TPU v7x, 256 devices: a whole 4x4x8 slice. The times are simulated.
256 devices in a mesh: enc: 8 (over z), mb: 2 (over core), tp: 16 (over y, x).
Axes of the slice: x: 4, y: 4, z: 8, core: 2. Of those that a mesh axis runs over, the one named last changes fastest.
Arguments:
- patches: bfloat16 [8, 2, 1024, 1280], P('enc', 'mb', 'tp'), may hold values from -6 to 6
- patch_counts: int32 [8, 2, 32], P('enc', 'mb'), may hold values from 4 to 32, as said below
- dest_pos: int32 [8, 2, 256], P('enc', 'mb'), may hold values from 0 to 2047, as said below
- merge_gain: float32 [1280], replicated, may hold values from 0.25 to 1.75
- merge_bias: float32 [1280], replicated, may hold values from -3 to 3
- up_weight: bfloat16 [5120, 5120], P(('enc', 'mb'), 'tp'), may hold values from -0.078125 to 0.078125
- up_bias: float32 [5120], replicated, may hold values from -3 to 3
- down_weight: bfloat16 [5120, 8192], P('tp', ('enc', 'mb')), may hold values from -0.078125 to 0.078125
- down_bias: float32 [8192], replicated, may hold values from -3 to 3
- text_embed: bfloat16 [8, 2, 2048, 8192], P('enc', 'mb', 'tp'), may hold values from -6 to 6
- norm_gain: float32 [8192], replicated, may hold values from 0.25 to 1.75
- kv_weight: bfloat16 [8192, 2048], P('tp'), may hold values from -0.0625 to 0.0625
- kv_bias: float32 [2048], replicated, may hold values from -3 to 3
Outputs:
- embedded: bfloat16 [8, 2, 2048, 8192], P('enc', 'mb', 'tp')
- keys_values: bfloat16 [8, 2, 2048, 2048], P('enc', 'mb', 'tp')
Inputs may be any that keep to these rules, and one draw needn't show every extreme that they name: `patch_counts`: each image's patch count is four times its merged rows; in every sequence some image has 32 patches. The image slots of enc index e and mb index m feed sequence (e, m); slot j of device t of tp is image t * 2 + j. `dest_pos`: the 8 slots of an image hold consecutive positions; slots past the image's merged rows are not live and their positions are used by no live slot; no two live slots of a sequence share a position.
All inputs are finite; a program needn't handle non-finite values.
Results may differ from a plain program's by a relative error of at most 0.02.
Values may be sent and summed in bfloat16 or wider, within the bound.
No kernel may reach another device: no remote copies, remote signals or barrier semaphores. Data moves between devices by JAX's collectives and lax.ppermute only.
A program may use at most 64 MiB of HBM per device.

v0:
```python
import jax
import jax.numpy as jnp
from jax import lax
from jax.sharding import PartitionSpec as P

SLOT = 8


def layer_norm(rows, gain, bias):
    values = rows.astype(jnp.float32)
    center = values - jnp.mean(values, axis=-1, keepdims=True)
    spread = jnp.mean(center * center, axis=-1, keepdims=True)
    return center * lax.rsqrt(spread + 1e-06) * gain + bias


def root_scale(values, gain):
    return (
        values * lax.rsqrt(jnp.mean(values * values, axis=-1, keepdims=True) + 1e-06) * gain
    ).astype(jnp.bfloat16)


def per_device(
    patches,
    patch_counts,
    dest_pos,
    merge_gain,
    merge_bias,
    up_weight,
    up_bias,
    down_weight,
    down_bias,
    text_embed,
    norm_gain,
    kv_weight,
    kv_bias,
):
    text = text_embed[0, 0]
    tokens = text.shape[0]
    normal = layer_norm(patches[0, 0], merge_gain, merge_bias).astype(jnp.bfloat16)
    merged = normal.reshape(normal.shape[0] // 4, normal.shape[1] * 4)
    group_rows = lax.all_gather(merged, "tp", axis=0, tiled=True)
    raised = jnp.dot(
        group_rows,
        lax.all_gather(up_weight, ("enc", "mb"), axis=0, tiled=True),
        preferred_element_type=jnp.float32,
    )
    unit_start = lax.axis_index("tp") * up_weight.shape[1]
    own_bias = lax.dynamic_slice_in_dim(up_bias, unit_start, up_weight.shape[1], 0)
    hidden = jax.nn.gelu(raised + own_bias, approximate=False).astype(jnp.bfloat16)
    down_full = lax.all_gather(down_weight, ("enc", "mb"), axis=1, tiled=True)
    rows = hidden
    own = lax.psum_scatter(
        jnp.dot(rows, down_full, preferred_element_type=jnp.float32).astype(jnp.bfloat16),
        "tp",
        scatter_dimension=0,
        tiled=True,
    ).astype(jnp.float32)
    visual = (own + down_bias).astype(jnp.bfloat16)
    visual_all = lax.all_gather(visual, "tp", axis=0, tiled=True)
    live_rows = patch_counts[0, 0] // 4
    live = (jnp.arange(SLOT, dtype=jnp.int32)[None, :] < live_rows[:, None]).reshape(-1)
    first = lax.axis_index("tp") * tokens
    places = first + jnp.arange(tokens, dtype=jnp.int32)
    select = (dest_pos[0, 0][None, :] == places[:, None]) & live[None, :]
    picked = jnp.dot(select.astype(jnp.bfloat16), visual_all, preferred_element_type=jnp.float32)
    present = jnp.any(select, axis=1)
    restored = picked.astype(jnp.bfloat16)
    embedded = jnp.where(present[:, None], restored, text)
    normed = root_scale(embedded.astype(jnp.float32), norm_gain)
    feature_rows = lax.all_to_all(normed, "tp", split_axis=1, concat_axis=0, tiled=True)
    rows = feature_rows
    kv_total = lax.psum_scatter(
        jnp.dot(rows, kv_weight, preferred_element_type=jnp.float32).astype(jnp.bfloat16),
        "tp",
        scatter_dimension=0,
        tiled=True,
    ).astype(jnp.float32)
    keys_values = (kv_total + kv_bias).astype(jnp.bfloat16)
    return (embedded[None, None], keys_values[None, None])


def solution(mesh):
    return jax.shard_map(
        per_device,
        mesh=mesh,
        in_specs=(
            P("enc", "mb", "tp", None),
            P("enc", "mb", None),
            P("enc", "mb", None),
            P(),
            P(),
            P(("enc", "mb"), "tp"),
            P(),
            P("tp", ("enc", "mb")),
            P(),
            P("enc", "mb", "tp", None),
            P(),
            P("tp", None),
            P(),
        ),
        out_specs=(P("enc", "mb", "tp", None), P("enc", "mb", "tp", None)),
        check_vma=False,
    )
```

profile of v0, /device:TPU:32, one launch (start us, length us, event | category | flops | bytes accessed | tf_op | source)
XLA Modules:
  0.0 449.3 jit_solution(9399251628535995408)
XLA Ops:
  7.2 1.2 convert_reduce_fusion
  8.4 1.1 fusion.9
  9.6 0.1 div.31
  9.6 1.0 reshape.103
  10.7 0.1 rsqrt.20
  10.8 0.1 mul.69
  10.9 0.1 copy.19
  11.0 0.1 sub.22
  11.2 0.7 add.86
  11.9 0.7 mul.72
  12.6 0.7 add_convert_fusion.2
  13.4 0.7 all-gather.7.cloned.1.call-update
  14.2 0.7 all-gather.9.cloned.1.call-update
  14.9 0.8 dynamic_slice.3
  15.7 51.8 %all-gather.5.cloned.1.call-done = bf16[256,5120]{1,0:T(8,128)(2,1)} async-done(((bf16[16,5120]{1,0:T(8,128)(2,1)}), bf16[256,5120]{1,0:T(8,128)(2,1)}) %all-gather.5.cloned.1.call-update) | async-done | bytes 2621456 | tf_op jit(solution)/shard_map/all_gather | solution.py:41
  67.4 42.7 %all-gather.7.cloned.1.call-done = bf16[5120,320]{1,0:T(8,128)(2,1)} async-done(((bf16[320,320]{1,0:T(8,128)(2,1)}), bf16[5120,320]{1,0:T(8,128)(2,1)}) %all-gather.7.cloned.1.call-update) | async-done | bytes 3276816 | tf_op jit(solution)/shard_map/all_gather | solution.py:44
  110.1 44.1 %all-gather.9.cloned.1.call-done = bf16[320,8192]{1,0:T(8,128)(2,1)} async-done(((bf16[320,512]{1,0:T(8,128)(2,1)}), bf16[320,8192]{1,0:T(8,128)(2,1)}) %all-gather.9.cloned.1.call-update) | async-done | bytes 5242896 | tf_op jit(solution)/shard_map/all_gather | solution.py:50
  154.2 12.1 %convolution_convert_fusion = bf16[256,8192]{1,0:T(8,128)(2,1)} fusion(bf16[320,8192]{1,0:T(8,128)(2,1)} %all-gather.9.cloned.1.call-done, bf16[256,5120]{1,0:T(8,128)(2,1)} %all-gather.5.cloned.1.call-done, bf16[5120,320]{1,0:T(8,128)(2,1)} %all-gather.7.cloned.1.call-done, f32[320]{0:T(512)S(1)} %dynamic_slice.3), kind=kOutput, calls=%fused_computation | convolution fusion | flops 2188541952 | bytes 15336704 | tf_op jit(solution)/shard_map/dot_general | solution.py:53
  166.4 81.5 %reduce-scatter.3.cloned.1.call-done = bf16[16,8192]{1,0:T(8,128)(2,1)} async-done(((bf16[256,8192]{1,0:T(8,128)(2,1)}), bf16[16,8192]{1,0:T(8,128)(2,1)}) %reduce-scatter.3.cloned.1.call-update) | async-done | bytes 262160 | tf_op jit(solution)/shard_map/reduce_scatter | solution.py:52
  247.9 1.7 add_convert_fusion.1
  249.7 0.1 iota_compare_fusion
  249.8 0.1 lt.26
  249.9 0.2 fusion.38
  250.1 56.9 %all-gather.11.cloned.1.call-done = bf16[256,8192]{1,0:T(8,128)(2,1)} async-done(((bf16[16,8192]{1,0:T(8,128)(2,1)}), bf16[256,8192]{1,0:T(8,128)(2,1)}) %all-gather.11.cloned.1.call-update) | async-done | bytes 4194320 | tf_op jit(solution)/shard_map/all_gather | solution.py:59
  307.0 4.0 fusion.1
  311.1 0.6 fusion.3
  311.7 0.7 copy-done.1
  312.4 0.2 copy.21
  312.6 33.4 %all_to_all.19 = bf16[128,16,512]{2,0,1:T(8,128)(2,1)S(1)} all-to-all(bf16[128,16,512]{2,0,1:T(8,128)(2,1)S(1)} %bitcast.40), channel_id=1, replica_groups=mesh['enc'=8,'mb'=2,'tp'=16] {'tp'}, dimensions={1} | all-to-all | bytes 4194304 | tf_op jit(solution)/shard_map/all_to_all | solution.py:70
  346.0 6.7 %convolution_convert_fusion.2 = bf16[2048,2048]{1,0:T(8,128)(2,1)} fusion(bf16[2048,512]{1,0:T(8,128)(2,1)S(1)} %bitcast.42, bf16[512,2048]{1,0:T(8,128)(2,1)S(1)} %copy-done), kind=kOutput, calls=%fused_computation.3 | convolution fusion | flops 4299161600 | bytes 12582912 | tf_op jit(solution)/shard_map/dot_general | solution.py:73
  352.8 87.8 %reduce-scatter.5.cloned.1.call-done = bf16[128,2048]{1,0:T(8,128)(2,1)} async-done(((bf16[2048,2048]{1,0:T(8,128)(2,1)}), bf16[128,2048]{1,0:T(8,128)(2,1)}) %reduce-scatter.5.cloned.1.call-update) | async-done | bytes 524304 | tf_op jit(solution)/shard_map/reduce_scatter | solution.py:72
  440.5 1.9 fusion.4
  (31 shorter events, 0.5 us)
Async XLA Ops:
  7.2 338.9 %copy-start = (bf16[512,2048]{1,0:T(8,128)(2,1)S(1)}, bf16[512,2048]{1,0:T(8,128)(2,1)}, u32[]{:S(2)}) copy-start(bf16[512,2048]{1,0:T(8,128)(2,1)} %param.24) | copy-start | bytes 6291460
  7.2 60.3 %all-gather.5.cloned.1.call-start = ((), (), s32[]{:S(2)}) async-start(), calls=%async_computation.3 | async-start | bytes 2785280 | tf_op jit(solution)/shard_map/all_gather | solution.py:41
  13.4 96.8 %all-gather.7.cloned.1.call-start = ((), (), s32[]{:S(2)}) async-start(), calls=%async_computation.4 | async-start | bytes 4177920 | tf_op jit(solution)/shard_map/all_gather | solution.py:44
  14.1 140.1 %all-gather.9.cloned.1.call-start = ((), (), s32[]{:S(2)}) async-start(), calls=%async_computation.5 | async-start | bytes 5570560 | tf_op jit(solution)/shard_map/all_gather | solution.py:50
  14.8 233.0 %reduce-scatter.3.cloned.1.call-start = ((), (), s32[]{:S(2)}) async-start(), calls=%async_computation.6 | async-start | bytes 4456448 | tf_op jit(solution)/shard_map/reduce_scatter | solution.py:52
  166.3 81.6 %copy-start.3 = (f32[8192]{0:T(1024)S(1)}, f32[8192]{0:T(1024)}, u32[]{:S(2)}) copy-start(f32[8192]{0:T(1024)} %param.21) | copy-start | bytes 98308
  166.3 83.3 %copy-start.6 = (s32[1,1,32]{2,1,0:T(1,128)S(1)}, s32[1,1,32]{2,1,0:T(1,128)}, u32[]{:S(2)}) copy-start(s32[1,1,32]{2,1,0:T(1,128)} %param.14) | copy-start | bytes 388
  166.3 83.6 %copy-start.5 = (s32[1,1,256]{2,1,0:T(1,128)S(1)}, s32[1,1,256]{2,1,0:T(1,128)}, u32[]{:S(2)}) copy-start(s32[1,1,256]{2,1,0:T(1,128)} %param.15) | copy-start | bytes 3076
  166.3 140.7 %all-gather.11.cloned.1.call-start = ((), (), s32[]{:S(2)}) async-start(), calls=%async_computation.7 | async-start | bytes 4456448 | tf_op jit(solution)/shard_map/all_gather | solution.py:59
  249.6 190.9 %reduce-scatter.5.cloned.1.call-start = ((), (), s32[]{:S(2)}) async-start(), calls=%async_computation.8 | async-start | bytes 8912896 | tf_op jit(solution)/shard_map/reduce_scatter | solution.py:72
  250.1 61.0 %copy-start.2 = (f32[8192]{0:T(1024)S(1)}, f32[8192]{0:T(1024)}, u32[]{:S(2)}) copy-start(f32[8192]{0:T(1024)} %param.23) | copy-start | bytes 98308
  311.0 1.3 copy-start.1
  352.7 87.8 %copy-start.4 = (f32[2048]{0:T(1024)S(1)}, f32[2048]{0:T(1024)}, u32[]{:S(2)}) copy-start(f32[2048]{0:T(1024)} %param.25) | copy-start | bytes 24580
Sparse Core Ops, SparseCore 0:
  13.5 53.9 all-gather.4
  69.3 40.8 all-gather.6
  112.0 42.1 all-gather.8
  166.5 81.3 reduce-scatter.2
  251.0 55.9 all-gather.10
  352.9 87.6 reduce-scatter.4
where the time goes:
time: 450 us; the launch traced here: 449 us
  waiting for transfers between devices  366 us (81%)
  blocking collectives  33.4 us (7%)
  matrix products  22.9 us (5%)
  between operations  14.3 us (3%)
  other arithmetic  7.55 us (2%)
  local copies, waits for them, and re-layouts  4.8 us (1%)
    reduce_scatter x1, waiting for transfers between devices, per_device(): lax.psum_scatter(jnp.dot(rows, kv_weight, preferred_element_type=jnp.floa...  87.8 us
    reduce_scatter x1, waiting for transfers between devices, per_device(): lax.psum_scatter(jnp.dot(rows, down_full, preferred_element_type=jnp.floa...  81.5 us
    all_gather x1, waiting for transfers between devices, per_device(): visual_all = lax.all_gather(visual, 'tp', axis=0, tiled=True)  56.9 us
    all_gather x1, waiting for transfers between devices, per_device(): group_rows = lax.all_gather(merged, 'tp', axis=0, tiled=True)  51.8 us
    all_gather x1, waiting for transfers between devices, per_device(): down_full = lax.all_gather(down_weight, ('enc', 'mb'), axis=1, tiled=True)  44.1 us
    all_gather x1, waiting for transfers between devices, per_device(): lax.all_gather(up_weight, ('enc', 'mb'), axis=0, tiled=True)  42.7 us
    all_to_all x1, blocking collectives, per_device(): lax.all_to_all(normed, 'tp', split_axis=1, concat_axis=0, tiled=True)  33.4 us
    dot_general x1, matrix products, per_device(): jnp.dot(rows, down_full, preferred_element_type=jnp.float32)  12.1 us
  transfers between devices with their start and end apart: 6, of which 6 were waited for; matrix products, arithmetic and copies ran while one was open for 0% of the time, Pallas kernels for 0%

commit v1 on v0

v1 whole, which is shorter than its diff:
```python
import jax
import jax.numpy as jnp
import numpy as np
from jax import lax
from jax.experimental import pallas as pl
from jax.experimental.pallas import tpu as pltpu
from jax.sharding import PartitionSpec as P

SLOT = 8
RING = (0, -1, 1, 2)
MIB = 1 << 20
BF16, F32 = jnp.bfloat16, jnp.float32


def place(core, tp, which, step):
    y, x = tp // 4, tp % 4
    if (core == 0) == (which == 1):
        return y * 4 + (x + step) % 4
    return (y + step) % 4 * 4 + x


TABLE = np.array(
    [
        [place(core, place(core, tp, 2, o2), 1, o1) for o2 in RING for o1 in RING]
        for core in range(2)
        for tp in range(16)
    ],
    np.int32,
)
HOPS = {
    (which, step): [(c * 16 + t, c * 16 + place(c, t, which, step)) for c in range(2) for t in range(16)]
    for which in (1, 2)
    for step in (1, -1)
}
SWAP = [(a * 16 + b, b * 16 + a) for a in range(16) for b in range(16)]


def hop(value, which, step):
    return lax.ppermute(value, ("mb", "tp"), HOPS[which, step])


def ring(value, which, axis=0):
    half = value.shape[axis] // 2
    right = hop(value, which, 1)
    left = hop(value, which, -1)
    far_a = hop(lax.slice_in_dim(right, 0, half, axis=axis), which, 1)
    far_b = hop(lax.slice_in_dim(left, half, 2 * half, axis=axis), which, -1)
    return right, left, far_a, far_b


def cost(flops, moved):
    return pl.CostEstimate(flops=flops, bytes_accessed=moved, transcendentals=0)


def params(mib):
    return pltpu.CompilerParams(vmem_limit_bytes=mib * MIB)


VMEM = pl.BlockSpec(memory_space=pltpu.VMEM)
SMEM = pl.BlockSpec(memory_space=pltpu.SMEM)
ANY = pl.BlockSpec(memory_space=pl.ANY)


def merge_kernel(p_ref, gain_ref, bias_ref, out_ref, rows):
    values = p_ref[...].astype(F32)
    center = values - jnp.mean(values, axis=-1, keepdims=True)
    spread = jnp.mean(center * center, axis=-1, keepdims=True)
    normal = center * lax.rsqrt(spread + 1e-06) * gain_ref[...] + bias_ref[...]
    for k in range(10):
        rows[k] = normal[:, k * 128 : (k + 1) * 128]
    for j in range(4):
        for k in range(10):
            start = j * 1280 + k * 128
            out_ref[:, start : start + 128] = rows[k, pl.ds(j, 16, stride=4), :].astype(BF16)


def merge(patches, gain, bias):
    return pl.pallas_call(
        merge_kernel,
        out_shape=jax.ShapeDtypeStruct((16, 5120), BF16),
        in_specs=[VMEM] * 3,
        out_specs=VMEM,
        scratch_shapes=[pltpu.VMEM((10, 64, 128), F32)],
        cost_estimate=cost(10**6, 330000),
    )(patches, gain, bias)


def pack_kernel(tab, text, to_right, to_left, own, sems):
    copies = []
    for j in range(4):
        at = pl.ds(j * 512, 512)

        def columns(i2):
            return pl.ds(pl.multiple_of(tab[i2 * 4 + j] * 512, 512), 512)

        copies += [
            (text.at[:, columns(2)], to_right.at[pl.ds(0, 128), at]),
            (text.at[pl.ds(0, 64), columns(3)], to_right.at[pl.ds(128, 64), at]),
            (text.at[pl.ds(64, 64), columns(3)], to_left.at[pl.ds(0, 64), at]),
            (text.at[:, columns(1)], to_left.at[pl.ds(64, 128), at]),
            (text.at[:, columns(0)], own.at[:, at]),
        ]
    copies = [pltpu.make_async_copy(a, b, sems.at[i]) for i, (a, b) in enumerate(copies)]
    for copy in copies:
        copy.start()
    for copy in copies:
        copy.wait()


def pack(tab, text):
    return pl.pallas_call(
        pack_kernel,
        out_shape=[jax.ShapeDtypeStruct((n, 2048), BF16) for n in (192, 192, 128)],
        in_specs=[SMEM, ANY],
        out_specs=[ANY] * 3,
        scratch_shapes=[pltpu.SemaphoreType.DMA((20,))],
        cost_estimate=cost(0, 4 * MIB),
    )(tab, text)


def up_kernel(tab, s0, s1, s2, s3a, s3b, weight, bias_ref, out_ref, rows, held, sems):
    copies = []
    for i2, piece in enumerate((s0, s1, s2, None)):
        for i1 in range(4):
            if piece is None:
                source = (s3a, s3b)[i1 // 2].at[pl.ds(i1 % 2 * 16, 16)]
            else:
                source = piece.at[pl.ds(i1 * 16, 16)]
            target = rows.at[pl.ds(pl.multiple_of(tab[i2 * 4 + i1] * 16, 16), 16)]
            copies.append((source, target))
    copies.append((weight, held))
    copies = [pltpu.make_async_copy(a, b, sems.at[i]) for i, (a, b) in enumerate(copies)]
    for copy in copies:
        copy.start()
    for copy in copies:
        copy.wait()
    raised = jnp.dot(rows[...], held[...], preferred_element_type=F32) + bias_ref[tab[0]]
    out_ref[...] = (0.5 * raised * (1.0 + lax.erf(raised * np.float32(0.5**0.5)))).astype(BF16)


def up(tab, pieces, weight, bias):
    return pl.pallas_call(
        up_kernel,
        out_shape=jax.ShapeDtypeStruct((256, 320), BF16),
        in_specs=[SMEM] + [ANY] * 6 + [VMEM],
        out_specs=VMEM,
        scratch_shapes=[
            pltpu.VMEM((256, 5120), BF16),
            pltpu.VMEM((5120, 320), BF16),
            pltpu.SemaphoreType.DMA((17,)),
        ],
        compiler_params=params(32),
        cost_estimate=cost(840 * 10**6, 6 * MIB),
    )(tab, *pieces, weight, bias)


def down_kernel(tab, h0, h1, h2, h3a, h3b, weight, bias_ref, out_ref, held, sems):
    copies = []
    for k in range(16):
        source = weight.at[pl.ds(pl.multiple_of(tab[k] * 320, 320), 320)]
        copies.append(pltpu.make_async_copy(source, held.at[pl.ds(k * 320, 320)], sems.at[k]))
    for copy in copies:
        copy.start()
    for copy in copies:
        copy.wait()
    total = bias_ref[tab[0]]
    for i2, piece in enumerate((h0[...], h1[...], h2[...], jnp.concatenate([h3a[...], h3b[...]], axis=0))):
        total = total + jnp.dot(piece, held[i2 * 1280 : (i2 + 1) * 1280, :], preferred_element_type=F32)
    out_ref[...] = total.astype(BF16)


def down(tab, pieces, weight, bias):
    return pl.pallas_call(
        down_kernel,
        out_shape=jax.ShapeDtypeStruct((256, 512), BF16),
        in_specs=[SMEM] + [VMEM] * 5 + [ANY] + [VMEM],
        out_specs=VMEM,
        scratch_shapes=[pltpu.VMEM((5120, 512), BF16), pltpu.SemaphoreType.DMA((16,))],
        compiler_params=params(32),
        cost_estimate=cost(1340 * 10**6, 8 * MIB),
    )(tab, *pieces, weight, bias)


def pick_kernel(tab, dest, v0, v1, v2, v3a, v3b, own, right, left, far_a, far_b, to_right, to_left, kept):
    visual = (v0[...], v1[...], v2[...], jnp.concatenate([v3a[...], v3b[...]], axis=0))
    targets = dest[...]

    def rows(i2, first, count):
        start = tab[i2 * 4] * 128 + first
        match = (lax.broadcasted_iota(jnp.int32, (count, 256), 0) + start) == targets
        select = match.astype(F32)
        return select.astype(BF16), jnp.sum(select, axis=1, keepdims=True) > 0.0

    def fill(i2, first, count, text, text_row, out, out_row):
        select, present = rows(i2, first, count)
        for j in range(4):
            at = slice(j * 512, (j + 1) * 512)
            picked = jnp.dot(select, visual[j], preferred_element_type=F32).astype(BF16)
            out[out_row : out_row + count, at] = jnp.where(present, picked, text[text_row : text_row + count, at])

    fill(2, 0, 128, left, 64, to_right, 0)
    fill(3, 0, 64, far_a, 0, to_right, 128)
    fill(3, 64, 64, far_b, 0, to_left, 0)
    fill(1, 0, 128, right, 0, to_left, 64)
    fill(0, 0, 128, own, 0, kept, 0)


def pick(tab, dest, visual, text):
    return pl.pallas_call(
        pick_kernel,
        out_shape=[jax.ShapeDtypeStruct((n, 2048), BF16) for n in (192, 192, 128)],
        in_specs=[SMEM] + [VMEM] * 11,
        out_specs=[VMEM] * 3,
        compiler_params=params(32),
        cost_estimate=cost(540 * 10**6, 6 * MIB),
    )(tab, dest, *visual, *text)


def product_kernel(tab, to_right, to_left, kept, gain, w0, w1, w2, w3a, w3b, far_a, far_b, right, left, own, scaled):
    @pl.when(pl.program_id(0) == 0)
    def _():
        for j in range(4):
            at = slice(j * 512, (j + 1) * 512)
            scale = gain[tab[j]]

            def times(ref, first, count):
                return (ref[first : first + count, at].astype(F32) * scale).astype(BF16)

            scaled[0:64, at] = times(to_right, 128, 64)
            scaled[64:128, at] = times(to_left, 0, 64)
            scaled[128:256, at] = times(to_right, 0, 128)
            scaled[256:384, at] = times(to_left, 64, 128)
            scaled[384:512, at] = times(kept, 0, 128)

    total = jnp.dot(scaled[:, 0:512], w0[...], preferred_element_type=F32)
    total = total + jnp.dot(scaled[:, 512:1024], w1[...], preferred_element_type=F32)
    total = total + jnp.dot(scaled[:, 1024:1536], w2[...], preferred_element_type=F32)
    total = total + jnp.dot(scaled[:, 1536:1792], w3a[...], preferred_element_type=F32)
    total = total + jnp.dot(scaled[:, 1792:2048], w3b[...], preferred_element_type=F32)
    far_a[...] = total[0:64].astype(BF16)
    far_b[...] = total[64:128].astype(BF16)
    right[...] = total[128:256].astype(BF16)
    left[...] = total[256:384].astype(BF16)
    own[...] = total[384:512]


def product(tab, picked, gain, weights):
    def block(count):
        return pl.BlockSpec((count, 512), lambda n: (0, n))

    return pl.pallas_call(
        product_kernel,
        out_shape=[jax.ShapeDtypeStruct((n, 2048), BF16) for n in (64, 64, 128, 128)]
        + [jax.ShapeDtypeStruct((128, 2048), F32)],
        grid=(4,),
        in_specs=[SMEM] + [VMEM] * 4 + [block(n) for n in (512, 512, 512, 256, 256)],
        out_specs=[block(n) for n in (64, 64, 128, 128, 128)],
        scratch_shapes=[pltpu.VMEM((512, 2048), BF16)],
        compiler_params=params(40),
        cost_estimate=cost(4300 * 10**6, 14 * MIB),
    )(tab, *picked, gain, *weights)


def place_kernel(tab, own, right, left, far_a, far_b, out, scale, sems):
    copies = []
    for j in range(4):
        at = pl.ds(j * 512, 512)

        def columns(i2):
            return pl.ds(pl.multiple_of(tab[i2 * 4 + j] * 512, 512), 512)

        copies += [
            (own.at[:, at], out.at[:, columns(0)]),
            (right.at[pl.ds(0, 128), at], out.at[:, columns(1)]),
            (left.at[pl.ds(64, 128), at], out.at[:, columns(2)]),
            (far_a.at[:, at], out.at[pl.ds(0, 64), columns(3)]),
            (far_b.at[:, at], out.at[pl.ds(64, 64), columns(3)]),
        ]
    copies = [pltpu.make_async_copy(a, b, sems.at[i]) for i, (a, b) in enumerate(copies)]
    for copy in copies:
        copy.start()

    def squares(values):
        values = values.astype(F32)
        return jnp.sum(values * values, axis=1, keepdims=True)

    far = jnp.concatenate([squares(far_a[...]), squares(far_b[...])], axis=0)
    total = squares(own[...]) + squares(right[0:128]) + squares(left[64:192]) + far
    scale[...] = jnp.broadcast_to(lax.rsqrt(total * (1.0 / 8192.0) + 1e-06), (128, 128))
    for copy in copies:
        copy.wait()


def place_rows(tab, pieces):
    return pl.pallas_call(
        place_kernel,
        out_shape=[jax.ShapeDtypeStruct((128, 8192), BF16), jax.ShapeDtypeStruct((128, 128), F32)],
        in_specs=[SMEM] + [VMEM] * 5,
        out_specs=[ANY, VMEM],
        scratch_shapes=[pltpu.SemaphoreType.DMA((20,))],
        compiler_params=params(32),
        cost_estimate=cost(4 * 10**6, 5 * MIB),
    )(tab, *pieces)


def per_device(
    patches,
    patch_counts,
    dest_pos,
    merge_gain,
    merge_bias,
    up_weight,
    up_bias,
    down_weight,
    down_bias,
    text_embed,
    norm_gain,
    kv_weight,
    kv_bias,
):
    tab = jnp.asarray(TABLE)[lax.axis_index("mb") * 16 + lax.axis_index("tp")]
    up_full = lax.all_gather(up_weight, ("enc", "mb"), axis=0, tiled=True)
    down_part = lax.ppermute(down_weight, ("enc", "mb", "tp"), SWAP)
    down_full = lax.all_gather(down_part, ("enc", "mb"), axis=0, tiled=True)

    merged = merge(patches[0, 0], merge_gain[None], merge_bias[None])
    right, left, far_a, far_b = ring(merged, 1, axis=1)
    near = jnp.concatenate([merged, right, left, jnp.concatenate([far_a, far_b], axis=1)], axis=0)
    group = (near, *ring(near, 2))

    text_right, text_left, text_own = pack(tab, text_embed[0, 0])
    right = hop(text_right, 2, 1)
    left = hop(text_left, 2, -1)
    text = (text_own, right, left, hop(right[128:192], 2, 1), hop(left[0:64], 2, -1))
    weights = (kv_weight, *ring(kv_weight, 1))

    hidden = up(tab, group, up_full, up_bias.reshape(16, 1, 320))
    right, left, far_a, far_b = ring(hidden, 1)
    near = jnp.concatenate([hidden, right, left, jnp.concatenate([far_a, far_b], axis=0)], axis=1)
    units = (near, *ring(near, 2))
    visual = down(tab, units, down_full, down_bias.reshape(16, 1, 512))
    visual = (visual, *ring(visual, 1))

    live_rows = patch_counts[0, 0] // 4
    live = (jnp.arange(SLOT, dtype=jnp.int32)[None, :] < live_rows[:, None]).reshape(-1)
    dest = jnp.where(live, dest_pos[0, 0], -1)[None]
    to_right, to_left, kept = pick(tab, dest, visual, text)
    right = hop(to_right, 2, 1)
    left = hop(to_left, 2, -1)
    pieces = (kept, right, left, hop(right[128:192], 2, 1), hop(left[0:64], 2, -1))

    far_a, far_b, to_right, to_left, own = product(
        tab, (to_right, to_left, kept), norm_gain.reshape(16, 1, 512), weights
    )
    far_a = hop(far_a, 2, 1).astype(F32)
    far_b = hop(far_b, 2, -1).astype(F32)
    to_right, to_left = to_right.astype(F32), to_left.astype(F32)
    to_right = jnp.concatenate([to_right[:64] + far_a, to_right[64:]], axis=0).astype(BF16)
    to_left = jnp.concatenate([to_left[:64], to_left[64:] + far_b], axis=0).astype(BF16)
    right = hop(to_right, 2, 1).astype(F32)
    left = hop(to_left, 2, -1).astype(F32)
    embedded, scale = place_rows(tab, pieces)
    keys_values = ((own + right + left) * scale[:, :1] + kv_bias).astype(BF16)
    return (embedded[None, None], keys_values[None, None])


def solution(mesh):
    return jax.shard_map(
        per_device,
        mesh=mesh,
        in_specs=(
            P("enc", "mb", "tp", None),
            P("enc", "mb", None),
            P("enc", "mb", None),
            P(),
            P(),
            P(("enc", "mb"), "tp"),
            P(),
            P("tp", ("enc", "mb")),
            P(),
            P("enc", "mb", "tp", None),
            P(),
            P("tp", None),
            P(),
        ),
        out_specs=(P("enc", "mb", "tp", None), P("enc", "mb", "tp", None)),
        check_vma=False,
    )
```

time: 450 us -> 302 us (0.67)
  waiting for transfers between devices: 366 us -> 103 us
  Pallas kernels: 0 us -> 89.4 us
  starting transfers between devices: 0.24 us -> 68.9 us
  blocking collectives: 33.4 us -> 0 us
  matrix products: 22.9 us -> 0 us
  local copies, waits for them, and re-layouts: 4.8 us -> 19.4 us
  other arithmetic: 7.55 us -> 2.33 us
    all_gather x4 -> x2, waiting for transfers between devices: 195 us -> 0.01 us  [the longest x1 0.01 us: per_device(): up_full = lax.all_gather(up_weight, ('enc', 'mb'), axis=0, tiled=True)]
    reduce_scatter x2 -> x0, waiting for transfers between devices: 169 us -> none  [the longest x1 87.8 us: per_device(): lax.psum_scatter(jnp.dot(rows, kv_weight, preferred_element_type=jnp.floa...]
    ppermute x0 -> x37, waiting for transfers between devices: none -> 103 us  [the longest x36 74.6 us: hop(): return lax.ppermute(value, ('mb', 'tp'), HOPS[which, step])]
    pallas_call x0 -> x7, Pallas kernels: none -> 89.4 us  [the longest x1 65.5 us: pack(): pl.pallas_call(pack_kernel, out_shape=[jax.ShapeDtypeStruct((n, 2048), BF...]
    ppermute x0 -> x37, starting transfers between devices: none -> 68.9 us  [the longest x36 64.4 us: hop(): return lax.ppermute(value, ('mb', 'tp'), HOPS[which, step])]
    all_to_all x1 -> x0, blocking collectives: 33.4 us -> none  [per_device(): lax.all_to_all(normed, 'tp', split_axis=1, concat_axis=0, tiled=True)]
    dot_general x3 -> x0, matrix products: 22.9 us -> none  [the longest x1 12.1 us: per_device(): jnp.dot(rows, down_full, preferred_element_type=jnp.float32)]
    unnamed x16 -> x34, local copies, waits for them, and re-layouts: 0.87 us -> 9.66 us
  transfers between devices with their start and end apart: 6 -> 39, of which waited for: 6 -> 16; matrix products, arithmetic and copies ran while one was open for 0% -> 4% of each run, Pallas kernels for 0% -> 28%
where the time goes in v1:
time: 302 us; the launch traced here: 298 us
  waiting for transfers between devices  103 us (34%)
  Pallas kernels  89.4 us (30%)
  starting transfers between devices  68.9 us (23%)
  local copies, waits for them, and re-layouts  19.4 us (6%)
  between operations  14.5 us (5%)
    ppermute x36, waiting for transfers between devices, hop(): return lax.ppermute(value, ('mb', 'tp'), HOPS[which, step])  74.6 us
    pallas_call x1, Pallas kernels, pack(): pl.pallas_call(pack_kernel, out_shape=[jax.ShapeDtypeStruct((n, 2048), BF...  65.5 us
    ppermute x36, starting transfers between devices, hop(): return lax.ppermute(value, ('mb', 'tp'), HOPS[which, step])  64.4 us
    ppermute x1, waiting for transfers between devices, per_device(): down_part = lax.ppermute(down_weight, ('enc', 'mb', 'tp'), SWAP)  28 us
    unnamed x34, local copies, waits for them, and re-layouts  9.66 us
    pallas_call x1, Pallas kernels, product(): pl.pallas_call(product_kernel, out_shape=[jax.ShapeDtypeStruct((n, 2048),...  7.2 us
    pallas_call x1, Pallas kernels, up(): pl.pallas_call(up_kernel, out_shape=jax.ShapeDtypeStruct((256, 320), BF16...  6.11 us
  transfers between devices with their start and end apart: 39, of which 16 were waited for; matrix products, arithmetic and copies ran while one was open for 4% of the time, Pallas kernels for 28%

profile of v1, /device:TPU:32, one launch (start us, length us, event | category | flops | bytes accessed | tf_op | source)
XLA Modules:
  0.0 297.8 jit_solution(5741165580820742439)
XLA Ops:
  7.9 4.5 %collective-permute-start.16 = (bf16[320,512]{1,0:T(8,128)(2,1)}, bf16[320,512]{1,0:T(8,128)(2,1)S(1)}, u32[]{:S(2)}, u32[]{:S(2)}) collective-permute-start(bf16[320,512]{1,0:T(8,128)(2,1)} %param.21), channel_id=1, source_target_pairs={{0,0},{1,16},{2,32},{3,48},{4,64},{5,80},{6,96},{7,112},{8,128},{9... | collective-permute-start | bytes 983048 | tf_op jit(solution)/shard_map/ppermute | solution.py:323
  12.4 28.0 %collective-permute-done.16 = bf16[320,512]{1,0:T(8,128)(2,1)S(1)} collective-permute-done((bf16[320,512]{1,0:T(8,128)(2,1)}, bf16[320,512]{1,0:T(8,128)(2,1)S(1)}, u32[]{:S(2)}, u32[]{:S(2)}) %collective-permute-start.16) | collective-permute-done | bytes 327712 | tf_op jit(solution)/shard_map/ppermute | solution.py:323
  46.3 2.5 collective-permute-start.1
  48.9 3.5 %collective-permute-done = bf16[16,5120]{1,0:T(8,128)(2,1)S(1)} collective-permute-done((bf16[16,5120]{1,0:T(8,128)(2,1)}, bf16[16,5120]{1,0:T(8,128)(2,1)S(1)}, u32[]{:S(2)}, u32[]{:S(2)}) %collective-permute-start) | collective-permute-done | bytes 163872 | tf_op jit(solution)/shard_map/ppermute | solution.py:39
  52.4 3.3 %collective-permute-start.3 = (bf16[16,2560]{1,0:T(8,128)(2,1)S(1)}, bf16[16,2560]{1,0:T(8,128)(2,1)S(1)}, u32[]{:S(2)}, u32[]{:S(2)}) collective-permute-start(bf16[16,2560]{1,0:T(8,128)(2,1)S(1)} %slice.95), channel_id=1, source_target_pairs={{0,3},{1,0},{2,1},{3,2},{4,7},{5,4},{6,5},{7,6},{8,11},{9,8},{10,9... | collective-permute-start | bytes 245768 | tf_op jit(solution)/shard_map/ppermute | solution.py:39
  59.0 11.5 %collective-permute-start.4 = (bf16[64,5120]{1,0:T(8,128)(2,1)S(1)}, bf16[64,5120]{1,0:T(8,128)(2,1)S(1)}, u32[]{:S(2)}, u32[]{:S(2)}) collective-permute-start(bf16[64,5120]{1,0:T(8,128)(2,1)S(1)} %maximum_maximum_fusion.s0), channel_id=1, source_target_pairs={{0,4},{1,5},{2,6},{3,7},{4,8},{5,9},{6,10},{7,11},{8,12},{9,13},{1... | collective-permute-start | bytes 1966088 | tf_op jit(solution)/shard_map/ppermute | solution.py:39
  70.5 3.3 %collective-permute-start.30 = (bf16[512,2048]{1,0:T(8,128)(2,1)}, bf16[512,2048]{1,0:T(8,128)(2,1)}, u32[]{:S(2)}, u32[]{:S(2)}) collective-permute-start(bf16[512,2048]{1,0:T(8,128)(2,1)} %w0.1), channel_id=1, source_target_pairs={{0,3},{1,0},{2,1},{3,2},{4,7},{5,4},{6,5},{7,6},{8,11},{9,8},{10,9... | collective-permute-start | bytes 6291464 | tf_op jit(solution)/shard_map/ppermute | solution.py:39
  73.8 11.8 %collective-permute-done.4.s1 = bf16[64,5120]{1,0:T(8,128)(2,1)S(1)} collective-permute-done((bf16[64,5120]{1,0:T(8,128)(2,1)S(1)}, bf16[64,5120]{1,0:T(8,128)(2,1)S(1)}, u32[]{:S(2)}, u32[]{:S(2)}) %collective-permute-start.4) | collective-permute-done | bytes 655392 | tf_op jit(solution)/shard_map/ppermute | solution.py:39
  85.7 2.6 collective-permute-start.6
  89.9 7.7 %collective-permute-done.6.s3a = bf16[32,5120]{1,0:T(8,128)(2,1)S(1)} collective-permute-done((bf16[32,5120]{1,0:T(8,128)(2,1)S(1)}, bf16[32,5120]{1,0:T(8,128)(2,1)S(1)}, u32[]{:S(2)}, u32[]{:S(2)}) %collective-permute-start.6) | collective-permute-done | bytes 327712 | tf_op jit(solution)/shard_map/ppermute | solution.py:39
  101.2 6.1 %shard_map.150 = bf16[256,320]{1,0:T(8,128)(2,1)S(1)} custom-call(s32[16]{0:T(128)S(1)} %dynamic-slice_bitcast_fusion.tab, bf16[64,5120]{1,0:T(8,128)(2,1)S(1)} %maximum_maximum_fusion.s0, bf16[64,5120]{1,0:T(8,128)(2,1)S(1)} %collective-permute-done.4.s1, bf16[64,5120]{1,0:T(8,128)(2,1)S(1)} %collective-permute-done.5.s2, ...), custom_call_target="tpu_custom_call" | custom-call | flops 840000000 | bytes 6291456 | tf_op jit(solution)/shard_map/pallas_call | solution.py:142
  107.4 3.4 %collective-permute-start.9 = (bf16[256,320]{1,0:T(8,128)(2,1)S(1)}, bf16[256,320]{1,0:T(8,128)(2,1)S(1)}, u32[]{:S(2)}, u32[]{:S(2)}) collective-permute-start(bf16[256,320]{1,0:T(8,128)(2,1)S(1)} %shard_map.150), channel_id=1, source_target_pairs={{0,3},{1,0},{2,1},{3,2},{4,7},{5,4},{6,5},{7,6},{8,11},{9,8},{10,9... | collective-permute-start | bytes 491528 | tf_op jit(solution)/shard_map/ppermute | solution.py:39
  110.8 3.6 %collective-permute-done.8 = bf16[256,320]{1,0:T(8,128)(2,1)S(1)} collective-permute-done((bf16[256,320]{1,0:T(8,128)(2,1)S(1)}, bf16[256,320]{1,0:T(8,128)(2,1)S(1)}, u32[]{:S(2)}, u32[]{:S(2)}) %collective-permute-start.8) | collective-permute-done | bytes 163872 | tf_op jit(solution)/shard_map/ppermute | solution.py:39
  114.7 3.3 %collective-permute-start.11 = (bf16[128,320]{1,0:T(8,128)(2,1)S(1)}, bf16[128,320]{1,0:T(8,128)(2,1)S(1)}, u32[]{:S(2)}, u32[]{:S(2)}) collective-permute-start(bf16[128,320]{1,0:T(8,128)(2,1)S(1)} %slice.99), channel_id=1, source_target_pairs={{0,3},{1,0},{2,1},{3,2},{4,7},{5,4},{6,5},{7,6},{8,11},{9,8},{10,9... | collective-permute-start | bytes 245768 | tf_op jit(solution)/shard_map/ppermute | solution.py:39
  118.0 3.5 %collective-permute-done.10 = bf16[128,320]{1,0:T(8,128)(2,1)S(1)} collective-permute-done((bf16[128,320]{1,0:T(8,128)(2,1)S(1)}, bf16[128,320]{1,0:T(8,128)(2,1)S(1)}, u32[]{:S(2)}, u32[]{:S(2)}) %collective-permute-start.10) | collective-permute-done | bytes 81952 | tf_op jit(solution)/shard_map/ppermute | solution.py:39
  122.1 3.2 %collective-permute-start.13 = (bf16[256,1280]{1,0:T(8,128)(2,1)S(1)}, bf16[256,1280]{1,0:T(8,128)(2,1)S(1)}, u32[]{:S(2)}, u32[]{:S(2)}) collective-permute-start(bf16[256,1280]{1,0:T(8,128)(2,1)S(1)} %concatenate.23.h0), channel_id=1, source_target_pairs={{0,12},{1,13},{2,14},{3,15},{4,0},{5,1},{6,2},{7,3},{8,4},{9,5},{1... | collective-permute-start | bytes 1966088 | tf_op jit(solution)/shard_map/ppermute | solution.py:39
  125.3 65.5 %shard_map.152 = (bf16[192,2048]{1,0:T(8,128)(2,1)}, bf16[192,2048]{1,0:T(8,128)(2,1)}, bf16[128,2048]{1,0:T(8,128)(2,1)}) custom-call(s32[16]{0:T(128)} %copy-done.8, bf16[128,8192]{1,0:T(8,128)(2,1)} %bitcast.21), custom_call_target="tpu_custom_call" | custom-call | bytes 4194304 | tf_op jit(solution)/shard_map/pallas_call | solution.py:111
  190.9 3.2 %collective-permute-start.22 = (bf16[192,2048]{1,0:T(8,128)(2,1)}, bf16[192,2048]{1,0:T(8,128)(2,1)S(1)}, u32[]{:S(2)}, u32[]{:S(2)}) collective-permute-start(bf16[192,2048]{1,0:T(8,128)(2,1)} %get-tuple-element.17), channel_id=1, source_target_pairs={{0,12},{1,13},{2,14},{3,15},{4,0},{5,1},{6,2},{7,3},{8,4},{9,5},{1... | collective-permute-start | bytes 2359304 | tf_op jit(solution)/shard_map/ppermute | solution.py:39
  194.3 3.3 %collective-permute-start.15 = (bf16[128,1280]{1,0:T(8,128)(2,1)S(1)}, bf16[128,1280]{1,0:T(8,128)(2,1)S(1)}, u32[]{:S(2)}, u32[]{:S(2)}) collective-permute-start(bf16[128,1280]{1,0:T(8,128)(2,1)S(1)} %slice.101), channel_id=1, source_target_pairs={{0,12},{1,13},{2,14},{3,15},{4,0},{5,1},{6,2},{7,3},{8,4},{9,5},{1... | collective-permute-start | bytes 983048 | tf_op jit(solution)/shard_map/ppermute | solution.py:39
  200.2 2.4 slice.109
  202.6 16.5 %collective-permute-done.14.h3a = bf16[128,1280]{1,0:T(8,128)(2,1)S(1)} collective-permute-done((bf16[128,1280]{1,0:T(8,128)(2,1)S(1)}, bf16[128,1280]{1,0:T(8,128)(2,1)S(1)}, u32[]{:S(2)}, u32[]{:S(2)}) %collective-permute-start.14) | collective-permute-done | bytes 327712 | tf_op jit(solution)/shard_map/ppermute | solution.py:39
  220.8 2.5 copy-done
  225.9 4.6 %shard_map.151.v0 = bf16[256,512]{1,0:T(8,128)(2,1)} custom-call(s32[16]{0:T(128)S(1)} %copy-done.9, bf16[256,1280]{1,0:T(8,128)(2,1)S(1)} %concatenate.23.h0, bf16[256,1280]{1,0:T(8,128)(2,1)S(1)} %collective-permute-done.12.h1, bf16[256,1280]{1,0:T(8,128)(2,1)S(1)} %collective-permute-done.13.h2, bf16[128,1280]{1,0:T(8,128)(2,1)S(1)} %copy-done.4, ...), custom_call_target="tpu_custom_call" | custom-call | flops 1340000000 | bytes 8388608 | tf_op jit(solution)/shard_map/pallas_call | solution.py:173
  234.9 3.6 %collective-permute-done.17.v1 = bf16[256,512]{1,0:T(8,128)(2,1)S(1)} collective-permute-done((bf16[256,512]{1,0:T(8,128)(2,1)}, bf16[256,512]{1,0:T(8,128)(2,1)S(1)}, u32[]{:S(2)}, u32[]{:S(2)}) %collective-permute-start.17) | collective-permute-done | bytes 262176 | tf_op jit(solution)/shard_map/ppermute | solution.py:39
  238.5 2.6 collective-permute-start.24
  241.6 3.3 %collective-permute-start.20 = (bf16[128,512]{1,0:T(8,128)(2,1)S(1)}, bf16[128,512]{1,0:T(8,128)(2,1)S(1)}, u32[]{:S(2)}, u32[]{:S(2)}) collective-permute-start(bf16[128,512]{1,0:T(8,128)(2,1)S(1)} %slice.103), channel_id=1, source_target_pairs={{0,3},{1,0},{2,1},{3,2},{4,7},{5,4},{6,5},{7,6},{8,11},{9,8},{10,9... | collective-permute-start | bytes 393224 | tf_op jit(solution)/shard_map/ppermute | solution.py:39
  245.3 3.9 %collective-permute-done.19.v3a = bf16[128,512]{1,0:T(8,128)(2,1)S(1)} collective-permute-done((bf16[128,512]{1,0:T(8,128)(2,1)S(1)}, bf16[128,512]{1,0:T(8,128)(2,1)S(1)}, u32[]{:S(2)}, u32[]{:S(2)}) %collective-permute-start.19) | collective-permute-done | bytes 131104 | tf_op jit(solution)/shard_map/ppermute | solution.py:39
  251.4 7.2 %shard_map.155 = (bf16[64,2048]{1,0:T(8,128)(2,1)S(1)}, bf16[64,2048]{1,0:T(8,128)(2,1)S(1)}, bf16[128,2048]{1,0:T(8,128)(2,1)S(1)}, bf16[128,2048]{1,0:T(8,128)(2,1)S(1)}, f32[128,2048]{1,0:T(8,128)S(1)}) custom-call(s32[16]{0:T(128)S(1)} %copy-done.9, bf16[192,2048]{1,0:T(8,128)(2,1)S(1)} %get-tuple-element.19.to_right, ...), custom_call_target="tpu_custom_call" | custom-call | flops 4300000256 | bytes 14680064 | tf_op jit(solution)/shard_map/pallas_call | solution.py:251
  266.5 8.0 %collective-permute-done.35 = bf16[64,2048]{1,0:T(8,128)(2,1)S(1)} collective-permute-done((bf16[64,2048]{1,0:T(8,128)(2,1)S(1)}, bf16[64,2048]{1,0:T(8,128)(2,1)S(1)}, u32[]{:S(2)}, u32[]{:S(2)}) %collective-permute-start.35) | collective-permute-done | bytes 262176 | tf_op jit(solution)/shard_map/ppermute | solution.py:39
  274.7 3.6 %collective-permute-start.36 = (bf16[128,2048]{1,0:T(8,128)(2,1)S(1)}, bf16[128,2048]{1,0:T(8,128)(2,1)S(1)}, u32[]{:S(2)}, u32[]{:S(2)}) collective-permute-start(bf16[128,2048]{1,0:T(8,128)(2,1)S(1)} %pad_maximum_fusion.1), channel_id=1, source_target_pairs={{0,12},{1,13},{2,14},{3,15},{4,0},{5,1},{6,2},{7,3},{8,4},{9,5},{1... | collective-permute-start | bytes 1572872 | tf_op jit(solution)/shard_map/ppermute | solution.py:39
  278.4 3.3 %collective-permute-start.28 = (bf16[64,2048]{1,0:T(8,128)(2,1)S(1)}, bf16[64,2048]{1,0:T(8,128)(2,1)S(1)}, u32[]{:S(2)}, u32[]{:S(2)}) collective-permute-start(bf16[64,2048]{1,0:T(8,128)(2,1)S(1)} %slice.107), channel_id=1, source_target_pairs={{0,12},{1,13},{2,14},{3,15},{4,0},{5,1},{6,2},{7,3},{8,4},{9,5},{1... | collective-permute-start | bytes 786440 | tf_op jit(solution)/shard_map/ppermute | solution.py:39
  281.7 4.2 %collective-permute-done.27.far_a = bf16[64,2048]{1,0:T(8,128)(2,1)S(1)} collective-permute-done((bf16[64,2048]{1,0:T(8,128)(2,1)S(1)}, bf16[64,2048]{1,0:T(8,128)(2,1)S(1)}, u32[]{:S(2)}, u32[]{:S(2)}) %collective-permute-start.27) | collective-permute-done | bytes 262176 | tf_op jit(solution)/shard_map/ppermute | solution.py:39
  (124 shorter events, 43.7 us)
Async XLA Ops:
  7.2 91.8 %all-gather.3.cloned.1.call-start = ((), (), s32[]{:S(2)}) async-start(), calls=%async_computation | async-start | bytes 4177920 | tf_op jit(solution)/shard_map/all_gather | solution.py:322
  7.9 212.9 %all-gather.5.cloned.1.call-start = ((), (), s32[]{:S(2)}) async-start(), calls=%async_computation.1 | async-start | bytes 5570560 | tf_op jit(solution)/shard_map/all_gather | solution.py:324
  7.9 32.5 %collective-permute-start.16 = (bf16[320,512]{1,0:T(8,128)(2,1)}, bf16[320,512]{1,0:T(8,128)(2,1)S(1)}, u32[]{:S(2)}, u32[]{:S(2)}) collective-permute-start(bf16[320,512]{1,0:T(8,128)(2,1)} %param.21), channel_id=1, source_target_pairs={{0,0},{1,16},{2,32},{3,48},{4,64},{5,80},{6,96},{7,112},{8,128},{9... | collective-permute-start | bytes 983048 | tf_op jit(solution)/shard_map/ppermute | solution.py:323
  59.0 26.7 %collective-permute-start.4 = (bf16[64,5120]{1,0:T(8,128)(2,1)S(1)}, bf16[64,5120]{1,0:T(8,128)(2,1)S(1)}, u32[]{:S(2)}, u32[]{:S(2)}) collective-permute-start(bf16[64,5120]{1,0:T(8,128)(2,1)S(1)} %maximum_maximum_fusion.s0), channel_id=1, source_target_pairs={{0,4},{1,5},{2,6},{3,7},{4,8},{5,9},{6,10},{7,11},{8,12},{9,13},{1... | collective-permute-start | bytes 1966088 | tf_op jit(solution)/shard_map/ppermute | solution.py:39
  70.5 17.8 %collective-permute-start.5 = (bf16[64,5120]{1,0:T(8,128)(2,1)S(1)}, bf16[64,5120]{1,0:T(8,128)(2,1)S(1)}, u32[]{:S(2)}, u32[]{:S(2)}) collective-permute-start(bf16[64,5120]{1,0:T(8,128)(2,1)S(1)} %maximum_maximum_fusion.s0), channel_id=1, source_target_pairs={{0,12},{1,13},{2,14},{3,15},{4,0},{5,1},{6,2},{7,3},{8,4},{9,5},{1... | collective-permute-start | bytes 1966088 | tf_op jit(solution)/shard_map/ppermute | solution.py:39
  70.5 123.8 %collective-permute-start.29 = (bf16[512,2048]{1,0:T(8,128)(2,1)}, bf16[512,2048]{1,0:T(8,128)(2,1)}, u32[]{:S(2)}, u32[]{:S(2)}) collective-permute-start(bf16[512,2048]{1,0:T(8,128)(2,1)} %w0.1), channel_id=1, source_target_pairs={{0,1},{1,2},{2,3},{3,0},{4,5},{5,6},{6,7},{7,4},{8,9},{9,10},{10,1... | collective-permute-start | bytes 6291464 | tf_op jit(solution)/shard_map/ppermute | solution.py:39
  70.5 129.4 %collective-permute-start.30 = (bf16[512,2048]{1,0:T(8,128)(2,1)}, bf16[512,2048]{1,0:T(8,128)(2,1)}, u32[]{:S(2)}, u32[]{:S(2)}) collective-permute-start(bf16[512,2048]{1,0:T(8,128)(2,1)} %w0.1), channel_id=1, source_target_pairs={{0,3},{1,0},{2,1},{3,2},{4,7},{5,4},{6,5},{7,6},{8,11},{9,8},{10,9... | collective-permute-start | bytes 6291464 | tf_op jit(solution)/shard_map/ppermute | solution.py:39
  85.7 11.9 %collective-permute-start.6 = (bf16[32,5120]{1,0:T(8,128)(2,1)S(1)}, bf16[32,5120]{1,0:T(8,128)(2,1)S(1)}, u32[]{:S(2)}, u32[]{:S(2)}) collective-permute-start(bf16[32,5120]{1,0:T(8,128)(2,1)S(1)} %slice.96), channel_id=1, source_target_pairs={{0,4},{1,5},{2,6},{3,7},{4,8},{5,9},{6,10},{7,11},{8,12},{9,13},{1... | collective-permute-start | bytes 983048 | tf_op jit(solution)/shard_map/ppermute | solution.py:39
  88.3 10.7 %collective-permute-start.7 = (bf16[32,5120]{1,0:T(8,128)(2,1)S(1)}, bf16[32,5120]{1,0:T(8,128)(2,1)S(1)}, u32[]{:S(2)}, u32[]{:S(2)}) collective-permute-start(bf16[32,5120]{1,0:T(8,128)(2,1)S(1)} %slice.97), channel_id=1, source_target_pairs={{0,12},{1,13},{2,14},{3,15},{4,0},{5,1},{6,2},{7,3},{8,4},{9,5},{1... | collective-permute-start | bytes 983048 | tf_op jit(solution)/shard_map/ppermute | solution.py:39
  107.4 7.2 %collective-permute-start.9 = (bf16[256,320]{1,0:T(8,128)(2,1)S(1)}, bf16[256,320]{1,0:T(8,128)(2,1)S(1)}, u32[]{:S(2)}, u32[]{:S(2)}) collective-permute-start(bf16[256,320]{1,0:T(8,128)(2,1)S(1)} %shard_map.150), channel_id=1, source_target_pairs={{0,3},{1,0},{2,1},{3,2},{4,7},{5,4},{6,5},{7,6},{8,11},{9,8},{10,9... | collective-permute-start | bytes 491528 | tf_op jit(solution)/shard_map/ppermute | solution.py:39
  114.4 7.1 %collective-permute-start.10 = (bf16[128,320]{1,0:T(8,128)(2,1)S(1)}, bf16[128,320]{1,0:T(8,128)(2,1)S(1)}, u32[]{:S(2)}, u32[]{:S(2)}) collective-permute-start(bf16[128,320]{1,0:T(8,128)(2,1)S(1)} %slice.98), channel_id=1, source_target_pairs={{0,1},{1,2},{2,3},{3,0},{4,5},{5,6},{6,7},{7,4},{8,9},{9,10},{10,1... | collective-permute-start | bytes 245768 | tf_op jit(solution)/shard_map/ppermute | solution.py:39
  122.0 68.9 %collective-permute-start.12 = (bf16[256,1280]{1,0:T(8,128)(2,1)S(1)}, bf16[256,1280]{1,0:T(8,128)(2,1)S(1)}, u32[]{:S(2)}, u32[]{:S(2)}) collective-permute-start(bf16[256,1280]{1,0:T(8,128)(2,1)S(1)} %concatenate.23.h0), channel_id=1, source_target_pairs={{0,4},{1,5},{2,6},{3,7},{4,8},{5,9},{6,10},{7,11},{8,12},{9,13},{1... | collective-permute-start | bytes 1966088 | tf_op jit(solution)/shard_map/ppermute | solution.py:39
  122.1 72.1 %collective-permute-start.13 = (bf16[256,1280]{1,0:T(8,128)(2,1)S(1)}, bf16[256,1280]{1,0:T(8,128)(2,1)S(1)}, u32[]{:S(2)}, u32[]{:S(2)}) collective-permute-start(bf16[256,1280]{1,0:T(8,128)(2,1)S(1)} %concatenate.23.h0), channel_id=1, source_target_pairs={{0,12},{1,13},{2,14},{3,15},{4,0},{5,1},{6,2},{7,3},{8,4},{9,5},{1... | collective-permute-start | bytes 1966088 | tf_op jit(solution)/shard_map/ppermute | solution.py:39
  190.8 41.7 %collective-permute-start.21 = (bf16[192,2048]{1,0:T(8,128)(2,1)}, bf16[192,2048]{1,0:T(8,128)(2,1)S(1)}, u32[]{:S(2)}, u32[]{:S(2)}) collective-permute-start(bf16[192,2048]{1,0:T(8,128)(2,1)} %get-tuple-element.16), channel_id=1, source_target_pairs={{0,4},{1,5},{2,6},{3,7},{4,8},{5,9},{6,10},{7,11},{8,12},{9,13},{1... | collective-permute-start | bytes 2359304 | tf_op jit(solution)/shard_map/ppermute | solution.py:39
  190.9 41.7 %collective-permute-start.22 = (bf16[192,2048]{1,0:T(8,128)(2,1)}, bf16[192,2048]{1,0:T(8,128)(2,1)S(1)}, u32[]{:S(2)}, u32[]{:S(2)}) collective-permute-start(bf16[192,2048]{1,0:T(8,128)(2,1)} %get-tuple-element.17), channel_id=1, source_target_pairs={{0,12},{1,13},{2,14},{3,15},{4,0},{5,1},{6,2},{7,3},{8,4},{9,5},{1... | collective-permute-start | bytes 2359304 | tf_op jit(solution)/shard_map/ppermute | solution.py:39
  194.2 24.9 %collective-permute-start.14 = (bf16[128,1280]{1,0:T(8,128)(2,1)S(1)}, bf16[128,1280]{1,0:T(8,128)(2,1)S(1)}, u32[]{:S(2)}, u32[]{:S(2)}) collective-permute-start(bf16[128,1280]{1,0:T(8,128)(2,1)S(1)} %slice.100), channel_id=1, source_target_pairs={{0,4},{1,5},{2,6},{3,7},{4,8},{5,9},{6,10},{7,11},{8,12},{9,13},{1... | collective-permute-start | bytes 983048 | tf_op jit(solution)/shard_map/ppermute | solution.py:39
  194.3 25.7 %collective-permute-start.15 = (bf16[128,1280]{1,0:T(8,128)(2,1)S(1)}, bf16[128,1280]{1,0:T(8,128)(2,1)S(1)}, u32[]{:S(2)}, u32[]{:S(2)}) collective-permute-start(bf16[128,1280]{1,0:T(8,128)(2,1)S(1)} %slice.101), channel_id=1, source_target_pairs={{0,12},{1,13},{2,14},{3,15},{4,0},{5,1},{6,2},{7,3},{8,4},{9,5},{1... | collective-permute-start | bytes 983048 | tf_op jit(solution)/shard_map/ppermute | solution.py:39
  199.9 51.5 %collective-permute-start.31 = (bf16[256,2048]{1,0:T(8,128)(2,1)}, bf16[256,2048]{1,0:T(8,128)(2,1)}, u32[]{:S(2)}, u32[]{:S(2)}) collective-permute-start(bf16[256,2048]{1,0:T(8,128)(2,1)} %slice.108), channel_id=1, source_target_pairs={{0,1},{1,2},{2,3},{3,0},{4,5},{5,6},{6,7},{7,4},{8,9},{9,10},{10,1... | collective-permute-start | bytes 3145736 | tf_op jit(solution)/shard_map/ppermute | solution.py:39
  219.9 31.6 %collective-permute-start.32 = (bf16[256,2048]{1,0:T(8,128)(2,1)}, bf16[256,2048]{1,0:T(8,128)(2,1)}, u32[]{:S(2)}, u32[]{:S(2)}) collective-permute-start(bf16[256,2048]{1,0:T(8,128)(2,1)} %slice.109), channel_id=1, source_target_pairs={{0,3},{1,0},{2,1},{3,2},{4,7},{5,4},{6,5},{7,6},{8,11},{9,8},{10,9... | collective-permute-start | bytes 3145736 | tf_op jit(solution)/shard_map/ppermute | solution.py:39
  230.6 7.9 %collective-permute-start.17 = (bf16[256,512]{1,0:T(8,128)(2,1)}, bf16[256,512]{1,0:T(8,128)(2,1)S(1)}, u32[]{:S(2)}, u32[]{:S(2)}) collective-permute-start(bf16[256,512]{1,0:T(8,128)(2,1)} %shard_map.151.v0), channel_id=1, source_target_pairs={{0,1},{1,2},{2,3},{3,0},{4,5},{5,6},{6,7},{7,4},{8,9},{9,10},{10,1... | collective-permute-start | bytes 786440 | tf_op jit(solution)/shard_map/ppermute | solution.py:39
  232.6 9.1 %collective-permute-start.23 = (bf16[64,2048]{1,0:T(8,128)(2,1)S(1)}, bf16[64,2048]{1,0:T(8,128)(2,1)S(1)}, u32[]{:S(2)}, u32[]{:S(2)}) collective-permute-start(bf16[64,2048]{1,0:T(8,128)(2,1)S(1)} %slice.104), channel_id=1, source_target_pairs={{0,4},{1,5},{2,6},{3,7},{4,8},{5,9},{6,10},{7,11},{8,12},{9,13},{1... | collective-permute-start | bytes 786440 | tf_op jit(solution)/shard_map/ppermute | solution.py:39
  232.7 8.6 %collective-permute-start.18 = (bf16[256,512]{1,0:T(8,128)(2,1)}, bf16[256,512]{1,0:T(8,128)(2,1)S(1)}, u32[]{:S(2)}, u32[]{:S(2)}) collective-permute-start(bf16[256,512]{1,0:T(8,128)(2,1)} %shard_map.151.v0), channel_id=1, source_target_pairs={{0,3},{1,0},{2,1},{3,2},{4,7},{5,4},{6,5},{7,6},{8,11},{9,8},{10,9... | collective-permute-start | bytes 786440 | tf_op jit(solution)/shard_map/ppermute | solution.py:39
  241.3 7.9 %collective-permute-start.19 = (bf16[128,512]{1,0:T(8,128)(2,1)S(1)}, bf16[128,512]{1,0:T(8,128)(2,1)S(1)}, u32[]{:S(2)}, u32[]{:S(2)}) collective-permute-start(bf16[128,512]{1,0:T(8,128)(2,1)S(1)} %slice.102), channel_id=1, source_target_pairs={{0,1},{1,2},{2,3},{3,0},{4,5},{5,6},{6,7},{7,4},{8,9},{9,10},{10,1... | collective-permute-start | bytes 393224 | tf_op jit(solution)/shard_map/ppermute | solution.py:39
  241.6 7.6 %collective-permute-start.20 = (bf16[128,512]{1,0:T(8,128)(2,1)S(1)}, bf16[128,512]{1,0:T(8,128)(2,1)S(1)}, u32[]{:S(2)}, u32[]{:S(2)}) collective-permute-start(bf16[128,512]{1,0:T(8,128)(2,1)S(1)} %slice.103), channel_id=1, source_target_pairs={{0,3},{1,0},{2,1},{3,2},{4,7},{5,4},{6,5},{7,6},{8,11},{9,8},{10,9... | collective-permute-start | bytes 393224 | tf_op jit(solution)/shard_map/ppermute | solution.py:39
  258.7 7.7 %collective-permute-start.33 = (bf16[64,2048]{1,0:T(8,128)(2,1)S(1)}, bf16[64,2048]{1,0:T(8,128)(2,1)S(1)}, u32[]{:S(2)}, u32[]{:S(2)}) collective-permute-start(bf16[64,2048]{1,0:T(8,128)(2,1)S(1)} %get-tuple-element.24), channel_id=1, source_target_pairs={{0,4},{1,5},{2,6},{3,7},{4,8},{5,9},{6,10},{7,11},{8,12},{9,13},{1... | collective-permute-start | bytes 786440 | tf_op jit(solution)/shard_map/ppermute | solution.py:39
  258.8 19.5 %collective-permute-start.25 = (bf16[192,2048]{1,0:T(8,128)(2,1)S(1)}, bf16[192,2048]{1,0:T(8,128)(2,1)S(1)}, u32[]{:S(2)}, u32[]{:S(2)}) collective-permute-start(bf16[192,2048]{1,0:T(8,128)(2,1)S(1)} %get-tuple-element.19.to_right), channel_id=1, source_target_pairs={{0,4},{1,5},{2,6},{3,7},{4,8},{5,9},{6,10},{7,11},{8,12},{9,13},{1... | collective-permute-start | bytes 2359304 | tf_op jit(solution)/shard_map/ppermute | solution.py:39
  259.8 18.6 %collective-permute-start.26 = (bf16[192,2048]{1,0:T(8,128)(2,1)S(1)}, bf16[192,2048]{1,0:T(8,128)(2,1)S(1)}, u32[]{:S(2)}, u32[]{:S(2)}) collective-permute-start(bf16[192,2048]{1,0:T(8,128)(2,1)S(1)} %get-tuple-element.20.to_left), channel_id=1, source_target_pairs={{0,12},{1,13},{2,14},{3,15},{4,0},{5,1},{6,2},{7,3},{8,4},{9,5},{1... | collective-permute-start | bytes 2359304 | tf_op jit(solution)/shard_map/ppermute | solution.py:39
  262.1 12.5 %collective-permute-start.35 = (bf16[64,2048]{1,0:T(8,128)(2,1)S(1)}, bf16[64,2048]{1,0:T(8,128)(2,1)S(1)}, u32[]{:S(2)}, u32[]{:S(2)}) collective-permute-start(bf16[64,2048]{1,0:T(8,128)(2,1)S(1)} %get-tuple-element.26), channel_id=1, source_target_pairs={{0,12},{1,13},{2,14},{3,15},{4,0},{5,1},{6,2},{7,3},{8,4},{9,5},{1... | collective-permute-start | bytes 786440 | tf_op jit(solution)/shard_map/ppermute | solution.py:39
  266.4 23.5 %collective-permute-start.34 = (bf16[128,2048]{1,0:T(8,128)(2,1)S(1)}, bf16[128,2048]{1,0:T(8,128)(2,1)S(1)}, u32[]{:S(2)}, u32[]{:S(2)}) collective-permute-start(bf16[128,2048]{1,0:T(8,128)(2,1)S(1)} %pad_maximum_fusion), channel_id=1, source_target_pairs={{0,4},{1,5},{2,6},{3,7},{4,8},{5,9},{6,10},{7,11},{8,12},{9,13},{1... | collective-permute-start | bytes 1572872 | tf_op jit(solution)/shard_map/ppermute | solution.py:39
  274.7 15.2 %collective-permute-start.36 = (bf16[128,2048]{1,0:T(8,128)(2,1)S(1)}, bf16[128,2048]{1,0:T(8,128)(2,1)S(1)}, u32[]{:S(2)}, u32[]{:S(2)}) collective-permute-start(bf16[128,2048]{1,0:T(8,128)(2,1)S(1)} %pad_maximum_fusion.1), channel_id=1, source_target_pairs={{0,12},{1,13},{2,14},{3,15},{4,0},{5,1},{6,2},{7,3},{8,4},{9,5},{1... | collective-permute-start | bytes 1572872 | tf_op jit(solution)/shard_map/ppermute | solution.py:39
  278.3 7.7 %collective-permute-start.27 = (bf16[64,2048]{1,0:T(8,128)(2,1)S(1)}, bf16[64,2048]{1,0:T(8,128)(2,1)S(1)}, u32[]{:S(2)}, u32[]{:S(2)}) collective-permute-start(bf16[64,2048]{1,0:T(8,128)(2,1)S(1)} %slice.106), channel_id=1, source_target_pairs={{0,4},{1,5},{2,6},{3,7},{4,8},{5,9},{6,10},{7,11},{8,12},{9,13},{1... | collective-permute-start | bytes 786440 | tf_op jit(solution)/shard_map/ppermute | solution.py:39
  278.4 9.3 %collective-permute-start.28 = (bf16[64,2048]{1,0:T(8,128)(2,1)S(1)}, bf16[64,2048]{1,0:T(8,128)(2,1)S(1)}, u32[]{:S(2)}, u32[]{:S(2)}) collective-permute-start(bf16[64,2048]{1,0:T(8,128)(2,1)S(1)} %slice.107), channel_id=1, source_target_pairs={{0,12},{1,13},{2,14},{3,15},{4,0},{5,1},{6,2},{7,3},{8,4},{9,5},{1... | collective-permute-start | bytes 786440 | tf_op jit(solution)/shard_map/ppermute | solution.py:39
  (24 other events, 186.5 us)
Sparse Core Ops, SparseCore 0:
  9.8 58.5 all-gather.2
  70.3 42.7 all-gather.4

commit v2 on v1

v2 whole, which is shorter than its diff:
```python
import jax
import jax.numpy as jnp
import numpy as np
from jax import lax
from jax.experimental import pallas as pl
from jax.experimental.pallas import tpu as pltpu
from jax.sharding import PartitionSpec as P

SLOT = 8
RING = (0, -1, 1, 2)
MIB = 1 << 20
BF16, F32 = jnp.bfloat16, jnp.float32


def place(core, tp, which, step):
    y, x = tp // 4, tp % 4
    if (core == 0) == (which == 1):
        return y * 4 + (x + step) % 4
    return (y + step) % 4 * 4 + x


TABLE = np.array(
    [
        [place(core, place(core, tp, 2, o2), 1, o1) for o2 in RING for o1 in RING]
        for core in range(2)
        for tp in range(16)
    ],
    np.int32,
)
HOPS = {
    (which, step): [(c * 16 + t, c * 16 + place(c, t, which, step)) for c in range(2) for t in range(16)]
    for which in (1, 2)
    for step in (1, -1, 2)
}
SHUFFLE = [(a * 16 + b, (a ^ b) * 16 + b) for a in range(16) for b in range(16)]
TURN = [(a * 16 + b, a * 16 + (a ^ b)) for a in range(16) for b in range(16)]


def hop(value, which, step):
    return lax.ppermute(value, ("mb", "tp"), HOPS[which, step])


def around(value, which):
    return hop(value, which, 1), hop(value, which, -1), hop(value, which, 2)


def after(value, *others):
    return lax.optimization_barrier((value, *others))[0]


def cost(flops, moved):
    return pl.CostEstimate(flops=flops, bytes_accessed=moved, transcendentals=0)


def params(mib):
    return pltpu.CompilerParams(vmem_limit_bytes=mib * MIB)


VMEM = pl.BlockSpec(memory_space=pltpu.VMEM)
SMEM = pl.BlockSpec(memory_space=pltpu.SMEM)
ANY = pl.BlockSpec(memory_space=pl.ANY)
HBM = pl.BlockSpec(memory_space=pltpu.HBM)


def merge_kernel(p_ref, gain_ref, bias_ref, out_ref, rows):
    values = p_ref[...].astype(F32)
    center = values - jnp.mean(values, axis=-1, keepdims=True)
    spread = jnp.mean(center * center, axis=-1, keepdims=True)
    normal = center * lax.rsqrt(spread + 1e-06) * gain_ref[...].reshape(1, 1280) + bias_ref[...].reshape(1, 1280)
    for k in range(10):
        rows[k] = normal[:, k * 128 : (k + 1) * 128]
    for j in range(4):
        for k in range(10):
            start = j * 1280 + k * 128
            out_ref[:, start : start + 128] = rows[k, pl.ds(j, 16, stride=4), :].astype(BF16)


def merge(patches, gain, bias):
    return pl.pallas_call(
        merge_kernel,
        out_shape=jax.ShapeDtypeStruct((16, 5120), BF16),
        in_specs=[VMEM] * 3,
        out_specs=VMEM,
        scratch_shapes=[pltpu.VMEM((10, 64, 128), F32)],
        compiler_params=params(8),
        cost_estimate=cost(10**6, 330000),
    )(patches, gain, bias)


def pack_kernel(tab, *refs):
    for source, target in zip(refs[:4], refs[4:]):
        target[...] = source[...]


def pack(tab, text):
    def columns(i2):
        return pl.BlockSpec((128, 512), lambda j, tab: (0, tab[i2 * 4 + j]))

    return pl.pallas_call(
        pack_kernel,
        out_shape=[jax.ShapeDtypeStruct((128, 2048), BF16)] * 4,
        grid_spec=pltpu.PrefetchScalarGridSpec(
            num_scalar_prefetch=1,
            grid=(4,),
            in_specs=[columns(i2) for i2 in range(4)],
            out_specs=[pl.BlockSpec((128, 512), lambda j, tab: (0, j))] * 4,
        ),
        compiler_params=params(8),
        cost_estimate=cost(0, 4 * MIB),
    )(tab, text, text, text, text)


def start(copies, sems):
    copies = [pltpu.make_async_copy(a, b, sems.at[i]) for i, (a, b) in enumerate(copies)]
    for copy in copies:
        copy.start()
    return copies


def up_kernel(tab, s0, s1, s2, s3, weight, bias_ref, out_ref, rows, held, sems):
    copies = [(piece, rows.at[pl.ds(i * 64, 64)]) for i, piece in enumerate((s0, s1, s2, s3))]
    copies += [(weight.at[pl.ds(k * 1024, 1024)], held.at[pl.ds(k * 1024, 1024)]) for k in range(5)]
    copies = start(copies, sems)
    for copy in copies[:4]:
        copy.wait()
    raised = bias_ref[tab[0]]
    for k in range(5):
        copies[4 + k].wait()
        at = slice(k * 1024, (k + 1) * 1024)
        raised = raised + jnp.dot(rows[:, at], held[at, :], preferred_element_type=F32)
    hidden = (0.5 * raised * (1.0 + lax.erf(raised * np.float32(0.5**0.5)))).astype(BF16)
    for k in range(16):
        out_ref[pl.ds(pl.multiple_of(tab[k] * 16, 16), 16), :] = hidden[k * 16 : (k + 1) * 16]


def up(tab, pieces, weight, bias):
    return pl.pallas_call(
        up_kernel,
        out_shape=jax.ShapeDtypeStruct((256, 320), BF16),
        in_specs=[SMEM] + [ANY] * 5 + [VMEM],
        out_specs=VMEM,
        scratch_shapes=[
            pltpu.VMEM((256, 5120), BF16),
            pltpu.VMEM((5120, 320), BF16),
            pltpu.SemaphoreType.DMA((9,)),
        ],
        compiler_params=params(56),
        cost_estimate=cost(840 * 10**6, 6 * MIB),
    )(tab, *pieces, weight, bias)


def down_kernel(tab, h0, h1, h2, h3, weight, bias_ref, out_ref, units, held, sems):
    copies = []
    for i2, piece in enumerate((h0, h1, h2, h3)):
        copies.append((piece, units.at[i2]))
        for i1 in range(4):
            k = i2 * 4 + i1
            source = weight.at[pl.ds(pl.multiple_of((tab[k] ^ tab[0]) * 320, 320), 320)]
            copies.append((source, held.at[pl.ds(k * 320, 320)]))
    copies = start(copies, sems)
    total = bias_ref[tab[0]]
    for i2 in range(4):
        for copy in copies[i2 * 5 : i2 * 5 + 5]:
            copy.wait()
        total = total + jnp.dot(units[i2], held[i2 * 1280 : (i2 + 1) * 1280, :], preferred_element_type=F32)
    out_ref[...] = total.astype(BF16)


def down(tab, pieces, weight, bias):
    return pl.pallas_call(
        down_kernel,
        out_shape=jax.ShapeDtypeStruct((256, 512), BF16),
        in_specs=[SMEM] + [ANY] * 5 + [VMEM],
        out_specs=VMEM,
        scratch_shapes=[
            pltpu.VMEM((4, 256, 1280), BF16),
            pltpu.VMEM((5120, 512), BF16),
            pltpu.SemaphoreType.DMA((20,)),
        ],
        compiler_params=params(56),
        cost_estimate=cost(1340 * 10**6, 8 * MIB),
    )(tab, *pieces, weight, bias)


def pick_kernel(tab, dest, v0, v1, v2, v3, *refs):
    visual = (v0[...], v1[...], v2[...], v3[...])
    targets = dest[...]
    for i2 in (3, 2, 1, 0):
        text, out = refs[i2], refs[4 + i2]
        match = (lax.broadcasted_iota(jnp.int32, (128, 256), 0) + tab[i2 * 4] * 128) == targets
        select = match.astype(F32)
        present = jnp.sum(select, axis=1, keepdims=True) > 0.0
        select = select.astype(BF16)
        for j in range(4):
            at = slice(j * 512, (j + 1) * 512)
            picked = jnp.dot(select, visual[j], preferred_element_type=F32).astype(BF16)
            out[:, at] = jnp.where(present, picked, text[:, at])


def pick(tab, dest, visual, text):
    return pl.pallas_call(
        pick_kernel,
        out_shape=[jax.ShapeDtypeStruct((128, 2048), BF16)] * 4,
        in_specs=[SMEM] + [VMEM] * 9,
        out_specs=[VMEM] * 4,
        compiler_params=params(32),
        cost_estimate=cost(540 * 10**6, 6 * MIB),
    )(tab, dest, *visual, *text)


def product_kernel(tab, e0, e1, e2, e3, gain, w0, w1, w2, w3a, w3b, own, left, right, far, scaled):
    @pl.when(pl.program_id(0) == 0)
    def _():
        for j in range(4):
            at = slice(j * 512, (j + 1) * 512)
            scale = gain[tab[j]]
            for i2, rows in enumerate((e0, e1, e2, e3)):
                scaled[i2 * 128 : (i2 + 1) * 128, at] = (rows[:, at].astype(F32) * scale).astype(BF16)

    total = jnp.dot(scaled[:, 0:512], w0[...], preferred_element_type=F32)
    total = total + jnp.dot(scaled[:, 512:1024], w1[...], preferred_element_type=F32)
    total = total + jnp.dot(scaled[:, 1024:1536], w2[...], preferred_element_type=F32)
    total = total + jnp.dot(scaled[:, 1536:1792], w3a[...], preferred_element_type=F32)
    total = total + jnp.dot(scaled[:, 1792:2048], w3b[...], preferred_element_type=F32)
    own[...] = total[0:128]
    left[...] = total[128:256].astype(BF16)
    right[...] = total[256:384].astype(BF16)
    far[...] = total[384:512].astype(BF16)


def product(tab, picked, gain, weights):
    def block(count):
        return pl.BlockSpec((count, 512), lambda n: (0, n))

    return pl.pallas_call(
        product_kernel,
        out_shape=[jax.ShapeDtypeStruct((128, 2048), F32)] + [jax.ShapeDtypeStruct((128, 2048), BF16)] * 3,
        grid=(4,),
        in_specs=[SMEM] + [VMEM] * 5 + [block(n) for n in (512, 512, 512, 256, 256)],
        out_specs=[block(128)] * 4,
        scratch_shapes=[pltpu.VMEM((512, 2048), BF16)],
        compiler_params=params(40),
        cost_estimate=cost(4300 * 10**6, 14 * MIB),
    )(tab, *picked, gain, *weights)


def place_kernel(tab, e0, e1, e2, e3, out, scale, sems):
    copies = []
    for i2, rows in enumerate((e0, e1, e2, e3)):
        for j in range(4):
            columns = pl.ds(pl.multiple_of(tab[i2 * 4 + j] * 512, 512), 512)
            copies.append((rows.at[:, pl.ds(j * 512, 512)], out.at[:, columns]))
    copies = start(copies, sems)
    total = 0.0
    for rows in (e0, e1, e2, e3):
        values = rows[...].astype(F32)
        total = total + jnp.sum(values * values, axis=1, keepdims=True)
    scale[...] = jnp.broadcast_to(lax.rsqrt(total * (1.0 / 8192.0) + 1e-06), (128, 128))
    for copy in copies:
        copy.wait()


def place_rows(tab, pieces):
    return pl.pallas_call(
        place_kernel,
        out_shape=[jax.ShapeDtypeStruct((128, 8192), BF16), jax.ShapeDtypeStruct((128, 128), F32)],
        in_specs=[SMEM] + [VMEM] * 4,
        out_specs=[ANY, VMEM],
        scratch_shapes=[pltpu.SemaphoreType.DMA((16,))],
        compiler_params=params(32),
        cost_estimate=cost(4 * 10**6, 30 * MIB),
    )(tab, *pieces)


def per_device(
    patches,
    patch_counts,
    dest_pos,
    merge_gain,
    merge_bias,
    up_weight,
    up_bias,
    down_weight,
    down_bias,
    text_embed,
    norm_gain,
    kv_weight,
    kv_bias,
):
    tab = jnp.asarray(TABLE)[lax.axis_index("mb") * 16 + lax.axis_index("tp")]
    up_full = lax.all_gather(up_weight, ("enc", "mb"), axis=0, tiled=True)
    down_part = lax.ppermute(down_weight, ("enc", "mb", "tp"), SHUFFLE)

    merged = merge(patches[0, 0], merge_gain, merge_bias)
    near = jnp.concatenate([merged, *around(merged, 1)], axis=0)
    down_part = lax.ppermute(after(down_part, near), ("enc", "mb", "tp"), TURN)
    group = (near, *around(near, 2))
    down_full = lax.all_gather(after(down_part, *group), ("enc", "mb"), axis=0, tiled=True)

    kv_weight = after(kv_weight, near)
    kv_right, kv_left = hop(kv_weight, 1, 1), hop(kv_weight, 1, -1)
    own, to_left, to_right, to_far = pack(tab, text_embed[0, 0])
    text = (own, hop(to_right, 2, 1), hop(to_left, 2, -1), hop(to_far, 2, 2))

    up_full = after(up_full, kv_right, kv_left, *text)
    hidden = up(tab, group, up_full, up_bias.reshape(16, 1, 320))
    near = jnp.concatenate([hidden, *around(hidden, 1)], axis=1)
    right, left = lax.optimization_barrier((kv_right, kv_left, near))[:2]
    weights = (kv_weight, kv_right, kv_left, hop(right[:256], 1, 1), hop(left[256:], 1, -1))
    units = (near, *around(near, 2))
    down_full = after(down_full, weights[3], weights[4])
    visual = down(tab, units, down_full, down_bias.reshape(16, 1, 512))
    visual = (visual, *around(visual, 1))

    live_rows = patch_counts[0, 0] // 4
    live = (jnp.arange(SLOT, dtype=jnp.int32)[None, :] < live_rows[:, None]).reshape(-1)
    dest = jnp.where(live, dest_pos[0, 0], -1)[None]
    picked = pick(tab, dest, visual, text)
    pieces = (picked[0], hop(picked[2], 2, 1), hop(picked[1], 2, -1), hop(picked[3], 2, 2))
    own, to_left, to_right, to_far = product(tab, picked, norm_gain.reshape(16, 1, 512), weights)
    sums = (hop(to_far, 2, 2), hop(to_right, 2, 1), hop(to_left, 2, -1))
    embedded, scale = place_rows(tab, pieces)
    total = own
    for value in sums:
        total = total + value.astype(F32)
    keys_values = (total * scale[:, :1] + kv_bias).astype(BF16)
    return (embedded[None, None], keys_values[None, None])


def solution(mesh):
    return jax.shard_map(
        per_device,
        mesh=mesh,
        in_specs=(
            P("enc", "mb", "tp", None),
            P("enc", "mb", None),
            P("enc", "mb", None),
            P(),
            P(),
            P(("enc", "mb"), "tp"),
            P(),
            P("tp", ("enc", "mb")),
            P(),
            P("enc", "mb", "tp", None),
            P(),
            P("tp", None),
            P(),
        ),
        out_specs=(P("enc", "mb", "tp", None), P("enc", "mb", "tp", None)),
        check_vma=False,
    )
```

time: 302 us -> 202 us (0.67)
  Pallas kernels: 89.4 us -> 24 us
  waiting for transfers between devices: 103 us -> 74.1 us
  local copies, waits for them, and re-layouts: 19.4 us -> 12.2 us
  starting transfers between devices: 68.9 us -> 72.6 us
    pallas_call x3, Pallas kernels: 74.8 us -> 10.7 us  [the longest x1 7.04 us: product(): pl.pallas_call(product_kernel, out_shape=[jax.ShapeDtypeStruct((128, 2048...]
    ppermute x1 -> x2, waiting for transfers between devices: 28 us -> 8.13 us  [the longest x1 8.13 us: per_device(): down_part = lax.ppermute(after(down_part, near), ('enc', 'mb', 'tp'), TURN)]
    ppermute x36 -> x28, waiting for transfers between devices: 74.6 us -> 65.2 us  [hop(): return lax.ppermute(value, ('mb', 'tp'), HOPS[which, step])]
    unnamed x34 -> x40, local copies, waits for them, and re-layouts: 9.66 us -> 6.5 us
    ppermute x36 -> x28, starting transfers between devices: 64.4 us -> 66.4 us  [hop(): return lax.ppermute(value, ('mb', 'tp'), HOPS[which, step])]
    ppermute x1 -> x2, starting transfers between devices: 4.48 us -> 6.16 us  [the longest x1 4.54 us: per_device(): down_part = lax.ppermute(after(down_part, near), ('enc', 'mb', 'tp'), TURN)]
  transfers between devices with their start and end apart: 39 -> 32, of which waited for: 16 -> 18; matrix products, arithmetic and copies ran while one was open for 4% -> 3% of each run, Pallas kernels for 28% -> 9%
where the time goes in v2:
time: 202 us; the launch traced here: 198 us
  waiting for transfers between devices  74.1 us (37%)
  starting transfers between devices  72.6 us (36%)
  Pallas kernels  24 us (12%)
  between operations  14.3 us (7%)
  local copies, waits for them, and re-layouts  12.2 us (6%)
    ppermute x28, starting transfers between devices, hop(): return lax.ppermute(value, ('mb', 'tp'), HOPS[which, step])  66.4 us
    ppermute x28, waiting for transfers between devices, hop(): return lax.ppermute(value, ('mb', 'tp'), HOPS[which, step])  65.2 us
    ppermute x1, waiting for transfers between devices, per_device(): down_part = lax.ppermute(after(down_part, near), ('enc', 'mb', 'tp'), TURN)  8.13 us
    pallas_call x1, Pallas kernels, product(): pl.pallas_call(product_kernel, out_shape=[jax.ShapeDtypeStruct((128, 2048...  7.04 us
    unnamed x40, local copies, waits for them, and re-layouts  6.5 us
    pallas_call x1, Pallas kernels, up(): pl.pallas_call(up_kernel, out_shape=jax.ShapeDtypeStruct((256, 320), BF16...  5.61 us
    pallas_call x1, Pallas kernels, down(): pl.pallas_call(down_kernel, out_shape=jax.ShapeDtypeStruct((256, 512), BF...  5.4 us
    ppermute x1, starting transfers between devices, per_device(): down_part = lax.ppermute(after(down_part, near), ('enc', 'mb', 'tp'), TURN)  4.54 us
  transfers between devices with their start and end apart: 32, of which 18 were waited for; matrix products, arithmetic and copies ran while one was open for 3% of the time, Pallas kernels for 9%

profile of v2, /device:TPU:32, one launch (start us, length us, event | category | flops | bytes accessed | tf_op | source)
XLA Modules:
  0.0 198.4 jit_solution(18017124180832730614)
XLA Ops:
  17.4 3.2 %collective-permute-done.2 = bf16[16,5120]{1,0:T(8,128)(2,1)S(1)} collective-permute-done((bf16[16,5120]{1,0:T(8,128)(2,1)S(1)}, bf16[16,5120]{1,0:T(8,128)(2,1)S(1)}, u32[]{:S(2)}, u32[]{:S(2)}) %collective-permute-start.2) | collective-permute-done | bytes 163872 | tf_op jit(solution)/shard_map/ppermute | solution.py:40
  20.7 1.9 collective-permute-start.3
  22.6 3.7 %collective-permute-start.4 = (bf16[64,5120]{1,0:T(8,128)(2,1)S(1)}, bf16[64,5120]{1,0:T(8,128)(2,1)}, u32[]{:S(2)}, u32[]{:S(2)}) collective-permute-start(bf16[64,5120]{1,0:T(8,128)(2,1)S(1)} %pad_maximum_fusion.s0), channel_id=1, source_target_pairs={{0,12},{1,13},{2,14},{3,15},{4,0},{5,1},{6,2},{7,3},{8,4},{9,5},{1... | collective-permute-start | bytes 1966088 | tf_op jit(solution)/shard_map/ppermute | solution.py:40
  26.3 3.0 %collective-permute-start.5 = (bf16[64,5120]{1,0:T(8,128)(2,1)S(1)}, bf16[64,5120]{1,0:T(8,128)(2,1)}, u32[]{:S(2)}, u32[]{:S(2)}) collective-permute-start(bf16[64,5120]{1,0:T(8,128)(2,1)S(1)} %pad_maximum_fusion.s0), channel_id=1, source_target_pairs={{0,8},{1,9},{2,10},{3,11},{4,12},{5,13},{6,14},{7,15},{8,0},{9,1},... | collective-permute-start | bytes 1966088 | tf_op jit(solution)/shard_map/ppermute | solution.py:40
  29.3 4.5 %collective-permute-start.18 = (bf16[320,512]{1,0:T(8,128)(2,1)S(1)}, bf16[320,512]{1,0:T(8,128)(2,1)}, u32[]{:S(2)}, u32[]{:S(2)}) collective-permute-start(bf16[320,512]{1,0:T(8,128)(2,1)S(1)} %collective-permute-done.17), channel_id=1, source_target_pairs={{0,0},{1,1},{2,2},{3,3},{4,4},{5,5},{6,6},{7,7},{8,8},{9,9},{10,10... | collective-permute-start | bytes 983048 | tf_op jit(solution)/shard_map/ppermute | solution.py:296
  33.8 8.1 %collective-permute-done.18 = bf16[320,512]{1,0:T(8,128)(2,1)} collective-permute-done((bf16[320,512]{1,0:T(8,128)(2,1)S(1)}, bf16[320,512]{1,0:T(8,128)(2,1)}, u32[]{:S(2)}, u32[]{:S(2)}) %collective-permute-start.18) | collective-permute-done | bytes 327712 | tf_op jit(solution)/shard_map/ppermute | solution.py:296
  43.4 3.2 %collective-permute-start.7 = (bf16[512,2048]{1,0:T(8,128)(2,1)}, bf16[512,2048]{1,0:T(8,128)(2,1)}, u32[]{:S(2)}, u32[]{:S(2)}) collective-permute-start(bf16[512,2048]{1,0:T(8,128)(2,1)} %w0), channel_id=1, source_target_pairs={{0,3},{1,0},{2,1},{3,2},{4,7},{5,4},{6,5},{7,6},{8,11},{9,8},{10,9... | collective-permute-start | bytes 6291464 | tf_op jit(solution)/shard_map/ppermute | solution.py:40
  47.4 2.4 %shard_map.150 = (bf16[128,2048]{1,0:T(8,128)(2,1)S(1)}, bf16[128,2048]{1,0:T(8,128)(2,1)S(1)}, bf16[128,2048]{1,0:T(8,128)(2,1)}, bf16[128,2048]{1,0:T(8,128)(2,1)}) custom-call(s32[16]{0:T(128)S(1)} %dynamic-slice_bitcast_fusion.tab, bf16[128,8192]{1,0:T(8,128)(2,1)S(1)} %bitcast.19, bf16[128,8192]{1,0:T(8,128)(2,1)S(1)} %bitcast.20, ...), custom_call_target="tpu_custom_call" | custom-call | bytes 4194304 | tf_op jit(solution)/shard_map/pallas_call | solution.py:99
  49.8 13.3 %collective-permute-start.10 = (bf16[128,2048]{1,0:T(8,128)(2,1)}, bf16[128,2048]{1,0:T(8,128)(2,1)S(1)}, u32[]{:S(2)}, u32[]{:S(2)}) collective-permute-start(bf16[128,2048]{1,0:T(8,128)(2,1)} %get-tuple-element.27), channel_id=1, source_target_pairs={{0,8},{1,9},{2,10},{3,11},{4,12},{5,13},{6,14},{7,15},{8,0},{9,1},... | collective-permute-start | bytes 1572872 | tf_op jit(solution)/shard_map/ppermute | solution.py:40
  63.1 3.2 %collective-permute-start.9 = (bf16[128,2048]{1,0:T(8,128)(2,1)S(1)}, bf16[128,2048]{1,0:T(8,128)(2,1)S(1)}, u32[]{:S(2)}, u32[]{:S(2)}) collective-permute-start(bf16[128,2048]{1,0:T(8,128)(2,1)S(1)} %get-tuple-element.26), channel_id=1, source_target_pairs={{0,12},{1,13},{2,14},{3,15},{4,0},{5,1},{6,2},{7,3},{8,4},{9,5},{1... | collective-permute-start | bytes 1572872 | tf_op jit(solution)/shard_map/ppermute | solution.py:40
  67.0 9.1 %collective-permute-done.10.refs_3_ = bf16[128,2048]{1,0:T(8,128)(2,1)S(1)} collective-permute-done((bf16[128,2048]{1,0:T(8,128)(2,1)}, bf16[128,2048]{1,0:T(8,128)(2,1)S(1)}, u32[]{:S(2)}, u32[]{:S(2)}) %collective-permute-start.10) | collective-permute-done | bytes 524320 | tf_op jit(solution)/shard_map/ppermute | solution.py:40
  76.1 10.9 %collective-permute-done.8.refs_1_ = bf16[128,2048]{1,0:T(8,128)(2,1)S(1)} collective-permute-done((bf16[128,2048]{1,0:T(8,128)(2,1)}, bf16[128,2048]{1,0:T(8,128)(2,1)S(1)}, u32[]{:S(2)}, u32[]{:S(2)}) %collective-permute-start.8) | collective-permute-done | bytes 524320 | tf_op jit(solution)/shard_map/ppermute | solution.py:40
  87.4 5.6 %shard_map.151 = bf16[256,320]{1,0:T(8,128)(2,1)} custom-call(s32[16]{0:T(128)} %copy-done.3, bf16[64,5120]{1,0:T(8,128)(2,1)} %copy-done.14, bf16[64,5120]{1,0:T(8,128)(2,1)} %copy-done.15, bf16[64,5120]{1,0:T(8,128)(2,1)} %collective-permute-done.4.s2, bf16[64,5120]{1,0:T(8,128)(2,1)} %collective-permute-done.5.s3, ...), custom_call_target="tpu_custom_call" | custom-call | flops 840000000 | bytes 6291456 | tf_op jit(solution)/shard_map/pallas_call | solution.py:137
  93.3 3.0 %collective-permute-start.12 = (bf16[256,320]{1,0:T(8,128)(2,1)}, bf16[256,320]{1,0:T(8,128)(2,1)S(1)}, u32[]{:S(2)}, u32[]{:S(2)}) collective-permute-start(bf16[256,320]{1,0:T(8,128)(2,1)} %shard_map.151), channel_id=1, source_target_pairs={{0,3},{1,0},{2,1},{3,2},{4,7},{5,4},{6,5},{7,6},{8,11},{9,8},{10,9... | collective-permute-start | bytes 491528 | tf_op jit(solution)/shard_map/ppermute | solution.py:40
  96.4 3.9 %collective-permute-done.11 = bf16[256,320]{1,0:T(8,128)(2,1)S(1)} collective-permute-done((bf16[256,320]{1,0:T(8,128)(2,1)}, bf16[256,320]{1,0:T(8,128)(2,1)S(1)}, u32[]{:S(2)}, u32[]{:S(2)}) %collective-permute-start.11) | collective-permute-done | bytes 163872 | tf_op jit(solution)/shard_map/ppermute | solution.py:40
  108.0 3.3 %collective-permute-start.20 = (bf16[256,2048]{1,0:T(8,128)(2,1)S(1)}, bf16[256,2048]{1,0:T(8,128)(2,1)S(1)}, u32[]{:S(2)}, u32[]{:S(2)}) collective-permute-start(bf16[256,2048]{1,0:T(8,128)(2,1)S(1)} %slice.10), channel_id=1, source_target_pairs={{0,3},{1,0},{2,1},{3,2},{4,7},{5,4},{6,5},{7,6},{8,11},{9,8},{10,9... | collective-permute-start | bytes 3145736 | tf_op jit(solution)/shard_map/ppermute | solution.py:40
  111.3 4.5 %collective-permute-start.14 = (bf16[256,1280]{1,0:T(8,128)(2,1)S(1)}, bf16[256,1280]{1,0:T(8,128)(2,1)}, u32[]{:S(2)}, u32[]{:S(2)}) collective-permute-start(bf16[256,1280]{1,0:T(8,128)(2,1)S(1)} %concatenate.7.h0), channel_id=1, source_target_pairs={{0,4},{1,5},{2,6},{3,7},{4,8},{5,9},{6,10},{7,11},{8,12},{9,13},{1... | collective-permute-start | bytes 1966088 | tf_op jit(solution)/shard_map/ppermute | solution.py:40
  115.8 3.0 %collective-permute-start.15 = (bf16[256,1280]{1,0:T(8,128)(2,1)S(1)}, bf16[256,1280]{1,0:T(8,128)(2,1)}, u32[]{:S(2)}, u32[]{:S(2)}) collective-permute-start(bf16[256,1280]{1,0:T(8,128)(2,1)S(1)} %concatenate.7.h0), channel_id=1, source_target_pairs={{0,12},{1,13},{2,14},{3,15},{4,0},{5,1},{6,2},{7,3},{8,4},{9,5},{1... | collective-permute-start | bytes 1966088 | tf_op jit(solution)/shard_map/ppermute | solution.py:40
  118.8 2.7 %collective-permute-start.16 = (bf16[256,1280]{1,0:T(8,128)(2,1)S(1)}, bf16[256,1280]{1,0:T(8,128)(2,1)}, u32[]{:S(2)}, u32[]{:S(2)}) collective-permute-start(bf16[256,1280]{1,0:T(8,128)(2,1)S(1)} %concatenate.7.h0), channel_id=1, source_target_pairs={{0,8},{1,9},{2,10},{3,11},{4,12},{5,13},{6,14},{7,15},{8,0},{9,1},... | collective-permute-start | bytes 1966088 | tf_op jit(solution)/shard_map/ppermute | solution.py:40
  121.4 6.6 %collective-permute-done.19.w3a = bf16[256,2048]{1,0:T(8,128)(2,1)S(1)} collective-permute-done((bf16[256,2048]{1,0:T(8,128)(2,1)S(1)}, bf16[256,2048]{1,0:T(8,128)(2,1)S(1)}, u32[]{:S(2)}, u32[]{:S(2)}) %collective-permute-start.19) | collective-permute-done | bytes 1048608 | tf_op jit(solution)/shard_map/ppermute | solution.py:40
  129.0 8.6 %collective-permute-done.20.w3b = bf16[256,2048]{1,0:T(8,128)(2,1)S(1)} collective-permute-done((bf16[256,2048]{1,0:T(8,128)(2,1)S(1)}, bf16[256,2048]{1,0:T(8,128)(2,1)S(1)}, u32[]{:S(2)}, u32[]{:S(2)}) %collective-permute-start.20) | collective-permute-done | bytes 1048608 | tf_op jit(solution)/shard_map/ppermute | solution.py:40
  139.1 5.4 %shard_map.152.v0 = bf16[256,512]{1,0:T(8,128)(2,1)} custom-call(s32[16]{0:T(128)} %copy-done.3, bf16[256,1280]{1,0:T(8,128)(2,1)} %copy-done.13, bf16[256,1280]{1,0:T(8,128)(2,1)} %collective-permute-done.14.h1, bf16[256,1280]{1,0:T(8,128)(2,1)} %collective-permute-done.15.h2, bf16[256,1280]{1,0:T(8,128)(2,1)} %collective-permute-done.16.h3, ...), custom_call_target="tpu_custom_call" | custom-call | flops 1340000000 | bytes 8388608 | tf_op jit(solution)/shard_map/pallas_call | solution.py:170
  144.5 2.0 collective-permute-start.21
  149.5 2.9 %collective-permute-done.21.v1 = bf16[256,512]{1,0:T(8,128)(2,1)S(1)} collective-permute-done((bf16[256,512]{1,0:T(8,128)(2,1)}, bf16[256,512]{1,0:T(8,128)(2,1)S(1)}, u32[]{:S(2)}, u32[]{:S(2)}) %collective-permute-start.21) | collective-permute-done | bytes 262176 | tf_op jit(solution)/shard_map/ppermute | solution.py:40
  153.1 3.6 %collective-permute-done.23.v3 = bf16[256,512]{1,0:T(8,128)(2,1)S(1)} collective-permute-done((bf16[256,512]{1,0:T(8,128)(2,1)}, bf16[256,512]{1,0:T(8,128)(2,1)S(1)}, u32[]{:S(2)}, u32[]{:S(2)}) %collective-permute-start.23) | collective-permute-done | bytes 262176 | tf_op jit(solution)/shard_map/ppermute | solution.py:40
  158.9 4.4 %collective-permute-start.24 = (bf16[128,2048]{1,0:T(8,128)(2,1)S(1)}, bf16[128,2048]{1,0:T(8,128)(2,1)S(1)}, u32[]{:S(2)}, u32[]{:S(2)}) collective-permute-start(bf16[128,2048]{1,0:T(8,128)(2,1)S(1)} %get-tuple-element.35.e2), channel_id=1, source_target_pairs={{0,4},{1,5},{2,6},{3,7},{4,8},{5,9},{6,10},{7,11},{8,12},{9,13},{1... | collective-permute-start | bytes 1572872 | tf_op jit(solution)/shard_map/ppermute | solution.py:40
  163.4 2.4 %collective-permute-start.26 = (bf16[128,2048]{1,0:T(8,128)(2,1)S(1)}, bf16[128,2048]{1,0:T(8,128)(2,1)S(1)}, u32[]{:S(2)}, u32[]{:S(2)}) collective-permute-start(bf16[128,2048]{1,0:T(8,128)(2,1)S(1)} %get-tuple-element.37.e3), channel_id=1, source_target_pairs={{0,8},{1,9},{2,10},{3,11},{4,12},{5,13},{6,14},{7,15},{8,0},{9,1},... | collective-permute-start | bytes 1572872 | tf_op jit(solution)/shard_map/ppermute | solution.py:40
  167.0 7.0 %shard_map.155 = (f32[128,2048]{1,0:T(8,128)S(1)}, bf16[128,2048]{1,0:T(8,128)(2,1)S(1)}, bf16[128,2048]{1,0:T(8,128)(2,1)S(1)}, bf16[128,2048]{1,0:T(8,128)(2,1)S(1)}) custom-call(s32[16]{0:T(128)S(1)} %copy-done.4, bf16[128,2048]{1,0:T(8,128)(2,1)S(1)} %get-tuple-element.34.e0, bf16[128,2048]{1,0:T(8,128)(2,1)S(1)} %get-tuple-element.36.e1, ...), custom_call_target="tpu_custom_call" | custom-call | flops 4300000256 | bytes 14680064 | tf_op jit(solution)/shard_map/pallas_call | solution.py:235
  175.3 2.0 %collective-permute-start.28 = (bf16[128,2048]{1,0:T(8,128)(2,1)S(1)}, bf16[128,2048]{1,0:T(8,128)(2,1)S(1)}, u32[]{:S(2)}, u32[]{:S(2)}) collective-permute-start(bf16[128,2048]{1,0:T(8,128)(2,1)S(1)} %get-tuple-element.41), channel_id=1, source_target_pairs={{0,4},{1,5},{2,6},{3,7},{4,8},{5,9},{6,10},{7,11},{8,12},{9,13},{1... | collective-permute-start | bytes 1572872 | tf_op jit(solution)/shard_map/ppermute | solution.py:40
  178.5 2.0 shard_map.154
  180.6 4.3 %collective-permute-done.27 = bf16[128,2048]{1,0:T(8,128)(2,1)S(1)} collective-permute-done((bf16[128,2048]{1,0:T(8,128)(2,1)S(1)}, bf16[128,2048]{1,0:T(8,128)(2,1)S(1)}, u32[]{:S(2)}, u32[]{:S(2)}) %collective-permute-start.27) | collective-permute-done | bytes 524320 | tf_op jit(solution)/shard_map/ppermute | solution.py:40
  184.9 5.5 %collective-permute-done.28 = bf16[128,2048]{1,0:T(8,128)(2,1)S(1)} collective-permute-done((bf16[128,2048]{1,0:T(8,128)(2,1)S(1)}, bf16[128,2048]{1,0:T(8,128)(2,1)S(1)}, u32[]{:S(2)}, u32[]{:S(2)}) %collective-permute-start.28) | collective-permute-done | bytes 524320 | tf_op jit(solution)/shard_map/ppermute | solution.py:40
  (93 shorter events, 34.9 us)
Async XLA Ops:
  7.2 80.3 %all-gather.3.cloned.1.call-start = ((), (), s32[]{:S(2)}) async-start(), calls=%async_computation | async-start | bytes 4177920 | tf_op jit(solution)/shard_map/all_gather | solution.py:291
  7.9 130.7 %all-gather.5.cloned.1.call-start = ((), (), s32[]{:S(2)}) async-start(), calls=%async_computation.1 | async-start | bytes 5570560 | tf_op jit(solution)/shard_map/all_gather | solution.py:298
  10.5 6.8 %collective-permute-start = (bf16[16,5120]{1,0:T(8,128)(2,1)S(1)}, bf16[16,5120]{1,0:T(8,128)(2,1)S(1)}, u32[]{:S(2)}, u32[]{:S(2)}) collective-permute-start(bf16[16,5120]{1,0:T(8,128)(2,1)S(1)} %shard_map.149), channel_id=1, source_target_pairs={{0,1},{1,2},{2,3},{3,0},{4,5},{5,6},{6,7},{7,4},{8,9},{9,10},{10,1... | collective-permute-start | bytes 491528 | tf_op jit(solution)/shard_map/ppermute | solution.py:40
  12.1 5.3 %collective-permute-start.1 = (bf16[16,5120]{1,0:T(8,128)(2,1)S(1)}, bf16[16,5120]{1,0:T(8,128)(2,1)S(1)}, u32[]{:S(2)}, u32[]{:S(2)}) collective-permute-start(bf16[16,5120]{1,0:T(8,128)(2,1)S(1)} %shard_map.149), channel_id=1, source_target_pairs={{0,3},{1,0},{2,1},{3,2},{4,7},{5,4},{6,5},{7,6},{8,11},{9,8},{10,9... | collective-permute-start | bytes 491528 | tf_op jit(solution)/shard_map/ppermute | solution.py:40
  13.9 6.8 %collective-permute-start.2 = (bf16[16,5120]{1,0:T(8,128)(2,1)S(1)}, bf16[16,5120]{1,0:T(8,128)(2,1)S(1)}, u32[]{:S(2)}, u32[]{:S(2)}) collective-permute-start(bf16[16,5120]{1,0:T(8,128)(2,1)S(1)} %shard_map.149), channel_id=1, source_target_pairs={{0,2},{1,3},{2,0},{3,1},{4,6},{5,7},{6,4},{7,5},{8,10},{9,11},{10,... | collective-permute-start | bytes 491528 | tf_op jit(solution)/shard_map/ppermute | solution.py:40
  15.7 13.6 %collective-permute-start.17 = (bf16[320,512]{1,0:T(8,128)(2,1)}, bf16[320,512]{1,0:T(8,128)(2,1)S(1)}, u32[]{:S(2)}, u32[]{:S(2)}) collective-permute-start(bf16[320,512]{1,0:T(8,128)(2,1)} %param.21), channel_id=1, source_target_pairs={{0,0},{1,17},{2,34},{3,51},{4,68},{5,85},{6,102},{7,119},{8,136},{... | collective-permute-start | bytes 983048 | tf_op jit(solution)/shard_map/ppermute | solution.py:292
  20.7 21.2 %collective-permute-start.3 = (bf16[64,5120]{1,0:T(8,128)(2,1)S(1)}, bf16[64,5120]{1,0:T(8,128)(2,1)S(1)}, u32[]{:S(2)}, u32[]{:S(2)}) collective-permute-start(bf16[64,5120]{1,0:T(8,128)(2,1)S(1)} %pad_maximum_fusion.s0), channel_id=1, source_target_pairs={{0,4},{1,5},{2,6},{3,7},{4,8},{5,9},{6,10},{7,11},{8,12},{9,13},{1... | collective-permute-start | bytes 1966088 | tf_op jit(solution)/shard_map/ppermute | solution.py:40
  22.6 19.3 %collective-permute-start.4 = (bf16[64,5120]{1,0:T(8,128)(2,1)S(1)}, bf16[64,5120]{1,0:T(8,128)(2,1)}, u32[]{:S(2)}, u32[]{:S(2)}) collective-permute-start(bf16[64,5120]{1,0:T(8,128)(2,1)S(1)} %pad_maximum_fusion.s0), channel_id=1, source_target_pairs={{0,12},{1,13},{2,14},{3,15},{4,0},{5,1},{6,2},{7,3},{8,4},{9,5},{1... | collective-permute-start | bytes 1966088 | tf_op jit(solution)/shard_map/ppermute | solution.py:40
  26.3 17.1 %collective-permute-start.5 = (bf16[64,5120]{1,0:T(8,128)(2,1)S(1)}, bf16[64,5120]{1,0:T(8,128)(2,1)}, u32[]{:S(2)}, u32[]{:S(2)}) collective-permute-start(bf16[64,5120]{1,0:T(8,128)(2,1)S(1)} %pad_maximum_fusion.s0), channel_id=1, source_target_pairs={{0,8},{1,9},{2,10},{3,11},{4,12},{5,13},{6,14},{7,15},{8,0},{9,1},... | collective-permute-start | bytes 1966088 | tf_op jit(solution)/shard_map/ppermute | solution.py:40
  29.3 12.7 %collective-permute-start.18 = (bf16[320,512]{1,0:T(8,128)(2,1)S(1)}, bf16[320,512]{1,0:T(8,128)(2,1)}, u32[]{:S(2)}, u32[]{:S(2)}) collective-permute-start(bf16[320,512]{1,0:T(8,128)(2,1)S(1)} %collective-permute-done.17), channel_id=1, source_target_pairs={{0,0},{1,1},{2,2},{3,3},{4,4},{5,5},{6,6},{7,7},{8,8},{9,9},{10,10... | collective-permute-start | bytes 983048 | tf_op jit(solution)/shard_map/ppermute | solution.py:296
  43.3 44.1 %collective-permute-start.6 = (bf16[512,2048]{1,0:T(8,128)(2,1)}, bf16[512,2048]{1,0:T(8,128)(2,1)}, u32[]{:S(2)}, u32[]{:S(2)}) collective-permute-start(bf16[512,2048]{1,0:T(8,128)(2,1)} %w0), channel_id=1, source_target_pairs={{0,1},{1,2},{2,3},{3,0},{4,5},{5,6},{6,7},{7,4},{8,9},{9,10},{10,1... | collective-permute-start | bytes 6291464 | tf_op jit(solution)/shard_map/ppermute | solution.py:40
  43.4 44.0 %collective-permute-start.7 = (bf16[512,2048]{1,0:T(8,128)(2,1)}, bf16[512,2048]{1,0:T(8,128)(2,1)}, u32[]{:S(2)}, u32[]{:S(2)}) collective-permute-start(bf16[512,2048]{1,0:T(8,128)(2,1)} %w0), channel_id=1, source_target_pairs={{0,3},{1,0},{2,1},{3,2},{4,7},{5,4},{6,5},{7,6},{8,11},{9,8},{10,9... | collective-permute-start | bytes 6291464 | tf_op jit(solution)/shard_map/ppermute | solution.py:40
  49.8 26.3 %collective-permute-start.10 = (bf16[128,2048]{1,0:T(8,128)(2,1)}, bf16[128,2048]{1,0:T(8,128)(2,1)S(1)}, u32[]{:S(2)}, u32[]{:S(2)}) collective-permute-start(bf16[128,2048]{1,0:T(8,128)(2,1)} %get-tuple-element.27), channel_id=1, source_target_pairs={{0,8},{1,9},{2,10},{3,11},{4,12},{5,13},{6,14},{7,15},{8,0},{9,1},... | collective-permute-start | bytes 1572872 | tf_op jit(solution)/shard_map/ppermute | solution.py:40
  63.1 23.9 %collective-permute-start.8 = (bf16[128,2048]{1,0:T(8,128)(2,1)}, bf16[128,2048]{1,0:T(8,128)(2,1)S(1)}, u32[]{:S(2)}, u32[]{:S(2)}) collective-permute-start(bf16[128,2048]{1,0:T(8,128)(2,1)} %get-tuple-element.25), channel_id=1, source_target_pairs={{0,4},{1,5},{2,6},{3,7},{4,8},{5,9},{6,10},{7,11},{8,12},{9,13},{1... | collective-permute-start | bytes 1572872 | tf_op jit(solution)/shard_map/ppermute | solution.py:40
  63.1 24.3 %collective-permute-start.9 = (bf16[128,2048]{1,0:T(8,128)(2,1)S(1)}, bf16[128,2048]{1,0:T(8,128)(2,1)S(1)}, u32[]{:S(2)}, u32[]{:S(2)}) collective-permute-start(bf16[128,2048]{1,0:T(8,128)(2,1)S(1)} %get-tuple-element.26), channel_id=1, source_target_pairs={{0,12},{1,13},{2,14},{3,15},{4,0},{5,1},{6,2},{7,3},{8,4},{9,5},{1... | collective-permute-start | bytes 1572872 | tf_op jit(solution)/shard_map/ppermute | solution.py:40
  93.1 7.2 %collective-permute-start.11 = (bf16[256,320]{1,0:T(8,128)(2,1)}, bf16[256,320]{1,0:T(8,128)(2,1)S(1)}, u32[]{:S(2)}, u32[]{:S(2)}) collective-permute-start(bf16[256,320]{1,0:T(8,128)(2,1)} %shard_map.151), channel_id=1, source_target_pairs={{0,1},{1,2},{2,3},{3,0},{4,5},{5,6},{6,7},{7,4},{8,9},{9,10},{10,1... | collective-permute-start | bytes 491528 | tf_op jit(solution)/shard_map/ppermute | solution.py:40
  93.3 8.6 %collective-permute-start.12 = (bf16[256,320]{1,0:T(8,128)(2,1)}, bf16[256,320]{1,0:T(8,128)(2,1)S(1)}, u32[]{:S(2)}, u32[]{:S(2)}) collective-permute-start(bf16[256,320]{1,0:T(8,128)(2,1)} %shard_map.151), channel_id=1, source_target_pairs={{0,3},{1,0},{2,1},{3,2},{4,7},{5,4},{6,5},{7,6},{8,11},{9,8},{10,9... | collective-permute-start | bytes 491528 | tf_op jit(solution)/shard_map/ppermute | solution.py:40
  96.4 7.4 %collective-permute-start.13 = (bf16[256,320]{1,0:T(8,128)(2,1)}, bf16[256,320]{1,0:T(8,128)(2,1)S(1)}, u32[]{:S(2)}, u32[]{:S(2)}) collective-permute-start(bf16[256,320]{1,0:T(8,128)(2,1)} %shard_map.151), channel_id=1, source_target_pairs={{0,2},{1,3},{2,0},{3,1},{4,6},{5,7},{6,4},{7,5},{8,10},{9,11},{10,... | collective-permute-start | bytes 491528 | tf_op jit(solution)/shard_map/ppermute | solution.py:40
  106.6 21.5 %collective-permute-start.19 = (bf16[256,2048]{1,0:T(8,128)(2,1)S(1)}, bf16[256,2048]{1,0:T(8,128)(2,1)S(1)}, u32[]{:S(2)}, u32[]{:S(2)}) collective-permute-start(bf16[256,2048]{1,0:T(8,128)(2,1)S(1)} %slice.9), channel_id=1, source_target_pairs={{0,1},{1,2},{2,3},{3,0},{4,5},{5,6},{6,7},{7,4},{8,9},{9,10},{10,1... | collective-permute-start | bytes 3145736 | tf_op jit(solution)/shard_map/ppermute | solution.py:40
  108.0 29.7 %collective-permute-start.20 = (bf16[256,2048]{1,0:T(8,128)(2,1)S(1)}, bf16[256,2048]{1,0:T(8,128)(2,1)S(1)}, u32[]{:S(2)}, u32[]{:S(2)}) collective-permute-start(bf16[256,2048]{1,0:T(8,128)(2,1)S(1)} %slice.10), channel_id=1, source_target_pairs={{0,3},{1,0},{2,1},{3,2},{4,7},{5,4},{6,5},{7,6},{8,11},{9,8},{10,9... | collective-permute-start | bytes 3145736 | tf_op jit(solution)/shard_map/ppermute | solution.py:40
  111.3 27.4 %collective-permute-start.14 = (bf16[256,1280]{1,0:T(8,128)(2,1)S(1)}, bf16[256,1280]{1,0:T(8,128)(2,1)}, u32[]{:S(2)}, u32[]{:S(2)}) collective-permute-start(bf16[256,1280]{1,0:T(8,128)(2,1)S(1)} %concatenate.7.h0), channel_id=1, source_target_pairs={{0,4},{1,5},{2,6},{3,7},{4,8},{5,9},{6,10},{7,11},{8,12},{9,13},{1... | collective-permute-start | bytes 1966088 | tf_op jit(solution)/shard_map/ppermute | solution.py:40
  115.8 23.4 %collective-permute-start.15 = (bf16[256,1280]{1,0:T(8,128)(2,1)S(1)}, bf16[256,1280]{1,0:T(8,128)(2,1)}, u32[]{:S(2)}, u32[]{:S(2)}) collective-permute-start(bf16[256,1280]{1,0:T(8,128)(2,1)S(1)} %concatenate.7.h0), channel_id=1, source_target_pairs={{0,12},{1,13},{2,14},{3,15},{4,0},{5,1},{6,2},{7,3},{8,4},{9,5},{1... | collective-permute-start | bytes 1966088 | tf_op jit(solution)/shard_map/ppermute | solution.py:40
  118.8 20.4 %collective-permute-start.16 = (bf16[256,1280]{1,0:T(8,128)(2,1)S(1)}, bf16[256,1280]{1,0:T(8,128)(2,1)}, u32[]{:S(2)}, u32[]{:S(2)}) collective-permute-start(bf16[256,1280]{1,0:T(8,128)(2,1)S(1)} %concatenate.7.h0), channel_id=1, source_target_pairs={{0,8},{1,9},{2,10},{3,11},{4,12},{5,13},{6,14},{7,15},{8,0},{9,1},... | collective-permute-start | bytes 1966088 | tf_op jit(solution)/shard_map/ppermute | solution.py:40
  144.5 7.9 %collective-permute-start.21 = (bf16[256,512]{1,0:T(8,128)(2,1)}, bf16[256,512]{1,0:T(8,128)(2,1)S(1)}, u32[]{:S(2)}, u32[]{:S(2)}) collective-permute-start(bf16[256,512]{1,0:T(8,128)(2,1)} %shard_map.152.v0), channel_id=1, source_target_pairs={{0,1},{1,2},{2,3},{3,0},{4,5},{5,6},{6,7},{7,4},{8,9},{9,10},{10,1... | collective-permute-start | bytes 786440 | tf_op jit(solution)/shard_map/ppermute | solution.py:40
  146.5 6.6 %collective-permute-start.22 = (bf16[256,512]{1,0:T(8,128)(2,1)}, bf16[256,512]{1,0:T(8,128)(2,1)S(1)}, u32[]{:S(2)}, u32[]{:S(2)}) collective-permute-start(bf16[256,512]{1,0:T(8,128)(2,1)} %shard_map.152.v0), channel_id=1, source_target_pairs={{0,3},{1,0},{2,1},{3,2},{4,7},{5,4},{6,5},{7,6},{8,11},{9,8},{10,9... | collective-permute-start | bytes 786440 | tf_op jit(solution)/shard_map/ppermute | solution.py:40
  148.0 8.7 %collective-permute-start.23 = (bf16[256,512]{1,0:T(8,128)(2,1)}, bf16[256,512]{1,0:T(8,128)(2,1)S(1)}, u32[]{:S(2)}, u32[]{:S(2)}) collective-permute-start(bf16[256,512]{1,0:T(8,128)(2,1)} %shard_map.152.v0), channel_id=1, source_target_pairs={{0,2},{1,3},{2,0},{3,1},{4,6},{5,7},{6,4},{7,5},{8,10},{9,11},{10,... | collective-permute-start | bytes 786440 | tf_op jit(solution)/shard_map/ppermute | solution.py:40
  158.9 18.4 %collective-permute-start.24 = (bf16[128,2048]{1,0:T(8,128)(2,1)S(1)}, bf16[128,2048]{1,0:T(8,128)(2,1)S(1)}, u32[]{:S(2)}, u32[]{:S(2)}) collective-permute-start(bf16[128,2048]{1,0:T(8,128)(2,1)S(1)} %get-tuple-element.35.e2), channel_id=1, source_target_pairs={{0,4},{1,5},{2,6},{3,7},{4,8},{5,9},{6,10},{7,11},{8,12},{9,13},{1... | collective-permute-start | bytes 1572872 | tf_op jit(solution)/shard_map/ppermute | solution.py:40
  163.4 15.2 %collective-permute-start.25 = (bf16[128,2048]{1,0:T(8,128)(2,1)S(1)}, bf16[128,2048]{1,0:T(8,128)(2,1)S(1)}, u32[]{:S(2)}, u32[]{:S(2)}) collective-permute-start(bf16[128,2048]{1,0:T(8,128)(2,1)S(1)} %get-tuple-element.36.e1), channel_id=1, source_target_pairs={{0,12},{1,13},{2,14},{3,15},{4,0},{5,1},{6,2},{7,3},{8,4},{9,5},{1... | collective-permute-start | bytes 1572872 | tf_op jit(solution)/shard_map/ppermute | solution.py:40
  163.4 15.2 %collective-permute-start.26 = (bf16[128,2048]{1,0:T(8,128)(2,1)S(1)}, bf16[128,2048]{1,0:T(8,128)(2,1)S(1)}, u32[]{:S(2)}, u32[]{:S(2)}) collective-permute-start(bf16[128,2048]{1,0:T(8,128)(2,1)S(1)} %get-tuple-element.37.e3), channel_id=1, source_target_pairs={{0,8},{1,9},{2,10},{3,11},{4,12},{5,13},{6,14},{7,15},{8,0},{9,1},... | collective-permute-start | bytes 1572872 | tf_op jit(solution)/shard_map/ppermute | solution.py:40
  174.0 10.9 %collective-permute-start.27 = (bf16[128,2048]{1,0:T(8,128)(2,1)S(1)}, bf16[128,2048]{1,0:T(8,128)(2,1)S(1)}, u32[]{:S(2)}, u32[]{:S(2)}) collective-permute-start(bf16[128,2048]{1,0:T(8,128)(2,1)S(1)} %get-tuple-element.40), channel_id=1, source_target_pairs={{0,8},{1,9},{2,10},{3,11},{4,12},{5,13},{6,14},{7,15},{8,0},{9,1},... | collective-permute-start | bytes 1572872 | tf_op jit(solution)/shard_map/ppermute | solution.py:40
  175.3 15.1 %collective-permute-start.28 = (bf16[128,2048]{1,0:T(8,128)(2,1)S(1)}, bf16[128,2048]{1,0:T(8,128)(2,1)S(1)}, u32[]{:S(2)}, u32[]{:S(2)}) collective-permute-start(bf16[128,2048]{1,0:T(8,128)(2,1)S(1)} %get-tuple-element.41), channel_id=1, source_target_pairs={{0,4},{1,5},{2,6},{3,7},{4,8},{5,9},{6,10},{7,11},{8,12},{9,13},{1... | collective-permute-start | bytes 1572872 | tf_op jit(solution)/shard_map/ppermute | solution.py:40
  177.3 13.1 %collective-permute-start.29 = (bf16[128,2048]{1,0:T(8,128)(2,1)S(1)}, bf16[128,2048]{1,0:T(8,128)(2,1)S(1)}, u32[]{:S(2)}, u32[]{:S(2)}) collective-permute-start(bf16[128,2048]{1,0:T(8,128)(2,1)S(1)} %get-tuple-element.42), channel_id=1, source_target_pairs={{0,12},{1,13},{2,14},{3,15},{4,0},{5,1},{6,2},{7,3},{8,4},{9,5},{1... | collective-permute-start | bytes 1572872 | tf_op jit(solution)/shard_map/ppermute | solution.py:40
  (20 other events, 217.4 us)
Sparse Core Ops, SparseCore 0:
  9.8 44.0 all-gather.2
  55.8 51.2 all-gather.4

commit v3 on v2

--- a/solution.py
+++ b/solution.py
@@ -295,20 +295,22 @@
     near = jnp.concatenate([merged, *around(merged, 1)], axis=0)
     down_part = lax.ppermute(after(down_part, near), ("enc", "mb", "tp"), TURN)
     group = (near, *around(near, 2))
-    down_full = lax.all_gather(after(down_part, *group), ("enc", "mb"), axis=0, tiled=True)
-
     kv_weight = after(kv_weight, near)
     kv_right, kv_left = hop(kv_weight, 1, 1), hop(kv_weight, 1, -1)
-    own, to_left, to_right, to_far = pack(tab, text_embed[0, 0])
-    text = (own, hop(to_right, 2, 1), hop(to_left, 2, -1), hop(to_far, 2, 2))
-
-    up_full = after(up_full, kv_right, kv_left, *text)
+    down_part = after(down_part, *group, kv_right, kv_left)
+    down_full = lax.all_gather(down_part, ("enc", "mb"), axis=0, tiled=True)
+    far_right, far_left = kv_right[:256], kv_left[256:]
+
+    up_full, far_right, far_left = lax.optimization_barrier((up_full, far_right, far_left))
     hidden = up(tab, group, up_full, up_bias.reshape(16, 1, 320))
     near = jnp.concatenate([hidden, *around(hidden, 1)], axis=1)
-    right, left = lax.optimization_barrier((kv_right, kv_left, near))[:2]
-    weights = (kv_weight, kv_right, kv_left, hop(right[:256], 1, 1), hop(left[256:], 1, -1))
+    far_right, far_left = lax.optimization_barrier((far_right, far_left, near))[:2]
+    weights = (kv_weight, kv_right, kv_left, hop(far_right, 1, 1), hop(far_left, 1, -1))
+    own, to_left, to_right, to_far = pack(tab, text_embed[0, 0])
     units = (near, *around(near, 2))
-    down_full = after(down_full, weights[3], weights[4])
+    to_left, to_right, to_far = lax.optimization_barrier((to_left, to_right, to_far, *units[1:3]))[:3]
+    text = (own, hop(to_right, 2, 1), hop(to_left, 2, -1), hop(to_far, 2, 2))
+    down_full = after(down_full, weights[3], weights[4], *text)
     visual = down(tab, units, down_full, down_bias.reshape(16, 1, 512))
     visual = (visual, *around(visual, 1))
 

time: 202 us -> 222 us (1.099)
  the two profiles are of different devices: /device:TPU:32 before, /device:TPU:134 now
where the time goes in v3:
time: 222 us
  waiting for transfers between devices  93.3 us (42%)
  starting transfers between devices  74.3 us (33%)
  Pallas kernels  22.9 us (10%)
  local copies, waits for them, and re-layouts  15.8 us (7%)
  between operations  14.3 us (6%)
    ppermute x28, waiting for transfers between devices, hop(): return lax.ppermute(value, ('mb', 'tp'), HOPS[which, step])  74.6 us
    ppermute x28, starting transfers between devices, hop(): return lax.ppermute(value, ('mb', 'tp'), HOPS[which, step])  57.5 us
    ppermute x1, waiting for transfers between devices, per_device(): down_part = lax.ppermute(down_weight, ('enc', 'mb', 'tp'), SHUFFLE)  15.4 us
    ppermute x1, starting transfers between devices, per_device(): down_part = lax.ppermute(after(down_part, near), ('enc', 'mb', 'tp'), TURN)  13.8 us
    unnamed x50, local copies, waits for them, and re-layouts  8.94 us
    pallas_call x1, Pallas kernels, product(): pl.pallas_call(product_kernel, out_shape=[jax.ShapeDtypeStruct((128, 2048...  7 us
    pallas_call x1, Pallas kernels, up(): pl.pallas_call(up_kernel, out_shape=jax.ShapeDtypeStruct((256, 320), BF16...  5.69 us
    pallas_call x1, Pallas kernels, down(): pl.pallas_call(down_kernel, out_shape=jax.ShapeDtypeStruct((256, 512), BF...  5.45 us
  transfers between devices with their start and end apart: 32, of which 21 were waited for; matrix products, arithmetic and copies ran while one was open for 3% of the time, Pallas kernels for 7%

profile of v3, /device:TPU:134, one launch (start us, length us, event | category | flops | bytes accessed | tf_op | source)
XLA Modules:
  0.0 221.9 jit_solution(17550323143679824392)
XLA Ops:
  21.6 3.0 %collective-permute-start.14 = (bf16[320,512]{1,0:T(8,128)(2,1)}, bf16[320,512]{1,0:T(8,128)(2,1)S(1)}, u32[]{:S(2)}, u32[]{:S(2)}) collective-permute-start(bf16[320,512]{1,0:T(8,128)(2,1)} %param.21), channel_id=1, source_target_pairs={{0,0},{1,17},{2,34},{3,51},{4,68},{5,85},{6,102},{7,119},{8,136},{... | collective-permute-start | bytes 983048 | tf_op jit(solution)/shard_map/ppermute | solution.py:292
  24.6 15.4 %collective-permute-done.14 = bf16[320,512]{1,0:T(8,128)(2,1)S(1)} collective-permute-done((bf16[320,512]{1,0:T(8,128)(2,1)}, bf16[320,512]{1,0:T(8,128)(2,1)S(1)}, u32[]{:S(2)}, u32[]{:S(2)}) %collective-permute-start.14) | collective-permute-done | bytes 327712 | tf_op jit(solution)/shard_map/ppermute | solution.py:292
  40.0 13.8 %collective-permute-start.15 = (bf16[320,512]{1,0:T(8,128)(2,1)S(1)}, bf16[320,512]{1,0:T(8,128)(2,1)}, u32[]{:S(2)}, u32[]{:S(2)}) collective-permute-start(bf16[320,512]{1,0:T(8,128)(2,1)S(1)} %collective-permute-done.14), channel_id=1, source_target_pairs={{0,0},{1,1},{2,2},{3,3},{4,4},{5,5},{6,6},{7,7},{8,8},{9,9},{10,10... | collective-permute-start | bytes 983048 | tf_op jit(solution)/shard_map/ppermute | solution.py:296
  53.9 3.2 %collective-permute-start.4 = (bf16[64,5120]{1,0:T(8,128)(2,1)S(1)}, bf16[64,5120]{1,0:T(8,128)(2,1)}, u32[]{:S(2)}, u32[]{:S(2)}) collective-permute-start(bf16[64,5120]{1,0:T(8,128)(2,1)S(1)} %pad_maximum_fusion.s0), channel_id=1, source_target_pairs={{0,12},{1,13},{2,14},{3,15},{4,0},{5,1},{6,2},{7,3},{8,4},{9,5},{1... | collective-permute-start | bytes 1966088 | tf_op jit(solution)/shard_map/ppermute | solution.py:40
  57.1 2.6 %collective-permute-done.15 = bf16[320,512]{1,0:T(8,128)(2,1)} collective-permute-done((bf16[320,512]{1,0:T(8,128)(2,1)S(1)}, bf16[320,512]{1,0:T(8,128)(2,1)}, u32[]{:S(2)}, u32[]{:S(2)}) %collective-permute-start.15) | collective-permute-done | bytes 327712 | tf_op jit(solution)/shard_map/ppermute | solution.py:296
  59.7 3.4 %collective-permute-start.5 = (bf16[64,5120]{1,0:T(8,128)(2,1)S(1)}, bf16[64,5120]{1,0:T(8,128)(2,1)S(1)}, u32[]{:S(2)}, u32[]{:S(2)}) collective-permute-start(bf16[64,5120]{1,0:T(8,128)(2,1)S(1)} %pad_maximum_fusion.s0), channel_id=1, source_target_pairs={{0,8},{1,9},{2,10},{3,11},{4,12},{5,13},{6,14},{7,15},{8,0},{9,1},... | collective-permute-start | bytes 1966088 | tf_op jit(solution)/shard_map/ppermute | solution.py:40
  63.1 3.4 %collective-permute-done.3.s1 = bf16[64,5120]{1,0:T(8,128)(2,1)S(1)} collective-permute-done((bf16[64,5120]{1,0:T(8,128)(2,1)S(1)}, bf16[64,5120]{1,0:T(8,128)(2,1)S(1)}, u32[]{:S(2)}, u32[]{:S(2)}) %collective-permute-start.3) | collective-permute-done | bytes 655392 | tf_op jit(solution)/shard_map/ppermute | solution.py:40
  66.8 6.7 %collective-permute-done.5.s3 = bf16[64,5120]{1,0:T(8,128)(2,1)S(1)} collective-permute-done((bf16[64,5120]{1,0:T(8,128)(2,1)S(1)}, bf16[64,5120]{1,0:T(8,128)(2,1)S(1)}, u32[]{:S(2)}, u32[]{:S(2)}) %collective-permute-start.5) | collective-permute-done | bytes 655392 | tf_op jit(solution)/shard_map/ppermute | solution.py:40
  77.5 2.4 %slice.13 = bf16[256,2048]{1,0:T(8,128)(2,1)} slice(bf16[512,2048]{1,0:T(8,128)(2,1)} %collective-permute-done.7.w2), slice={[256:512], [0:2048]} | slice | bytes 2097152 | tf_op jit(solution)/shard_map/slice | solution.py:302
  79.9 5.7 %shard_map.150 = bf16[256,320]{1,0:T(8,128)(2,1)} custom-call(s32[16]{0:T(128)} %dynamic-slice_bitcast_fusion.tab, bf16[64,5120]{1,0:T(8,128)(2,1)} %copy-done.16, bf16[64,5120]{1,0:T(8,128)(2,1)} %copy-done.19, bf16[64,5120]{1,0:T(8,128)(2,1)} %collective-permute-done.4.s2, bf16[64,5120]{1,0:T(8,128)(2,1)} %copy-done.20, ...), custom_call_target="tpu_custom_call" | custom-call | flops 840000000 | bytes 6291456 | tf_op jit(solution)/shard_map/pallas_call | solution.py:137
  85.6 2.7 %collective-permute-start.10 = (bf16[256,320]{1,0:T(8,128)(2,1)}, bf16[256,320]{1,0:T(8,128)(2,1)S(1)}, u32[]{:S(2)}, u32[]{:S(2)}) collective-permute-start(bf16[256,320]{1,0:T(8,128)(2,1)} %shard_map.150), channel_id=1, source_target_pairs={{0,2},{1,3},{2,0},{3,1},{4,6},{5,7},{6,4},{7,5},{8,10},{9,11},{10,... | collective-permute-start | bytes 491528 | tf_op jit(solution)/shard_map/ppermute | solution.py:40
  90.3 2.7 %collective-permute-done.10 = bf16[256,320]{1,0:T(8,128)(2,1)S(1)} collective-permute-done((bf16[256,320]{1,0:T(8,128)(2,1)}, bf16[256,320]{1,0:T(8,128)(2,1)S(1)}, u32[]{:S(2)}, u32[]{:S(2)}) %collective-permute-start.10) | collective-permute-done | bytes 163872 | tf_op jit(solution)/shard_map/ppermute | solution.py:40
  94.2 2.0 collective-permute-done.9
  99.3 2.1 collective-permute-start.12
  102.8 2.8 %collective-permute-start.13 = (bf16[256,1280]{1,0:T(8,128)(2,1)S(1)}, bf16[256,1280]{1,0:T(8,128)(2,1)}, u32[]{:S(2)}, u32[]{:S(2)}) collective-permute-start(bf16[256,1280]{1,0:T(8,128)(2,1)S(1)} %concatenate.7.h0), channel_id=1, source_target_pairs={{0,8},{1,9},{2,10},{3,11},{4,12},{5,13},{6,14},{7,15},{8,0},{9,1},... | collective-permute-start | bytes 1966088 | tf_op jit(solution)/shard_map/ppermute | solution.py:40
  106.9 15.2 %collective-permute-done.11.h1 = bf16[256,1280]{1,0:T(8,128)(2,1)S(1)} collective-permute-done((bf16[256,1280]{1,0:T(8,128)(2,1)S(1)}, bf16[256,1280]{1,0:T(8,128)(2,1)S(1)}, u32[]{:S(2)}, u32[]{:S(2)}) %collective-permute-start.11) | collective-permute-done | bytes 655392 | tf_op jit(solution)/shard_map/ppermute | solution.py:40
  123.4 3.8 %collective-permute-start.19 = (bf16[128,2048]{1,0:T(8,128)(2,1)S(1)}, bf16[128,2048]{1,0:T(8,128)(2,1)S(1)}, u32[]{:S(2)}, u32[]{:S(2)}) collective-permute-start(bf16[128,2048]{1,0:T(8,128)(2,1)S(1)} %get-tuple-element.41), channel_id=1, source_target_pairs={{0,12},{1,13},{2,14},{3,15},{4,0},{5,1},{6,2},{7,3},{8,4},{9,5},{1... | collective-permute-start | bytes 1572872 | tf_op jit(solution)/shard_map/ppermute | solution.py:40
  127.3 5.1 %collective-permute-done.16.w3a = bf16[256,2048]{1,0:T(8,128)(2,1)S(1)} collective-permute-done((bf16[256,2048]{1,0:T(8,128)(2,1)}, bf16[256,2048]{1,0:T(8,128)(2,1)S(1)}, u32[]{:S(2)}, u32[]{:S(2)}) %collective-permute-start.16) | collective-permute-done | bytes 1048608 | tf_op jit(solution)/shard_map/ppermute | solution.py:40
  133.4 2.3 %collective-permute-done.17.w3b = bf16[256,2048]{1,0:T(8,128)(2,1)S(1)} collective-permute-done((bf16[256,2048]{1,0:T(8,128)(2,1)}, bf16[256,2048]{1,0:T(8,128)(2,1)S(1)}, u32[]{:S(2)}, u32[]{:S(2)}) %collective-permute-start.17) | collective-permute-done | bytes 1048608 | tf_op jit(solution)/shard_map/ppermute | solution.py:40
  136.6 7.4 %collective-permute-done.20.refs_3_ = bf16[128,2048]{1,0:T(8,128)(2,1)S(1)} collective-permute-done((bf16[128,2048]{1,0:T(8,128)(2,1)S(1)}, bf16[128,2048]{1,0:T(8,128)(2,1)S(1)}, u32[]{:S(2)}, u32[]{:S(2)}) %collective-permute-start.20) | collective-permute-done | bytes 524320 | tf_op jit(solution)/shard_map/ppermute | solution.py:40
  144.1 5.4 %shard_map.152.v0 = bf16[256,512]{1,0:T(8,128)(2,1)} custom-call(s32[16]{0:T(128)} %dynamic-slice_bitcast_fusion.tab, bf16[256,1280]{1,0:T(8,128)(2,1)} %copy-done.15, bf16[256,1280]{1,0:T(8,128)(2,1)} %copy-done.17, bf16[256,1280]{1,0:T(8,128)(2,1)} %copy-done.18, bf16[256,1280]{1,0:T(8,128)(2,1)} %collective-permute-done.13.h3, ...), custom_call_target="tpu_custom_call" | custom-call | flops 1340000000 | bytes 8388608 | tf_op jit(solution)/shard_map/pallas_call | solution.py:170
  149.5 4.7 %collective-permute-start.21 = (bf16[256,512]{1,0:T(8,128)(2,1)}, bf16[256,512]{1,0:T(8,128)(2,1)S(1)}, u32[]{:S(2)}, u32[]{:S(2)}) collective-permute-start(bf16[256,512]{1,0:T(8,128)(2,1)} %shard_map.152.v0), channel_id=1, source_target_pairs={{0,1},{1,2},{2,3},{3,0},{4,5},{5,6},{6,7},{7,4},{8,9},{9,10},{10,1... | collective-permute-start | bytes 786440 | tf_op jit(solution)/shard_map/ppermute | solution.py:40
  156.0 6.8 %collective-permute-done.21.v1 = bf16[256,512]{1,0:T(8,128)(2,1)S(1)} collective-permute-done((bf16[256,512]{1,0:T(8,128)(2,1)}, bf16[256,512]{1,0:T(8,128)(2,1)S(1)}, u32[]{:S(2)}, u32[]{:S(2)}) %collective-permute-start.21) | collective-permute-done | bytes 262176 | tf_op jit(solution)/shard_map/ppermute | solution.py:40
  162.8 3.8 %collective-permute-done.22.v2 = bf16[256,512]{1,0:T(8,128)(2,1)S(1)} collective-permute-done((bf16[256,512]{1,0:T(8,128)(2,1)}, bf16[256,512]{1,0:T(8,128)(2,1)S(1)}, u32[]{:S(2)}, u32[]{:S(2)}) %collective-permute-start.22) | collective-permute-done | bytes 262176 | tf_op jit(solution)/shard_map/ppermute | solution.py:40
  166.5 2.3 %collective-permute-done.23.v3 = bf16[256,512]{1,0:T(8,128)(2,1)S(1)} collective-permute-done((bf16[256,512]{1,0:T(8,128)(2,1)}, bf16[256,512]{1,0:T(8,128)(2,1)S(1)}, u32[]{:S(2)}, u32[]{:S(2)}) %collective-permute-start.23) | collective-permute-done | bytes 262176 | tf_op jit(solution)/shard_map/ppermute | solution.py:40
  171.0 12.0 %collective-permute-start.24 = (bf16[128,2048]{1,0:T(8,128)(2,1)S(1)}, bf16[128,2048]{1,0:T(8,128)(2,1)S(1)}, u32[]{:S(2)}, u32[]{:S(2)}) collective-permute-start(bf16[128,2048]{1,0:T(8,128)(2,1)S(1)} %get-tuple-element.45.e2), channel_id=1, source_target_pairs={{0,4},{1,5},{2,6},{3,7},{4,8},{5,9},{6,10},{7,11},{8,12},{9,13},{1... | collective-permute-start | bytes 1572872 | tf_op jit(solution)/shard_map/ppermute | solution.py:40
  183.0 3.3 %collective-permute-start.25 = (bf16[128,2048]{1,0:T(8,128)(2,1)S(1)}, bf16[128,2048]{1,0:T(8,128)(2,1)S(1)}, u32[]{:S(2)}, u32[]{:S(2)}) collective-permute-start(bf16[128,2048]{1,0:T(8,128)(2,1)S(1)} %get-tuple-element.46.e1), channel_id=1, source_target_pairs={{0,12},{1,13},{2,14},{3,15},{4,0},{5,1},{6,2},{7,3},{8,4},{9,5},{1... | collective-permute-start | bytes 1572872 | tf_op jit(solution)/shard_map/ppermute | solution.py:40
  190.5 7.0 %shard_map.155 = (f32[128,2048]{1,0:T(8,128)S(1)}, bf16[128,2048]{1,0:T(8,128)(2,1)S(1)}, bf16[128,2048]{1,0:T(8,128)(2,1)S(1)}, bf16[128,2048]{1,0:T(8,128)(2,1)S(1)}) custom-call(s32[16]{0:T(128)S(1)} %copy-done.6, bf16[128,2048]{1,0:T(8,128)(2,1)S(1)} %get-tuple-element.44.e0, bf16[128,2048]{1,0:T(8,128)(2,1)S(1)} %get-tuple-element.46.e1, ...), custom_call_target="tpu_custom_call" | custom-call | flops 4300000256 | bytes 14680064 | tf_op jit(solution)/shard_map/pallas_call | solution.py:235
  197.5 2.2 %collective-permute-start.27 = (bf16[128,2048]{1,0:T(8,128)(2,1)S(1)}, bf16[128,2048]{1,0:T(8,128)(2,1)S(1)}, u32[]{:S(2)}, u32[]{:S(2)}) collective-permute-start(bf16[128,2048]{1,0:T(8,128)(2,1)S(1)} %get-tuple-element.50), channel_id=1, source_target_pairs={{0,8},{1,9},{2,10},{3,11},{4,12},{5,13},{6,14},{7,15},{8,0},{9,1},... | collective-permute-start | bytes 1572872 | tf_op jit(solution)/shard_map/ppermute | solution.py:40
  199.8 3.2 %collective-permute-start.29 = (bf16[128,2048]{1,0:T(8,128)(2,1)S(1)}, bf16[128,2048]{1,0:T(8,128)(2,1)S(1)}, u32[]{:S(2)}, u32[]{:S(2)}) collective-permute-start(bf16[128,2048]{1,0:T(8,128)(2,1)S(1)} %get-tuple-element.52), channel_id=1, source_target_pairs={{0,12},{1,13},{2,14},{3,15},{4,0},{5,1},{6,2},{7,3},{8,4},{9,5},{1... | collective-permute-start | bytes 1572872 | tf_op jit(solution)/shard_map/ppermute | solution.py:40
  205.1 3.3 %collective-permute-done.27 = bf16[128,2048]{1,0:T(8,128)(2,1)S(1)} collective-permute-done((bf16[128,2048]{1,0:T(8,128)(2,1)S(1)}, bf16[128,2048]{1,0:T(8,128)(2,1)S(1)}, u32[]{:S(2)}, u32[]{:S(2)}) %collective-permute-start.27) | collective-permute-done | bytes 524320 | tf_op jit(solution)/shard_map/ppermute | solution.py:40
  208.4 5.5 %collective-permute-done.28 = bf16[128,2048]{1,0:T(8,128)(2,1)S(1)} collective-permute-done((bf16[128,2048]{1,0:T(8,128)(2,1)S(1)}, bf16[128,2048]{1,0:T(8,128)(2,1)S(1)}, u32[]{:S(2)}, u32[]{:S(2)}) %collective-permute-start.28) | collective-permute-done | bytes 524320 | tf_op jit(solution)/shard_map/ppermute | solution.py:40
  (103 shorter events, 42.3 us)
Async XLA Ops:
  7.2 72.7 %all-gather.3.cloned.1.call-start = ((), (), s32[]{:S(2)}) async-start(), calls=%async_computation | async-start | bytes 4177920 | tf_op jit(solution)/shard_map/all_gather | solution.py:291
  7.9 136.1 %all-gather.5.cloned.1.call-start = ((), (), s32[]{:S(2)}) async-start(), calls=%async_computation.1 | async-start | bytes 5570560 | tf_op jit(solution)/shard_map/all_gather | solution.py:301
  10.5 5.4 %collective-permute-start = (bf16[16,5120]{1,0:T(8,128)(2,1)S(1)}, bf16[16,5120]{1,0:T(8,128)(2,1)S(1)}, u32[]{:S(2)}, u32[]{:S(2)}) collective-permute-start(bf16[16,5120]{1,0:T(8,128)(2,1)S(1)} %shard_map.149), channel_id=1, source_target_pairs={{0,1},{1,2},{2,3},{3,0},{4,5},{5,6},{6,7},{7,4},{8,9},{9,10},{10,1... | collective-permute-start | bytes 491528 | tf_op jit(solution)/shard_map/ppermute | solution.py:40
  11.1 6.5 %collective-permute-start.1 = (bf16[16,5120]{1,0:T(8,128)(2,1)S(1)}, bf16[16,5120]{1,0:T(8,128)(2,1)S(1)}, u32[]{:S(2)}, u32[]{:S(2)}) collective-permute-start(bf16[16,5120]{1,0:T(8,128)(2,1)S(1)} %shard_map.149), channel_id=1, source_target_pairs={{0,3},{1,0},{2,1},{3,2},{4,7},{5,4},{6,5},{7,6},{8,11},{9,8},{10,9... | collective-permute-start | bytes 491528 | tf_op jit(solution)/shard_map/ppermute | solution.py:40
  12.6 6.8 %collective-permute-start.2 = (bf16[16,5120]{1,0:T(8,128)(2,1)S(1)}, bf16[16,5120]{1,0:T(8,128)(2,1)S(1)}, u32[]{:S(2)}, u32[]{:S(2)}) collective-permute-start(bf16[16,5120]{1,0:T(8,128)(2,1)S(1)} %shard_map.149), channel_id=1, source_target_pairs={{0,2},{1,3},{2,0},{3,1},{4,6},{5,7},{6,4},{7,5},{8,10},{9,11},{10,... | collective-permute-start | bytes 491528 | tf_op jit(solution)/shard_map/ppermute | solution.py:40
  19.5 54.0 %collective-permute-start.6 = (bf16[512,2048]{1,0:T(8,128)(2,1)}, bf16[512,2048]{1,0:T(8,128)(2,1)S(1)}, u32[]{:S(2)}, u32[]{:S(2)}) collective-permute-start(bf16[512,2048]{1,0:T(8,128)(2,1)} %w0), channel_id=1, source_target_pairs={{0,1},{1,2},{2,3},{3,0},{4,5},{5,6},{6,7},{7,4},{8,9},{9,10},{10,1... | collective-permute-start | bytes 6291464 | tf_op jit(solution)/shard_map/ppermute | solution.py:40
  21.3 53.1 %collective-permute-start.7 = (bf16[512,2048]{1,0:T(8,128)(2,1)}, bf16[512,2048]{1,0:T(8,128)(2,1)}, u32[]{:S(2)}, u32[]{:S(2)}) collective-permute-start(bf16[512,2048]{1,0:T(8,128)(2,1)} %w0), channel_id=1, source_target_pairs={{0,3},{1,0},{2,1},{3,2},{4,7},{5,4},{6,5},{7,6},{8,11},{9,8},{10,9... | collective-permute-start | bytes 6291464 | tf_op jit(solution)/shard_map/ppermute | solution.py:40
  21.6 18.3 %collective-permute-start.14 = (bf16[320,512]{1,0:T(8,128)(2,1)}, bf16[320,512]{1,0:T(8,128)(2,1)S(1)}, u32[]{:S(2)}, u32[]{:S(2)}) collective-permute-start(bf16[320,512]{1,0:T(8,128)(2,1)} %param.21), channel_id=1, source_target_pairs={{0,0},{1,17},{2,34},{3,51},{4,68},{5,85},{6,102},{7,119},{8,136},{... | collective-permute-start | bytes 983048 | tf_op jit(solution)/shard_map/ppermute | solution.py:292
  40.0 19.8 %collective-permute-start.15 = (bf16[320,512]{1,0:T(8,128)(2,1)S(1)}, bf16[320,512]{1,0:T(8,128)(2,1)}, u32[]{:S(2)}, u32[]{:S(2)}) collective-permute-start(bf16[320,512]{1,0:T(8,128)(2,1)S(1)} %collective-permute-done.14), channel_id=1, source_target_pairs={{0,0},{1,1},{2,2},{3,3},{4,4},{5,5},{6,6},{7,7},{8,8},{9,9},{10,10... | collective-permute-start | bytes 983048 | tf_op jit(solution)/shard_map/ppermute | solution.py:296
  53.8 12.8 %collective-permute-start.3 = (bf16[64,5120]{1,0:T(8,128)(2,1)S(1)}, bf16[64,5120]{1,0:T(8,128)(2,1)S(1)}, u32[]{:S(2)}, u32[]{:S(2)}) collective-permute-start(bf16[64,5120]{1,0:T(8,128)(2,1)S(1)} %pad_maximum_fusion.s0), channel_id=1, source_target_pairs={{0,4},{1,5},{2,6},{3,7},{4,8},{5,9},{6,10},{7,11},{8,12},{9,13},{1... | collective-permute-start | bytes 1966088 | tf_op jit(solution)/shard_map/ppermute | solution.py:40
  53.9 13.0 %collective-permute-start.4 = (bf16[64,5120]{1,0:T(8,128)(2,1)S(1)}, bf16[64,5120]{1,0:T(8,128)(2,1)}, u32[]{:S(2)}, u32[]{:S(2)}) collective-permute-start(bf16[64,5120]{1,0:T(8,128)(2,1)S(1)} %pad_maximum_fusion.s0), channel_id=1, source_target_pairs={{0,12},{1,13},{2,14},{3,15},{4,0},{5,1},{6,2},{7,3},{8,4},{9,5},{1... | collective-permute-start | bytes 1966088 | tf_op jit(solution)/shard_map/ppermute | solution.py:40
  59.7 13.8 %collective-permute-start.5 = (bf16[64,5120]{1,0:T(8,128)(2,1)S(1)}, bf16[64,5120]{1,0:T(8,128)(2,1)S(1)}, u32[]{:S(2)}, u32[]{:S(2)}) collective-permute-start(bf16[64,5120]{1,0:T(8,128)(2,1)S(1)} %pad_maximum_fusion.s0), channel_id=1, source_target_pairs={{0,8},{1,9},{2,10},{3,11},{4,12},{5,13},{6,14},{7,15},{8,0},{9,1},... | collective-permute-start | bytes 1966088 | tf_op jit(solution)/shard_map/ppermute | solution.py:40
  85.6 7.5 %collective-permute-start.10 = (bf16[256,320]{1,0:T(8,128)(2,1)}, bf16[256,320]{1,0:T(8,128)(2,1)S(1)}, u32[]{:S(2)}, u32[]{:S(2)}) collective-permute-start(bf16[256,320]{1,0:T(8,128)(2,1)} %shard_map.150), channel_id=1, source_target_pairs={{0,2},{1,3},{2,0},{3,1},{4,6},{5,7},{6,4},{7,5},{8,10},{9,11},{10,... | collective-permute-start | bytes 491528 | tf_op jit(solution)/shard_map/ppermute | solution.py:40
  88.3 5.9 %collective-permute-start.8 = (bf16[256,320]{1,0:T(8,128)(2,1)}, bf16[256,320]{1,0:T(8,128)(2,1)S(1)}, u32[]{:S(2)}, u32[]{:S(2)}) collective-permute-start(bf16[256,320]{1,0:T(8,128)(2,1)} %shard_map.150), channel_id=1, source_target_pairs={{0,1},{1,2},{2,3},{3,0},{4,5},{5,6},{6,7},{7,4},{8,9},{9,10},{10,1... | collective-permute-start | bytes 491528 | tf_op jit(solution)/shard_map/ppermute | solution.py:40
  89.1 7.1 %collective-permute-start.9 = (bf16[256,320]{1,0:T(8,128)(2,1)}, bf16[256,320]{1,0:T(8,128)(2,1)S(1)}, u32[]{:S(2)}, u32[]{:S(2)}) collective-permute-start(bf16[256,320]{1,0:T(8,128)(2,1)} %shard_map.150), channel_id=1, source_target_pairs={{0,3},{1,0},{2,1},{3,2},{4,7},{5,4},{6,5},{7,6},{8,11},{9,8},{10,9... | collective-permute-start | bytes 491528 | tf_op jit(solution)/shard_map/ppermute | solution.py:40
  97.5 34.9 %collective-permute-start.16 = (bf16[256,2048]{1,0:T(8,128)(2,1)}, bf16[256,2048]{1,0:T(8,128)(2,1)S(1)}, u32[]{:S(2)}, u32[]{:S(2)}) collective-permute-start(bf16[256,2048]{1,0:T(8,128)(2,1)} %slice.12), channel_id=1, source_target_pairs={{0,1},{1,2},{2,3},{3,0},{4,5},{5,6},{6,7},{7,4},{8,9},{9,10},{10,1... | collective-permute-start | bytes 3145736 | tf_op jit(solution)/shard_map/ppermute | solution.py:40
  98.1 24.0 %collective-permute-start.11 = (bf16[256,1280]{1,0:T(8,128)(2,1)S(1)}, bf16[256,1280]{1,0:T(8,128)(2,1)S(1)}, u32[]{:S(2)}, u32[]{:S(2)}) collective-permute-start(bf16[256,1280]{1,0:T(8,128)(2,1)S(1)} %concatenate.7.h0), channel_id=1, source_target_pairs={{0,4},{1,5},{2,6},{3,7},{4,8},{5,9},{6,10},{7,11},{8,12},{9,13},{1... | collective-permute-start | bytes 1966088 | tf_op jit(solution)/shard_map/ppermute | solution.py:40
  99.3 24.2 %collective-permute-start.12 = (bf16[256,1280]{1,0:T(8,128)(2,1)S(1)}, bf16[256,1280]{1,0:T(8,128)(2,1)S(1)}, u32[]{:S(2)}, u32[]{:S(2)}) collective-permute-start(bf16[256,1280]{1,0:T(8,128)(2,1)S(1)} %concatenate.7.h0), channel_id=1, source_target_pairs={{0,12},{1,13},{2,14},{3,15},{4,0},{5,1},{6,2},{7,3},{8,4},{9,5},{1... | collective-permute-start | bytes 1966088 | tf_op jit(solution)/shard_map/ppermute | solution.py:40
  101.4 34.3 %collective-permute-start.17 = (bf16[256,2048]{1,0:T(8,128)(2,1)}, bf16[256,2048]{1,0:T(8,128)(2,1)S(1)}, u32[]{:S(2)}, u32[]{:S(2)}) collective-permute-start(bf16[256,2048]{1,0:T(8,128)(2,1)} %slice.13), channel_id=1, source_target_pairs={{0,3},{1,0},{2,1},{3,2},{4,7},{5,4},{6,5},{7,6},{8,11},{9,8},{10,9... | collective-permute-start | bytes 3145736 | tf_op jit(solution)/shard_map/ppermute | solution.py:40
  102.8 41.2 %collective-permute-start.13 = (bf16[256,1280]{1,0:T(8,128)(2,1)S(1)}, bf16[256,1280]{1,0:T(8,128)(2,1)}, u32[]{:S(2)}, u32[]{:S(2)}) collective-permute-start(bf16[256,1280]{1,0:T(8,128)(2,1)S(1)} %concatenate.7.h0), channel_id=1, source_target_pairs={{0,8},{1,9},{2,10},{3,11},{4,12},{5,13},{6,14},{7,15},{8,0},{9,1},... | collective-permute-start | bytes 1966088 | tf_op jit(solution)/shard_map/ppermute | solution.py:40
  123.4 13.2 %collective-permute-start.18 = (bf16[128,2048]{1,0:T(8,128)(2,1)S(1)}, bf16[128,2048]{1,0:T(8,128)(2,1)S(1)}, u32[]{:S(2)}, u32[]{:S(2)}) collective-permute-start(bf16[128,2048]{1,0:T(8,128)(2,1)S(1)} %get-tuple-element.40), channel_id=1, source_target_pairs={{0,4},{1,5},{2,6},{3,7},{4,8},{5,9},{6,10},{7,11},{8,12},{9,13},{1... | collective-permute-start | bytes 1572872 | tf_op jit(solution)/shard_map/ppermute | solution.py:40
  123.4 13.2 %collective-permute-start.19 = (bf16[128,2048]{1,0:T(8,128)(2,1)S(1)}, bf16[128,2048]{1,0:T(8,128)(2,1)S(1)}, u32[]{:S(2)}, u32[]{:S(2)}) collective-permute-start(bf16[128,2048]{1,0:T(8,128)(2,1)S(1)} %get-tuple-element.41), channel_id=1, source_target_pairs={{0,12},{1,13},{2,14},{3,15},{4,0},{5,1},{6,2},{7,3},{8,4},{9,5},{1... | collective-permute-start | bytes 1572872 | tf_op jit(solution)/shard_map/ppermute | solution.py:40
  133.4 10.7 %collective-permute-start.20 = (bf16[128,2048]{1,0:T(8,128)(2,1)S(1)}, bf16[128,2048]{1,0:T(8,128)(2,1)S(1)}, u32[]{:S(2)}, u32[]{:S(2)}) collective-permute-start(bf16[128,2048]{1,0:T(8,128)(2,1)S(1)} %get-tuple-element.42), channel_id=1, source_target_pairs={{0,8},{1,9},{2,10},{3,11},{4,12},{5,13},{6,14},{7,15},{8,0},{9,1},... | collective-permute-start | bytes 1572872 | tf_op jit(solution)/shard_map/ppermute | solution.py:40
  149.5 13.2 %collective-permute-start.21 = (bf16[256,512]{1,0:T(8,128)(2,1)}, bf16[256,512]{1,0:T(8,128)(2,1)S(1)}, u32[]{:S(2)}, u32[]{:S(2)}) collective-permute-start(bf16[256,512]{1,0:T(8,128)(2,1)} %shard_map.152.v0), channel_id=1, source_target_pairs={{0,1},{1,2},{2,3},{3,0},{4,5},{5,6},{6,7},{7,4},{8,9},{9,10},{10,1... | collective-permute-start | bytes 786440 | tf_op jit(solution)/shard_map/ppermute | solution.py:40
  154.3 12.3 %collective-permute-start.22 = (bf16[256,512]{1,0:T(8,128)(2,1)}, bf16[256,512]{1,0:T(8,128)(2,1)S(1)}, u32[]{:S(2)}, u32[]{:S(2)}) collective-permute-start(bf16[256,512]{1,0:T(8,128)(2,1)} %shard_map.152.v0), channel_id=1, source_target_pairs={{0,3},{1,0},{2,1},{3,2},{4,7},{5,4},{6,5},{7,6},{8,11},{9,8},{10,9... | collective-permute-start | bytes 786440 | tf_op jit(solution)/shard_map/ppermute | solution.py:40
  154.3 14.5 %collective-permute-start.23 = (bf16[256,512]{1,0:T(8,128)(2,1)}, bf16[256,512]{1,0:T(8,128)(2,1)S(1)}, u32[]{:S(2)}, u32[]{:S(2)}) collective-permute-start(bf16[256,512]{1,0:T(8,128)(2,1)} %shard_map.152.v0), channel_id=1, source_target_pairs={{0,2},{1,3},{2,0},{3,1},{4,6},{5,7},{6,4},{7,5},{8,10},{9,11},{10,... | collective-permute-start | bytes 786440 | tf_op jit(solution)/shard_map/ppermute | solution.py:40
  171.0 28.8 %collective-permute-start.24 = (bf16[128,2048]{1,0:T(8,128)(2,1)S(1)}, bf16[128,2048]{1,0:T(8,128)(2,1)S(1)}, u32[]{:S(2)}, u32[]{:S(2)}) collective-permute-start(bf16[128,2048]{1,0:T(8,128)(2,1)S(1)} %get-tuple-element.45.e2), channel_id=1, source_target_pairs={{0,4},{1,5},{2,6},{3,7},{4,8},{5,9},{6,10},{7,11},{8,12},{9,13},{1... | collective-permute-start | bytes 1572872 | tf_op jit(solution)/shard_map/ppermute | solution.py:40
  183.0 20.0 %collective-permute-start.25 = (bf16[128,2048]{1,0:T(8,128)(2,1)S(1)}, bf16[128,2048]{1,0:T(8,128)(2,1)S(1)}, u32[]{:S(2)}, u32[]{:S(2)}) collective-permute-start(bf16[128,2048]{1,0:T(8,128)(2,1)S(1)} %get-tuple-element.46.e1), channel_id=1, source_target_pairs={{0,12},{1,13},{2,14},{3,15},{4,0},{5,1},{6,2},{7,3},{8,4},{9,5},{1... | collective-permute-start | bytes 1572872 | tf_op jit(solution)/shard_map/ppermute | solution.py:40
  186.3 16.7 %collective-permute-start.26 = (bf16[128,2048]{1,0:T(8,128)(2,1)S(1)}, bf16[128,2048]{1,0:T(8,128)(2,1)S(1)}, u32[]{:S(2)}, u32[]{:S(2)}) collective-permute-start(bf16[128,2048]{1,0:T(8,128)(2,1)S(1)} %get-tuple-element.47.e3), channel_id=1, source_target_pairs={{0,8},{1,9},{2,10},{3,11},{4,12},{5,13},{6,14},{7,15},{8,0},{9,1},... | collective-permute-start | bytes 1572872 | tf_op jit(solution)/shard_map/ppermute | solution.py:40
  197.5 10.9 %collective-permute-start.27 = (bf16[128,2048]{1,0:T(8,128)(2,1)S(1)}, bf16[128,2048]{1,0:T(8,128)(2,1)S(1)}, u32[]{:S(2)}, u32[]{:S(2)}) collective-permute-start(bf16[128,2048]{1,0:T(8,128)(2,1)S(1)} %get-tuple-element.50), channel_id=1, source_target_pairs={{0,8},{1,9},{2,10},{3,11},{4,12},{5,13},{6,14},{7,15},{8,0},{9,1},... | collective-permute-start | bytes 1572872 | tf_op jit(solution)/shard_map/ppermute | solution.py:40
  199.8 14.1 %collective-permute-start.28 = (bf16[128,2048]{1,0:T(8,128)(2,1)S(1)}, bf16[128,2048]{1,0:T(8,128)(2,1)S(1)}, u32[]{:S(2)}, u32[]{:S(2)}) collective-permute-start(bf16[128,2048]{1,0:T(8,128)(2,1)S(1)} %get-tuple-element.51), channel_id=1, source_target_pairs={{0,4},{1,5},{2,6},{3,7},{4,8},{5,9},{6,10},{7,11},{8,12},{9,13},{1... | collective-permute-start | bytes 1572872 | tf_op jit(solution)/shard_map/ppermute | solution.py:40
  199.8 14.1 %collective-permute-start.29 = (bf16[128,2048]{1,0:T(8,128)(2,1)S(1)}, bf16[128,2048]{1,0:T(8,128)(2,1)S(1)}, u32[]{:S(2)}, u32[]{:S(2)}) collective-permute-start(bf16[128,2048]{1,0:T(8,128)(2,1)S(1)} %get-tuple-element.52), channel_id=1, source_target_pairs={{0,12},{1,13},{2,14},{3,15},{4,0},{5,1},{6,2},{7,3},{8,4},{9,5},{1... | collective-permute-start | bytes 1572872 | tf_op jit(solution)/shard_map/ppermute | solution.py:40
  (25 other events, 395.7 us)
Sparse Core Ops, SparseCore 0:
  9.8 44.5 all-gather.2
  74.6 45.7 all-gather.4

commit v4 on v3

--- a/solution.py
+++ b/solution.py
@@ -288,14 +288,15 @@
     kv_bias,
 ):
     tab = jnp.asarray(TABLE)[lax.axis_index("mb") * 16 + lax.axis_index("tp")]
+    merged = merge(patches[0, 0], merge_gain, merge_bias)
+    down_part = lax.ppermute(down_weight, ("enc", "mb", "tp"), SHUFFLE)
+    up_weight = after(up_weight, down_part, merged)
     up_full = lax.all_gather(up_weight, ("enc", "mb"), axis=0, tiled=True)
-    down_part = lax.ppermute(down_weight, ("enc", "mb", "tp"), SHUFFLE)
-
-    merged = merge(patches[0, 0], merge_gain, merge_bias)
+    down_part = lax.ppermute(down_part, ("enc", "mb", "tp"), TURN)
+
     near = jnp.concatenate([merged, *around(merged, 1)], axis=0)
-    down_part = lax.ppermute(after(down_part, near), ("enc", "mb", "tp"), TURN)
+    near, kv_weight, down_part = lax.optimization_barrier((near, kv_weight, down_part))
     group = (near, *around(near, 2))
-    kv_weight = after(kv_weight, near)
     kv_right, kv_left = hop(kv_weight, 1, 1), hop(kv_weight, 1, -1)
     down_part = after(down_part, *group, kv_right, kv_left)
     down_full = lax.all_gather(down_part, ("enc", "mb"), axis=0, tiled=True)
@@ -308,11 +309,11 @@
     weights = (kv_weight, kv_right, kv_left, hop(far_right, 1, 1), hop(far_left, 1, -1))
     own, to_left, to_right, to_far = pack(tab, text_embed[0, 0])
     units = (near, *around(near, 2))
-    to_left, to_right, to_far = lax.optimization_barrier((to_left, to_right, to_far, *units[1:3]))[:3]
+    to_left, to_right, to_far = lax.optimization_barrier((to_left, to_right, to_far, *units))[:3]
     text = (own, hop(to_right, 2, 1), hop(to_left, 2, -1), hop(to_far, 2, 2))
-    down_full = after(down_full, weights[3], weights[4], *text)
+    down_full = after(down_full, weights[3], weights[4])
     visual = down(tab, units, down_full, down_bias.reshape(16, 1, 512))
-    visual = (visual, *around(visual, 1))
+    visual = (visual, *around(after(visual, *text), 1))
 
     live_rows = patch_counts[0, 0] // 4
     live = (jnp.arange(SLOT, dtype=jnp.int32)[None, :] < live_rows[:, None]).reshape(-1)

time: 222 us -> 220 us (level)
  the two profiles are of different devices: /device:TPU:134 before, /device:TPU:32 now
where the time goes in v4:
time: 220 us; the launch traced here: 219 us
  waiting for transfers between devices  91.5 us (42%)
  starting transfers between devices  70.7 us (32%)
  Pallas kernels  24.1 us (11%)
  local copies, waits for them, and re-layouts  17.5 us (8%)
  between operations  14.3 us (6%)
    ppermute x28, waiting for transfers between devices, hop(): return lax.ppermute(value, ('mb', 'tp'), HOPS[which, step])  85.9 us
    ppermute x28, starting transfers between devices, hop(): return lax.ppermute(value, ('mb', 'tp'), HOPS[which, step])  65.9 us
    unnamed x54, local copies, waits for them, and re-layouts  9.7 us
    pallas_call x1, Pallas kernels, product(): pl.pallas_call(product_kernel, out_shape=[jax.ShapeDtypeStruct((128, 2048...  6.99 us
    pallas_call x1, Pallas kernels, up(): pl.pallas_call(up_kernel, out_shape=jax.ShapeDtypeStruct((256, 320), BF16...  5.69 us
    ppermute x1, waiting for transfers between devices, per_device(): down_part = lax.ppermute(down_part, ('enc', 'mb', 'tp'), TURN)  5.53 us
    pallas_call x1, Pallas kernels, down(): pl.pallas_call(down_kernel, out_shape=jax.ShapeDtypeStruct((256, 512), BF...  5.48 us
  transfers between devices with their start and end apart: 32, of which 19 were waited for; matrix products, arithmetic and copies ran while one was open for 4% of the time, Pallas kernels for 10%

profile of v4, /device:TPU:32, one launch (start us, length us, event | category | flops | bytes accessed | tf_op | source)
XLA Modules:
  0.0 219.3 jit_solution(15622192644000044415)
XLA Ops:
  11.5 10.4 %collective-permute-start.2 = (bf16[16,5120]{1,0:T(8,128)(2,1)S(1)}, bf16[16,5120]{1,0:T(8,128)(2,1)S(1)}, u32[]{:S(2)}, u32[]{:S(2)}) collective-permute-start(bf16[16,5120]{1,0:T(8,128)(2,1)S(1)} %shard_map.149), channel_id=1, source_target_pairs={{0,2},{1,3},{2,0},{3,1},{4,6},{5,7},{6,4},{7,5},{8,10},{9,11},{10,... | collective-permute-start | bytes 491528 | tf_op jit(solution)/shard_map/ppermute | solution.py:40
  24.0 3.1 %collective-permute-start.4 = (bf16[320,512]{1,0:T(8,128)(2,1)S(1)}, bf16[320,512]{1,0:T(8,128)(2,1)S(1)}, u32[]{:S(2)}, u32[]{:S(2)}) collective-permute-start(bf16[320,512]{1,0:T(8,128)(2,1)S(1)} %collective-permute-done.3), channel_id=1, source_target_pairs={{0,0},{1,1},{2,2},{3,3},{4,4},{5,5},{6,6},{7,7},{8,8},{9,9},{10,10... | collective-permute-start | bytes 983048 | tf_op jit(solution)/shard_map/ppermute | solution.py:295
  28.9 5.5 %collective-permute-done.4 = bf16[320,512]{1,0:T(8,128)(2,1)S(1)} collective-permute-done((bf16[320,512]{1,0:T(8,128)(2,1)S(1)}, bf16[320,512]{1,0:T(8,128)(2,1)S(1)}, u32[]{:S(2)}, u32[]{:S(2)}) %collective-permute-start.4) | collective-permute-done | bytes 327712 | tf_op jit(solution)/shard_map/ppermute | solution.py:295
  36.3 2.1 collective-permute-start.9
  38.4 8.9 %collective-permute-start.5 = (bf16[64,5120]{1,0:T(8,128)(2,1)S(1)}, bf16[64,5120]{1,0:T(8,128)(2,1)S(1)}, u32[]{:S(2)}, u32[]{:S(2)}) collective-permute-start(bf16[64,5120]{1,0:T(8,128)(2,1)S(1)} %pad_maximum_fusion.s0), channel_id=1, source_target_pairs={{0,4},{1,5},{2,6},{3,7},{4,8},{5,9},{6,10},{7,11},{8,12},{9,13},{1... | collective-permute-start | bytes 1966088 | tf_op jit(solution)/shard_map/ppermute | solution.py:40
  47.3 4.5 %collective-permute-start.6 = (bf16[64,5120]{1,0:T(8,128)(2,1)S(1)}, bf16[64,5120]{1,0:T(8,128)(2,1)S(1)}, u32[]{:S(2)}, u32[]{:S(2)}) collective-permute-start(bf16[64,5120]{1,0:T(8,128)(2,1)S(1)} %pad_maximum_fusion.s0), channel_id=1, source_target_pairs={{0,12},{1,13},{2,14},{3,15},{4,0},{5,1},{6,2},{7,3},{8,4},{9,5},{1... | collective-permute-start | bytes 1966088 | tf_op jit(solution)/shard_map/ppermute | solution.py:40
  51.8 3.6 %collective-permute-start.7 = (bf16[64,5120]{1,0:T(8,128)(2,1)S(1)}, bf16[64,5120]{1,0:T(8,128)(2,1)S(1)}, u32[]{:S(2)}, u32[]{:S(2)}) collective-permute-start(bf16[64,5120]{1,0:T(8,128)(2,1)S(1)} %pad_maximum_fusion.s0), channel_id=1, source_target_pairs={{0,8},{1,9},{2,10},{3,11},{4,12},{5,13},{6,14},{7,15},{8,0},{9,1},... | collective-permute-start | bytes 1966088 | tf_op jit(solution)/shard_map/ppermute | solution.py:40
  55.5 12.0 %collective-permute-done.5.s1 = bf16[64,5120]{1,0:T(8,128)(2,1)S(1)} collective-permute-done((bf16[64,5120]{1,0:T(8,128)(2,1)S(1)}, bf16[64,5120]{1,0:T(8,128)(2,1)S(1)}, u32[]{:S(2)}, u32[]{:S(2)}) %collective-permute-start.5) | collective-permute-done | bytes 655392 | tf_op jit(solution)/shard_map/ppermute | solution.py:40
  69.1 14.1 %collective-permute-done.7.s3 = bf16[64,5120]{1,0:T(8,128)(2,1)S(1)} collective-permute-done((bf16[64,5120]{1,0:T(8,128)(2,1)S(1)}, bf16[64,5120]{1,0:T(8,128)(2,1)S(1)}, u32[]{:S(2)}, u32[]{:S(2)}) %collective-permute-start.7) | collective-permute-done | bytes 655392 | tf_op jit(solution)/shard_map/ppermute | solution.py:40
  87.3 2.4 %slice.13 = bf16[256,2048]{1,0:T(8,128)(2,1)} slice(bf16[512,2048]{1,0:T(8,128)(2,1)} %collective-permute-done.9.w2), slice={[256:512], [0:2048]} | slice | bytes 2097152 | tf_op jit(solution)/shard_map/slice | solution.py:303
  89.7 5.7 %shard_map.150 = bf16[256,320]{1,0:T(8,128)(2,1)} custom-call(s32[16]{0:T(128)} %dynamic-slice_bitcast_fusion.tab, bf16[64,5120]{1,0:T(8,128)(2,1)} %copy-done.15, bf16[64,5120]{1,0:T(8,128)(2,1)} %copy-done.19, bf16[64,5120]{1,0:T(8,128)(2,1)} %copy-done.20, bf16[64,5120]{1,0:T(8,128)(2,1)} %copy-done.21, ...), custom_call_target="tpu_custom_call" | custom-call | flops 840000000 | bytes 6291456 | tf_op jit(solution)/shard_map/pallas_call | solution.py:137
  95.5 3.2 %collective-permute-start.11 = (bf16[256,320]{1,0:T(8,128)(2,1)}, bf16[256,320]{1,0:T(8,128)(2,1)S(1)}, u32[]{:S(2)}, u32[]{:S(2)}) collective-permute-start(bf16[256,320]{1,0:T(8,128)(2,1)} %shard_map.150), channel_id=1, source_target_pairs={{0,3},{1,0},{2,1},{3,2},{4,7},{5,4},{6,5},{7,6},{8,11},{9,8},{10,9... | collective-permute-start | bytes 491528 | tf_op jit(solution)/shard_map/ppermute | solution.py:40
  98.7 3.9 %collective-permute-done.10 = bf16[256,320]{1,0:T(8,128)(2,1)S(1)} collective-permute-done((bf16[256,320]{1,0:T(8,128)(2,1)}, bf16[256,320]{1,0:T(8,128)(2,1)S(1)}, u32[]{:S(2)}, u32[]{:S(2)}) %collective-permute-start.10) | collective-permute-done | bytes 163872 | tf_op jit(solution)/shard_map/ppermute | solution.py:40
  106.1 2.0 concatenate.7.h0
  109.6 4.5 %collective-permute-start.14 = (bf16[256,1280]{1,0:T(8,128)(2,1)}, bf16[256,1280]{1,0:T(8,128)(2,1)S(1)}, u32[]{:S(2)}, u32[]{:S(2)}) collective-permute-start(bf16[256,1280]{1,0:T(8,128)(2,1)} %concatenate.7.h0), channel_id=1, source_target_pairs={{0,12},{1,13},{2,14},{3,15},{4,0},{5,1},{6,2},{7,3},{8,4},{9,5},{1... | collective-permute-start | bytes 1966088 | tf_op jit(solution)/shard_map/ppermute | solution.py:40
  114.2 3.6 %collective-permute-start.15 = (bf16[256,1280]{1,0:T(8,128)(2,1)}, bf16[256,1280]{1,0:T(8,128)(2,1)S(1)}, u32[]{:S(2)}, u32[]{:S(2)}) collective-permute-start(bf16[256,1280]{1,0:T(8,128)(2,1)} %concatenate.7.h0), channel_id=1, source_target_pairs={{0,8},{1,9},{2,10},{3,11},{4,12},{5,13},{6,14},{7,15},{8,0},{9,1},... | collective-permute-start | bytes 1966088 | tf_op jit(solution)/shard_map/ppermute | solution.py:40
  119.0 2.0 collective-permute-start.17
  121.1 2.4 %shard_map.152 = (bf16[128,2048]{1,0:T(8,128)(2,1)S(1)}, bf16[128,2048]{1,0:T(8,128)(2,1)}, bf16[128,2048]{1,0:T(8,128)(2,1)}, bf16[128,2048]{1,0:T(8,128)(2,1)S(1)}) custom-call(s32[16]{0:T(128)S(1)} %copy-done.5, bf16[128,8192]{1,0:T(8,128)(2,1)S(1)} %bitcast.19, bf16[128,8192]{1,0:T(8,128)(2,1)S(1)} %bitcast.20, bf16[128,8192]{1,0:T(8,128)(2,1)S(1)} %bitcast.21, ...), custom_call_target="tpu_custom_call" | custom-call | bytes 4194304 | tf_op jit(solution)/shard_map/pallas_call | solution.py:99
  123.5 4.3 %collective-permute-done.13.h1 = bf16[256,1280]{1,0:T(8,128)(2,1)S(1)} collective-permute-done((bf16[256,1280]{1,0:T(8,128)(2,1)}, bf16[256,1280]{1,0:T(8,128)(2,1)S(1)}, u32[]{:S(2)}, u32[]{:S(2)}) %collective-permute-start.13) | collective-permute-done | bytes 655392 | tf_op jit(solution)/shard_map/ppermute | solution.py:40
  127.8 3.6 %collective-permute-done.14.h2 = bf16[256,1280]{1,0:T(8,128)(2,1)S(1)} collective-permute-done((bf16[256,1280]{1,0:T(8,128)(2,1)}, bf16[256,1280]{1,0:T(8,128)(2,1)S(1)}, u32[]{:S(2)}, u32[]{:S(2)}) %collective-permute-start.14) | collective-permute-done | bytes 655392 | tf_op jit(solution)/shard_map/ppermute | solution.py:40
  131.4 11.4 %collective-permute-done.15.h3 = bf16[256,1280]{1,0:T(8,128)(2,1)S(1)} collective-permute-done((bf16[256,1280]{1,0:T(8,128)(2,1)}, bf16[256,1280]{1,0:T(8,128)(2,1)S(1)}, u32[]{:S(2)}, u32[]{:S(2)}) %collective-permute-start.15) | collective-permute-done | bytes 655392 | tf_op jit(solution)/shard_map/ppermute | solution.py:40
  149.1 5.5 %shard_map.151.v0 = bf16[256,512]{1,0:T(8,128)(2,1)} custom-call(s32[16]{0:T(128)} %dynamic-slice_bitcast_fusion.tab, bf16[256,1280]{1,0:T(8,128)(2,1)} %concatenate.7.h0, bf16[256,1280]{1,0:T(8,128)(2,1)} %copy-done.16, bf16[256,1280]{1,0:T(8,128)(2,1)} %copy-done.17, bf16[256,1280]{1,0:T(8,128)(2,1)} %copy-done.18, ...), custom_call_target="tpu_custom_call" | custom-call | flops 1340000000 | bytes 8388608 | tf_op jit(solution)/shard_map/pallas_call | solution.py:170
  155.8 6.7 %collective-permute-done.20.refs_3_ = bf16[128,2048]{1,0:T(8,128)(2,1)S(1)} collective-permute-done((bf16[128,2048]{1,0:T(8,128)(2,1)S(1)}, bf16[128,2048]{1,0:T(8,128)(2,1)S(1)}, u32[]{:S(2)}, u32[]{:S(2)}) %collective-permute-start.20) | collective-permute-done | bytes 524320 | tf_op jit(solution)/shard_map/ppermute | solution.py:40
  166.4 3.9 %collective-permute-done.21.v1 = bf16[256,512]{1,0:T(8,128)(2,1)S(1)} collective-permute-done((bf16[256,512]{1,0:T(8,128)(2,1)}, bf16[256,512]{1,0:T(8,128)(2,1)S(1)}, u32[]{:S(2)}, u32[]{:S(2)}) %collective-permute-start.21) | collective-permute-done | bytes 262176 | tf_op jit(solution)/shard_map/ppermute | solution.py:40
  170.7 5.9 %collective-permute-done.23.v3 = bf16[256,512]{1,0:T(8,128)(2,1)S(1)} collective-permute-done((bf16[256,512]{1,0:T(8,128)(2,1)}, bf16[256,512]{1,0:T(8,128)(2,1)S(1)}, u32[]{:S(2)}, u32[]{:S(2)}) %collective-permute-start.23) | collective-permute-done | bytes 262176 | tf_op jit(solution)/shard_map/ppermute | solution.py:40
  178.9 1.8 collective-permute-start.24
  185.7 7.0 %shard_map.155 = (f32[128,2048]{1,0:T(8,128)S(1)}, bf16[128,2048]{1,0:T(8,128)(2,1)S(1)}, bf16[128,2048]{1,0:T(8,128)(2,1)S(1)}, bf16[128,2048]{1,0:T(8,128)(2,1)S(1)}) custom-call(s32[16]{0:T(128)S(1)} %copy-done.6, bf16[128,2048]{1,0:T(8,128)(2,1)S(1)} %get-tuple-element.50.e0, bf16[128,2048]{1,0:T(8,128)(2,1)S(1)} %get-tuple-element.52.e1, ...), custom_call_target="tpu_custom_call" | custom-call | flops 4300000256 | bytes 14680064 | tf_op jit(solution)/shard_map/pallas_call | solution.py:235
  192.7 2.6 %collective-permute-start.29 = (bf16[128,2048]{1,0:T(8,128)(2,1)S(1)}, bf16[128,2048]{1,0:T(8,128)(2,1)S(1)}, u32[]{:S(2)}, u32[]{:S(2)}) collective-permute-start(bf16[128,2048]{1,0:T(8,128)(2,1)S(1)} %get-tuple-element.58), channel_id=1, source_target_pairs={{0,12},{1,13},{2,14},{3,15},{4,0},{5,1},{6,2},{7,3},{8,4},{9,5},{1... | collective-permute-start | bytes 1572872 | tf_op jit(solution)/shard_map/ppermute | solution.py:40
  195.3 2.3 %collective-permute-start.27 = (bf16[128,2048]{1,0:T(8,128)(2,1)S(1)}, bf16[128,2048]{1,0:T(8,128)(2,1)S(1)}, u32[]{:S(2)}, u32[]{:S(2)}) collective-permute-start(bf16[128,2048]{1,0:T(8,128)(2,1)S(1)} %get-tuple-element.56), channel_id=1, source_target_pairs={{0,8},{1,9},{2,10},{3,11},{4,12},{5,13},{6,14},{7,15},{8,0},{9,1},... | collective-permute-start | bytes 1572872 | tf_op jit(solution)/shard_map/ppermute | solution.py:40
  197.7 2.0 shard_map.154
  199.8 7.9 %collective-permute-done.29 = bf16[128,2048]{1,0:T(8,128)(2,1)S(1)} collective-permute-done((bf16[128,2048]{1,0:T(8,128)(2,1)S(1)}, bf16[128,2048]{1,0:T(8,128)(2,1)S(1)}, u32[]{:S(2)}, u32[]{:S(2)}) %collective-permute-start.29) | collective-permute-done | bytes 524320 | tf_op jit(solution)/shard_map/ppermute | solution.py:40
  207.7 3.7 %collective-permute-done.28 = bf16[128,2048]{1,0:T(8,128)(2,1)S(1)} collective-permute-done((bf16[128,2048]{1,0:T(8,128)(2,1)S(1)}, bf16[128,2048]{1,0:T(8,128)(2,1)S(1)}, u32[]{:S(2)}, u32[]{:S(2)}) %collective-permute-start.28) | collective-permute-done | bytes 524320 | tf_op jit(solution)/shard_map/ppermute | solution.py:40
  (107 shorter events, 42.3 us)
Async XLA Ops:
  7.2 82.5 %all-gather.3.cloned.1.call-start = ((), (), s32[]{:S(2)}) async-start(), calls=%async_computation | async-start | bytes 4177920 | tf_op jit(solution)/shard_map/all_gather | solution.py:294
  7.2 4.2 %collective-permute-start.3 = (bf16[320,512]{1,0:T(8,128)(2,1)}, bf16[320,512]{1,0:T(8,128)(2,1)S(1)}, u32[]{:S(2)}, u32[]{:S(2)}) collective-permute-start(bf16[320,512]{1,0:T(8,128)(2,1)} %param.21), channel_id=1, source_target_pairs={{0,0},{1,17},{2,34},{3,51},{4,68},{5,85},{6,102},{7,119},{8,136},{... | collective-permute-start | bytes 983048 | tf_op jit(solution)/shard_map/ppermute | solution.py:292
  11.5 137.6 %all-gather.5.cloned.1.call-start = ((), (), s32[]{:S(2)}) async-start(), calls=%async_computation.1 | async-start | bytes 5570560 | tf_op jit(solution)/shard_map/all_gather | solution.py:302
  11.5 15.5 %collective-permute-start.2 = (bf16[16,5120]{1,0:T(8,128)(2,1)S(1)}, bf16[16,5120]{1,0:T(8,128)(2,1)S(1)}, u32[]{:S(2)}, u32[]{:S(2)}) collective-permute-start(bf16[16,5120]{1,0:T(8,128)(2,1)S(1)} %shard_map.149), channel_id=1, source_target_pairs={{0,2},{1,3},{2,0},{3,1},{4,6},{5,7},{6,4},{7,5},{8,10},{9,11},{10,... | collective-permute-start | bytes 491528 | tf_op jit(solution)/shard_map/ppermute | solution.py:40
  21.9 6.2 %collective-permute-start.1 = (bf16[16,5120]{1,0:T(8,128)(2,1)S(1)}, bf16[16,5120]{1,0:T(8,128)(2,1)S(1)}, u32[]{:S(2)}, u32[]{:S(2)}) collective-permute-start(bf16[16,5120]{1,0:T(8,128)(2,1)S(1)} %shard_map.149), channel_id=1, source_target_pairs={{0,3},{1,0},{2,1},{3,2},{4,7},{5,4},{6,5},{7,6},{8,11},{9,8},{10,9... | collective-permute-start | bytes 491528 | tf_op jit(solution)/shard_map/ppermute | solution.py:40
  22.3 6.5 %collective-permute-start = (bf16[16,5120]{1,0:T(8,128)(2,1)S(1)}, bf16[16,5120]{1,0:T(8,128)(2,1)S(1)}, u32[]{:S(2)}, u32[]{:S(2)}) collective-permute-start(bf16[16,5120]{1,0:T(8,128)(2,1)S(1)} %shard_map.149), channel_id=1, source_target_pairs={{0,1},{1,2},{2,3},{3,0},{4,5},{5,6},{6,7},{7,4},{8,9},{9,10},{10,1... | collective-permute-start | bytes 491528 | tf_op jit(solution)/shard_map/ppermute | solution.py:40
  24.0 10.5 %collective-permute-start.4 = (bf16[320,512]{1,0:T(8,128)(2,1)S(1)}, bf16[320,512]{1,0:T(8,128)(2,1)S(1)}, u32[]{:S(2)}, u32[]{:S(2)}) collective-permute-start(bf16[320,512]{1,0:T(8,128)(2,1)S(1)} %collective-permute-done.3), channel_id=1, source_target_pairs={{0,0},{1,1},{2,2},{3,3},{4,4},{5,5},{6,6},{7,7},{8,8},{9,9},{10,10... | collective-permute-start | bytes 983048 | tf_op jit(solution)/shard_map/ppermute | solution.py:295
  35.2 48.0 %collective-permute-start.8 = (bf16[512,2048]{1,0:T(8,128)(2,1)}, bf16[512,2048]{1,0:T(8,128)(2,1)S(1)}, u32[]{:S(2)}, u32[]{:S(2)}) collective-permute-start(bf16[512,2048]{1,0:T(8,128)(2,1)} %w0), channel_id=1, source_target_pairs={{0,1},{1,2},{2,3},{3,0},{4,5},{5,6},{6,7},{7,4},{8,9},{9,10},{10,1... | collective-permute-start | bytes 6291464 | tf_op jit(solution)/shard_map/ppermute | solution.py:40
  36.3 47.7 %collective-permute-start.9 = (bf16[512,2048]{1,0:T(8,128)(2,1)}, bf16[512,2048]{1,0:T(8,128)(2,1)}, u32[]{:S(2)}, u32[]{:S(2)}) collective-permute-start(bf16[512,2048]{1,0:T(8,128)(2,1)} %w0), channel_id=1, source_target_pairs={{0,3},{1,0},{2,1},{3,2},{4,7},{5,4},{6,5},{7,6},{8,11},{9,8},{10,9... | collective-permute-start | bytes 6291464 | tf_op jit(solution)/shard_map/ppermute | solution.py:40
  38.4 29.1 %collective-permute-start.5 = (bf16[64,5120]{1,0:T(8,128)(2,1)S(1)}, bf16[64,5120]{1,0:T(8,128)(2,1)S(1)}, u32[]{:S(2)}, u32[]{:S(2)}) collective-permute-start(bf16[64,5120]{1,0:T(8,128)(2,1)S(1)} %pad_maximum_fusion.s0), channel_id=1, source_target_pairs={{0,4},{1,5},{2,6},{3,7},{4,8},{5,9},{6,10},{7,11},{8,12},{9,13},{1... | collective-permute-start | bytes 1966088 | tf_op jit(solution)/shard_map/ppermute | solution.py:40
  47.3 21.8 %collective-permute-start.6 = (bf16[64,5120]{1,0:T(8,128)(2,1)S(1)}, bf16[64,5120]{1,0:T(8,128)(2,1)S(1)}, u32[]{:S(2)}, u32[]{:S(2)}) collective-permute-start(bf16[64,5120]{1,0:T(8,128)(2,1)S(1)} %pad_maximum_fusion.s0), channel_id=1, source_target_pairs={{0,12},{1,13},{2,14},{3,15},{4,0},{5,1},{6,2},{7,3},{8,4},{9,5},{1... | collective-permute-start | bytes 1966088 | tf_op jit(solution)/shard_map/ppermute | solution.py:40
  51.8 31.3 %collective-permute-start.7 = (bf16[64,5120]{1,0:T(8,128)(2,1)S(1)}, bf16[64,5120]{1,0:T(8,128)(2,1)S(1)}, u32[]{:S(2)}, u32[]{:S(2)}) collective-permute-start(bf16[64,5120]{1,0:T(8,128)(2,1)S(1)} %pad_maximum_fusion.s0), channel_id=1, source_target_pairs={{0,8},{1,9},{2,10},{3,11},{4,12},{5,13},{6,14},{7,15},{8,0},{9,1},... | collective-permute-start | bytes 1966088 | tf_op jit(solution)/shard_map/ppermute | solution.py:40
  95.4 7.2 %collective-permute-start.10 = (bf16[256,320]{1,0:T(8,128)(2,1)}, bf16[256,320]{1,0:T(8,128)(2,1)S(1)}, u32[]{:S(2)}, u32[]{:S(2)}) collective-permute-start(bf16[256,320]{1,0:T(8,128)(2,1)} %shard_map.150), channel_id=1, source_target_pairs={{0,1},{1,2},{2,3},{3,0},{4,5},{5,6},{6,7},{7,4},{8,9},{9,10},{10,1... | collective-permute-start | bytes 491528 | tf_op jit(solution)/shard_map/ppermute | solution.py:40
  95.5 8.8 %collective-permute-start.11 = (bf16[256,320]{1,0:T(8,128)(2,1)}, bf16[256,320]{1,0:T(8,128)(2,1)S(1)}, u32[]{:S(2)}, u32[]{:S(2)}) collective-permute-start(bf16[256,320]{1,0:T(8,128)(2,1)} %shard_map.150), channel_id=1, source_target_pairs={{0,3},{1,0},{2,1},{3,2},{4,7},{5,4},{6,5},{7,6},{8,11},{9,8},{10,9... | collective-permute-start | bytes 491528 | tf_op jit(solution)/shard_map/ppermute | solution.py:40
  98.7 7.4 %collective-permute-start.12 = (bf16[256,320]{1,0:T(8,128)(2,1)}, bf16[256,320]{1,0:T(8,128)(2,1)S(1)}, u32[]{:S(2)}, u32[]{:S(2)}) collective-permute-start(bf16[256,320]{1,0:T(8,128)(2,1)} %shard_map.150), channel_id=1, source_target_pairs={{0,2},{1,3},{2,0},{3,1},{4,6},{5,7},{6,4},{7,5},{8,10},{9,11},{10,... | collective-permute-start | bytes 491528 | tf_op jit(solution)/shard_map/ppermute | solution.py:40
  108.1 19.7 %collective-permute-start.13 = (bf16[256,1280]{1,0:T(8,128)(2,1)}, bf16[256,1280]{1,0:T(8,128)(2,1)S(1)}, u32[]{:S(2)}, u32[]{:S(2)}) collective-permute-start(bf16[256,1280]{1,0:T(8,128)(2,1)} %concatenate.7.h0), channel_id=1, source_target_pairs={{0,4},{1,5},{2,6},{3,7},{4,8},{5,9},{6,10},{7,11},{8,12},{9,13},{1... | collective-permute-start | bytes 1966088 | tf_op jit(solution)/shard_map/ppermute | solution.py:40
  109.6 21.8 %collective-permute-start.14 = (bf16[256,1280]{1,0:T(8,128)(2,1)}, bf16[256,1280]{1,0:T(8,128)(2,1)S(1)}, u32[]{:S(2)}, u32[]{:S(2)}) collective-permute-start(bf16[256,1280]{1,0:T(8,128)(2,1)} %concatenate.7.h0), channel_id=1, source_target_pairs={{0,12},{1,13},{2,14},{3,15},{4,0},{5,1},{6,2},{7,3},{8,4},{9,5},{1... | collective-permute-start | bytes 1966088 | tf_op jit(solution)/shard_map/ppermute | solution.py:40
  114.2 28.6 %collective-permute-start.15 = (bf16[256,1280]{1,0:T(8,128)(2,1)}, bf16[256,1280]{1,0:T(8,128)(2,1)S(1)}, u32[]{:S(2)}, u32[]{:S(2)}) collective-permute-start(bf16[256,1280]{1,0:T(8,128)(2,1)} %concatenate.7.h0), channel_id=1, source_target_pairs={{0,8},{1,9},{2,10},{3,11},{4,12},{5,13},{6,14},{7,15},{8,0},{9,1},... | collective-permute-start | bytes 1966088 | tf_op jit(solution)/shard_map/ppermute | solution.py:40
  117.8 29.3 %collective-permute-start.16 = (bf16[256,2048]{1,0:T(8,128)(2,1)}, bf16[256,2048]{1,0:T(8,128)(2,1)S(1)}, u32[]{:S(2)}, u32[]{:S(2)}) collective-permute-start(bf16[256,2048]{1,0:T(8,128)(2,1)} %slice.12), channel_id=1, source_target_pairs={{0,1},{1,2},{2,3},{3,0},{4,5},{5,6},{6,7},{7,4},{8,9},{9,10},{10,1... | collective-permute-start | bytes 3145736 | tf_op jit(solution)/shard_map/ppermute | solution.py:40
  119.0 29.0 %collective-permute-start.17 = (bf16[256,2048]{1,0:T(8,128)(2,1)}, bf16[256,2048]{1,0:T(8,128)(2,1)S(1)}, u32[]{:S(2)}, u32[]{:S(2)}) collective-permute-start(bf16[256,2048]{1,0:T(8,128)(2,1)} %slice.13), channel_id=1, source_target_pairs={{0,3},{1,0},{2,1},{3,2},{4,7},{5,4},{6,5},{7,6},{8,11},{9,8},{10,9... | collective-permute-start | bytes 3145736 | tf_op jit(solution)/shard_map/ppermute | solution.py:40
  142.8 11.8 %collective-permute-start.18 = (bf16[128,2048]{1,0:T(8,128)(2,1)}, bf16[128,2048]{1,0:T(8,128)(2,1)S(1)}, u32[]{:S(2)}, u32[]{:S(2)}) collective-permute-start(bf16[128,2048]{1,0:T(8,128)(2,1)} %get-tuple-element.46), channel_id=1, source_target_pairs={{0,4},{1,5},{2,6},{3,7},{4,8},{5,9},{6,10},{7,11},{8,12},{9,13},{1... | collective-permute-start | bytes 1572872 | tf_op jit(solution)/shard_map/ppermute | solution.py:40
  144.2 11.6 %collective-permute-start.19 = (bf16[128,2048]{1,0:T(8,128)(2,1)}, bf16[128,2048]{1,0:T(8,128)(2,1)S(1)}, u32[]{:S(2)}, u32[]{:S(2)}) collective-permute-start(bf16[128,2048]{1,0:T(8,128)(2,1)} %get-tuple-element.47), channel_id=1, source_target_pairs={{0,12},{1,13},{2,14},{3,15},{4,0},{5,1},{6,2},{7,3},{8,4},{9,5},{1... | collective-permute-start | bytes 1572872 | tf_op jit(solution)/shard_map/ppermute | solution.py:40
  146.1 16.5 %collective-permute-start.20 = (bf16[128,2048]{1,0:T(8,128)(2,1)S(1)}, bf16[128,2048]{1,0:T(8,128)(2,1)S(1)}, u32[]{:S(2)}, u32[]{:S(2)}) collective-permute-start(bf16[128,2048]{1,0:T(8,128)(2,1)S(1)} %get-tuple-element.48), channel_id=1, source_target_pairs={{0,8},{1,9},{2,10},{3,11},{4,12},{5,13},{6,14},{7,15},{8,0},{9,1},... | collective-permute-start | bytes 1572872 | tf_op jit(solution)/shard_map/ppermute | solution.py:40
  162.5 7.8 %collective-permute-start.21 = (bf16[256,512]{1,0:T(8,128)(2,1)}, bf16[256,512]{1,0:T(8,128)(2,1)S(1)}, u32[]{:S(2)}, u32[]{:S(2)}) collective-permute-start(bf16[256,512]{1,0:T(8,128)(2,1)} %shard_map.151.v0), channel_id=1, source_target_pairs={{0,1},{1,2},{2,3},{3,0},{4,5},{5,6},{6,7},{7,4},{8,9},{9,10},{10,1... | collective-permute-start | bytes 786440 | tf_op jit(solution)/shard_map/ppermute | solution.py:40
  164.2 6.6 %collective-permute-start.22 = (bf16[256,512]{1,0:T(8,128)(2,1)}, bf16[256,512]{1,0:T(8,128)(2,1)S(1)}, u32[]{:S(2)}, u32[]{:S(2)}) collective-permute-start(bf16[256,512]{1,0:T(8,128)(2,1)} %shard_map.151.v0), channel_id=1, source_target_pairs={{0,3},{1,0},{2,1},{3,2},{4,7},{5,4},{6,5},{7,6},{8,11},{9,8},{10,9... | collective-permute-start | bytes 786440 | tf_op jit(solution)/shard_map/ppermute | solution.py:40
  165.8 10.8 %collective-permute-start.23 = (bf16[256,512]{1,0:T(8,128)(2,1)}, bf16[256,512]{1,0:T(8,128)(2,1)S(1)}, u32[]{:S(2)}, u32[]{:S(2)}) collective-permute-start(bf16[256,512]{1,0:T(8,128)(2,1)} %shard_map.151.v0), channel_id=1, source_target_pairs={{0,2},{1,3},{2,0},{3,1},{4,6},{5,7},{6,4},{7,5},{8,10},{9,11},{10,... | collective-permute-start | bytes 786440 | tf_op jit(solution)/shard_map/ppermute | solution.py:40
  178.9 16.5 %collective-permute-start.24 = (bf16[128,2048]{1,0:T(8,128)(2,1)S(1)}, bf16[128,2048]{1,0:T(8,128)(2,1)S(1)}, u32[]{:S(2)}, u32[]{:S(2)}) collective-permute-start(bf16[128,2048]{1,0:T(8,128)(2,1)S(1)} %get-tuple-element.51.e2), channel_id=1, source_target_pairs={{0,4},{1,5},{2,6},{3,7},{4,8},{5,9},{6,10},{7,11},{8,12},{9,13},{1... | collective-permute-start | bytes 1572872 | tf_op jit(solution)/shard_map/ppermute | solution.py:40
  180.7 17.0 %collective-permute-start.25 = (bf16[128,2048]{1,0:T(8,128)(2,1)S(1)}, bf16[128,2048]{1,0:T(8,128)(2,1)S(1)}, u32[]{:S(2)}, u32[]{:S(2)}) collective-permute-start(bf16[128,2048]{1,0:T(8,128)(2,1)S(1)} %get-tuple-element.52.e1), channel_id=1, source_target_pairs={{0,12},{1,13},{2,14},{3,15},{4,0},{5,1},{6,2},{7,3},{8,4},{9,5},{1... | collective-permute-start | bytes 1572872 | tf_op jit(solution)/shard_map/ppermute | solution.py:40
  182.2 15.5 %collective-permute-start.26 = (bf16[128,2048]{1,0:T(8,128)(2,1)S(1)}, bf16[128,2048]{1,0:T(8,128)(2,1)S(1)}, u32[]{:S(2)}, u32[]{:S(2)}) collective-permute-start(bf16[128,2048]{1,0:T(8,128)(2,1)S(1)} %get-tuple-element.53.e3), channel_id=1, source_target_pairs={{0,8},{1,9},{2,10},{3,11},{4,12},{5,13},{6,14},{7,15},{8,0},{9,1},... | collective-permute-start | bytes 1572872 | tf_op jit(solution)/shard_map/ppermute | solution.py:40
  192.7 15.0 %collective-permute-start.29 = (bf16[128,2048]{1,0:T(8,128)(2,1)S(1)}, bf16[128,2048]{1,0:T(8,128)(2,1)S(1)}, u32[]{:S(2)}, u32[]{:S(2)}) collective-permute-start(bf16[128,2048]{1,0:T(8,128)(2,1)S(1)} %get-tuple-element.58), channel_id=1, source_target_pairs={{0,12},{1,13},{2,14},{3,15},{4,0},{5,1},{6,2},{7,3},{8,4},{9,5},{1... | collective-permute-start | bytes 1572872 | tf_op jit(solution)/shard_map/ppermute | solution.py:40
  195.3 16.0 %collective-permute-start.28 = (bf16[128,2048]{1,0:T(8,128)(2,1)S(1)}, bf16[128,2048]{1,0:T(8,128)(2,1)S(1)}, u32[]{:S(2)}, u32[]{:S(2)}) collective-permute-start(bf16[128,2048]{1,0:T(8,128)(2,1)S(1)} %get-tuple-element.57), channel_id=1, source_target_pairs={{0,4},{1,5},{2,6},{3,7},{4,8},{5,9},{6,10},{7,11},{8,12},{9,13},{1... | collective-permute-start | bytes 1572872 | tf_op jit(solution)/shard_map/ppermute | solution.py:40
  195.3 16.0 %collective-permute-start.27 = (bf16[128,2048]{1,0:T(8,128)(2,1)S(1)}, bf16[128,2048]{1,0:T(8,128)(2,1)S(1)}, u32[]{:S(2)}, u32[]{:S(2)}) collective-permute-start(bf16[128,2048]{1,0:T(8,128)(2,1)S(1)} %get-tuple-element.56), channel_id=1, source_target_pairs={{0,8},{1,9},{2,10},{3,11},{4,12},{5,13},{6,14},{7,15},{8,0},{9,1},... | collective-permute-start | bytes 1572872 | tf_op jit(solution)/shard_map/ppermute | solution.py:40
  (27 other events, 416.1 us)
Sparse Core Ops, SparseCore 0:
  11.6 61.2 all-gather.2
  84.2 50.6 all-gather.4

commit v5 on v3

--- a/solution.py
+++ b/solution.py
@@ -44,6 +44,18 @@
     return hop(value, which, 1), hop(value, which, -1), hop(value, which, 2)
 
 
+def ring(value, which):
+    half = value.shape[0] // 2
+    right, left = hop(value, which, 1), hop(value, which, -1)
+    return right, left, hop(right[:half], which, 1), hop(left[half:], which, -1)
+
+
+def trade(to_right, to_left, to_far):
+    right = hop(to_right, 2, 1)
+    left = hop(to_left, 2, -1)
+    return right, left, hop(to_far, 2, 2), hop(left[128:192], 2, -1)
+
+
 def after(value, *others):
     return lax.optimization_barrier((value, *others))[0]
 
@@ -87,23 +99,27 @@
     )(patches, gain, bias)
 
 
-def pack_kernel(tab, *refs):
-    for source, target in zip(refs[:4], refs[4:]):
-        target[...] = source[...]
+def pack_kernel(tab, own, left, right, far, kept, to_left, to_right, to_far):
+    kept[...] = own[...]
+    to_left[0:128] = left[...]
+    to_left[128:192] = far[64:128]
+    to_right[...] = right[...]
+    to_far[...] = far[0:64]
 
 
 def pack(tab, text):
     def columns(i2):
         return pl.BlockSpec((128, 512), lambda j, tab: (0, tab[i2 * 4 + j]))
 
+    rows = (128, 192, 128, 64)
     return pl.pallas_call(
         pack_kernel,
-        out_shape=[jax.ShapeDtypeStruct((128, 2048), BF16)] * 4,
+        out_shape=[jax.ShapeDtypeStruct((n, 2048), BF16) for n in rows],
         grid_spec=pltpu.PrefetchScalarGridSpec(
             num_scalar_prefetch=1,
             grid=(4,),
             in_specs=[columns(i2) for i2 in range(4)],
-            out_specs=[pl.BlockSpec((128, 512), lambda j, tab: (0, j))] * 4,
+            out_specs=[pl.BlockSpec((n, 512), lambda j, tab: (0, j)) for n in rows],
         ),
         compiler_params=params(8),
         cost_estimate=cost(0, 4 * MIB),
@@ -117,15 +133,16 @@
     return copies
 
 
-def up_kernel(tab, s0, s1, s2, s3, weight, bias_ref, out_ref, rows, held, sems):
-    copies = [(piece, rows.at[pl.ds(i * 64, 64)]) for i, piece in enumerate((s0, s1, s2, s3))]
+def up_kernel(tab, s0, s1, s2, s3a, s3b, weight, bias_ref, out_ref, rows, held, sems):
+    copies = [(piece, rows.at[pl.ds(i * 64, 64)]) for i, piece in enumerate((s0, s1, s2))]
+    copies += [(s3a, rows.at[pl.ds(192, 32)]), (s3b, rows.at[pl.ds(224, 32)])]
     copies += [(weight.at[pl.ds(k * 1024, 1024)], held.at[pl.ds(k * 1024, 1024)]) for k in range(5)]
     copies = start(copies, sems)
-    for copy in copies[:4]:
+    for copy in copies[:5]:
         copy.wait()
     raised = bias_ref[tab[0]]
     for k in range(5):
-        copies[4 + k].wait()
+        copies[5 + k].wait()
         at = slice(k * 1024, (k + 1) * 1024)
         raised = raised + jnp.dot(rows[:, at], held[at, :], preferred_element_type=F32)
     hidden = (0.5 * raised * (1.0 + lax.erf(raised * np.float32(0.5**0.5)))).astype(BF16)
@@ -137,30 +154,31 @@
     return pl.pallas_call(
         up_kernel,
         out_shape=jax.ShapeDtypeStruct((256, 320), BF16),
-        in_specs=[SMEM] + [ANY] * 5 + [VMEM],
+        in_specs=[SMEM] + [ANY] * 6 + [VMEM],
         out_specs=VMEM,
         scratch_shapes=[
             pltpu.VMEM((256, 5120), BF16),
             pltpu.VMEM((5120, 320), BF16),
-            pltpu.SemaphoreType.DMA((9,)),
+            pltpu.SemaphoreType.DMA((10,)),
         ],
         compiler_params=params(56),
         cost_estimate=cost(840 * 10**6, 6 * MIB),
     )(tab, *pieces, weight, bias)
 
 
-def down_kernel(tab, h0, h1, h2, h3, weight, bias_ref, out_ref, units, held, sems):
+def down_kernel(tab, h0, h1, h2, h3a, h3b, weight, bias_ref, out_ref, units, held, sems):
     copies = []
-    for i2, piece in enumerate((h0, h1, h2, h3)):
-        copies.append((piece, units.at[i2]))
-        for i1 in range(4):
-            k = i2 * 4 + i1
-            source = weight.at[pl.ds(pl.multiple_of((tab[k] ^ tab[0]) * 320, 320), 320)]
-            copies.append((source, held.at[pl.ds(k * 320, 320)]))
+    for k in range(16):
+        source = weight.at[pl.ds(pl.multiple_of((tab[k] ^ tab[0]) * 320, 320), 320)]
+        copies.append((source, held.at[pl.ds(k * 320, 320)]))
+        if k % 4 == 3 and k < 15:
+            copies.append(((h0, h1, h2)[k // 4], units.at[k // 4]))
+    copies.append((h3a, units.at[3, pl.ds(0, 128)]))
+    copies.append((h3b, units.at[3, pl.ds(128, 128)]))
     copies = start(copies, sems)
     total = bias_ref[tab[0]]
     for i2 in range(4):
-        for copy in copies[i2 * 5 : i2 * 5 + 5]:
+        for copy in copies[i2 * 5 : i2 * 5 + 5 + i2 // 3]:
             copy.wait()
         total = total + jnp.dot(units[i2], held[i2 * 1280 : (i2 + 1) * 1280, :], preferred_element_type=F32)
     out_ref[...] = total.astype(BF16)
@@ -170,52 +188,61 @@
     return pl.pallas_call(
         down_kernel,
         out_shape=jax.ShapeDtypeStruct((256, 512), BF16),
-        in_specs=[SMEM] + [ANY] * 5 + [VMEM],
+        in_specs=[SMEM] + [ANY] * 6 + [VMEM],
         out_specs=VMEM,
         scratch_shapes=[
             pltpu.VMEM((4, 256, 1280), BF16),
             pltpu.VMEM((5120, 512), BF16),
-            pltpu.SemaphoreType.DMA((20,)),
+            pltpu.SemaphoreType.DMA((21,)),
         ],
         compiler_params=params(56),
         cost_estimate=cost(1340 * 10**6, 8 * MIB),
     )(tab, *pieces, weight, bias)
 
 
-def pick_kernel(tab, dest, v0, v1, v2, v3, *refs):
+def pick_kernel(tab, dest, v0, v1, v2, v3, own, right, left, far_a, far_b, kept, to_left, to_right):
     visual = (v0[...], v1[...], v2[...], v3[...])
     targets = dest[...]
-    for i2 in (3, 2, 1, 0):
-        text, out = refs[i2], refs[4 + i2]
-        match = (lax.broadcasted_iota(jnp.int32, (128, 256), 0) + tab[i2 * 4] * 128) == targets
-        select = match.astype(F32)
+
+    def fill(i2, first, count, text, out, out_row):
+        rows = lax.broadcasted_iota(jnp.int32, (count, 256), 0) + (tab[i2 * 4] * 128 + first)
+        select = (rows == targets).astype(F32)
         present = jnp.sum(select, axis=1, keepdims=True) > 0.0
         select = select.astype(BF16)
         for j in range(4):
             at = slice(j * 512, (j + 1) * 512)
             picked = jnp.dot(select, visual[j], preferred_element_type=F32).astype(BF16)
-            out[:, at] = jnp.where(present, picked, text[:, at])
+            out[out_row : out_row + count, at] = jnp.where(present, picked, text[0:count, at])
+
+    fill(3, 0, 64, far_a, to_left, 128)
+    fill(3, 64, 64, far_b, to_left, 192)
+    fill(1, 0, 128, right, to_left, 0)
+    fill(2, 0, 128, left, to_right, 0)
+    fill(0, 0, 128, own, kept, 0)
 
 
 def pick(tab, dest, visual, text):
     return pl.pallas_call(
         pick_kernel,
-        out_shape=[jax.ShapeDtypeStruct((128, 2048), BF16)] * 4,
-        in_specs=[SMEM] + [VMEM] * 9,
-        out_specs=[VMEM] * 4,
+        out_shape=[jax.ShapeDtypeStruct((n, 2048), BF16) for n in (128, 256, 128)],
+        in_specs=[SMEM] + [VMEM] * 10,
+        out_specs=[VMEM] * 3,
         compiler_params=params(32),
         cost_estimate=cost(540 * 10**6, 6 * MIB),
     )(tab, dest, *visual, *text)
 
 
-def product_kernel(tab, e0, e1, e2, e3, gain, w0, w1, w2, w3a, w3b, own, left, right, far, scaled):
+def product_kernel(tab, kept, to_left, to_right, gain, w0, w1, w2, w3a, w3b, own, left, far, right, scaled):
     @pl.when(pl.program_id(0) == 0)
     def _():
         for j in range(4):
             at = slice(j * 512, (j + 1) * 512)
             scale = gain[tab[j]]
-            for i2, rows in enumerate((e0, e1, e2, e3)):
-                scaled[i2 * 128 : (i2 + 1) * 128, at] = (rows[:, at].astype(F32) * scale).astype(BF16)
+            row = 0
+            for rows in (kept, to_left, to_right):
+                count = rows.shape[0]
+                scaled[row : row + count, at] = (rows[:, at].astype(F32) * scale).astype(BF16)
+                row += count
 
     total = jnp.dot(scaled[:, 0:512], w0[...], preferred_element_type=F32)
     total = total + jnp.dot(scaled[:, 512:1024], w1[...], preferred_element_type=F32)
@@ -224,8 +251,8 @@
     total = total + jnp.dot(scaled[:, 1792:2048], w3b[...], preferred_element_type=F32)
     own[...] = total[0:128]
     left[...] = total[128:256].astype(BF16)
-    right[...] = total[256:384].astype(BF16)
-    far[...] = total[384:512].astype(BF16)
+    far[...] = total[256:384].astype(BF16)
+    right[...] = total[384:512].astype(BF16)
 
 
 def product(tab, picked, gain, weights):
@@ -236,7 +263,7 @@
         product_kernel,
         out_shape=[jax.ShapeDtypeStruct((128, 2048), F32)] + [jax.ShapeDtypeStruct((128, 2048), BF16)] * 3,
         grid=(4,),
-        in_specs=[SMEM] + [VMEM] * 5 + [block(n) for n in (512, 512, 512, 256, 256)],
+        in_specs=[SMEM] + [VMEM] * 4 + [block(n) for n in (512, 512, 512, 256, 256)],
         out_specs=[block(128)] * 4,
         scratch_shapes=[pltpu.VMEM((512, 2048), BF16)],
         compiler_params=params(40),
@@ -244,16 +271,16 @@
     )(tab, *picked, gain, *weights)
 
 
-def place_kernel(tab, e0, e1, e2, e3, out, scale, sems):
+def place_kernel(tab, own, right, left, far, out, scale, sems):
     copies = []
-    for i2, rows in enumerate((e0, e1, e2, e3)):
+    total = 0.0
+    for i2, rows in enumerate((own, right, left, far)):
         for j in range(4):
             columns = pl.ds(pl.multiple_of(tab[i2 * 4 + j] * 512, 512), 512)
-            copies.append((rows.at[:, pl.ds(j * 512, 512)], out.at[:, columns]))
+            copies.append((rows.at[pl.ds(0, 128), pl.ds(j * 512, 512)], out.at[:, columns]))
     copies = start(copies, sems)
-    total = 0.0
-    for rows in (e0, e1, e2, e3):
-        values = rows[...].astype(F32)
+    for rows in (own, right, left, far):
+        values = rows[0:128].astype(F32)
         total = total + jnp.sum(values * values, axis=1, keepdims=True)
     scale[...] = jnp.broadcast_to(lax.rsqrt(total * (1.0 / 8192.0) + 1e-06), (128, 128))
     for copy in copies:
@@ -294,10 +321,10 @@
     merged = merge(patches[0, 0], merge_gain, merge_bias)
     near = jnp.concatenate([merged, *around(merged, 1)], axis=0)
     down_part = lax.ppermute(after(down_part, near), ("enc", "mb", "tp"), TURN)
-    group = (near, *around(near, 2))
     kv_weight = after(kv_weight, near)
     kv_right, kv_left = hop(kv_weight, 1, 1), hop(kv_weight, 1, -1)
-    down_part = after(down_part, *group, kv_right, kv_left)
+    group = (near, *ring(near, 2))
+    down_part = after(down_part, *group[:3])
     down_full = lax.all_gather(down_part, ("enc", "mb"), axis=0, tiled=True)
     far_right, far_left = kv_right[:256], kv_left[256:]
 
@@ -306,20 +333,21 @@
     near = jnp.concatenate([hidden, *around(hidden, 1)], axis=1)
     far_right, far_left = lax.optimization_barrier((far_right, far_left, near))[:2]
     weights = (kv_weight, kv_right, kv_left, hop(far_right, 1, 1), hop(far_left, 1, -1))
+    units = (near, *ring(near, 2))
     own, to_left, to_right, to_far = pack(tab, text_embed[0, 0])
-    units = (near, *around(near, 2))
-    to_left, to_right, to_far = lax.optimization_barrier((to_left, to_right, to_far, *units[1:3]))[:3]
-    text = (own, hop(to_right, 2, 1), hop(to_left, 2, -1), hop(to_far, 2, 2))
-    down_full = after(down_full, weights[3], weights[4], *text)
+    to_left, to_right, to_far = lax.optimization_barrier((to_left, to_right, to_far, *units))[:3]
+    text = (own, *trade(to_right, to_left, to_far))
+    down_full = after(down_full, weights[3], weights[4])
     visual = down(tab, units, down_full, down_bias.reshape(16, 1, 512))
-    visual = (visual, *around(visual, 1))
+    visual = (visual, *around(after(visual, *text), 1))
 
     live_rows = patch_counts[0, 0] // 4
     live = (jnp.arange(SLOT, dtype=jnp.int32)[None, :] < live_rows[:, None]).reshape(-1)
     dest = jnp.where(live, dest_pos[0, 0], -1)[None]
     picked = pick(tab, dest, visual, text)
-    pieces = (picked[0], hop(picked[2], 2, 1), hop(picked[1], 2, -1), hop(picked[3], 2, 2))
-    own, to_left, to_right, to_far = product(tab, picked, norm_gain.reshape(16, 1, 512), weights)
+    right, left = hop(picked[2], 2, 1), hop(picked[1], 2, -1)
+    own, to_left, to_far, to_right = product(tab, picked, norm_gain.reshape(16, 1, 512), weights)
+    pieces = (picked[0], right, left, hop(after(left, to_far)[128:256], 2, -1))
     sums = (hop(to_far, 2, 2), hop(to_right, 2, 1), hop(to_left, 2, -1))
     embedded, scale = place_rows(tab, pieces)
     total = own

time: 222 us -> 228 us (1.027)
  the two profiles are of different devices: /device:TPU:134 before, /device:TPU:218 now
where the time goes in v5:
time: 228 us; the launch traced here: 227 us
  waiting for transfers between devices  122 us (54%)
  starting transfers between devices  46.2 us (20%)
  Pallas kernels  25.3 us (11%)
  local copies, waits for them, and re-layouts  17.6 us (8%)
  between operations  14.4 us (6%)
    ppermute x31, waiting for transfers between devices, hop(): return lax.ppermute(value, ('mb', 'tp'), HOPS[which, step])  90 us
    ppermute x31, starting transfers between devices, hop(): return lax.ppermute(value, ('mb', 'tp'), HOPS[which, step])  42.3 us
    ppermute x1, waiting for transfers between devices, per_device(): down_part = lax.ppermute(down_weight, ('enc', 'mb', 'tp'), SHUFFLE)  20.9 us
    ppermute x1, waiting for transfers between devices, per_device(): down_part = lax.ppermute(after(down_part, near), ('enc', 'mb', 'tp'), TURN)  10.6 us
    unnamed x56, local copies, waits for them, and re-layouts  7.51 us
    pallas_call x1, Pallas kernels, product(): pl.pallas_call(product_kernel, out_shape=[jax.ShapeDtypeStruct((128, 2048...  6.99 us
    pallas_call x1, Pallas kernels, up(): pl.pallas_call(up_kernel, out_shape=jax.ShapeDtypeStruct((256, 320), BF16...  5.62 us
    pallas_call x1, Pallas kernels, down(): pl.pallas_call(down_kernel, out_shape=jax.ShapeDtypeStruct((256, 512), BF...  5.56 us
  transfers between devices with their start and end apart: 35, of which 22 were waited for; matrix products, arithmetic and copies ran while one was open for 5% of the time, Pallas kernels for 10%

profile of v5, /device:TPU:218, one launch (start us, length us, event | category | flops | bytes accessed | tf_op | source)
XLA Modules:
  0.0 227.0 jit_solution(4487055927373432078)
XLA Ops:
  10.5 2.2 collective-permute-start.2
  21.7 20.9 %collective-permute-done.16 = bf16[320,512]{1,0:T(8,128)(2,1)S(1)} collective-permute-done((bf16[320,512]{1,0:T(8,128)(2,1)}, bf16[320,512]{1,0:T(8,128)(2,1)S(1)}, u32[]{:S(2)}, u32[]{:S(2)}) %collective-permute-start.16) | collective-permute-done | bytes 327712 | tf_op jit(solution)/shard_map/ppermute | solution.py:319
  44.4 10.6 %collective-permute-done.17 = bf16[320,512]{1,0:T(8,128)(2,1)S(1)} collective-permute-done((bf16[320,512]{1,0:T(8,128)(2,1)S(1)}, bf16[320,512]{1,0:T(8,128)(2,1)S(1)}, u32[]{:S(2)}, u32[]{:S(2)}) %collective-permute-start.17) | collective-permute-done | bytes 327712 | tf_op jit(solution)/shard_map/ppermute | solution.py:323
  56.2 2.0 collective-permute-start.8
  60.7 2.0 collective-permute-start.6
  64.6 19.0 %collective-permute-done.7.w1 = bf16[512,2048]{1,0:T(8,128)(2,1)S(1)} collective-permute-done((bf16[512,2048]{1,0:T(8,128)(2,1)}, bf16[512,2048]{1,0:T(8,128)(2,1)S(1)}, u32[]{:S(2)}, u32[]{:S(2)}) %collective-permute-start.7) | collective-permute-done | bytes 2097184 | tf_op jit(solution)/shard_map/ppermute | solution.py:40
  85.4 2.4 %slice.39 = bf16[256,2048]{1,0:T(8,128)(2,1)} slice(bf16[512,2048]{1,0:T(8,128)(2,1)} %collective-permute-done.8.w2), slice={[256:512], [0:2048]} | slice | bytes 2097152 | tf_op jit(solution)/shard_map/slice | solution.py:329
  87.8 5.6 %shard_map.150 = bf16[256,320]{1,0:T(8,128)(2,1)} custom-call(s32[16]{0:T(128)} %dynamic-slice_bitcast_fusion.tab, bf16[64,5120]{1,0:T(8,128)(2,1)} %copy-done.16, bf16[64,5120]{1,0:T(8,128)(2,1)} %copy-done.19, bf16[64,5120]{1,0:T(8,128)(2,1)} %copy-done.20, bf16[32,5120]{1,0:T(8,128)(2,1)} %collective-permute-done.5.s3a, ...), custom_call_target="tpu_custom_call" | custom-call | flops 840000000 | bytes 6291456 | tf_op jit(solution)/shard_map/pallas_call | solution.py:154
  93.6 2.0 collective-permute-start.10
  95.6 2.5 %collective-permute-start.11 = (bf16[256,320]{1,0:T(8,128)(2,1)}, bf16[256,320]{1,0:T(8,128)(2,1)S(1)}, u32[]{:S(2)}, u32[]{:S(2)}) collective-permute-start(bf16[256,320]{1,0:T(8,128)(2,1)} %shard_map.150), channel_id=1, source_target_pairs={{0,2},{1,3},{2,0},{3,1},{4,6},{5,7},{6,4},{7,5},{8,10},{9,11},{10,... | collective-permute-start | bytes 491528 | tf_op jit(solution)/shard_map/ppermute | solution.py:40
  100.4 3.5 %collective-permute-done.11 = bf16[256,320]{1,0:T(8,128)(2,1)S(1)} collective-permute-done((bf16[256,320]{1,0:T(8,128)(2,1)}, bf16[256,320]{1,0:T(8,128)(2,1)S(1)}, u32[]{:S(2)}, u32[]{:S(2)}) %collective-permute-start.11) | collective-permute-done | bytes 163872 | tf_op jit(solution)/shard_map/ppermute | solution.py:40
  105.3 2.8 %collective-permute-start.12 = (bf16[256,1280]{1,0:T(8,128)(2,1)S(1)}, bf16[256,1280]{1,0:T(8,128)(2,1)S(1)}, u32[]{:S(2)}, u32[]{:S(2)}) collective-permute-start(bf16[256,1280]{1,0:T(8,128)(2,1)S(1)} %concatenate.7.h0), channel_id=1, source_target_pairs={{0,4},{1,5},{2,6},{3,7},{4,8},{5,9},{6,10},{7,11},{8,12},{9,13},{1... | collective-permute-start | bytes 1966088 | tf_op jit(solution)/shard_map/ppermute | solution.py:40
  108.0 8.7 %collective-permute-done.12.h1 = bf16[256,1280]{1,0:T(8,128)(2,1)S(1)} collective-permute-done((bf16[256,1280]{1,0:T(8,128)(2,1)S(1)}, bf16[256,1280]{1,0:T(8,128)(2,1)S(1)}, u32[]{:S(2)}, u32[]{:S(2)}) %collective-permute-start.12) | collective-permute-done | bytes 655392 | tf_op jit(solution)/shard_map/ppermute | solution.py:40
  116.8 3.8 %collective-permute-start.14 = (bf16[128,1280]{1,0:T(8,128)(2,1)S(1)}, bf16[128,1280]{1,0:T(8,128)(2,1)S(1)}, u32[]{:S(2)}, u32[]{:S(2)}) collective-permute-start(bf16[128,1280]{1,0:T(8,128)(2,1)S(1)} %slice.40), channel_id=1, source_target_pairs={{0,4},{1,5},{2,6},{3,7},{4,8},{5,9},{6,10},{7,11},{8,12},{9,13},{1... | collective-permute-start | bytes 983048 | tf_op jit(solution)/shard_map/ppermute | solution.py:40
  122.1 2.1 collective-permute-start.19
  124.2 2.4 %shard_map.152 = (bf16[128,2048]{1,0:T(8,128)(2,1)S(1)}, bf16[192,2048]{1,0:T(8,128)(2,1)S(1)}, bf16[128,2048]{1,0:T(8,128)(2,1)}, bf16[64,2048]{1,0:T(8,128)(2,1)}) custom-call(s32[16]{0:T(128)S(1)} %copy-done.5, bf16[128,8192]{1,0:T(8,128)(2,1)S(1)} %bitcast.19, bf16[128,8192]{1,0:T(8,128)(2,1)S(1)} %bitcast.20, bf16[128,8192]{1,0:T(8,128)(2,1)S(1)} %bitcast.21, ...), custom_call_target="tpu_custom_call" | custom-call | bytes 4194304 | tf_op jit(solution)/shard_map/pallas_call | solution.py:115
  126.6 2.1 collective-permute-done.14.h3a
  128.7 4.0 %collective-permute-done.15.h3b = bf16[128,1280]{1,0:T(8,128)(2,1)S(1)} collective-permute-done((bf16[128,1280]{1,0:T(8,128)(2,1)S(1)}, bf16[128,1280]{1,0:T(8,128)(2,1)S(1)}, u32[]{:S(2)}, u32[]{:S(2)}) %collective-permute-start.15) | collective-permute-done | bytes 327712 | tf_op jit(solution)/shard_map/ppermute | solution.py:40
  132.7 3.2 %collective-permute-start.20 = (bf16[128,2048]{1,0:T(8,128)(2,1)}, bf16[128,2048]{1,0:T(8,128)(2,1)}, u32[]{:S(2)}, u32[]{:S(2)}) collective-permute-start(bf16[128,2048]{1,0:T(8,128)(2,1)} %get-tuple-element.42), channel_id=1, source_target_pairs={{0,4},{1,5},{2,6},{3,7},{4,8},{5,9},{6,10},{7,11},{8,12},{9,13},{1... | collective-permute-start | bytes 1572872 | tf_op jit(solution)/shard_map/ppermute | solution.py:40
  135.9 12.8 %collective-permute-done.21.left = bf16[192,2048]{1,0:T(8,128)(2,1)S(1)} collective-permute-done((bf16[192,2048]{1,0:T(8,128)(2,1)S(1)}, bf16[192,2048]{1,0:T(8,128)(2,1)S(1)}, u32[]{:S(2)}, u32[]{:S(2)}) %collective-permute-start.21) | collective-permute-done | bytes 786464 | tf_op jit(solution)/shard_map/ppermute | solution.py:40
  151.4 5.6 %shard_map.151.v0 = bf16[256,512]{1,0:T(8,128)(2,1)} custom-call(s32[16]{0:T(128)} %dynamic-slice_bitcast_fusion.tab, bf16[256,1280]{1,0:T(8,128)(2,1)} %copy-done.15, bf16[256,1280]{1,0:T(8,128)(2,1)} %copy-done.17, bf16[256,1280]{1,0:T(8,128)(2,1)} %copy-done.18, bf16[128,1280]{1,0:T(8,128)(2,1)} %copy-done.21, bf16[128,1280]{1,0:T(8,128)(2,1)} %copy-done.22, ...), custom_call_target="tpu_custom_call" | custom-call | flops 1340000000 | bytes 8388608 | tf_op jit(solution)/shard_map/pallas_call | solution.py:188
  157.0 2.3 collective-permute-done.23.far_b
  162.3 2.9 %collective-permute-start.26 = (bf16[256,512]{1,0:T(8,128)(2,1)}, bf16[256,512]{1,0:T(8,128)(2,1)}, u32[]{:S(2)}, u32[]{:S(2)}) collective-permute-start(bf16[256,512]{1,0:T(8,128)(2,1)} %shard_map.151.v0), channel_id=1, source_target_pairs={{0,2},{1,3},{2,0},{3,1},{4,6},{5,7},{6,4},{7,5},{8,10},{9,11},{10,... | collective-permute-start | bytes 786440 | tf_op jit(solution)/shard_map/ppermute | solution.py:40
  167.0 4.4 %collective-permute-done.25.v2 = bf16[256,512]{1,0:T(8,128)(2,1)} collective-permute-done((bf16[256,512]{1,0:T(8,128)(2,1)}, bf16[256,512]{1,0:T(8,128)(2,1)}, u32[]{:S(2)}, u32[]{:S(2)}) %collective-permute-start.25) | collective-permute-done | bytes 262176 | tf_op jit(solution)/shard_map/ppermute | solution.py:40
  171.4 6.2 %collective-permute-done.26.v3 = bf16[256,512]{1,0:T(8,128)(2,1)} collective-permute-done((bf16[256,512]{1,0:T(8,128)(2,1)}, bf16[256,512]{1,0:T(8,128)(2,1)}, u32[]{:S(2)}, u32[]{:S(2)}) %collective-permute-start.26) | collective-permute-done | bytes 262176 | tf_op jit(solution)/shard_map/ppermute | solution.py:40
  178.6 2.5 %shard_map.153 = (bf16[128,2048]{1,0:T(8,128)(2,1)S(1)}, bf16[256,2048]{1,0:T(8,128)(2,1)S(1)}, bf16[128,2048]{1,0:T(8,128)(2,1)S(1)}) custom-call(s32[16]{0:T(128)S(1)} %copy-done.6, s32[1,256]{1,0:T(1,128)S(1)} %bitcast_select_fusion.dest, bf16[256,512]{1,0:T(8,128)(2,1)S(1)} %copy-done.1, bf16[256,512]{1,0:T(8,128)(2,1)} %collective-permute-done.24.v1, ...), custom_call_target="tpu_custom_call" | custom-call | flops 540000000 | bytes 6291456 | tf_op jit(solution)/shard_map/pallas_call | solution.py:225
  181.2 3.2 %collective-permute-start.27 = (bf16[128,2048]{1,0:T(8,128)(2,1)S(1)}, bf16[128,2048]{1,0:T(8,128)(2,1)S(1)}, u32[]{:S(2)}, u32[]{:S(2)}) collective-permute-start(bf16[128,2048]{1,0:T(8,128)(2,1)S(1)} %get-tuple-element.47.to_right), channel_id=1, source_target_pairs={{0,4},{1,5},{2,6},{3,7},{4,8},{5,9},{6,10},{7,11},{8,12},{9,13},{1... | collective-permute-start | bytes 1572872 | tf_op jit(solution)/shard_map/ppermute | solution.py:40
  185.7 7.0 %shard_map.154 = (f32[128,2048]{1,0:T(8,128)S(1)}, bf16[128,2048]{1,0:T(8,128)(2,1)S(1)}, bf16[128,2048]{1,0:T(8,128)(2,1)S(1)}, bf16[128,2048]{1,0:T(8,128)(2,1)S(1)}) custom-call(s32[16]{0:T(128)S(1)} %copy-done.6, bf16[128,2048]{1,0:T(8,128)(2,1)S(1)} %get-tuple-element.46.kept.own, bf16[256,2048]{1,0:T(8,128)(2,1)S(1)} %get-tuple-element.48.to_left, ...), custom_call_target="tpu_custom_call" | custom-call | flops 4300000256 | bytes 14680064 | tf_op jit(solution)/shard_map/pallas_call | solution.py:262
  192.7 4.5 %collective-permute-done.28.left = bf16[256,2048]{1,0:T(8,128)(2,1)S(1)} collective-permute-done((bf16[256,2048]{1,0:T(8,128)(2,1)S(1)}, bf16[256,2048]{1,0:T(8,128)(2,1)S(1)}, u32[]{:S(2)}, u32[]{:S(2)}) %collective-permute-start.28) | collective-permute-done | bytes 1048608 | tf_op jit(solution)/shard_map/ppermute | solution.py:40
  197.4 3.2 %collective-permute-start.31 = (bf16[128,2048]{1,0:T(8,128)(2,1)S(1)}, bf16[128,2048]{1,0:T(8,128)(2,1)S(1)}, u32[]{:S(2)}, u32[]{:S(2)}) collective-permute-start(bf16[128,2048]{1,0:T(8,128)(2,1)S(1)} %get-tuple-element.53), channel_id=1, source_target_pairs={{0,4},{1,5},{2,6},{3,7},{4,8},{5,9},{6,10},{7,11},{8,12},{9,13},{1... | collective-permute-start | bytes 1572872 | tf_op jit(solution)/shard_map/ppermute | solution.py:40
  202.0 5.7 %collective-permute-done.29.far = bf16[128,2048]{1,0:T(8,128)(2,1)S(1)} collective-permute-done((bf16[128,2048]{1,0:T(8,128)(2,1)S(1)}, bf16[128,2048]{1,0:T(8,128)(2,1)S(1)}, u32[]{:S(2)}, u32[]{:S(2)}) %collective-permute-start.29) | collective-permute-done | bytes 524320 | tf_op jit(solution)/shard_map/ppermute | solution.py:40
  209.8 9.1 %collective-permute-done.32 = bf16[128,2048]{1,0:T(8,128)(2,1)S(1)} collective-permute-done((bf16[128,2048]{1,0:T(8,128)(2,1)S(1)}, bf16[128,2048]{1,0:T(8,128)(2,1)S(1)}, u32[]{:S(2)}, u32[]{:S(2)}) %collective-permute-start.32) | collective-permute-done | bytes 524320 | tf_op jit(solution)/shard_map/ppermute | solution.py:40
  (121 shorter events, 41.4 us)
Async XLA Ops:
  7.2 80.6 %all-gather.3.cloned.1.call-start = ((), (), s32[]{:S(2)}) async-start(), calls=%async_computation | async-start | bytes 4177920 | tf_op jit(solution)/shard_map/all_gather | solution.py:318
  7.9 143.5 %all-gather.5.cloned.1.call-start = ((), (), s32[]{:S(2)}) async-start(), calls=%async_computation.1 | async-start | bytes 5570560 | tf_op jit(solution)/shard_map/all_gather | solution.py:328
  10.5 7.0 %collective-permute-start.2 = (bf16[16,5120]{1,0:T(8,128)(2,1)S(1)}, bf16[16,5120]{1,0:T(8,128)(2,1)S(1)}, u32[]{:S(2)}, u32[]{:S(2)}) collective-permute-start(bf16[16,5120]{1,0:T(8,128)(2,1)S(1)} %shard_map.149), channel_id=1, source_target_pairs={{0,2},{1,3},{2,0},{3,1},{4,6},{5,7},{6,4},{7,5},{8,10},{9,11},{10,... | collective-permute-start | bytes 491528 | tf_op jit(solution)/shard_map/ppermute | solution.py:40
  14.8 27.7 %collective-permute-start.16 = (bf16[320,512]{1,0:T(8,128)(2,1)}, bf16[320,512]{1,0:T(8,128)(2,1)S(1)}, u32[]{:S(2)}, u32[]{:S(2)}) collective-permute-start(bf16[320,512]{1,0:T(8,128)(2,1)} %param.21), channel_id=1, source_target_pairs={{0,0},{1,17},{2,34},{3,51},{4,68},{5,85},{6,102},{7,119},{8,136},{... | collective-permute-start | bytes 983048 | tf_op jit(solution)/shard_map/ppermute | solution.py:319
  19.6 35.5 %collective-permute-start.3 = (bf16[64,5120]{1,0:T(8,128)(2,1)S(1)}, bf16[64,5120]{1,0:T(8,128)(2,1)S(1)}, u32[]{:S(2)}, u32[]{:S(2)}) collective-permute-start(bf16[64,5120]{1,0:T(8,128)(2,1)S(1)} %pad_maximum_fusion.s0), channel_id=1, source_target_pairs={{0,4},{1,5},{2,6},{3,7},{4,8},{5,9},{6,10},{7,11},{8,12},{9,13},{1... | collective-permute-start | bytes 1966088 | tf_op jit(solution)/shard_map/ppermute | solution.py:40
  19.9 35.2 %collective-permute-start.4 = (bf16[64,5120]{1,0:T(8,128)(2,1)S(1)}, bf16[64,5120]{1,0:T(8,128)(2,1)S(1)}, u32[]{:S(2)}, u32[]{:S(2)}) collective-permute-start(bf16[64,5120]{1,0:T(8,128)(2,1)S(1)} %pad_maximum_fusion.s0), channel_id=1, source_target_pairs={{0,12},{1,13},{2,14},{3,15},{4,0},{5,1},{6,2},{7,3},{8,4},{9,5},{1... | collective-permute-start | bytes 1966088 | tf_op jit(solution)/shard_map/ppermute | solution.py:40
  42.5 12.5 %collective-permute-start.17 = (bf16[320,512]{1,0:T(8,128)(2,1)S(1)}, bf16[320,512]{1,0:T(8,128)(2,1)S(1)}, u32[]{:S(2)}, u32[]{:S(2)}) collective-permute-start(bf16[320,512]{1,0:T(8,128)(2,1)S(1)} %collective-permute-done.16), channel_id=1, source_target_pairs={{0,0},{1,1},{2,2},{3,3},{4,4},{5,5},{6,6},{7,7},{8,8},{9,9},{10,10... | collective-permute-start | bytes 983048 | tf_op jit(solution)/shard_map/ppermute | solution.py:323
  56.1 27.5 %collective-permute-start.7 = (bf16[512,2048]{1,0:T(8,128)(2,1)}, bf16[512,2048]{1,0:T(8,128)(2,1)S(1)}, u32[]{:S(2)}, u32[]{:S(2)}) collective-permute-start(bf16[512,2048]{1,0:T(8,128)(2,1)} %w0), channel_id=1, source_target_pairs={{0,1},{1,2},{2,3},{3,0},{4,5},{5,6},{6,7},{7,4},{8,9},{9,10},{10,1... | collective-permute-start | bytes 6291464 | tf_op jit(solution)/shard_map/ppermute | solution.py:40
  56.2 29.2 %collective-permute-start.8 = (bf16[512,2048]{1,0:T(8,128)(2,1)}, bf16[512,2048]{1,0:T(8,128)(2,1)}, u32[]{:S(2)}, u32[]{:S(2)}) collective-permute-start(bf16[512,2048]{1,0:T(8,128)(2,1)} %w0), channel_id=1, source_target_pairs={{0,3},{1,0},{2,1},{3,2},{4,7},{5,4},{6,5},{7,6},{8,11},{9,8},{10,9... | collective-permute-start | bytes 6291464 | tf_op jit(solution)/shard_map/ppermute | solution.py:40
  58.9 28.8 %collective-permute-start.5 = (bf16[32,5120]{1,0:T(8,128)(2,1)}, bf16[32,5120]{1,0:T(8,128)(2,1)}, u32[]{:S(2)}, u32[]{:S(2)}) collective-permute-start(bf16[32,5120]{1,0:T(8,128)(2,1)} %slice.36), channel_id=1, source_target_pairs={{0,4},{1,5},{2,6},{3,7},{4,8},{5,9},{6,10},{7,11},{8,12},{9,13},{1... | collective-permute-start | bytes 983048 | tf_op jit(solution)/shard_map/ppermute | solution.py:40
  60.7 27.1 %collective-permute-start.6 = (bf16[32,5120]{1,0:T(8,128)(2,1)}, bf16[32,5120]{1,0:T(8,128)(2,1)}, u32[]{:S(2)}, u32[]{:S(2)}) collective-permute-start(bf16[32,5120]{1,0:T(8,128)(2,1)} %slice.37), channel_id=1, source_target_pairs={{0,12},{1,13},{2,14},{3,15},{4,0},{5,1},{6,2},{7,3},{8,4},{9,5},{1... | collective-permute-start | bytes 983048 | tf_op jit(solution)/shard_map/ppermute | solution.py:40
  93.6 6.9 %collective-permute-start.10 = (bf16[256,320]{1,0:T(8,128)(2,1)}, bf16[256,320]{1,0:T(8,128)(2,1)S(1)}, u32[]{:S(2)}, u32[]{:S(2)}) collective-permute-start(bf16[256,320]{1,0:T(8,128)(2,1)} %shard_map.150), channel_id=1, source_target_pairs={{0,3},{1,0},{2,1},{3,2},{4,7},{5,4},{6,5},{7,6},{8,11},{9,8},{10,9... | collective-permute-start | bytes 491528 | tf_op jit(solution)/shard_map/ppermute | solution.py:40
  95.6 8.4 %collective-permute-start.11 = (bf16[256,320]{1,0:T(8,128)(2,1)}, bf16[256,320]{1,0:T(8,128)(2,1)S(1)}, u32[]{:S(2)}, u32[]{:S(2)}) collective-permute-start(bf16[256,320]{1,0:T(8,128)(2,1)} %shard_map.150), channel_id=1, source_target_pairs={{0,2},{1,3},{2,0},{3,1},{4,6},{5,7},{6,4},{7,5},{8,10},{9,11},{10,... | collective-permute-start | bytes 491528 | tf_op jit(solution)/shard_map/ppermute | solution.py:40
  105.3 11.5 %collective-permute-start.12 = (bf16[256,1280]{1,0:T(8,128)(2,1)S(1)}, bf16[256,1280]{1,0:T(8,128)(2,1)S(1)}, u32[]{:S(2)}, u32[]{:S(2)}) collective-permute-start(bf16[256,1280]{1,0:T(8,128)(2,1)S(1)} %concatenate.7.h0), channel_id=1, source_target_pairs={{0,4},{1,5},{2,6},{3,7},{4,8},{5,9},{6,10},{7,11},{8,12},{9,13},{1... | collective-permute-start | bytes 1966088 | tf_op jit(solution)/shard_map/ppermute | solution.py:40
  108.0 12.7 %collective-permute-start.13 = (bf16[256,1280]{1,0:T(8,128)(2,1)S(1)}, bf16[256,1280]{1,0:T(8,128)(2,1)S(1)}, u32[]{:S(2)}, u32[]{:S(2)}) collective-permute-start(bf16[256,1280]{1,0:T(8,128)(2,1)S(1)} %concatenate.7.h0), channel_id=1, source_target_pairs={{0,12},{1,13},{2,14},{3,15},{4,0},{5,1},{6,2},{7,3},{8,4},{9,5},{1... | collective-permute-start | bytes 1966088 | tf_op jit(solution)/shard_map/ppermute | solution.py:40
  116.8 11.9 %collective-permute-start.14 = (bf16[128,1280]{1,0:T(8,128)(2,1)S(1)}, bf16[128,1280]{1,0:T(8,128)(2,1)S(1)}, u32[]{:S(2)}, u32[]{:S(2)}) collective-permute-start(bf16[128,1280]{1,0:T(8,128)(2,1)S(1)} %slice.40), channel_id=1, source_target_pairs={{0,4},{1,5},{2,6},{3,7},{4,8},{5,9},{6,10},{7,11},{8,12},{9,13},{1... | collective-permute-start | bytes 983048 | tf_op jit(solution)/shard_map/ppermute | solution.py:40
  120.7 11.9 %collective-permute-start.15 = (bf16[128,1280]{1,0:T(8,128)(2,1)S(1)}, bf16[128,1280]{1,0:T(8,128)(2,1)S(1)}, u32[]{:S(2)}, u32[]{:S(2)}) collective-permute-start(bf16[128,1280]{1,0:T(8,128)(2,1)S(1)} %slice.41), channel_id=1, source_target_pairs={{0,12},{1,13},{2,14},{3,15},{4,0},{5,1},{6,2},{7,3},{8,4},{9,5},{1... | collective-permute-start | bytes 983048 | tf_op jit(solution)/shard_map/ppermute | solution.py:40
  120.8 28.6 %collective-permute-start.18 = (bf16[256,2048]{1,0:T(8,128)(2,1)}, bf16[256,2048]{1,0:T(8,128)(2,1)S(1)}, u32[]{:S(2)}, u32[]{:S(2)}) collective-permute-start(bf16[256,2048]{1,0:T(8,128)(2,1)} %slice.38), channel_id=1, source_target_pairs={{0,1},{1,2},{2,3},{3,0},{4,5},{5,6},{6,7},{7,4},{8,9},{9,10},{10,1... | collective-permute-start | bytes 3145736 | tf_op jit(solution)/shard_map/ppermute | solution.py:40
  122.1 28.4 %collective-permute-start.19 = (bf16[256,2048]{1,0:T(8,128)(2,1)}, bf16[256,2048]{1,0:T(8,128)(2,1)S(1)}, u32[]{:S(2)}, u32[]{:S(2)}) collective-permute-start(bf16[256,2048]{1,0:T(8,128)(2,1)} %slice.39), channel_id=1, source_target_pairs={{0,3},{1,0},{2,1},{3,2},{4,7},{5,4},{6,5},{7,6},{8,11},{9,8},{10,9... | collective-permute-start | bytes 3145736 | tf_op jit(solution)/shard_map/ppermute | solution.py:40
  132.7 16.0 %collective-permute-start.21 = (bf16[192,2048]{1,0:T(8,128)(2,1)S(1)}, bf16[192,2048]{1,0:T(8,128)(2,1)S(1)}, u32[]{:S(2)}, u32[]{:S(2)}) collective-permute-start(bf16[192,2048]{1,0:T(8,128)(2,1)S(1)} %get-tuple-element.43), channel_id=1, source_target_pairs={{0,12},{1,13},{2,14},{3,15},{4,0},{5,1},{6,2},{7,3},{8,4},{9,5},{1... | collective-permute-start | bytes 2359304 | tf_op jit(solution)/shard_map/ppermute | solution.py:40
  132.7 24.4 %collective-permute-start.20 = (bf16[128,2048]{1,0:T(8,128)(2,1)}, bf16[128,2048]{1,0:T(8,128)(2,1)}, u32[]{:S(2)}, u32[]{:S(2)}) collective-permute-start(bf16[128,2048]{1,0:T(8,128)(2,1)} %get-tuple-element.42), channel_id=1, source_target_pairs={{0,4},{1,5},{2,6},{3,7},{4,8},{5,9},{6,10},{7,11},{8,12},{9,13},{1... | collective-permute-start | bytes 1572872 | tf_op jit(solution)/shard_map/ppermute | solution.py:40
  135.9 21.1 %collective-permute-start.22 = (bf16[64,2048]{1,0:T(8,128)(2,1)}, bf16[64,2048]{1,0:T(8,128)(2,1)}, u32[]{:S(2)}, u32[]{:S(2)}) collective-permute-start(bf16[64,2048]{1,0:T(8,128)(2,1)} %get-tuple-element.44), channel_id=1, source_target_pairs={{0,8},{1,9},{2,10},{3,11},{4,12},{5,13},{6,14},{7,15},{8,0},{9,1},... | collective-permute-start | bytes 786440 | tf_op jit(solution)/shard_map/ppermute | solution.py:40
  149.4 9.9 %collective-permute-start.23 = (bf16[64,2048]{1,0:T(8,128)(2,1)}, bf16[64,2048]{1,0:T(8,128)(2,1)}, u32[]{:S(2)}, u32[]{:S(2)}) collective-permute-start(bf16[64,2048]{1,0:T(8,128)(2,1)} %slice.42), channel_id=1, source_target_pairs={{0,12},{1,13},{2,14},{3,15},{4,0},{5,1},{6,2},{7,3},{8,4},{9,5},{1... | collective-permute-start | bytes 786440 | tf_op jit(solution)/shard_map/ppermute | solution.py:40
  159.3 7.7 %collective-permute-start.24 = (bf16[256,512]{1,0:T(8,128)(2,1)}, bf16[256,512]{1,0:T(8,128)(2,1)}, u32[]{:S(2)}, u32[]{:S(2)}) collective-permute-start(bf16[256,512]{1,0:T(8,128)(2,1)} %shard_map.151.v0), channel_id=1, source_target_pairs={{0,1},{1,2},{2,3},{3,0},{4,5},{5,6},{6,7},{7,4},{8,9},{9,10},{10,1... | collective-permute-start | bytes 786440 | tf_op jit(solution)/shard_map/ppermute | solution.py:40
  161.3 10.1 %collective-permute-start.25 = (bf16[256,512]{1,0:T(8,128)(2,1)}, bf16[256,512]{1,0:T(8,128)(2,1)}, u32[]{:S(2)}, u32[]{:S(2)}) collective-permute-start(bf16[256,512]{1,0:T(8,128)(2,1)} %shard_map.151.v0), channel_id=1, source_target_pairs={{0,3},{1,0},{2,1},{3,2},{4,7},{5,4},{6,5},{7,6},{8,11},{9,8},{10,9... | collective-permute-start | bytes 786440 | tf_op jit(solution)/shard_map/ppermute | solution.py:40
  162.3 15.2 %collective-permute-start.26 = (bf16[256,512]{1,0:T(8,128)(2,1)}, bf16[256,512]{1,0:T(8,128)(2,1)}, u32[]{:S(2)}, u32[]{:S(2)}) collective-permute-start(bf16[256,512]{1,0:T(8,128)(2,1)} %shard_map.151.v0), channel_id=1, source_target_pairs={{0,2},{1,3},{2,0},{3,1},{4,6},{5,7},{6,4},{7,5},{8,10},{9,11},{10,... | collective-permute-start | bytes 786440 | tf_op jit(solution)/shard_map/ppermute | solution.py:40
  181.1 16.1 %collective-permute-start.28 = (bf16[256,2048]{1,0:T(8,128)(2,1)S(1)}, bf16[256,2048]{1,0:T(8,128)(2,1)S(1)}, u32[]{:S(2)}, u32[]{:S(2)}) collective-permute-start(bf16[256,2048]{1,0:T(8,128)(2,1)S(1)} %get-tuple-element.48.to_left), channel_id=1, source_target_pairs={{0,12},{1,13},{2,14},{3,15},{4,0},{5,1},{6,2},{7,3},{8,4},{9,5},{1... | collective-permute-start | bytes 3145736 | tf_op jit(solution)/shard_map/ppermute | solution.py:40
  181.2 20.8 %collective-permute-start.27 = (bf16[128,2048]{1,0:T(8,128)(2,1)S(1)}, bf16[128,2048]{1,0:T(8,128)(2,1)S(1)}, u32[]{:S(2)}, u32[]{:S(2)}) collective-permute-start(bf16[128,2048]{1,0:T(8,128)(2,1)S(1)} %get-tuple-element.47.to_right), channel_id=1, source_target_pairs={{0,4},{1,5},{2,6},{3,7},{4,8},{5,9},{6,10},{7,11},{8,12},{9,13},{1... | collective-permute-start | bytes 1572872 | tf_op jit(solution)/shard_map/ppermute | solution.py:40
  197.3 10.5 %collective-permute-start.29 = (bf16[128,2048]{1,0:T(8,128)(2,1)S(1)}, bf16[128,2048]{1,0:T(8,128)(2,1)S(1)}, u32[]{:S(2)}, u32[]{:S(2)}) collective-permute-start(bf16[128,2048]{1,0:T(8,128)(2,1)S(1)} %slice.34), channel_id=1, source_target_pairs={{0,12},{1,13},{2,14},{3,15},{4,0},{5,1},{6,2},{7,3},{8,4},{9,5},{1... | collective-permute-start | bytes 1572872 | tf_op jit(solution)/shard_map/ppermute | solution.py:40
  197.3 21.6 %collective-permute-start.32 = (bf16[128,2048]{1,0:T(8,128)(2,1)S(1)}, bf16[128,2048]{1,0:T(8,128)(2,1)S(1)}, u32[]{:S(2)}, u32[]{:S(2)}) collective-permute-start(bf16[128,2048]{1,0:T(8,128)(2,1)S(1)} %get-tuple-element.54), channel_id=1, source_target_pairs={{0,12},{1,13},{2,14},{3,15},{4,0},{5,1},{6,2},{7,3},{8,4},{9,5},{1... | collective-permute-start | bytes 1572872 | tf_op jit(solution)/shard_map/ppermute | solution.py:40
  197.4 21.5 %collective-permute-start.31 = (bf16[128,2048]{1,0:T(8,128)(2,1)S(1)}, bf16[128,2048]{1,0:T(8,128)(2,1)S(1)}, u32[]{:S(2)}, u32[]{:S(2)}) collective-permute-start(bf16[128,2048]{1,0:T(8,128)(2,1)S(1)} %get-tuple-element.53), channel_id=1, source_target_pairs={{0,4},{1,5},{2,6},{3,7},{4,8},{5,9},{6,10},{7,11},{8,12},{9,13},{1... | collective-permute-start | bytes 1572872 | tf_op jit(solution)/shard_map/ppermute | solution.py:40
  200.7 18.3 %collective-permute-start.30 = (bf16[128,2048]{1,0:T(8,128)(2,1)S(1)}, bf16[128,2048]{1,0:T(8,128)(2,1)S(1)}, u32[]{:S(2)}, u32[]{:S(2)}) collective-permute-start(bf16[128,2048]{1,0:T(8,128)(2,1)S(1)} %get-tuple-element.49), channel_id=1, source_target_pairs={{0,8},{1,9},{2,10},{3,11},{4,12},{5,13},{6,14},{7,15},{8,0},{9,1},... | collective-permute-start | bytes 1572872 | tf_op jit(solution)/shard_map/ppermute | solution.py:40
  (31 other events, 472.7 us)
Sparse Core Ops, SparseCore 0:
  9.8 49.2 all-gather.2
  60.9 41.6 all-gather.4

commit v6 on v2

--- a/solution.py
+++ b/solution.py
@@ -32,8 +32,20 @@
     for which in (1, 2)
     for step in (1, -1, 2)
 }
-SHUFFLE = [(a * 16 + b, (a ^ b) * 16 + b) for a in range(16) for b in range(16)]
-TURN = [(a * 16 + b, a * 16 + (a ^ b)) for a in range(16) for b in range(16)]
+LINES = {
+    (axis, step): [
+        (c * 16 + t, c * 16 + place(1 if axis == "y" else 0, t, 1, step)) for c in range(2) for t in range(16)
+    ]
+    for axis in "yx"
+    for step in (1, -1, 2)
+}
+SHUFFLE = [
+    ((z * 2 + c) * 16 + y * 4 + x, ((y * 2 + z % 2) * 2 + c) * 16 + z // 2 * 4 + x)
+    for z in range(8)
+    for c in range(2)
+    for y in range(4)
+    for x in range(4)
+]
 
 
 def hop(value, which, step):
@@ -42,6 +54,10 @@
 
 def around(value, which):
     return hop(value, which, 1), hop(value, which, -1), hop(value, which, 2)
+
+
+def line(value, axis, step):
+    return lax.ppermute(value, ("mb", "tp"), LINES[axis, step])
 
 
 def after(value, *others):
@@ -149,37 +165,40 @@
     )(tab, *pieces, weight, bias)
 
 
-def down_kernel(tab, h0, h1, h2, h3, weight, bias_ref, out_ref, units, held, sems):
+def down_kernel(nat, h0, h1, h2, h3, weight, own, left, right, far, units, held, sems):
     copies = []
-    for i2, piece in enumerate((h0, h1, h2, h3)):
-        copies.append((piece, units.at[i2]))
-        for i1 in range(4):
-            k = i2 * 4 + i1
-            source = weight.at[pl.ds(pl.multiple_of((tab[k] ^ tab[0]) * 320, 320), 320)]
-            copies.append((source, held.at[pl.ds(k * 320, 320)]))
+    for k, piece in enumerate((h0, h1, h2, h3)):
+        copies.append((piece, units.at[k]))
+        for j in range(4):
+            slot = nat[k * 4] // 4 * 4 + nat[j] % 4
+            source = weight.at[pl.ds(pl.multiple_of(slot * 320, 320), 320)]
+            copies.append((source, held.at[k, :, pl.ds(j * 512, 512)]))
     copies = start(copies, sems)
-    total = bias_ref[tab[0]]
-    for i2 in range(4):
-        for copy in copies[i2 * 5 : i2 * 5 + 5]:
+    total = 0.0
+    for k in range(4):
+        for copy in copies[k * 5 : k * 5 + 5]:
             copy.wait()
-        total = total + jnp.dot(units[i2], held[i2 * 1280 : (i2 + 1) * 1280, :], preferred_element_type=F32)
-    out_ref[...] = total.astype(BF16)
-
-
-def down(tab, pieces, weight, bias):
+        total = total + jnp.dot(units[k], held[k], preferred_element_type=F32)
+    own[...] = total[:, 0:512]
+    left[...] = total[:, 512:1024].astype(BF16)
+    right[...] = total[:, 1024:1536].astype(BF16)
+    far[...] = total[:, 1536:2048].astype(BF16)
+
+
+def down(nat, pieces, weight):
     return pl.pallas_call(
         down_kernel,
-        out_shape=jax.ShapeDtypeStruct((256, 512), BF16),
-        in_specs=[SMEM] + [ANY] * 5 + [VMEM],
-        out_specs=VMEM,
+        out_shape=[jax.ShapeDtypeStruct((256, 512), F32)] + [jax.ShapeDtypeStruct((256, 512), BF16)] * 3,
+        in_specs=[SMEM] + [ANY] * 5,
+        out_specs=[VMEM] * 4,
         scratch_shapes=[
-            pltpu.VMEM((4, 256, 1280), BF16),
-            pltpu.VMEM((5120, 512), BF16),
+            pltpu.VMEM((4, 256, 320), BF16),
+            pltpu.VMEM((4, 320, 2048), BF16),
             pltpu.SemaphoreType.DMA((20,)),
         ],
         compiler_params=params(56),
         cost_estimate=cost(1340 * 10**6, 8 * MIB),
-    )(tab, *pieces, weight, bias)
+    )(nat, *pieces, weight)
 
 
 def pick_kernel(tab, dest, v0, v1, v2, v3, *refs):
@@ -288,28 +307,33 @@
     kv_bias,
 ):
     tab = jnp.asarray(TABLE)[lax.axis_index("mb") * 16 + lax.axis_index("tp")]
+    nat = jnp.asarray(TABLE)[lax.axis_index("tp")]
     up_full = lax.all_gather(up_weight, ("enc", "mb"), axis=0, tiled=True)
     down_part = lax.ppermute(down_weight, ("enc", "mb", "tp"), SHUFFLE)
 
     merged = merge(patches[0, 0], merge_gain, merge_bias)
     near = jnp.concatenate([merged, *around(merged, 1)], axis=0)
-    down_part = lax.ppermute(after(down_part, near), ("enc", "mb", "tp"), TURN)
     group = (near, *around(near, 2))
     down_full = lax.all_gather(after(down_part, *group), ("enc", "mb"), axis=0, tiled=True)
 
-    kv_weight = after(kv_weight, near)
+    kv_weight = after(kv_weight, *group)
     kv_right, kv_left = hop(kv_weight, 1, 1), hop(kv_weight, 1, -1)
+    far_right, far_left = kv_right[:256], kv_left[256:]
     own, to_left, to_right, to_far = pack(tab, text_embed[0, 0])
+    hidden = up(tab, group, up_full, up_bias.reshape(16, 1, 320))
+    units = (hidden, line(hidden, "y", 1), line(hidden, "y", -1), line(hidden, "y", 2))
+    moved = (*units, far_right, far_left, to_left, to_right, to_far)
+    *units, far_right, far_left, to_left, to_right, to_far = lax.optimization_barrier(moved)
+
+    weights = (kv_weight, kv_right, kv_left, hop(far_right, 1, 1), hop(far_left, 1, -1))
     text = (own, hop(to_right, 2, 1), hop(to_left, 2, -1), hop(to_far, 2, 2))
-
-    up_full = after(up_full, kv_right, kv_left, *text)
-    hidden = up(tab, group, up_full, up_bias.reshape(16, 1, 320))
-    near = jnp.concatenate([hidden, *around(hidden, 1)], axis=1)
-    right, left = lax.optimization_barrier((kv_right, kv_left, near))[:2]
-    weights = (kv_weight, kv_right, kv_left, hop(right[:256], 1, 1), hop(left[256:], 1, -1))
-    units = (near, *around(near, 2))
-    down_full = after(down_full, weights[3], weights[4])
-    visual = down(tab, units, down_full, down_bias.reshape(16, 1, 512))
+    down_full = after(down_full, weights[3], weights[4], *text)
+    own, to_left, to_right, to_far = down(nat, units, down_full)
+    bias = lax.dynamic_slice_in_dim(down_bias, lax.axis_index("tp") * 512, 512, 0)
+    total = own + bias
+    for value in (line(to_far, "x", 2), line(to_right, "x", 1), line(to_left, "x", -1)):
+        total = total + value.astype(F32)
+    visual = total.astype(BF16)
     visual = (visual, *around(visual, 1))
 
     live_rows = patch_counts[0, 0] // 4

time: 202 us -> 198 us (0.980); the launches traced: 198 us -> 197 us
  starting transfers between devices: 72.6 us -> 47.9 us
  waiting for transfers between devices: 74.1 us -> 95.8 us
    ppermute x28 -> x22, starting transfers between devices: 66.4 us -> 35.6 us  [hop(): return lax.ppermute(value, ('mb', 'tp'), HOPS[which, step])]
    all_gather x1, waiting for transfers between devices: 0.01 us -> 13.5 us  [per_device(): up_full = lax.all_gather(up_weight, ('enc', 'mb'), axis=0, tiled=True)]
    ppermute x1 -> x6, waiting for transfers between devices: 8.13 us -> 14.4 us  [line(): return lax.ppermute(value, ('mb', 'tp'), LINES[axis, step])]
    ppermute x1 -> x6, starting transfers between devices: 4.54 us -> 10.6 us  [line(): return lax.ppermute(value, ('mb', 'tp'), LINES[axis, step])]
    ppermute x28 -> x22, waiting for transfers between devices: 65.2 us -> 67.2 us  [hop(): return lax.ppermute(value, ('mb', 'tp'), HOPS[which, step])]
    unnamed x40 -> x50, local copies, waits for them, and re-layouts: 6.5 us -> 8 us
  transfers between devices with their start and end apart: 32 -> 31, of which waited for: 18 -> 20; matrix products, arithmetic and copies ran while one was open for 3% -> 3% of each run, Pallas kernels for 9% -> 8%
where the time goes in v6:
time: 198 us; the launch traced here: 197 us
  waiting for transfers between devices  95.8 us (48%)
  starting transfers between devices  47.9 us (24%)
  Pallas kernels  23.5 us (12%)
  between operations  14.3 us (7%)
  local copies, waits for them, and re-layouts  13 us (7%)
  other arithmetic  2.52 us (1%)
    ppermute x22, waiting for transfers between devices, hop(): return lax.ppermute(value, ('mb', 'tp'), HOPS[which, step])  67.2 us
    ppermute x22, starting transfers between devices, hop(): return lax.ppermute(value, ('mb', 'tp'), HOPS[which, step])  35.6 us
    ppermute x6, waiting for transfers between devices, line(): return lax.ppermute(value, ('mb', 'tp'), LINES[axis, step])  14.4 us
    all_gather x1, waiting for transfers between devices, per_device(): up_full = lax.all_gather(up_weight, ('enc', 'mb'), axis=0, tiled=True)  13.5 us
    ppermute x6, starting transfers between devices, line(): return lax.ppermute(value, ('mb', 'tp'), LINES[axis, step])  10.6 us
    unnamed x50, local copies, waits for them, and re-layouts  8 us
    pallas_call x1, Pallas kernels, product(): pl.pallas_call(product_kernel, out_shape=[jax.ShapeDtypeStruct((128, 2048...  7 us
    pallas_call x1, Pallas kernels, down(): pl.pallas_call(down_kernel, out_shape=[jax.ShapeDtypeStruct((256, 512), F...  5.98 us
  transfers between devices with their start and end apart: 31, of which 20 were waited for; matrix products, arithmetic and copies ran while one was open for 3% of the time, Pallas kernels for 8%

profile of v6, /device:TPU:32, one launch (start us, length us, event | category | flops | bytes accessed | tf_op | source)
XLA Modules:
  0.0 197.0 jit_solution(2405488400392752924)
XLA Ops:
  13.9 1.8 collective-permute-start.2
  17.4 3.2 %collective-permute-done.2 = bf16[16,5120]{1,0:T(8,128)(2,1)S(1)} collective-permute-done((bf16[16,5120]{1,0:T(8,128)(2,1)S(1)}, bf16[16,5120]{1,0:T(8,128)(2,1)S(1)}, u32[]{:S(2)}, u32[]{:S(2)}) %collective-permute-start.2) | collective-permute-done | bytes 163872 | tf_op jit(solution)/shard_map/ppermute | solution.py:52
  24.1 2.0 %collective-permute-start.5 = (bf16[64,5120]{1,0:T(8,128)(2,1)S(1)}, bf16[64,5120]{1,0:T(8,128)(2,1)S(1)}, u32[]{:S(2)}, u32[]{:S(2)}) collective-permute-start(bf16[64,5120]{1,0:T(8,128)(2,1)S(1)} %pad_maximum_fusion.s0), channel_id=1, source_target_pairs={{0,8},{1,9},{2,10},{3,11},{4,12},{5,13},{6,14},{7,15},{8,0},{9,1},... | collective-permute-start | bytes 1966088 | tf_op jit(solution)/shard_map/ppermute | solution.py:52
  27.7 6.3 %collective-permute-done.3.s1 = bf16[64,5120]{1,0:T(8,128)(2,1)S(1)} collective-permute-done((bf16[64,5120]{1,0:T(8,128)(2,1)S(1)}, bf16[64,5120]{1,0:T(8,128)(2,1)S(1)}, u32[]{:S(2)}, u32[]{:S(2)}) %collective-permute-start.3) | collective-permute-done | bytes 655392 | tf_op jit(solution)/shard_map/ppermute | solution.py:52
  34.0 7.0 %collective-permute-done.4.s2 = bf16[64,5120]{1,0:T(8,128)(2,1)S(1)} collective-permute-done((bf16[64,5120]{1,0:T(8,128)(2,1)S(1)}, bf16[64,5120]{1,0:T(8,128)(2,1)S(1)}, u32[]{:S(2)}, u32[]{:S(2)}) %collective-permute-start.4) | collective-permute-done | bytes 655392 | tf_op jit(solution)/shard_map/ppermute | solution.py:52
  40.9 10.6 %collective-permute-done.5.s3 = bf16[64,5120]{1,0:T(8,128)(2,1)S(1)} collective-permute-done((bf16[64,5120]{1,0:T(8,128)(2,1)S(1)}, bf16[64,5120]{1,0:T(8,128)(2,1)S(1)}, u32[]{:S(2)}, u32[]{:S(2)}) %collective-permute-start.5) | collective-permute-done | bytes 655392 | tf_op jit(solution)/shard_map/ppermute | solution.py:52
  53.1 2.6 %collective-permute-start.10 = (bf16[512,2048]{1,0:T(8,128)(2,1)}, bf16[512,2048]{1,0:T(8,128)(2,1)}, u32[]{:S(2)}, u32[]{:S(2)}) collective-permute-start(bf16[512,2048]{1,0:T(8,128)(2,1)} %w0), channel_id=1, source_target_pairs={{0,3},{1,0},{2,1},{3,2},{4,7},{5,4},{6,5},{7,6},{8,11},{9,8},{10,9... | collective-permute-start | bytes 6291464 | tf_op jit(solution)/shard_map/ppermute | solution.py:52
  57.8 13.5 %all-gather.3.cloned.1.call-done.weight = bf16[5120,320]{1,0:T(8,128)(2,1)} async-done(((bf16[320,320]{1,0:T(8,128)(2,1)}), bf16[5120,320]{1,0:T(8,128)(2,1)}) %all-gather.3.cloned.1.call-update) | async-done | bytes 3276816 | tf_op jit(solution)/shard_map/all_gather | solution.py:311
  71.3 5.7 %shard_map.150.h0 = bf16[256,320]{1,0:T(8,128)(2,1)} custom-call(s32[16]{0:T(128)} %get-tuple-element.63.tab, bf16[64,5120]{1,0:T(8,128)(2,1)} %copy-done.13, bf16[64,5120]{1,0:T(8,128)(2,1)} %copy-done.14, bf16[64,5120]{1,0:T(8,128)(2,1)} %copy-done.15, bf16[64,5120]{1,0:T(8,128)(2,1)} %copy-done.16, bf16[5120,320]{1,0:T(8,128)(2,1)} %all-gather.3.cloned.1.call-done.weight, ...), custom_call_target="tpu_custom_call" | custom-call | flops 840000000 | bytes 6291456 | tf_op jit(solution)/shard_map/pallas_call | solution.py:153
  78.3 2.1 %collective-permute-start.7 = (bf16[256,320]{1,0:T(8,128)(2,1)}, bf16[256,320]{1,0:T(8,128)(2,1)S(1)}, u32[]{:S(2)}, u32[]{:S(2)}) collective-permute-start(bf16[256,320]{1,0:T(8,128)(2,1)} %shard_map.150.h0), channel_id=1, source_target_pairs={{0,12},{1,13},{2,14},{3,15},{4,0},{5,1},{6,2},{7,3},{8,4},{9,5},{1... | collective-permute-start | bytes 491528 | tf_op jit(solution)/shard_map/ppermute | solution.py:60
  80.3 2.2 %collective-permute-start.8 = (bf16[256,320]{1,0:T(8,128)(2,1)}, bf16[256,320]{1,0:T(8,128)(2,1)S(1)}, u32[]{:S(2)}, u32[]{:S(2)}) collective-permute-start(bf16[256,320]{1,0:T(8,128)(2,1)} %shard_map.150.h0), channel_id=1, source_target_pairs={{0,8},{1,9},{2,10},{3,11},{4,12},{5,13},{6,14},{7,15},{8,0},{9,1},... | collective-permute-start | bytes 491528 | tf_op jit(solution)/shard_map/ppermute | solution.py:60
  84.0 1.9 slice.13
  86.5 5.4 %collective-permute-done.8.h3 = bf16[256,320]{1,0:T(8,128)(2,1)S(1)} collective-permute-done((bf16[256,320]{1,0:T(8,128)(2,1)}, bf16[256,320]{1,0:T(8,128)(2,1)S(1)}, u32[]{:S(2)}, u32[]{:S(2)}) %collective-permute-start.8) | collective-permute-done | bytes 163872 | tf_op jit(solution)/shard_map/ppermute | solution.py:60
  93.0 2.2 %collective-permute-start.13 = (bf16[256,2048]{1,0:T(8,128)(2,1)S(1)}, bf16[256,2048]{1,0:T(8,128)(2,1)S(1)}, u32[]{:S(2)}, u32[]{:S(2)}) collective-permute-start(bf16[256,2048]{1,0:T(8,128)(2,1)S(1)} %slice.13), channel_id=1, source_target_pairs={{0,3},{1,0},{2,1},{3,2},{4,7},{5,4},{6,5},{7,6},{8,11},{9,8},{10,9... | collective-permute-start | bytes 3145736 | tf_op jit(solution)/shard_map/ppermute | solution.py:52
  96.6 1.8 collective-permute-start.15
  99.2 11.9 %collective-permute-done.14.refs_1_ = bf16[128,2048]{1,0:T(8,128)(2,1)S(1)} collective-permute-done((bf16[128,2048]{1,0:T(8,128)(2,1)S(1)}, bf16[128,2048]{1,0:T(8,128)(2,1)S(1)}, u32[]{:S(2)}, u32[]{:S(2)}) %collective-permute-start.14) | collective-permute-done | bytes 524320 | tf_op jit(solution)/shard_map/ppermute | solution.py:52
  111.4 10.7 %collective-permute-done.16.refs_3_ = bf16[128,2048]{1,0:T(8,128)(2,1)S(1)} collective-permute-done((bf16[128,2048]{1,0:T(8,128)(2,1)S(1)}, bf16[128,2048]{1,0:T(8,128)(2,1)S(1)}, u32[]{:S(2)}, u32[]{:S(2)}) %collective-permute-start.16) | collective-permute-done | bytes 524320 | tf_op jit(solution)/shard_map/ppermute | solution.py:52
  124.1 6.0 %shard_map.152 = (f32[256,512]{1,0:T(8,128)}, bf16[256,512]{1,0:T(8,128)(2,1)}, bf16[256,512]{1,0:T(8,128)(2,1)}, bf16[256,512]{1,0:T(8,128)(2,1)}) custom-call(s32[16]{0:T(128)} %get-tuple-element.62.nat, bf16[256,320]{1,0:T(8,128)(2,1)} %shard_map.150.h0, bf16[256,320]{1,0:T(8,128)(2,1)} %copy-done.18, bf16[256,320]{1,0:T(8,128)(2,1)} %copy-done.19, ...), custom_call_target="tpu_custom_call" | custom-call | flops 1340000000 | bytes 8388608 | tf_op jit(solution)/shard_map/pallas_call | solution.py:189
  130.1 1.8 collective-permute-start.17
  131.9 3.2 %collective-permute-start.19 = (bf16[256,512]{1,0:T(8,128)(2,1)}, bf16[256,512]{1,0:T(8,128)(2,1)S(1)}, u32[]{:S(2)}, u32[]{:S(2)}) collective-permute-start(bf16[256,512]{1,0:T(8,128)(2,1)} %get-tuple-element.51), channel_id=1, source_target_pairs={{0,3},{1,0},{2,1},{3,2},{4,7},{5,4},{6,5},{7,6},{8,11},{9,8},{10,9... | collective-permute-start | bytes 786440 | tf_op jit(solution)/shard_map/ppermute | solution.py:60
  135.9 5.2 %collective-permute-done.17 = bf16[256,512]{1,0:T(8,128)(2,1)S(1)} collective-permute-done((bf16[256,512]{1,0:T(8,128)(2,1)}, bf16[256,512]{1,0:T(8,128)(2,1)S(1)}, u32[]{:S(2)}, u32[]{:S(2)}) %collective-permute-start.17) | collective-permute-done | bytes 262176 | tf_op jit(solution)/shard_map/ppermute | solution.py:60
  141.1 3.2 %collective-permute-done.18 = bf16[256,512]{1,0:T(8,128)(2,1)S(1)} collective-permute-done((bf16[256,512]{1,0:T(8,128)(2,1)}, bf16[256,512]{1,0:T(8,128)(2,1)S(1)}, u32[]{:S(2)}, u32[]{:S(2)}) %collective-permute-start.18) | collective-permute-done | bytes 262176 | tf_op jit(solution)/shard_map/ppermute | solution.py:60
  147.0 1.8 collective-permute-start.21
  149.9 3.3 %collective-permute-done.20.v1 = bf16[256,512]{1,0:T(8,128)(2,1)S(1)} collective-permute-done((bf16[256,512]{1,0:T(8,128)(2,1)S(1)}, bf16[256,512]{1,0:T(8,128)(2,1)S(1)}, u32[]{:S(2)}, u32[]{:S(2)}) %collective-permute-start.20) | collective-permute-done | bytes 262176 | tf_op jit(solution)/shard_map/ppermute | solution.py:52
  153.2 2.4 %collective-permute-done.21.v2 = bf16[256,512]{1,0:T(8,128)(2,1)S(1)} collective-permute-done((bf16[256,512]{1,0:T(8,128)(2,1)S(1)}, bf16[256,512]{1,0:T(8,128)(2,1)S(1)}, u32[]{:S(2)}, u32[]{:S(2)}) %collective-permute-start.21) | collective-permute-done | bytes 262176 | tf_op jit(solution)/shard_map/ppermute | solution.py:52
  158.6 2.7 %collective-permute-start.24 = (bf16[128,2048]{1,0:T(8,128)(2,1)S(1)}, bf16[128,2048]{1,0:T(8,128)(2,1)S(1)}, u32[]{:S(2)}, u32[]{:S(2)}) collective-permute-start(bf16[128,2048]{1,0:T(8,128)(2,1)S(1)} %get-tuple-element.54.e1), channel_id=1, source_target_pairs={{0,12},{1,13},{2,14},{3,15},{4,0},{5,1},{6,2},{7,3},{8,4},{9,5},{1... | collective-permute-start | bytes 1572872 | tf_op jit(solution)/shard_map/ppermute | solution.py:52
  165.4 7.0 %shard_map.155 = (f32[128,2048]{1,0:T(8,128)S(1)}, bf16[128,2048]{1,0:T(8,128)(2,1)S(1)}, bf16[128,2048]{1,0:T(8,128)(2,1)S(1)}, bf16[128,2048]{1,0:T(8,128)(2,1)S(1)}) custom-call(s32[16]{0:T(128)S(1)} %copy-done.4, bf16[128,2048]{1,0:T(8,128)(2,1)S(1)} %get-tuple-element.52.e0, bf16[128,2048]{1,0:T(8,128)(2,1)S(1)} %get-tuple-element.54.e1, ...), custom_call_target="tpu_custom_call" | custom-call | flops 4300000256 | bytes 14680064 | tf_op jit(solution)/shard_map/pallas_call | solution.py:254
  172.4 2.6 %collective-permute-start.26 = (bf16[128,2048]{1,0:T(8,128)(2,1)S(1)}, bf16[128,2048]{1,0:T(8,128)(2,1)S(1)}, u32[]{:S(2)}, u32[]{:S(2)}) collective-permute-start(bf16[128,2048]{1,0:T(8,128)(2,1)S(1)} %get-tuple-element.58), channel_id=1, source_target_pairs={{0,8},{1,9},{2,10},{3,11},{4,12},{5,13},{6,14},{7,15},{8,0},{9,1},... | collective-permute-start | bytes 1572872 | tf_op jit(solution)/shard_map/ppermute | solution.py:52
  175.0 3.2 %collective-permute-start.28 = (bf16[128,2048]{1,0:T(8,128)(2,1)S(1)}, bf16[128,2048]{1,0:T(8,128)(2,1)S(1)}, u32[]{:S(2)}, u32[]{:S(2)}) collective-permute-start(bf16[128,2048]{1,0:T(8,128)(2,1)S(1)} %get-tuple-element.60), channel_id=1, source_target_pairs={{0,12},{1,13},{2,14},{3,15},{4,0},{5,1},{6,2},{7,3},{8,4},{9,5},{1... | collective-permute-start | bytes 1572872 | tf_op jit(solution)/shard_map/ppermute | solution.py:52
  178.2 2.0 %shard_map.154 = (bf16[128,8192]{1,0:T(8,128)(2,1)}, f32[128,128]{1,0:T(8,128)S(1)}) custom-call(s32[16]{0:T(128)S(1)} %copy-done.4, bf16[128,2048]{1,0:T(8,128)(2,1)S(1)} %get-tuple-element.52.e0, bf16[128,2048]{1,0:T(8,128)(2,1)S(1)} %collective-permute-done.23.e1, bf16[128,2048]{1,0:T(8,128)(2,1)S(1)} %collective-permute-done.24.e2, ...), custom_call_target="tpu_custom_call" | custom-call | flops 4000000 | bytes 31457280 | tf_op jit(solution)/shard_map/pallas_call | solution.py:283
  180.3 3.1 %collective-permute-done.26 = bf16[128,2048]{1,0:T(8,128)(2,1)S(1)} collective-permute-done((bf16[128,2048]{1,0:T(8,128)(2,1)S(1)}, bf16[128,2048]{1,0:T(8,128)(2,1)S(1)}, u32[]{:S(2)}, u32[]{:S(2)}) %collective-permute-start.26) | collective-permute-done | bytes 524320 | tf_op jit(solution)/shard_map/ppermute | solution.py:52
  183.5 5.5 %collective-permute-done.27 = bf16[128,2048]{1,0:T(8,128)(2,1)S(1)} collective-permute-done((bf16[128,2048]{1,0:T(8,128)(2,1)S(1)}, bf16[128,2048]{1,0:T(8,128)(2,1)S(1)}, u32[]{:S(2)}, u32[]{:S(2)}) %collective-permute-start.27) | collective-permute-done | bytes 524320 | tf_op jit(solution)/shard_map/ppermute | solution.py:52
  (102 shorter events, 38.7 us)
Async XLA Ops:
  7.2 64.1 %all-gather.3.cloned.1.call-start = ((), (), s32[]{:S(2)}) async-start(), calls=%async_computation | async-start | bytes 4177920 | tf_op jit(solution)/shard_map/all_gather | solution.py:311
  7.9 116.1 %all-gather.5.cloned.1.call-start = ((), (), s32[]{:S(2)}) async-start(), calls=%async_computation.1 | async-start | bytes 5570560 | tf_op jit(solution)/shard_map/all_gather | solution.py:317
  10.5 6.6 %collective-permute-start = (bf16[16,5120]{1,0:T(8,128)(2,1)S(1)}, bf16[16,5120]{1,0:T(8,128)(2,1)S(1)}, u32[]{:S(2)}, u32[]{:S(2)}) collective-permute-start(bf16[16,5120]{1,0:T(8,128)(2,1)S(1)} %shard_map.149), channel_id=1, source_target_pairs={{0,1},{1,2},{2,3},{3,0},{4,5},{5,6},{6,7},{7,4},{8,9},{9,10},{10,1... | collective-permute-start | bytes 491528 | tf_op jit(solution)/shard_map/ppermute | solution.py:52
  12.1 5.3 %collective-permute-start.1 = (bf16[16,5120]{1,0:T(8,128)(2,1)S(1)}, bf16[16,5120]{1,0:T(8,128)(2,1)S(1)}, u32[]{:S(2)}, u32[]{:S(2)}) collective-permute-start(bf16[16,5120]{1,0:T(8,128)(2,1)S(1)} %shard_map.149), channel_id=1, source_target_pairs={{0,3},{1,0},{2,1},{3,2},{4,7},{5,4},{6,5},{7,6},{8,11},{9,8},{10,9... | collective-permute-start | bytes 491528 | tf_op jit(solution)/shard_map/ppermute | solution.py:52
  13.9 6.8 %collective-permute-start.2 = (bf16[16,5120]{1,0:T(8,128)(2,1)S(1)}, bf16[16,5120]{1,0:T(8,128)(2,1)S(1)}, u32[]{:S(2)}, u32[]{:S(2)}) collective-permute-start(bf16[16,5120]{1,0:T(8,128)(2,1)S(1)} %shard_map.149), channel_id=1, source_target_pairs={{0,2},{1,3},{2,0},{3,1},{4,6},{5,7},{6,4},{7,5},{8,10},{9,11},{10,... | collective-permute-start | bytes 491528 | tf_op jit(solution)/shard_map/ppermute | solution.py:52
  20.7 50.6 %copy-start.13 = (bf16[64,5120]{1,0:T(8,128)(2,1)}, bf16[64,5120]{1,0:T(8,128)(2,1)S(1)}, u32[]{:S(2)}) copy-start(bf16[64,5120]{1,0:T(8,128)(2,1)S(1)} %pad_maximum_fusion.s0) | copy-start | bytes 1966084
  20.7 13.2 %collective-permute-start.3 = (bf16[64,5120]{1,0:T(8,128)(2,1)S(1)}, bf16[64,5120]{1,0:T(8,128)(2,1)S(1)}, u32[]{:S(2)}, u32[]{:S(2)}) collective-permute-start(bf16[64,5120]{1,0:T(8,128)(2,1)S(1)} %pad_maximum_fusion.s0), channel_id=1, source_target_pairs={{0,4},{1,5},{2,6},{3,7},{4,8},{5,9},{6,10},{7,11},{8,12},{9,13},{1... | collective-permute-start | bytes 1966088 | tf_op jit(solution)/shard_map/ppermute | solution.py:52
  22.4 18.6 %collective-permute-start.4 = (bf16[64,5120]{1,0:T(8,128)(2,1)S(1)}, bf16[64,5120]{1,0:T(8,128)(2,1)S(1)}, u32[]{:S(2)}, u32[]{:S(2)}) collective-permute-start(bf16[64,5120]{1,0:T(8,128)(2,1)S(1)} %pad_maximum_fusion.s0), channel_id=1, source_target_pairs={{0,12},{1,13},{2,14},{3,15},{4,0},{5,1},{6,2},{7,3},{8,4},{9,5},{1... | collective-permute-start | bytes 1966088 | tf_op jit(solution)/shard_map/ppermute | solution.py:52
  24.1 27.5 %collective-permute-start.5 = (bf16[64,5120]{1,0:T(8,128)(2,1)S(1)}, bf16[64,5120]{1,0:T(8,128)(2,1)S(1)}, u32[]{:S(2)}, u32[]{:S(2)}) collective-permute-start(bf16[64,5120]{1,0:T(8,128)(2,1)S(1)} %pad_maximum_fusion.s0), channel_id=1, source_target_pairs={{0,8},{1,9},{2,10},{3,11},{4,12},{5,13},{6,14},{7,15},{8,0},{9,1},... | collective-permute-start | bytes 1966088 | tf_op jit(solution)/shard_map/ppermute | solution.py:52
  26.0 1.6 collective-permute-start.11
  52.4 31.4 %collective-permute-start.9 = (bf16[512,2048]{1,0:T(8,128)(2,1)}, bf16[512,2048]{1,0:T(8,128)(2,1)S(1)}, u32[]{:S(2)}, u32[]{:S(2)}) collective-permute-start(bf16[512,2048]{1,0:T(8,128)(2,1)} %w0), channel_id=1, source_target_pairs={{0,1},{1,2},{2,3},{3,0},{4,5},{5,6},{6,7},{7,4},{8,9},{9,10},{10,1... | collective-permute-start | bytes 6291464 | tf_op jit(solution)/shard_map/ppermute | solution.py:52
  53.1 30.8 %collective-permute-start.10 = (bf16[512,2048]{1,0:T(8,128)(2,1)}, bf16[512,2048]{1,0:T(8,128)(2,1)}, u32[]{:S(2)}, u32[]{:S(2)}) collective-permute-start(bf16[512,2048]{1,0:T(8,128)(2,1)} %w0), channel_id=1, source_target_pairs={{0,3},{1,0},{2,1},{3,2},{4,7},{5,4},{6,5},{7,6},{8,11},{9,8},{10,9... | collective-permute-start | bytes 6291464 | tf_op jit(solution)/shard_map/ppermute | solution.py:52
  77.0 9.3 %collective-permute-start.6 = (bf16[256,320]{1,0:T(8,128)(2,1)}, bf16[256,320]{1,0:T(8,128)(2,1)S(1)}, u32[]{:S(2)}, u32[]{:S(2)}) collective-permute-start(bf16[256,320]{1,0:T(8,128)(2,1)} %shard_map.150.h0), channel_id=1, source_target_pairs={{0,4},{1,5},{2,6},{3,7},{4,8},{5,9},{6,10},{7,11},{8,12},{9,13},{1... | collective-permute-start | bytes 491528 | tf_op jit(solution)/shard_map/ppermute | solution.py:60
  78.3 8.3 %collective-permute-start.7 = (bf16[256,320]{1,0:T(8,128)(2,1)}, bf16[256,320]{1,0:T(8,128)(2,1)S(1)}, u32[]{:S(2)}, u32[]{:S(2)}) collective-permute-start(bf16[256,320]{1,0:T(8,128)(2,1)} %shard_map.150.h0), channel_id=1, source_target_pairs={{0,12},{1,13},{2,14},{3,15},{4,0},{5,1},{6,2},{7,3},{8,4},{9,5},{1... | collective-permute-start | bytes 491528 | tf_op jit(solution)/shard_map/ppermute | solution.py:60
  80.3 11.6 %collective-permute-start.8 = (bf16[256,320]{1,0:T(8,128)(2,1)}, bf16[256,320]{1,0:T(8,128)(2,1)S(1)}, u32[]{:S(2)}, u32[]{:S(2)}) collective-permute-start(bf16[256,320]{1,0:T(8,128)(2,1)} %shard_map.150.h0), channel_id=1, source_target_pairs={{0,8},{1,9},{2,10},{3,11},{4,12},{5,13},{6,14},{7,15},{8,0},{9,1},... | collective-permute-start | bytes 491528 | tf_op jit(solution)/shard_map/ppermute | solution.py:60
  91.9 30.1 %collective-permute-start.12 = (bf16[256,2048]{1,0:T(8,128)(2,1)S(1)}, bf16[256,2048]{1,0:T(8,128)(2,1)S(1)}, u32[]{:S(2)}, u32[]{:S(2)}) collective-permute-start(bf16[256,2048]{1,0:T(8,128)(2,1)S(1)} %slice.12), channel_id=1, source_target_pairs={{0,1},{1,2},{2,3},{3,0},{4,5},{5,6},{6,7},{7,4},{8,9},{9,10},{10,1... | collective-permute-start | bytes 3145736 | tf_op jit(solution)/shard_map/ppermute | solution.py:52
  93.0 30.1 %collective-permute-start.13 = (bf16[256,2048]{1,0:T(8,128)(2,1)S(1)}, bf16[256,2048]{1,0:T(8,128)(2,1)S(1)}, u32[]{:S(2)}, u32[]{:S(2)}) collective-permute-start(bf16[256,2048]{1,0:T(8,128)(2,1)S(1)} %slice.13), channel_id=1, source_target_pairs={{0,3},{1,0},{2,1},{3,2},{4,7},{5,4},{6,5},{7,6},{8,11},{9,8},{10,9... | collective-permute-start | bytes 3145736 | tf_op jit(solution)/shard_map/ppermute | solution.py:52
  95.2 15.9 %collective-permute-start.14 = (bf16[128,2048]{1,0:T(8,128)(2,1)S(1)}, bf16[128,2048]{1,0:T(8,128)(2,1)S(1)}, u32[]{:S(2)}, u32[]{:S(2)}) collective-permute-start(bf16[128,2048]{1,0:T(8,128)(2,1)S(1)} %get-tuple-element.44), channel_id=1, source_target_pairs={{0,4},{1,5},{2,6},{3,7},{4,8},{5,9},{6,10},{7,11},{8,12},{9,13},{1... | collective-permute-start | bytes 1572872 | tf_op jit(solution)/shard_map/ppermute | solution.py:52
  96.6 14.8 %collective-permute-start.15 = (bf16[128,2048]{1,0:T(8,128)(2,1)S(1)}, bf16[128,2048]{1,0:T(8,128)(2,1)S(1)}, u32[]{:S(2)}, u32[]{:S(2)}) collective-permute-start(bf16[128,2048]{1,0:T(8,128)(2,1)S(1)} %get-tuple-element.45), channel_id=1, source_target_pairs={{0,12},{1,13},{2,14},{3,15},{4,0},{5,1},{6,2},{7,3},{8,4},{9,5},{1... | collective-permute-start | bytes 1572872 | tf_op jit(solution)/shard_map/ppermute | solution.py:52
  98.4 23.6 %collective-permute-start.16 = (bf16[128,2048]{1,0:T(8,128)(2,1)S(1)}, bf16[128,2048]{1,0:T(8,128)(2,1)S(1)}, u32[]{:S(2)}, u32[]{:S(2)}) collective-permute-start(bf16[128,2048]{1,0:T(8,128)(2,1)S(1)} %get-tuple-element.46), channel_id=1, source_target_pairs={{0,8},{1,9},{2,10},{3,11},{4,12},{5,13},{6,14},{7,15},{8,0},{9,1},... | collective-permute-start | bytes 1572872 | tf_op jit(solution)/shard_map/ppermute | solution.py:52
  130.1 11.0 %collective-permute-start.17 = (bf16[256,512]{1,0:T(8,128)(2,1)}, bf16[256,512]{1,0:T(8,128)(2,1)S(1)}, u32[]{:S(2)}, u32[]{:S(2)}) collective-permute-start(bf16[256,512]{1,0:T(8,128)(2,1)} %get-tuple-element.49), channel_id=1, source_target_pairs={{0,2},{1,3},{2,0},{3,1},{4,6},{5,7},{6,4},{7,5},{8,10},{9,11},{10,... | collective-permute-start | bytes 786440 | tf_op jit(solution)/shard_map/ppermute | solution.py:60
  131.9 12.4 %collective-permute-start.18 = (bf16[256,512]{1,0:T(8,128)(2,1)}, bf16[256,512]{1,0:T(8,128)(2,1)S(1)}, u32[]{:S(2)}, u32[]{:S(2)}) collective-permute-start(bf16[256,512]{1,0:T(8,128)(2,1)} %get-tuple-element.50), channel_id=1, source_target_pairs={{0,1},{1,2},{2,3},{3,0},{4,5},{5,6},{6,7},{7,4},{8,9},{9,10},{10,1... | collective-permute-start | bytes 786440 | tf_op jit(solution)/shard_map/ppermute | solution.py:60
  131.9 12.4 %collective-permute-start.19 = (bf16[256,512]{1,0:T(8,128)(2,1)}, bf16[256,512]{1,0:T(8,128)(2,1)S(1)}, u32[]{:S(2)}, u32[]{:S(2)}) collective-permute-start(bf16[256,512]{1,0:T(8,128)(2,1)} %get-tuple-element.51), channel_id=1, source_target_pairs={{0,3},{1,0},{2,1},{3,2},{4,7},{5,4},{6,5},{7,6},{8,11},{9,8},{10,9... | collective-permute-start | bytes 786440 | tf_op jit(solution)/shard_map/ppermute | solution.py:60
  145.5 7.7 %collective-permute-start.20 = (bf16[256,512]{1,0:T(8,128)(2,1)S(1)}, bf16[256,512]{1,0:T(8,128)(2,1)S(1)}, u32[]{:S(2)}, u32[]{:S(2)}) collective-permute-start(bf16[256,512]{1,0:T(8,128)(2,1)S(1)} %add_convert_fusion.1.v0), channel_id=1, source_target_pairs={{0,1},{1,2},{2,3},{3,0},{4,5},{5,6},{6,7},{7,4},{8,9},{9,10},{10,1... | collective-permute-start | bytes 786440 | tf_op jit(solution)/shard_map/ppermute | solution.py:52
  147.0 8.5 %collective-permute-start.21 = (bf16[256,512]{1,0:T(8,128)(2,1)S(1)}, bf16[256,512]{1,0:T(8,128)(2,1)S(1)}, u32[]{:S(2)}, u32[]{:S(2)}) collective-permute-start(bf16[256,512]{1,0:T(8,128)(2,1)S(1)} %add_convert_fusion.1.v0), channel_id=1, source_target_pairs={{0,3},{1,0},{2,1},{3,2},{4,7},{5,4},{6,5},{7,6},{8,11},{9,8},{10,9... | collective-permute-start | bytes 786440 | tf_op jit(solution)/shard_map/ppermute | solution.py:52
  148.8 7.9 %collective-permute-start.22 = (bf16[256,512]{1,0:T(8,128)(2,1)S(1)}, bf16[256,512]{1,0:T(8,128)(2,1)S(1)}, u32[]{:S(2)}, u32[]{:S(2)}) collective-permute-start(bf16[256,512]{1,0:T(8,128)(2,1)S(1)} %add_convert_fusion.1.v0), channel_id=1, source_target_pairs={{0,2},{1,3},{2,0},{3,1},{4,6},{5,7},{6,4},{7,5},{8,10},{9,11},{10,... | collective-permute-start | bytes 786440 | tf_op jit(solution)/shard_map/ppermute | solution.py:52
  158.0 17.0 %collective-permute-start.23 = (bf16[128,2048]{1,0:T(8,128)(2,1)S(1)}, bf16[128,2048]{1,0:T(8,128)(2,1)S(1)}, u32[]{:S(2)}, u32[]{:S(2)}) collective-permute-start(bf16[128,2048]{1,0:T(8,128)(2,1)S(1)} %get-tuple-element.53.e2), channel_id=1, source_target_pairs={{0,4},{1,5},{2,6},{3,7},{4,8},{5,9},{6,10},{7,11},{8,12},{9,13},{1... | collective-permute-start | bytes 1572872 | tf_op jit(solution)/shard_map/ppermute | solution.py:52
  158.6 19.7 %collective-permute-start.24 = (bf16[128,2048]{1,0:T(8,128)(2,1)S(1)}, bf16[128,2048]{1,0:T(8,128)(2,1)S(1)}, u32[]{:S(2)}, u32[]{:S(2)}) collective-permute-start(bf16[128,2048]{1,0:T(8,128)(2,1)S(1)} %get-tuple-element.54.e1), channel_id=1, source_target_pairs={{0,12},{1,13},{2,14},{3,15},{4,0},{5,1},{6,2},{7,3},{8,4},{9,5},{1... | collective-permute-start | bytes 1572872 | tf_op jit(solution)/shard_map/ppermute | solution.py:52
  161.3 16.9 %collective-permute-start.25 = (bf16[128,2048]{1,0:T(8,128)(2,1)S(1)}, bf16[128,2048]{1,0:T(8,128)(2,1)S(1)}, u32[]{:S(2)}, u32[]{:S(2)}) collective-permute-start(bf16[128,2048]{1,0:T(8,128)(2,1)S(1)} %get-tuple-element.55.e3), channel_id=1, source_target_pairs={{0,8},{1,9},{2,10},{3,11},{4,12},{5,13},{6,14},{7,15},{8,0},{9,1},... | collective-permute-start | bytes 1572872 | tf_op jit(solution)/shard_map/ppermute | solution.py:52
  172.4 11.1 %collective-permute-start.26 = (bf16[128,2048]{1,0:T(8,128)(2,1)S(1)}, bf16[128,2048]{1,0:T(8,128)(2,1)S(1)}, u32[]{:S(2)}, u32[]{:S(2)}) collective-permute-start(bf16[128,2048]{1,0:T(8,128)(2,1)S(1)} %get-tuple-element.58), channel_id=1, source_target_pairs={{0,8},{1,9},{2,10},{3,11},{4,12},{5,13},{6,14},{7,15},{8,0},{9,1},... | collective-permute-start | bytes 1572872 | tf_op jit(solution)/shard_map/ppermute | solution.py:52
  175.0 14.0 %collective-permute-start.27 = (bf16[128,2048]{1,0:T(8,128)(2,1)S(1)}, bf16[128,2048]{1,0:T(8,128)(2,1)S(1)}, u32[]{:S(2)}, u32[]{:S(2)}) collective-permute-start(bf16[128,2048]{1,0:T(8,128)(2,1)S(1)} %get-tuple-element.59), channel_id=1, source_target_pairs={{0,4},{1,5},{2,6},{3,7},{4,8},{5,9},{6,10},{7,11},{8,12},{9,13},{1... | collective-permute-start | bytes 1572872 | tf_op jit(solution)/shard_map/ppermute | solution.py:52
  175.0 14.0 %collective-permute-start.28 = (bf16[128,2048]{1,0:T(8,128)(2,1)S(1)}, bf16[128,2048]{1,0:T(8,128)(2,1)S(1)}, u32[]{:S(2)}, u32[]{:S(2)}) collective-permute-start(bf16[128,2048]{1,0:T(8,128)(2,1)S(1)} %get-tuple-element.60), channel_id=1, source_target_pairs={{0,12},{1,13},{2,14},{3,15},{4,0},{5,1},{6,2},{7,3},{8,4},{9,5},{1... | collective-permute-start | bytes 1572872 | tf_op jit(solution)/shard_map/ppermute | solution.py:52
  (24 other events, 358.1 us)
Sparse Core Ops, SparseCore 0:
  9.8 61.4 all-gather.2
  73.7 42.3 all-gather.4

commit v7 on v6

--- a/solution.py
+++ b/solution.py
@@ -40,7 +40,7 @@
     for step in (1, -1, 2)
 }
 SHUFFLE = [
-    ((z * 2 + c) * 16 + y * 4 + x, ((y * 2 + z % 2) * 2 + c) * 16 + z // 2 * 4 + x)
+    ((z * 2 + c) * 16 + y * 4 + x, (z // 2 * 4 + x) * 16 + y * 4 + z % 2 * 2 + c)
     for z in range(8)
     for c in range(2)
     for y in range(4)
@@ -170,7 +170,7 @@
     for k, piece in enumerate((h0, h1, h2, h3)):
         copies.append((piece, units.at[k]))
         for j in range(4):
-            slot = nat[k * 4] // 4 * 4 + nat[j] % 4
+            slot = nat[j * 4] // 4 * 4 + nat[k] % 4
             source = weight.at[pl.ds(pl.multiple_of(slot * 320, 320), 320)]
             copies.append((source, held.at[k, :, pl.ds(j * 512, 512)]))
     copies = start(copies, sems)
@@ -258,7 +258,7 @@
         in_specs=[SMEM] + [VMEM] * 5 + [block(n) for n in (512, 512, 512, 256, 256)],
         out_specs=[block(128)] * 4,
         scratch_shapes=[pltpu.VMEM((512, 2048), BF16)],
-        compiler_params=params(40),
+        compiler_params=params(56),
         cost_estimate=cost(4300 * 10**6, 14 * MIB),
     )(tab, *picked, gain, *weights)
 
@@ -321,7 +321,7 @@
     far_right, far_left = kv_right[:256], kv_left[256:]
     own, to_left, to_right, to_far = pack(tab, text_embed[0, 0])
     hidden = up(tab, group, up_full, up_bias.reshape(16, 1, 320))
-    units = (hidden, line(hidden, "y", 1), line(hidden, "y", -1), line(hidden, "y", 2))
+    units = (hidden, line(hidden, "x", 1), line(hidden, "x", -1), line(hidden, "x", 2))
     moved = (*units, far_right, far_left, to_left, to_right, to_far)
     *units, far_right, far_left, to_left, to_right, to_far = lax.optimization_barrier(moved)
 
@@ -331,7 +331,7 @@
     own, to_left, to_right, to_far = down(nat, units, down_full)
     bias = lax.dynamic_slice_in_dim(down_bias, lax.axis_index("tp") * 512, 512, 0)
     total = own + bias
-    for value in (line(to_far, "x", 2), line(to_right, "x", 1), line(to_left, "x", -1)):
+    for value in (line(to_far, "y", 2), line(to_right, "y", 1), line(to_left, "y", -1)):
         total = total + value.astype(F32)
     visual = total.astype(BF16)
     visual = (visual, *around(visual, 1))

time: 198 us -> 188 us (0.949)
  the two profiles are of different devices: /device:TPU:32 before, /device:TPU:224 now
where the time goes in v7:
time: 188 us; the launch traced here: 187 us
  waiting for transfers between devices  80.4 us (43%)
  starting transfers between devices  53.9 us (29%)
  Pallas kernels  25.8 us (14%)
  between operations  14.3 us (8%)
  local copies, waits for them, and re-layouts  10.4 us (6%)
  other arithmetic  2.49 us (1%)
    ppermute x22, waiting for transfers between devices, hop(): return lax.ppermute(value, ('mb', 'tp'), HOPS[which, step])  50.3 us
    ppermute x22, starting transfers between devices, hop(): return lax.ppermute(value, ('mb', 'tp'), HOPS[which, step])  39.4 us
    ppermute x1, waiting for transfers between devices, per_device(): down_part = lax.ppermute(down_weight, ('enc', 'mb', 'tp'), SHUFFLE)  17.3 us
    ppermute x6, waiting for transfers between devices, line(): return lax.ppermute(value, ('mb', 'tp'), LINES[axis, step])  11.2 us
    ppermute x6, starting transfers between devices, line(): return lax.ppermute(value, ('mb', 'tp'), LINES[axis, step])  10.3 us
    pallas_call x1, Pallas kernels, product(): pl.pallas_call(product_kernel, out_shape=[jax.ShapeDtypeStruct((128, 2048...  9.34 us
    pallas_call x1, Pallas kernels, down(): pl.pallas_call(down_kernel, out_shape=[jax.ShapeDtypeStruct((256, 512), F...  5.96 us
    pallas_call x1, Pallas kernels, up(): pl.pallas_call(up_kernel, out_shape=jax.ShapeDtypeStruct((256, 320), BF16...  5.68 us
  transfers between devices with their start and end apart: 31, of which 19 were waited for; matrix products, arithmetic and copies ran while one was open for 3% of the time, Pallas kernels for 10%

profile of v7, /device:TPU:224, one launch (start us, length us, event | category | flops | bytes accessed | tf_op | source)
XLA Modules:
  0.0 187.4 jit_solution(16121706994462512708)
XLA Ops:
  12.1 1.7 collective-permute-start.1
  13.9 1.8 collective-permute-start.2
  17.4 3.2 %collective-permute-done.2 = bf16[16,5120]{1,0:T(8,128)(2,1)S(1)} collective-permute-done((bf16[16,5120]{1,0:T(8,128)(2,1)S(1)}, bf16[16,5120]{1,0:T(8,128)(2,1)S(1)}, u32[]{:S(2)}, u32[]{:S(2)}) %collective-permute-start.2) | collective-permute-done | bytes 163872 | tf_op jit(solution)/shard_map/ppermute | solution.py:52
  22.4 1.7 collective-permute-start.4
  24.1 2.0 %collective-permute-start.5 = (bf16[64,5120]{1,0:T(8,128)(2,1)S(1)}, bf16[64,5120]{1,0:T(8,128)(2,1)S(1)}, u32[]{:S(2)}, u32[]{:S(2)}) collective-permute-start(bf16[64,5120]{1,0:T(8,128)(2,1)S(1)} %pad_maximum_fusion.s0), channel_id=1, source_target_pairs={{0,8},{1,9},{2,10},{3,11},{4,12},{5,13},{6,14},{7,15},{8,0},{9,1},... | collective-permute-start | bytes 1966088 | tf_op jit(solution)/shard_map/ppermute | solution.py:52
  26.0 4.2 %collective-permute-start.11 = (bf16[320,512]{1,0:T(8,128)(2,1)}, bf16[320,512]{1,0:T(8,128)(2,1)S(1)}, u32[]{:S(2)}, u32[]{:S(2)}) collective-permute-start(bf16[320,512]{1,0:T(8,128)(2,1)} %param.21), channel_id=1, source_target_pairs={{0,0},{1,16},{2,32},{3,48},{4,4},{5,20},{6,36},{7,52},{8,8},{9,24}... | collective-permute-start | bytes 983048 | tf_op jit(solution)/shard_map/ppermute | solution.py:312
  30.2 17.3 %collective-permute-done.11 = bf16[320,512]{1,0:T(8,128)(2,1)S(1)} collective-permute-done((bf16[320,512]{1,0:T(8,128)(2,1)}, bf16[320,512]{1,0:T(8,128)(2,1)S(1)}, u32[]{:S(2)}, u32[]{:S(2)}) %collective-permute-start.11) | collective-permute-done | bytes 327712 | tf_op jit(solution)/shard_map/ppermute | solution.py:312
  48.3 3.2 %collective-permute-start.10 = (bf16[512,2048]{1,0:T(8,128)(2,1)}, bf16[512,2048]{1,0:T(8,128)(2,1)}, u32[]{:S(2)}, u32[]{:S(2)}) collective-permute-start(bf16[512,2048]{1,0:T(8,128)(2,1)} %w0), channel_id=1, source_target_pairs={{0,3},{1,0},{2,1},{3,2},{4,7},{5,4},{6,5},{7,6},{8,11},{9,8},{10,9... | collective-permute-start | bytes 6291464 | tf_op jit(solution)/shard_map/ppermute | solution.py:52
  54.5 5.7 %shard_map.150.h0 = bf16[256,320]{1,0:T(8,128)(2,1)} custom-call(s32[16]{0:T(128)} %get-tuple-element.63.tab, bf16[64,5120]{1,0:T(8,128)(2,1)} %copy-done.11, bf16[64,5120]{1,0:T(8,128)(2,1)} %copy-done.13, bf16[64,5120]{1,0:T(8,128)(2,1)} %copy-done.14, bf16[64,5120]{1,0:T(8,128)(2,1)} %copy-done.15, bf16[5120,320]{1,0:T(8,128)(2,1)} %all-gather.3.cloned.1.call-done.weight, ...), custom_call_target="tpu_custom_call" | custom-call | flops 840000000 | bytes 6291456 | tf_op jit(solution)/shard_map/pallas_call | solution.py:153
  60.6 2.9 %collective-permute-start.7 = (bf16[256,320]{1,0:T(8,128)(2,1)}, bf16[256,320]{1,0:T(8,128)(2,1)S(1)}, u32[]{:S(2)}, u32[]{:S(2)}) collective-permute-start(bf16[256,320]{1,0:T(8,128)(2,1)} %shard_map.150.h0), channel_id=1, source_target_pairs={{0,3},{1,0},{2,1},{3,2},{4,7},{5,4},{6,5},{7,6},{8,11},{9,8},{10,9... | collective-permute-start | bytes 491528 | tf_op jit(solution)/shard_map/ppermute | solution.py:60
  63.5 2.1 %collective-permute-start.8 = (bf16[256,320]{1,0:T(8,128)(2,1)}, bf16[256,320]{1,0:T(8,128)(2,1)S(1)}, u32[]{:S(2)}, u32[]{:S(2)}) collective-permute-start(bf16[256,320]{1,0:T(8,128)(2,1)} %shard_map.150.h0), channel_id=1, source_target_pairs={{0,2},{1,3},{2,0},{3,1},{4,6},{5,7},{6,4},{7,5},{8,10},{9,11},{10,... | collective-permute-start | bytes 491528 | tf_op jit(solution)/shard_map/ppermute | solution.py:60
  66.9 13.1 %collective-permute-done.9.w1 = bf16[512,2048]{1,0:T(8,128)(2,1)} collective-permute-done((bf16[512,2048]{1,0:T(8,128)(2,1)}, bf16[512,2048]{1,0:T(8,128)(2,1)}, u32[]{:S(2)}, u32[]{:S(2)}) %collective-permute-start.9) | collective-permute-done | bytes 2097184 | tf_op jit(solution)/shard_map/ppermute | solution.py:52
  82.7 1.7 collective-permute-done.6.h1
  85.4 2.1 %collective-permute-start.12 = (bf16[256,2048]{1,0:T(8,128)(2,1)S(1)}, bf16[256,2048]{1,0:T(8,128)(2,1)S(1)}, u32[]{:S(2)}, u32[]{:S(2)}) collective-permute-start(bf16[256,2048]{1,0:T(8,128)(2,1)S(1)} %slice.12), channel_id=1, source_target_pairs={{0,1},{1,2},{2,3},{3,0},{4,5},{5,6},{6,7},{7,4},{8,9},{9,10},{10,1... | collective-permute-start | bytes 3145736 | tf_op jit(solution)/shard_map/ppermute | solution.py:52
  87.4 1.8 collective-permute-start.13
  89.3 2.1 %collective-permute-start.14 = (bf16[128,2048]{1,0:T(8,128)(2,1)S(1)}, bf16[128,2048]{1,0:T(8,128)(2,1)S(1)}, u32[]{:S(2)}, u32[]{:S(2)}) collective-permute-start(bf16[128,2048]{1,0:T(8,128)(2,1)S(1)} %get-tuple-element.44), channel_id=1, source_target_pairs={{0,4},{1,5},{2,6},{3,7},{4,8},{5,9},{6,10},{7,11},{8,12},{9,13},{1... | collective-permute-start | bytes 1572872 | tf_op jit(solution)/shard_map/ppermute | solution.py:52
  93.9 5.8 %collective-permute-done.14.refs_1_ = bf16[128,2048]{1,0:T(8,128)(2,1)S(1)} collective-permute-done((bf16[128,2048]{1,0:T(8,128)(2,1)S(1)}, bf16[128,2048]{1,0:T(8,128)(2,1)S(1)}, u32[]{:S(2)}, u32[]{:S(2)}) %collective-permute-start.14) | collective-permute-done | bytes 524320 | tf_op jit(solution)/shard_map/ppermute | solution.py:52
  100.6 5.3 %collective-permute-done.16.refs_3_ = bf16[128,2048]{1,0:T(8,128)(2,1)S(1)} collective-permute-done((bf16[128,2048]{1,0:T(8,128)(2,1)S(1)}, bf16[128,2048]{1,0:T(8,128)(2,1)S(1)}, u32[]{:S(2)}, u32[]{:S(2)}) %collective-permute-start.16) | collective-permute-done | bytes 524320 | tf_op jit(solution)/shard_map/ppermute | solution.py:52
  107.7 6.0 %shard_map.152 = (f32[256,512]{1,0:T(8,128)}, bf16[256,512]{1,0:T(8,128)(2,1)}, bf16[256,512]{1,0:T(8,128)(2,1)}, bf16[256,512]{1,0:T(8,128)(2,1)}) custom-call(s32[16]{0:T(128)} %get-tuple-element.62.nat, bf16[256,320]{1,0:T(8,128)(2,1)} %shard_map.150.h0, bf16[256,320]{1,0:T(8,128)(2,1)} %copy-done.17, bf16[256,320]{1,0:T(8,128)(2,1)} %copy-done.18, ...), custom_call_target="tpu_custom_call" | custom-call | flops 1340000000 | bytes 8388608 | tf_op jit(solution)/shard_map/pallas_call | solution.py:189
  116.8 1.7 collective-permute-start.19
  119.3 3.0 %collective-permute-done.17 = bf16[256,512]{1,0:T(8,128)(2,1)S(1)} collective-permute-done((bf16[256,512]{1,0:T(8,128)(2,1)}, bf16[256,512]{1,0:T(8,128)(2,1)S(1)}, u32[]{:S(2)}, u32[]{:S(2)}) %collective-permute-start.17) | collective-permute-done | bytes 262176 | tf_op jit(solution)/shard_map/ppermute | solution.py:60
  122.3 5.6 %collective-permute-done.18 = bf16[256,512]{1,0:T(8,128)(2,1)S(1)} collective-permute-done((bf16[256,512]{1,0:T(8,128)(2,1)}, bf16[256,512]{1,0:T(8,128)(2,1)S(1)}, u32[]{:S(2)}, u32[]{:S(2)}) %collective-permute-start.18) | collective-permute-done | bytes 262176 | tf_op jit(solution)/shard_map/ppermute | solution.py:60
  129.2 3.2 %collective-permute-start.21 = (bf16[256,512]{1,0:T(8,128)(2,1)S(1)}, bf16[256,512]{1,0:T(8,128)(2,1)S(1)}, u32[]{:S(2)}, u32[]{:S(2)}) collective-permute-start(bf16[256,512]{1,0:T(8,128)(2,1)S(1)} %add_convert_fusion.1.v0), channel_id=1, source_target_pairs={{0,3},{1,0},{2,1},{3,2},{4,7},{5,4},{6,5},{7,6},{8,11},{9,8},{10,9... | collective-permute-start | bytes 786440 | tf_op jit(solution)/shard_map/ppermute | solution.py:52
  132.8 4.7 %collective-permute-done.20.v1 = bf16[256,512]{1,0:T(8,128)(2,1)S(1)} collective-permute-done((bf16[256,512]{1,0:T(8,128)(2,1)S(1)}, bf16[256,512]{1,0:T(8,128)(2,1)S(1)}, u32[]{:S(2)}, u32[]{:S(2)}) %collective-permute-start.20) | collective-permute-done | bytes 262176 | tf_op jit(solution)/shard_map/ppermute | solution.py:52
  138.8 4.3 %collective-permute-done.22.v3 = bf16[256,512]{1,0:T(8,128)(2,1)S(1)} collective-permute-done((bf16[256,512]{1,0:T(8,128)(2,1)S(1)}, bf16[256,512]{1,0:T(8,128)(2,1)S(1)}, u32[]{:S(2)}, u32[]{:S(2)}) %collective-permute-start.22) | collective-permute-done | bytes 262176 | tf_op jit(solution)/shard_map/ppermute | solution.py:52
  146.2 5.6 %collective-permute-start.24 = (bf16[128,2048]{1,0:T(8,128)(2,1)S(1)}, bf16[128,2048]{1,0:T(8,128)(2,1)S(1)}, u32[]{:S(2)}, u32[]{:S(2)}) collective-permute-start(bf16[128,2048]{1,0:T(8,128)(2,1)S(1)} %get-tuple-element.54.e1), channel_id=1, source_target_pairs={{0,12},{1,13},{2,14},{3,15},{4,0},{5,1},{6,2},{7,3},{8,4},{9,5},{1... | collective-permute-start | bytes 1572872 | tf_op jit(solution)/shard_map/ppermute | solution.py:52
  153.2 9.3 %shard_map.155 = (f32[128,2048]{1,0:T(8,128)}, bf16[128,2048]{1,0:T(8,128)(2,1)}, bf16[128,2048]{1,0:T(8,128)(2,1)}, bf16[128,2048]{1,0:T(8,128)(2,1)}) custom-call(s32[16]{0:T(128)} %get-tuple-element.63.tab, bf16[128,2048]{1,0:T(8,128)(2,1)} %copy-done.1, bf16[128,2048]{1,0:T(8,128)(2,1)} %copy-done.9, bf16[128,2048]{1,0:T(8,128)(2,1)} %copy-done.10, ...), custom_call_target="tpu_custom_call" | custom-call | flops 4300000256 | bytes 14680064 | tf_op jit(solution)/shard_map/pallas_call | solution.py:254
  162.6 2.5 %collective-permute-start.26 = (bf16[128,2048]{1,0:T(8,128)(2,1)}, bf16[128,2048]{1,0:T(8,128)(2,1)S(1)}, u32[]{:S(2)}, u32[]{:S(2)}) collective-permute-start(bf16[128,2048]{1,0:T(8,128)(2,1)} %get-tuple-element.58), channel_id=1, source_target_pairs={{0,8},{1,9},{2,10},{3,11},{4,12},{5,13},{6,14},{7,15},{8,0},{9,1},... | collective-permute-start | bytes 1572872 | tf_op jit(solution)/shard_map/ppermute | solution.py:52
  165.1 3.2 %collective-permute-start.28 = (bf16[128,2048]{1,0:T(8,128)(2,1)}, bf16[128,2048]{1,0:T(8,128)(2,1)S(1)}, u32[]{:S(2)}, u32[]{:S(2)}) collective-permute-start(bf16[128,2048]{1,0:T(8,128)(2,1)} %get-tuple-element.60), channel_id=1, source_target_pairs={{0,12},{1,13},{2,14},{3,15},{4,0},{5,1},{6,2},{7,3},{8,4},{9,5},{1... | collective-permute-start | bytes 1572872 | tf_op jit(solution)/shard_map/ppermute | solution.py:52
  168.3 2.0 %shard_map.154 = (bf16[128,8192]{1,0:T(8,128)(2,1)}, f32[128,128]{1,0:T(8,128)S(1)}) custom-call(s32[16]{0:T(128)S(1)} %copy-done.5, bf16[128,2048]{1,0:T(8,128)(2,1)S(1)} %copy-done.2, bf16[128,2048]{1,0:T(8,128)(2,1)S(1)} %collective-permute-done.23.e1, bf16[128,2048]{1,0:T(8,128)(2,1)S(1)} %collective-permute-done.24.e2, ...), custom_call_target="tpu_custom_call" | custom-call | flops 4000000 | bytes 31457280 | tf_op jit(solution)/shard_map/pallas_call | solution.py:283
  170.4 3.5 %collective-permute-done.26 = bf16[128,2048]{1,0:T(8,128)(2,1)S(1)} collective-permute-done((bf16[128,2048]{1,0:T(8,128)(2,1)}, bf16[128,2048]{1,0:T(8,128)(2,1)S(1)}, u32[]{:S(2)}, u32[]{:S(2)}) %collective-permute-start.26) | collective-permute-done | bytes 524320 | tf_op jit(solution)/shard_map/ppermute | solution.py:52
  173.9 5.5 %collective-permute-done.27 = bf16[128,2048]{1,0:T(8,128)(2,1)S(1)} collective-permute-done((bf16[128,2048]{1,0:T(8,128)(2,1)}, bf16[128,2048]{1,0:T(8,128)(2,1)S(1)}, u32[]{:S(2)}, u32[]{:S(2)}) %collective-permute-start.27) | collective-permute-done | bytes 524320 | tf_op jit(solution)/shard_map/ppermute | solution.py:52
  (102 shorter events, 35.0 us)
Async XLA Ops:
  7.2 44.4 %copy-start.20 = (f32[5120]{0:T(1024)S(1)}, f32[5120]{0:T(1024)}, u32[]{:S(2)}) copy-start(f32[5120]{0:T(1024)} %param.20) | copy-start | bytes 61444
  7.2 47.3 %all-gather.3.cloned.1.call-start = ((), (), s32[]{:S(2)}) async-start(), calls=%async_computation | async-start | bytes 4177920 | tf_op jit(solution)/shard_map/all_gather | solution.py:311
  7.9 99.7 %all-gather.5.cloned.1.call-start = ((), (), s32[]{:S(2)}) async-start(), calls=%async_computation.1 | async-start | bytes 5570560 | tf_op jit(solution)/shard_map/all_gather | solution.py:317
  10.5 6.6 %collective-permute-start = (bf16[16,5120]{1,0:T(8,128)(2,1)S(1)}, bf16[16,5120]{1,0:T(8,128)(2,1)S(1)}, u32[]{:S(2)}, u32[]{:S(2)}) collective-permute-start(bf16[16,5120]{1,0:T(8,128)(2,1)S(1)} %shard_map.149), channel_id=1, source_target_pairs={{0,1},{1,2},{2,3},{3,0},{4,5},{5,6},{6,7},{7,4},{8,9},{9,10},{10,1... | collective-permute-start | bytes 491528 | tf_op jit(solution)/shard_map/ppermute | solution.py:52
  12.1 5.3 %collective-permute-start.1 = (bf16[16,5120]{1,0:T(8,128)(2,1)S(1)}, bf16[16,5120]{1,0:T(8,128)(2,1)S(1)}, u32[]{:S(2)}, u32[]{:S(2)}) collective-permute-start(bf16[16,5120]{1,0:T(8,128)(2,1)S(1)} %shard_map.149), channel_id=1, source_target_pairs={{0,3},{1,0},{2,1},{3,2},{4,7},{5,4},{6,5},{7,6},{8,11},{9,8},{10,9... | collective-permute-start | bytes 491528 | tf_op jit(solution)/shard_map/ppermute | solution.py:52
  13.9 6.8 %collective-permute-start.2 = (bf16[16,5120]{1,0:T(8,128)(2,1)S(1)}, bf16[16,5120]{1,0:T(8,128)(2,1)S(1)}, u32[]{:S(2)}, u32[]{:S(2)}) collective-permute-start(bf16[16,5120]{1,0:T(8,128)(2,1)S(1)} %shard_map.149), channel_id=1, source_target_pairs={{0,2},{1,3},{2,0},{3,1},{4,6},{5,7},{6,4},{7,5},{8,10},{9,11},{10,... | collective-permute-start | bytes 491528 | tf_op jit(solution)/shard_map/ppermute | solution.py:52
  20.7 26.7 %collective-permute-start.3 = (bf16[64,5120]{1,0:T(8,128)(2,1)S(1)}, bf16[64,5120]{1,0:T(8,128)(2,1)S(1)}, u32[]{:S(2)}, u32[]{:S(2)}) collective-permute-start(bf16[64,5120]{1,0:T(8,128)(2,1)S(1)} %pad_maximum_fusion.s0), channel_id=1, source_target_pairs={{0,4},{1,5},{2,6},{3,7},{4,8},{5,9},{6,10},{7,11},{8,12},{9,13},{1... | collective-permute-start | bytes 1966088 | tf_op jit(solution)/shard_map/ppermute | solution.py:52
  22.4 25.1 %collective-permute-start.4 = (bf16[64,5120]{1,0:T(8,128)(2,1)S(1)}, bf16[64,5120]{1,0:T(8,128)(2,1)S(1)}, u32[]{:S(2)}, u32[]{:S(2)}) collective-permute-start(bf16[64,5120]{1,0:T(8,128)(2,1)S(1)} %pad_maximum_fusion.s0), channel_id=1, source_target_pairs={{0,12},{1,13},{2,14},{3,15},{4,0},{5,1},{6,2},{7,3},{8,4},{9,5},{1... | collective-permute-start | bytes 1966088 | tf_op jit(solution)/shard_map/ppermute | solution.py:52
  24.1 23.5 %collective-permute-start.5 = (bf16[64,5120]{1,0:T(8,128)(2,1)S(1)}, bf16[64,5120]{1,0:T(8,128)(2,1)S(1)}, u32[]{:S(2)}, u32[]{:S(2)}) collective-permute-start(bf16[64,5120]{1,0:T(8,128)(2,1)S(1)} %pad_maximum_fusion.s0), channel_id=1, source_target_pairs={{0,8},{1,9},{2,10},{3,11},{4,12},{5,13},{6,14},{7,15},{8,0},{9,1},... | collective-permute-start | bytes 1966088 | tf_op jit(solution)/shard_map/ppermute | solution.py:52
  26.0 21.4 %collective-permute-start.11 = (bf16[320,512]{1,0:T(8,128)(2,1)}, bf16[320,512]{1,0:T(8,128)(2,1)S(1)}, u32[]{:S(2)}, u32[]{:S(2)}) collective-permute-start(bf16[320,512]{1,0:T(8,128)(2,1)} %param.21), channel_id=1, source_target_pairs={{0,0},{1,16},{2,32},{3,48},{4,4},{5,20},{6,36},{7,52},{8,8},{9,24}... | collective-permute-start | bytes 983048 | tf_op jit(solution)/shard_map/ppermute | solution.py:312
  48.2 31.9 %collective-permute-start.9 = (bf16[512,2048]{1,0:T(8,128)(2,1)}, bf16[512,2048]{1,0:T(8,128)(2,1)}, u32[]{:S(2)}, u32[]{:S(2)}) collective-permute-start(bf16[512,2048]{1,0:T(8,128)(2,1)} %w0), channel_id=1, source_target_pairs={{0,1},{1,2},{2,3},{3,0},{4,5},{5,6},{6,7},{7,4},{8,9},{9,10},{10,1... | collective-permute-start | bytes 6291464 | tf_op jit(solution)/shard_map/ppermute | solution.py:52
  48.3 33.1 %collective-permute-start.10 = (bf16[512,2048]{1,0:T(8,128)(2,1)}, bf16[512,2048]{1,0:T(8,128)(2,1)}, u32[]{:S(2)}, u32[]{:S(2)}) collective-permute-start(bf16[512,2048]{1,0:T(8,128)(2,1)} %w0), channel_id=1, source_target_pairs={{0,3},{1,0},{2,1},{3,2},{4,7},{5,4},{6,5},{7,6},{8,11},{9,8},{10,9... | collective-permute-start | bytes 6291464 | tf_op jit(solution)/shard_map/ppermute | solution.py:52
  60.2 24.3 %collective-permute-start.6 = (bf16[256,320]{1,0:T(8,128)(2,1)}, bf16[256,320]{1,0:T(8,128)(2,1)S(1)}, u32[]{:S(2)}, u32[]{:S(2)}) collective-permute-start(bf16[256,320]{1,0:T(8,128)(2,1)} %shard_map.150.h0), channel_id=1, source_target_pairs={{0,1},{1,2},{2,3},{3,0},{4,5},{5,6},{6,7},{7,4},{8,9},{9,10},{10,1... | collective-permute-start | bytes 491528 | tf_op jit(solution)/shard_map/ppermute | solution.py:60
  60.6 24.7 %collective-permute-start.7 = (bf16[256,320]{1,0:T(8,128)(2,1)}, bf16[256,320]{1,0:T(8,128)(2,1)S(1)}, u32[]{:S(2)}, u32[]{:S(2)}) collective-permute-start(bf16[256,320]{1,0:T(8,128)(2,1)} %shard_map.150.h0), channel_id=1, source_target_pairs={{0,3},{1,0},{2,1},{3,2},{4,7},{5,4},{6,5},{7,6},{8,11},{9,8},{10,9... | collective-permute-start | bytes 491528 | tf_op jit(solution)/shard_map/ppermute | solution.py:60
  63.5 21.8 %collective-permute-start.8 = (bf16[256,320]{1,0:T(8,128)(2,1)}, bf16[256,320]{1,0:T(8,128)(2,1)S(1)}, u32[]{:S(2)}, u32[]{:S(2)}) collective-permute-start(bf16[256,320]{1,0:T(8,128)(2,1)} %shard_map.150.h0), channel_id=1, source_target_pairs={{0,2},{1,3},{2,0},{3,1},{4,6},{5,7},{6,4},{7,5},{8,10},{9,11},{10,... | collective-permute-start | bytes 491528 | tf_op jit(solution)/shard_map/ppermute | solution.py:60
  85.4 21.3 %collective-permute-start.12 = (bf16[256,2048]{1,0:T(8,128)(2,1)S(1)}, bf16[256,2048]{1,0:T(8,128)(2,1)S(1)}, u32[]{:S(2)}, u32[]{:S(2)}) collective-permute-start(bf16[256,2048]{1,0:T(8,128)(2,1)S(1)} %slice.12), channel_id=1, source_target_pairs={{0,1},{1,2},{2,3},{3,0},{4,5},{5,6},{6,7},{7,4},{8,9},{9,10},{10,1... | collective-permute-start | bytes 3145736 | tf_op jit(solution)/shard_map/ppermute | solution.py:52
  87.4 20.2 %collective-permute-start.13 = (bf16[256,2048]{1,0:T(8,128)(2,1)S(1)}, bf16[256,2048]{1,0:T(8,128)(2,1)}, u32[]{:S(2)}, u32[]{:S(2)}) collective-permute-start(bf16[256,2048]{1,0:T(8,128)(2,1)S(1)} %slice.13), channel_id=1, source_target_pairs={{0,3},{1,0},{2,1},{3,2},{4,7},{5,4},{6,5},{7,6},{8,11},{9,8},{10,9... | collective-permute-start | bytes 3145736 | tf_op jit(solution)/shard_map/ppermute | solution.py:52
  89.3 10.4 %collective-permute-start.14 = (bf16[128,2048]{1,0:T(8,128)(2,1)S(1)}, bf16[128,2048]{1,0:T(8,128)(2,1)S(1)}, u32[]{:S(2)}, u32[]{:S(2)}) collective-permute-start(bf16[128,2048]{1,0:T(8,128)(2,1)S(1)} %get-tuple-element.44), channel_id=1, source_target_pairs={{0,4},{1,5},{2,6},{3,7},{4,8},{5,9},{6,10},{7,11},{8,12},{9,13},{1... | collective-permute-start | bytes 1572872 | tf_op jit(solution)/shard_map/ppermute | solution.py:52
  91.4 9.2 %collective-permute-start.15 = (bf16[128,2048]{1,0:T(8,128)(2,1)S(1)}, bf16[128,2048]{1,0:T(8,128)(2,1)S(1)}, u32[]{:S(2)}, u32[]{:S(2)}) collective-permute-start(bf16[128,2048]{1,0:T(8,128)(2,1)S(1)} %get-tuple-element.45), channel_id=1, source_target_pairs={{0,12},{1,13},{2,14},{3,15},{4,0},{5,1},{6,2},{7,3},{8,4},{9,5},{1... | collective-permute-start | bytes 1572872 | tf_op jit(solution)/shard_map/ppermute | solution.py:52
  92.5 13.4 %collective-permute-start.16 = (bf16[128,2048]{1,0:T(8,128)(2,1)S(1)}, bf16[128,2048]{1,0:T(8,128)(2,1)S(1)}, u32[]{:S(2)}, u32[]{:S(2)}) collective-permute-start(bf16[128,2048]{1,0:T(8,128)(2,1)S(1)} %get-tuple-element.46), channel_id=1, source_target_pairs={{0,8},{1,9},{2,10},{3,11},{4,12},{5,13},{6,14},{7,15},{8,0},{9,1},... | collective-permute-start | bytes 1572872 | tf_op jit(solution)/shard_map/ppermute | solution.py:52
  113.6 8.6 %collective-permute-start.17 = (bf16[256,512]{1,0:T(8,128)(2,1)}, bf16[256,512]{1,0:T(8,128)(2,1)S(1)}, u32[]{:S(2)}, u32[]{:S(2)}) collective-permute-start(bf16[256,512]{1,0:T(8,128)(2,1)} %get-tuple-element.49), channel_id=1, source_target_pairs={{0,8},{1,9},{2,10},{3,11},{4,12},{5,13},{6,14},{7,15},{8,0},{9,1},... | collective-permute-start | bytes 786440 | tf_op jit(solution)/shard_map/ppermute | solution.py:60
  115.3 12.6 %collective-permute-start.18 = (bf16[256,512]{1,0:T(8,128)(2,1)}, bf16[256,512]{1,0:T(8,128)(2,1)S(1)}, u32[]{:S(2)}, u32[]{:S(2)}) collective-permute-start(bf16[256,512]{1,0:T(8,128)(2,1)} %get-tuple-element.50), channel_id=1, source_target_pairs={{0,4},{1,5},{2,6},{3,7},{4,8},{5,9},{6,10},{7,11},{8,12},{9,13},{1... | collective-permute-start | bytes 786440 | tf_op jit(solution)/shard_map/ppermute | solution.py:60
  116.8 11.1 %collective-permute-start.19 = (bf16[256,512]{1,0:T(8,128)(2,1)}, bf16[256,512]{1,0:T(8,128)(2,1)S(1)}, u32[]{:S(2)}, u32[]{:S(2)}) collective-permute-start(bf16[256,512]{1,0:T(8,128)(2,1)} %get-tuple-element.51), channel_id=1, source_target_pairs={{0,12},{1,13},{2,14},{3,15},{4,0},{5,1},{6,2},{7,3},{8,4},{9,5},{1... | collective-permute-start | bytes 786440 | tf_op jit(solution)/shard_map/ppermute | solution.py:60
  129.1 8.4 %collective-permute-start.20 = (bf16[256,512]{1,0:T(8,128)(2,1)S(1)}, bf16[256,512]{1,0:T(8,128)(2,1)S(1)}, u32[]{:S(2)}, u32[]{:S(2)}) collective-permute-start(bf16[256,512]{1,0:T(8,128)(2,1)S(1)} %add_convert_fusion.1.v0), channel_id=1, source_target_pairs={{0,1},{1,2},{2,3},{3,0},{4,5},{5,6},{6,7},{7,4},{8,9},{9,10},{10,1... | collective-permute-start | bytes 786440 | tf_op jit(solution)/shard_map/ppermute | solution.py:52
  129.2 9.6 %collective-permute-start.21 = (bf16[256,512]{1,0:T(8,128)(2,1)S(1)}, bf16[256,512]{1,0:T(8,128)(2,1)S(1)}, u32[]{:S(2)}, u32[]{:S(2)}) collective-permute-start(bf16[256,512]{1,0:T(8,128)(2,1)S(1)} %add_convert_fusion.1.v0), channel_id=1, source_target_pairs={{0,3},{1,0},{2,1},{3,2},{4,7},{5,4},{6,5},{7,6},{8,11},{9,8},{10,9... | collective-permute-start | bytes 786440 | tf_op jit(solution)/shard_map/ppermute | solution.py:52
  132.4 10.7 %collective-permute-start.22 = (bf16[256,512]{1,0:T(8,128)(2,1)S(1)}, bf16[256,512]{1,0:T(8,128)(2,1)S(1)}, u32[]{:S(2)}, u32[]{:S(2)}) collective-permute-start(bf16[256,512]{1,0:T(8,128)(2,1)S(1)} %add_convert_fusion.1.v0), channel_id=1, source_target_pairs={{0,2},{1,3},{2,0},{3,1},{4,6},{5,7},{6,4},{7,5},{8,10},{9,11},{10,... | collective-permute-start | bytes 786440 | tf_op jit(solution)/shard_map/ppermute | solution.py:52
  145.2 19.8 %collective-permute-start.23 = (bf16[128,2048]{1,0:T(8,128)(2,1)S(1)}, bf16[128,2048]{1,0:T(8,128)(2,1)S(1)}, u32[]{:S(2)}, u32[]{:S(2)}) collective-permute-start(bf16[128,2048]{1,0:T(8,128)(2,1)S(1)} %get-tuple-element.53.e2), channel_id=1, source_target_pairs={{0,4},{1,5},{2,6},{3,7},{4,8},{5,9},{6,10},{7,11},{8,12},{9,13},{1... | collective-permute-start | bytes 1572872 | tf_op jit(solution)/shard_map/ppermute | solution.py:52
  146.2 22.1 %collective-permute-start.24 = (bf16[128,2048]{1,0:T(8,128)(2,1)S(1)}, bf16[128,2048]{1,0:T(8,128)(2,1)S(1)}, u32[]{:S(2)}, u32[]{:S(2)}) collective-permute-start(bf16[128,2048]{1,0:T(8,128)(2,1)S(1)} %get-tuple-element.54.e1), channel_id=1, source_target_pairs={{0,12},{1,13},{2,14},{3,15},{4,0},{5,1},{6,2},{7,3},{8,4},{9,5},{1... | collective-permute-start | bytes 1572872 | tf_op jit(solution)/shard_map/ppermute | solution.py:52
  151.8 16.5 %collective-permute-start.25 = (bf16[128,2048]{1,0:T(8,128)(2,1)S(1)}, bf16[128,2048]{1,0:T(8,128)(2,1)S(1)}, u32[]{:S(2)}, u32[]{:S(2)}) collective-permute-start(bf16[128,2048]{1,0:T(8,128)(2,1)S(1)} %get-tuple-element.55.e3), channel_id=1, source_target_pairs={{0,8},{1,9},{2,10},{3,11},{4,12},{5,13},{6,14},{7,15},{8,0},{9,1},... | collective-permute-start | bytes 1572872 | tf_op jit(solution)/shard_map/ppermute | solution.py:52
  162.6 11.3 %collective-permute-start.26 = (bf16[128,2048]{1,0:T(8,128)(2,1)}, bf16[128,2048]{1,0:T(8,128)(2,1)S(1)}, u32[]{:S(2)}, u32[]{:S(2)}) collective-permute-start(bf16[128,2048]{1,0:T(8,128)(2,1)} %get-tuple-element.58), channel_id=1, source_target_pairs={{0,8},{1,9},{2,10},{3,11},{4,12},{5,13},{6,14},{7,15},{8,0},{9,1},... | collective-permute-start | bytes 1572872 | tf_op jit(solution)/shard_map/ppermute | solution.py:52
  165.0 14.4 %collective-permute-start.27 = (bf16[128,2048]{1,0:T(8,128)(2,1)}, bf16[128,2048]{1,0:T(8,128)(2,1)S(1)}, u32[]{:S(2)}, u32[]{:S(2)}) collective-permute-start(bf16[128,2048]{1,0:T(8,128)(2,1)} %get-tuple-element.59), channel_id=1, source_target_pairs={{0,4},{1,5},{2,6},{3,7},{4,8},{5,9},{6,10},{7,11},{8,12},{9,13},{1... | collective-permute-start | bytes 1572872 | tf_op jit(solution)/shard_map/ppermute | solution.py:52
  165.1 14.4 %collective-permute-start.28 = (bf16[128,2048]{1,0:T(8,128)(2,1)}, bf16[128,2048]{1,0:T(8,128)(2,1)S(1)}, u32[]{:S(2)}, u32[]{:S(2)}) collective-permute-start(bf16[128,2048]{1,0:T(8,128)(2,1)} %get-tuple-element.60), channel_id=1, source_target_pairs={{0,12},{1,13},{2,14},{3,15},{4,0},{5,1},{6,2},{7,3},{8,4},{9,5},{1... | collective-permute-start | bytes 1572872 | tf_op jit(solution)/shard_map/ppermute | solution.py:52
  (24 other events, 274.2 us)
Sparse Core Ops, SparseCore 0:
  9.8 44.6 all-gather.2
  56.9 42.2 all-gather.4

commit v8 on v7

--- a/solution.py
+++ b/solution.py
@@ -47,6 +47,26 @@
     for x in range(4)
 ]
 
+OTHER = [(0, 1), (1, 0)]
+CLIMB = [(z * 2 + c, (z + 1 - 2 * c) % 8 * 2 + c) for z in range(8) for c in range(2)]
+
+
+def climbed(z, core, other):
+    step = -1 if (core == 0) != other else 1
+    first = core ^ int(other)
+    near = [(z + step * k) % 8 * 2 + (first ^ j) for k in (1, 2, 3) for j in (0, 1)]
+    return near + [(z + 4) % 8 * 2 + first]
+
+
+STACK = np.array(
+    [
+        [z * 2 + c, z * 2 + 1 - c] + climbed(z, c, False) + climbed(z, c, True)
+        for z in range(8)
+        for c in range(2)
+    ],
+    np.int32,
+)
+
 
 def hop(value, which, step):
     return lax.ppermute(value, ("mb", "tp"), HOPS[which, step])
@@ -133,36 +153,34 @@
     return copies
 
 
-def up_kernel(tab, s0, s1, s2, s3, weight, bias_ref, out_ref, rows, held, sems):
+def up_kernel(tab, stack, s0, s1, s2, s3, *rest):
+    *weights, bias_ref, out_ref, rows, held, sems = rest
     copies = [(piece, rows.at[pl.ds(i * 64, 64)]) for i, piece in enumerate((s0, s1, s2, s3))]
-    copies += [(weight.at[pl.ds(k * 1024, 1024)], held.at[pl.ds(k * 1024, 1024)]) for k in range(5)]
-    copies = start(copies, sems)
-    for copy in copies[:4]:
+    blocks = list(weights[:2]) + [w.at[k] for w in weights[2:] for k in range(w.shape[0])]
+    for k, block in enumerate(blocks):
+        copies.append((block, held.at[pl.ds(pl.multiple_of(stack[k] * 320, 320), 320)]))
+    for copy in start(copies, sems):
         copy.wait()
-    raised = bias_ref[tab[0]]
-    for k in range(5):
-        copies[4 + k].wait()
-        at = slice(k * 1024, (k + 1) * 1024)
-        raised = raised + jnp.dot(rows[:, at], held[at, :], preferred_element_type=F32)
+    raised = bias_ref[tab[0]] + jnp.dot(rows[...], held[...], preferred_element_type=F32)
     hidden = (0.5 * raised * (1.0 + lax.erf(raised * np.float32(0.5**0.5)))).astype(BF16)
     for k in range(16):
         out_ref[pl.ds(pl.multiple_of(tab[k] * 16, 16), 16), :] = hidden[k * 16 : (k + 1) * 16]
 
 
-def up(tab, pieces, weight, bias):
+def up(tab, stack, pieces, weights, bias):
     return pl.pallas_call(
         up_kernel,
         out_shape=jax.ShapeDtypeStruct((256, 320), BF16),
-        in_specs=[SMEM] + [ANY] * 5 + [VMEM],
+        in_specs=[SMEM] * 2 + [ANY] * 14 + [VMEM],
         out_specs=VMEM,
         scratch_shapes=[
             pltpu.VMEM((256, 5120), BF16),
             pltpu.VMEM((5120, 320), BF16),
-            pltpu.SemaphoreType.DMA((9,)),
+            pltpu.SemaphoreType.DMA((20,)),
         ],
-        compiler_params=params(56),
+        compiler_params=params(24),
         cost_estimate=cost(840 * 10**6, 6 * MIB),
-    )(tab, *pieces, weight, bias)
+    )(tab, stack, *pieces, *weights, bias)
 
 
 def down_kernel(nat, h0, h1, h2, h3, weight, own, left, right, far, units, held, sems):
@@ -308,19 +326,32 @@
 ):
     tab = jnp.asarray(TABLE)[lax.axis_index("mb") * 16 + lax.axis_index("tp")]
     nat = jnp.asarray(TABLE)[lax.axis_index("tp")]
-    up_full = lax.all_gather(up_weight, ("enc", "mb"), axis=0, tiled=True)
+    stack = jnp.asarray(STACK)[lax.axis_index("enc") * 2 + lax.axis_index("mb")]
+
+    def climb(value):
+        return lax.ppermute(value, ("enc", "mb"), CLIMB)
+
+    def cross(value):
+        return lax.ppermute(value, "mb", OTHER)
+
     down_part = lax.ppermute(down_weight, ("enc", "mb", "tp"), SHUFFLE)
-
-    merged = merge(patches[0, 0], merge_gain, merge_bias)
+    up_other = cross(up_weight)
+    first = climb(jnp.stack([up_weight, up_other]))
+    merged = merge(after(patches[0, 0], up_other), merge_gain, merge_bias)
     near = jnp.concatenate([merged, *around(merged, 1)], axis=0)
+    near, first, down_part = lax.optimization_barrier((near, first, down_part))
+    down_full = lax.all_gather(down_part, ("enc", "mb"), axis=0, tiled=True)
+    second = climb(first)
     group = (near, *around(near, 2))
-    down_full = lax.all_gather(after(down_part, *group), ("enc", "mb"), axis=0, tiled=True)
-
-    kv_weight = after(kv_weight, *group)
+    third = climb(second)
+    climbed = (first, second, third, climb(third[:1]))
+    up_weights = (up_weight, up_other, *climbed, *[cross(value) for value in climbed])
+
+    kv_weight = after(kv_weight, *group, third)
     kv_right, kv_left = hop(kv_weight, 1, 1), hop(kv_weight, 1, -1)
     far_right, far_left = kv_right[:256], kv_left[256:]
     own, to_left, to_right, to_far = pack(tab, text_embed[0, 0])
-    hidden = up(tab, group, up_full, up_bias.reshape(16, 1, 320))
+    hidden = up(tab, stack, group, up_weights, up_bias.reshape(16, 1, 320))
     units = (hidden, line(hidden, "x", 1), line(hidden, "x", -1), line(hidden, "x", 2))
     moved = (*units, far_right, far_left, to_left, to_right, to_far)
     *units, far_right, far_left, to_left, to_right, to_far = lax.optimization_barrier(moved)

time: 188 us -> 210 us (1.12)
  the two profiles are of different devices: /device:TPU:224 before, /device:TPU:32 now
where the time goes in v8:
time: 210 us; the launch traced here: 207 us
  waiting for transfers between devices  89.8 us (43%)
  starting transfers between devices  57.6 us (27%)
  Pallas kernels  27 us (13%)
  local copies, waits for them, and re-layouts  14.4 us (7%)
  between operations  14.4 us (7%)
  other arithmetic  3.54 us (2%)
    ppermute x22, waiting for transfers between devices, hop(): return lax.ppermute(value, ('mb', 'tp'), HOPS[which, step])  42.8 us
    ppermute x22, starting transfers between devices, hop(): return lax.ppermute(value, ('mb', 'tp'), HOPS[which, step])  36.6 us
    ppermute x4, waiting for transfers between devices, climb(): return lax.ppermute(value, ('enc', 'mb'), CLIMB)  21.8 us
    ppermute x6, waiting for transfers between devices, line(): return lax.ppermute(value, ('mb', 'tp'), LINES[axis, step])  15.2 us
    ppermute x6, starting transfers between devices, line(): return lax.ppermute(value, ('mb', 'tp'), LINES[axis, step])  9.92 us
    pallas_call x1, Pallas kernels, product(): pl.pallas_call(product_kernel, out_shape=[jax.ShapeDtypeStruct((128, 2048...  9.27 us
    ppermute x1, waiting for transfers between devices, per_device(): down_part = lax.ppermute(down_weight, ('enc', 'mb', 'tp'), SHUFFLE)  8.23 us
    unnamed x54, local copies, waits for them, and re-layouts  8.01 us
  transfers between devices with their start and end apart: 39, of which 21 were waited for; matrix products, arithmetic and copies ran while one was open for 4% of the time, Pallas kernels for 9%

profile of v8, /device:TPU:32, one launch (start us, length us, event | category | flops | bytes accessed | tf_op | source)
XLA Modules:
  0.0 206.7 jit_solution(16401183006954509536)
XLA Ops:
  14.9 1.8 collective-permute-start.3
  16.7 4.9 %collective-permute-start.5 = (bf16[320,512]{1,0:T(8,128)(2,1)}, bf16[320,512]{1,0:T(8,128)(2,1)S(1)}, u32[]{:S(2)}, u32[]{:S(2)}) collective-permute-start(bf16[320,512]{1,0:T(8,128)(2,1)} %param.22), channel_id=1, source_target_pairs={{0,0},{1,16},{2,32},{3,48},{4,4},{5,20},{6,36},{7,52},{8,8},{9,24}... | collective-permute-start | bytes 983048 | tf_op jit(solution)/shard_map/ppermute | solution.py:337
  22.9 8.2 %collective-permute-done.5 = bf16[320,512]{1,0:T(8,128)(2,1)S(1)} collective-permute-done((bf16[320,512]{1,0:T(8,128)(2,1)}, bf16[320,512]{1,0:T(8,128)(2,1)S(1)}, u32[]{:S(2)}, u32[]{:S(2)}) %collective-permute-start.5) | collective-permute-done | bytes 327712 | tf_op jit(solution)/shard_map/ppermute | solution.py:337
  33.2 2.1 %collective-permute-start.7 = (bf16[64,5120]{1,0:T(8,128)(2,1)S(1)}, bf16[64,5120]{1,0:T(8,128)(2,1)S(1)}, u32[]{:S(2)}, u32[]{:S(2)}) collective-permute-start(bf16[64,5120]{1,0:T(8,128)(2,1)S(1)} %pad_maximum_fusion.s0), channel_id=1, source_target_pairs={{0,12},{1,13},{2,14},{3,15},{4,0},{5,1},{6,2},{7,3},{8,4},{9,5},{1... | collective-permute-start | bytes 1966088 | tf_op jit(solution)/shard_map/ppermute | solution.py:72
  36.7 5.4 %collective-permute-done.9.rest_3_ = bf16[2,320,320]{2,1,0:T(8,128)(2,1)} collective-permute-done((bf16[2,320,320]{2,1,0:T(8,128)(2,1)}, bf16[2,320,320]{2,1,0:T(8,128)(2,1)}, u32[]{:S(2)}, u32[]{:S(2)}) %collective-permute-start.9) | collective-permute-done | bytes 409632 | tf_op jit(solution)/shard_map/ppermute | solution.py:332
  43.8 6.6 %collective-permute-done.7.s2 = bf16[64,5120]{1,0:T(8,128)(2,1)S(1)} collective-permute-done((bf16[64,5120]{1,0:T(8,128)(2,1)S(1)}, bf16[64,5120]{1,0:T(8,128)(2,1)S(1)}, u32[]{:S(2)}, u32[]{:S(2)}) %collective-permute-start.7) | collective-permute-done | bytes 655392 | tf_op jit(solution)/shard_map/ppermute | solution.py:72
  52.3 7.6 %collective-permute-done.10.rest_4_ = bf16[2,320,320]{2,1,0:T(8,128)(2,1)S(1)} collective-permute-done((bf16[2,320,320]{2,1,0:T(8,128)(2,1)}, bf16[2,320,320]{2,1,0:T(8,128)(2,1)S(1)}, u32[]{:S(2)}, u32[]{:S(2)}) %collective-permute-start.10) | collective-permute-done | bytes 409632 | tf_op jit(solution)/shard_map/ppermute | solution.py:332
  59.9 5.0 %collective-permute-start.20 = (bf16[512,2048]{1,0:T(8,128)(2,1)}, bf16[512,2048]{1,0:T(8,128)(2,1)}, u32[]{:S(2)}, u32[]{:S(2)}) collective-permute-start(bf16[512,2048]{1,0:T(8,128)(2,1)} %w0), channel_id=1, source_target_pairs={{0,3},{1,0},{2,1},{3,2},{4,7},{5,4},{6,5},{7,6},{8,11},{9,8},{10,9... | collective-permute-start | bytes 6291464 | tf_op jit(solution)/shard_map/ppermute | solution.py:72
  67.0 4.1 %collective-permute-start.13 = (bf16[2,320,320]{2,1,0:T(8,128)(2,1)}, bf16[2,320,320]{2,1,0:T(8,128)(2,1)}, u32[]{:S(2)}, u32[]{:S(2)}) collective-permute-start(bf16[2,320,320]{2,1,0:T(8,128)(2,1)} %collective-permute-done.9.rest_3_), channel_id=1, source_target_pairs={{0,16},{16,0},{1,17},{17,1},{2,18},{18,2},{3,19},{19,3},{4,20},{20... | collective-permute-start | bytes 1228808 | tf_op jit(solution)/shard_map/ppermute | solution.py:335
  72.0 8.3 %collective-permute-done.11.rest_5_ = bf16[1,320,320]{2,1,0:T(8,128)(2,1)S(1)} collective-permute-done((bf16[1,320,320]{2,1,0:T(8,128)(2,1)}, bf16[1,320,320]{2,1,0:T(8,128)(2,1)S(1)}, u32[]{:S(2)}, u32[]{:S(2)}) %collective-permute-start.11) | collective-permute-done | bytes 204832 | tf_op jit(solution)/shard_map/ppermute | solution.py:332
  84.5 7.0 %shard_map.159.h0 = bf16[256,320]{1,0:T(8,128)(2,1)S(1)} custom-call(s32[16]{0:T(128)S(1)} %get-tuple-element.69.tab, s32[16]{0:T(128)S(1)} %fusion.3.stack, bf16[64,5120]{1,0:T(8,128)(2,1)S(1)} %pad_maximum_fusion.s0, bf16[64,5120]{1,0:T(8,128)(2,1)S(1)} %collective-permute-done.6.s1, bf16[64,5120]{1,0:T(8,128)(2,1)S(1)} %collective-permute-done.7.s2, ...), custom_call_target="tpu_custom_call" | custom-call | flops 840000000 | bytes 6291456 | tf_op jit(solution)/shard_map/pallas_call | solution.py:171
  91.5 3.2 %collective-permute-start.17 = (bf16[256,320]{1,0:T(8,128)(2,1)S(1)}, bf16[256,320]{1,0:T(8,128)(2,1)S(1)}, u32[]{:S(2)}, u32[]{:S(2)}) collective-permute-start(bf16[256,320]{1,0:T(8,128)(2,1)S(1)} %shard_map.159.h0), channel_id=1, source_target_pairs={{0,3},{1,0},{2,1},{3,2},{4,7},{5,4},{6,5},{7,6},{8,11},{9,8},{10,9... | collective-permute-start | bytes 491528 | tf_op jit(solution)/shard_map/ppermute | solution.py:80
  100.0 3.5 %collective-permute-done.17.h2 = bf16[256,320]{1,0:T(8,128)(2,1)S(1)} collective-permute-done((bf16[256,320]{1,0:T(8,128)(2,1)S(1)}, bf16[256,320]{1,0:T(8,128)(2,1)S(1)}, u32[]{:S(2)}, u32[]{:S(2)}) %collective-permute-start.17) | collective-permute-done | bytes 163872 | tf_op jit(solution)/shard_map/ppermute | solution.py:80
  105.8 2.1 %collective-permute-start.22 = (bf16[256,2048]{1,0:T(8,128)(2,1)S(1)}, bf16[256,2048]{1,0:T(8,128)(2,1)}, u32[]{:S(2)}, u32[]{:S(2)}) collective-permute-start(bf16[256,2048]{1,0:T(8,128)(2,1)S(1)} %slice.18), channel_id=1, source_target_pairs={{0,3},{1,0},{2,1},{3,2},{4,7},{5,4},{6,5},{7,6},{8,11},{9,8},{10,9... | collective-permute-start | bytes 3145736 | tf_op jit(solution)/shard_map/ppermute | solution.py:72
  108.7 2.4 %collective-permute-start.24 = (bf16[128,2048]{1,0:T(8,128)(2,1)S(1)}, bf16[128,2048]{1,0:T(8,128)(2,1)S(1)}, u32[]{:S(2)}, u32[]{:S(2)}) collective-permute-start(bf16[128,2048]{1,0:T(8,128)(2,1)S(1)} %get-tuple-element.51), channel_id=1, source_target_pairs={{0,12},{1,13},{2,14},{3,15},{4,0},{5,1},{6,2},{7,3},{8,4},{9,5},{1... | collective-permute-start | bytes 1572872 | tf_op jit(solution)/shard_map/ppermute | solution.py:72
  111.7 12.4 %collective-permute-done.23.refs_1_ = bf16[128,2048]{1,0:T(8,128)(2,1)S(1)} collective-permute-done((bf16[128,2048]{1,0:T(8,128)(2,1)S(1)}, bf16[128,2048]{1,0:T(8,128)(2,1)S(1)}, u32[]{:S(2)}, u32[]{:S(2)}) %collective-permute-start.23) | collective-permute-done | bytes 524320 | tf_op jit(solution)/shard_map/ppermute | solution.py:72
  124.1 6.4 %collective-permute-done.25.refs_3_ = bf16[128,2048]{1,0:T(8,128)(2,1)S(1)} collective-permute-done((bf16[128,2048]{1,0:T(8,128)(2,1)S(1)}, bf16[128,2048]{1,0:T(8,128)(2,1)S(1)}, u32[]{:S(2)}, u32[]{:S(2)}) %collective-permute-start.25) | collective-permute-done | bytes 524320 | tf_op jit(solution)/shard_map/ppermute | solution.py:72
  131.6 6.0 %shard_map.161 = (f32[256,512]{1,0:T(8,128)}, bf16[256,512]{1,0:T(8,128)(2,1)}, bf16[256,512]{1,0:T(8,128)(2,1)}, bf16[256,512]{1,0:T(8,128)(2,1)}) custom-call(s32[16]{0:T(128)} %get-tuple-element.68.nat, bf16[256,320]{1,0:T(8,128)(2,1)} %copy-done.2, bf16[256,320]{1,0:T(8,128)(2,1)} %copy-done.19, bf16[256,320]{1,0:T(8,128)(2,1)} %copy-done.20, ...), custom_call_target="tpu_custom_call" | custom-call | flops 1340000000 | bytes 8388608 | tf_op jit(solution)/shard_map/pallas_call | solution.py:207
  137.6 2.4 %collective-permute-start.26 = (bf16[256,512]{1,0:T(8,128)(2,1)}, bf16[256,512]{1,0:T(8,128)(2,1)S(1)}, u32[]{:S(2)}, u32[]{:S(2)}) collective-permute-start(bf16[256,512]{1,0:T(8,128)(2,1)} %get-tuple-element.55), channel_id=1, source_target_pairs={{0,8},{1,9},{2,10},{3,11},{4,12},{5,13},{6,14},{7,15},{8,0},{9,1},... | collective-permute-start | bytes 786440 | tf_op jit(solution)/shard_map/ppermute | solution.py:80
  140.7 2.5 %collective-permute-start.28 = (bf16[256,512]{1,0:T(8,128)(2,1)}, bf16[256,512]{1,0:T(8,128)(2,1)S(1)}, u32[]{:S(2)}, u32[]{:S(2)}) collective-permute-start(bf16[256,512]{1,0:T(8,128)(2,1)} %get-tuple-element.57), channel_id=1, source_target_pairs={{0,12},{1,13},{2,14},{3,15},{4,0},{5,1},{6,2},{7,3},{8,4},{9,5},{1... | collective-permute-start | bytes 786440 | tf_op jit(solution)/shard_map/ppermute | solution.py:80
  144.0 3.7 %collective-permute-done.26 = bf16[256,512]{1,0:T(8,128)(2,1)S(1)} collective-permute-done((bf16[256,512]{1,0:T(8,128)(2,1)}, bf16[256,512]{1,0:T(8,128)(2,1)S(1)}, u32[]{:S(2)}, u32[]{:S(2)}) %collective-permute-start.26) | collective-permute-done | bytes 262176 | tf_op jit(solution)/shard_map/ppermute | solution.py:80
  147.7 6.5 %collective-permute-done.27 = bf16[256,512]{1,0:T(8,128)(2,1)S(1)} collective-permute-done((bf16[256,512]{1,0:T(8,128)(2,1)}, bf16[256,512]{1,0:T(8,128)(2,1)S(1)}, u32[]{:S(2)}, u32[]{:S(2)}) %collective-permute-start.27) | collective-permute-done | bytes 262176 | tf_op jit(solution)/shard_map/ppermute | solution.py:80
  156.7 2.2 %collective-permute-start.30 = (bf16[256,512]{1,0:T(8,128)(2,1)S(1)}, bf16[256,512]{1,0:T(8,128)(2,1)S(1)}, u32[]{:S(2)}, u32[]{:S(2)}) collective-permute-start(bf16[256,512]{1,0:T(8,128)(2,1)S(1)} %add_convert_fusion.1.v0), channel_id=1, source_target_pairs={{0,3},{1,0},{2,1},{3,2},{4,7},{5,4},{6,5},{7,6},{8,11},{9,8},{10,9... | collective-permute-start | bytes 786440 | tf_op jit(solution)/shard_map/ppermute | solution.py:72
  160.2 3.1 %collective-permute-done.29.v1 = bf16[256,512]{1,0:T(8,128)(2,1)S(1)} collective-permute-done((bf16[256,512]{1,0:T(8,128)(2,1)S(1)}, bf16[256,512]{1,0:T(8,128)(2,1)S(1)}, u32[]{:S(2)}, u32[]{:S(2)}) %collective-permute-start.29) | collective-permute-done | bytes 262176 | tf_op jit(solution)/shard_map/ppermute | solution.py:72
  163.3 2.4 %collective-permute-done.30.v2 = bf16[256,512]{1,0:T(8,128)(2,1)S(1)} collective-permute-done((bf16[256,512]{1,0:T(8,128)(2,1)S(1)}, bf16[256,512]{1,0:T(8,128)(2,1)S(1)}, u32[]{:S(2)}, u32[]{:S(2)}) %collective-permute-start.30) | collective-permute-done | bytes 262176 | tf_op jit(solution)/shard_map/ppermute | solution.py:72
  169.6 2.9 %collective-permute-start.33 = (bf16[128,2048]{1,0:T(8,128)(2,1)S(1)}, bf16[128,2048]{1,0:T(8,128)(2,1)S(1)}, u32[]{:S(2)}, u32[]{:S(2)}) collective-permute-start(bf16[128,2048]{1,0:T(8,128)(2,1)S(1)} %get-tuple-element.60.e1), channel_id=1, source_target_pairs={{0,12},{1,13},{2,14},{3,15},{4,0},{5,1},{6,2},{7,3},{8,4},{9,5},{1... | collective-permute-start | bytes 1572872 | tf_op jit(solution)/shard_map/ppermute | solution.py:72
  172.8 9.3 %shard_map.164 = (f32[128,2048]{1,0:T(8,128)}, bf16[128,2048]{1,0:T(8,128)(2,1)}, bf16[128,2048]{1,0:T(8,128)(2,1)}, bf16[128,2048]{1,0:T(8,128)(2,1)}) custom-call(s32[16]{0:T(128)} %copy-done.10, bf16[128,2048]{1,0:T(8,128)(2,1)} %copy-done.5, bf16[128,2048]{1,0:T(8,128)(2,1)} %copy-done.15, bf16[128,2048]{1,0:T(8,128)(2,1)} %copy-done.16, ...), custom_call_target="tpu_custom_call" | custom-call | flops 4300000256 | bytes 14680064 | tf_op jit(solution)/shard_map/pallas_call | solution.py:272
  182.1 3.4 %collective-permute-start.35 = (bf16[128,2048]{1,0:T(8,128)(2,1)}, bf16[128,2048]{1,0:T(8,128)(2,1)S(1)}, u32[]{:S(2)}, u32[]{:S(2)}) collective-permute-start(bf16[128,2048]{1,0:T(8,128)(2,1)} %get-tuple-element.64), channel_id=1, source_target_pairs={{0,8},{1,9},{2,10},{3,11},{4,12},{5,13},{6,14},{7,15},{8,0},{9,1},... | collective-permute-start | bytes 1572872 | tf_op jit(solution)/shard_map/ppermute | solution.py:72
  185.4 3.2 %collective-permute-start.37 = (bf16[128,2048]{1,0:T(8,128)(2,1)}, bf16[128,2048]{1,0:T(8,128)(2,1)S(1)}, u32[]{:S(2)}, u32[]{:S(2)}) collective-permute-start(bf16[128,2048]{1,0:T(8,128)(2,1)} %get-tuple-element.66), channel_id=1, source_target_pairs={{0,12},{1,13},{2,14},{3,15},{4,0},{5,1},{6,2},{7,3},{8,4},{9,5},{1... | collective-permute-start | bytes 1572872 | tf_op jit(solution)/shard_map/ppermute | solution.py:72
  188.7 2.0 shard_map.163
  190.8 2.3 %collective-permute-done.35 = bf16[128,2048]{1,0:T(8,128)(2,1)S(1)} collective-permute-done((bf16[128,2048]{1,0:T(8,128)(2,1)}, bf16[128,2048]{1,0:T(8,128)(2,1)S(1)}, u32[]{:S(2)}, u32[]{:S(2)}) %collective-permute-start.35) | collective-permute-done | bytes 524320 | tf_op jit(solution)/shard_map/ppermute | solution.py:72
  193.1 5.5 %collective-permute-done.36 = bf16[128,2048]{1,0:T(8,128)(2,1)S(1)} collective-permute-done((bf16[128,2048]{1,0:T(8,128)(2,1)}, bf16[128,2048]{1,0:T(8,128)(2,1)S(1)}, u32[]{:S(2)}, u32[]{:S(2)}) %collective-permute-start.36) | collective-permute-done | bytes 524320 | tf_op jit(solution)/shard_map/ppermute | solution.py:72
  (124 shorter events, 43.9 us)
Async XLA Ops:
  7.2 124.4 %all-gather.2.cloned.1.call-start = ((), (), s32[]{:S(2)}) async-start(), calls=%async_computation | async-start | bytes 5570560 | tf_op jit(solution)/shard_map/all_gather | solution.py:343
  11.6 11.2 %collective-permute-start.1 = (bf16[16,5120]{1,0:T(8,128)(2,1)S(1)}, bf16[16,5120]{1,0:T(8,128)(2,1)S(1)}, u32[]{:S(2)}, u32[]{:S(2)}) collective-permute-start(bf16[16,5120]{1,0:T(8,128)(2,1)S(1)} %shard_map.158), channel_id=1, source_target_pairs={{0,1},{1,2},{2,3},{3,0},{4,5},{5,6},{6,7},{7,4},{8,9},{9,10},{10,1... | collective-permute-start | bytes 491528 | tf_op jit(solution)/shard_map/ppermute | solution.py:72
  13.2 9.6 %collective-permute-start.2 = (bf16[16,5120]{1,0:T(8,128)(2,1)S(1)}, bf16[16,5120]{1,0:T(8,128)(2,1)S(1)}, u32[]{:S(2)}, u32[]{:S(2)}) collective-permute-start(bf16[16,5120]{1,0:T(8,128)(2,1)S(1)} %shard_map.158), channel_id=1, source_target_pairs={{0,3},{1,0},{2,1},{3,2},{4,7},{5,4},{6,5},{7,6},{8,11},{9,8},{10,9... | collective-permute-start | bytes 491528 | tf_op jit(solution)/shard_map/ppermute | solution.py:72
  16.7 14.4 %collective-permute-start.5 = (bf16[320,512]{1,0:T(8,128)(2,1)}, bf16[320,512]{1,0:T(8,128)(2,1)S(1)}, u32[]{:S(2)}, u32[]{:S(2)}) collective-permute-start(bf16[320,512]{1,0:T(8,128)(2,1)} %param.22), channel_id=1, source_target_pairs={{0,0},{1,16},{2,32},{3,48},{4,4},{5,20},{6,36},{7,52},{8,8},{9,24}... | collective-permute-start | bytes 983048 | tf_op jit(solution)/shard_map/ppermute | solution.py:337
  22.7 9.0 %collective-permute-start.4 = (bf16[2,320,320]{2,1,0:T(8,128)(2,1)S(1)}, bf16[2,320,320]{2,1,0:T(8,128)(2,1)}, u32[]{:S(2)}, u32[]{:S(2)}) collective-permute-start(bf16[2,320,320]{2,1,0:T(8,128)(2,1)S(1)} %pad_maximum_fusion.1), channel_id=1, source_target_pairs={{0,32},{16,240},{32,64},{48,16},{64,96},{80,48},{96,128},{112,80},... | collective-permute-start | bytes 1228808 | tf_op jit(solution)/shard_map/ppermute | solution.py:332
  31.9 10.2 %collective-permute-start.9 = (bf16[2,320,320]{2,1,0:T(8,128)(2,1)}, bf16[2,320,320]{2,1,0:T(8,128)(2,1)}, u32[]{:S(2)}, u32[]{:S(2)}) collective-permute-start(bf16[2,320,320]{2,1,0:T(8,128)(2,1)} %collective-permute-done.4.rest_2_), channel_id=1, source_target_pairs={{0,32},{16,240},{32,64},{48,16},{64,96},{80,48},{96,128},{112,80},... | collective-permute-start | bytes 1228808 | tf_op jit(solution)/shard_map/ppermute | solution.py:332
  31.9 11.9 %collective-permute-start.6 = (bf16[64,5120]{1,0:T(8,128)(2,1)S(1)}, bf16[64,5120]{1,0:T(8,128)(2,1)S(1)}, u32[]{:S(2)}, u32[]{:S(2)}) collective-permute-start(bf16[64,5120]{1,0:T(8,128)(2,1)S(1)} %pad_maximum_fusion.s0), channel_id=1, source_target_pairs={{0,4},{1,5},{2,6},{3,7},{4,8},{5,9},{6,10},{7,11},{8,12},{9,13},{1... | collective-permute-start | bytes 1966088 | tf_op jit(solution)/shard_map/ppermute | solution.py:72
  33.2 17.3 %collective-permute-start.7 = (bf16[64,5120]{1,0:T(8,128)(2,1)S(1)}, bf16[64,5120]{1,0:T(8,128)(2,1)S(1)}, u32[]{:S(2)}, u32[]{:S(2)}) collective-permute-start(bf16[64,5120]{1,0:T(8,128)(2,1)S(1)} %pad_maximum_fusion.s0), channel_id=1, source_target_pairs={{0,12},{1,13},{2,14},{3,15},{4,0},{5,1},{6,2},{7,3},{8,4},{9,5},{1... | collective-permute-start | bytes 1966088 | tf_op jit(solution)/shard_map/ppermute | solution.py:72
  35.3 16.2 %collective-permute-start.8 = (bf16[64,5120]{1,0:T(8,128)(2,1)S(1)}, bf16[64,5120]{1,0:T(8,128)(2,1)S(1)}, u32[]{:S(2)}, u32[]{:S(2)}) collective-permute-start(bf16[64,5120]{1,0:T(8,128)(2,1)S(1)} %pad_maximum_fusion.s0), channel_id=1, source_target_pairs={{0,8},{1,9},{2,10},{3,11},{4,12},{5,13},{6,14},{7,15},{8,0},{9,1},... | collective-permute-start | bytes 1966088 | tf_op jit(solution)/shard_map/ppermute | solution.py:72
  42.1 17.9 %collective-permute-start.10 = (bf16[2,320,320]{2,1,0:T(8,128)(2,1)}, bf16[2,320,320]{2,1,0:T(8,128)(2,1)S(1)}, u32[]{:S(2)}, u32[]{:S(2)}) collective-permute-start(bf16[2,320,320]{2,1,0:T(8,128)(2,1)} %collective-permute-done.9.rest_3_), channel_id=1, source_target_pairs={{0,32},{16,240},{32,64},{48,16},{64,96},{80,48},{96,128},{112,80},... | collective-permute-start | bytes 1228808 | tf_op jit(solution)/shard_map/ppermute | solution.py:332
  59.9 37.0 %collective-permute-start.19 = (bf16[512,2048]{1,0:T(8,128)(2,1)}, bf16[512,2048]{1,0:T(8,128)(2,1)}, u32[]{:S(2)}, u32[]{:S(2)}) collective-permute-start(bf16[512,2048]{1,0:T(8,128)(2,1)} %w0), channel_id=1, source_target_pairs={{0,1},{1,2},{2,3},{3,0},{4,5},{5,6},{6,7},{7,4},{8,9},{9,10},{10,1... | collective-permute-start | bytes 6291464 | tf_op jit(solution)/shard_map/ppermute | solution.py:72
  59.9 38.3 %collective-permute-start.20 = (bf16[512,2048]{1,0:T(8,128)(2,1)}, bf16[512,2048]{1,0:T(8,128)(2,1)}, u32[]{:S(2)}, u32[]{:S(2)}) collective-permute-start(bf16[512,2048]{1,0:T(8,128)(2,1)} %w0), channel_id=1, source_target_pairs={{0,3},{1,0},{2,1},{3,2},{4,7},{5,4},{6,5},{7,6},{8,11},{9,8},{10,9... | collective-permute-start | bytes 6291464 | tf_op jit(solution)/shard_map/ppermute | solution.py:72
  65.7 14.6 %collective-permute-start.11 = (bf16[1,320,320]{2,1,0:T(8,128)(2,1)}, bf16[1,320,320]{2,1,0:T(8,128)(2,1)S(1)}, u32[]{:S(2)}, u32[]{:S(2)}) collective-permute-start(bf16[1,320,320]{2,1,0:T(8,128)(2,1)} %slice.16), channel_id=1, source_target_pairs={{0,32},{16,240},{32,64},{48,16},{64,96},{80,48},{96,128},{112,80},... | collective-permute-start | bytes 614408 | tf_op jit(solution)/shard_map/ppermute | solution.py:332
  67.0 15.3 %collective-permute-start.13 = (bf16[2,320,320]{2,1,0:T(8,128)(2,1)}, bf16[2,320,320]{2,1,0:T(8,128)(2,1)}, u32[]{:S(2)}, u32[]{:S(2)}) collective-permute-start(bf16[2,320,320]{2,1,0:T(8,128)(2,1)} %collective-permute-done.9.rest_3_), channel_id=1, source_target_pairs={{0,16},{16,0},{1,17},{17,1},{2,18},{18,2},{3,19},{19,3},{4,20},{20... | collective-permute-start | bytes 1228808 | tf_op jit(solution)/shard_map/ppermute | solution.py:335
  71.9 10.4 %collective-permute-start.14 = (bf16[2,320,320]{2,1,0:T(8,128)(2,1)S(1)}, bf16[2,320,320]{2,1,0:T(8,128)(2,1)}, u32[]{:S(2)}, u32[]{:S(2)}) collective-permute-start(bf16[2,320,320]{2,1,0:T(8,128)(2,1)S(1)} %collective-permute-done.10.rest_4_), channel_id=1, source_target_pairs={{0,16},{16,0},{1,17},{17,1},{2,18},{18,2},{3,19},{19,3},{4,20},{20... | collective-permute-start | bytes 1228808 | tf_op jit(solution)/shard_map/ppermute | solution.py:335
  91.5 11.9 %collective-permute-start.17 = (bf16[256,320]{1,0:T(8,128)(2,1)S(1)}, bf16[256,320]{1,0:T(8,128)(2,1)S(1)}, u32[]{:S(2)}, u32[]{:S(2)}) collective-permute-start(bf16[256,320]{1,0:T(8,128)(2,1)S(1)} %shard_map.159.h0), channel_id=1, source_target_pairs={{0,3},{1,0},{2,1},{3,2},{4,7},{5,4},{6,5},{7,6},{8,11},{9,8},{10,9... | collective-permute-start | bytes 491528 | tf_op jit(solution)/shard_map/ppermute | solution.py:80
  94.8 9.9 %collective-permute-start.18 = (bf16[256,320]{1,0:T(8,128)(2,1)S(1)}, bf16[256,320]{1,0:T(8,128)(2,1)S(1)}, u32[]{:S(2)}, u32[]{:S(2)}) collective-permute-start(bf16[256,320]{1,0:T(8,128)(2,1)S(1)} %shard_map.159.h0), channel_id=1, source_target_pairs={{0,2},{1,3},{2,0},{3,1},{4,6},{5,7},{6,4},{7,5},{8,10},{9,11},{10,... | collective-permute-start | bytes 491528 | tf_op jit(solution)/shard_map/ppermute | solution.py:80
  104.6 25.9 %collective-permute-start.21 = (bf16[256,2048]{1,0:T(8,128)(2,1)S(1)}, bf16[256,2048]{1,0:T(8,128)(2,1)S(1)}, u32[]{:S(2)}, u32[]{:S(2)}) collective-permute-start(bf16[256,2048]{1,0:T(8,128)(2,1)S(1)} %slice.17), channel_id=1, source_target_pairs={{0,1},{1,2},{2,3},{3,0},{4,5},{5,6},{6,7},{7,4},{8,9},{9,10},{10,1... | collective-permute-start | bytes 3145736 | tf_op jit(solution)/shard_map/ppermute | solution.py:72
  105.8 25.8 %collective-permute-start.22 = (bf16[256,2048]{1,0:T(8,128)(2,1)S(1)}, bf16[256,2048]{1,0:T(8,128)(2,1)}, u32[]{:S(2)}, u32[]{:S(2)}) collective-permute-start(bf16[256,2048]{1,0:T(8,128)(2,1)S(1)} %slice.18), channel_id=1, source_target_pairs={{0,3},{1,0},{2,1},{3,2},{4,7},{5,4},{6,5},{7,6},{8,11},{9,8},{10,9... | collective-permute-start | bytes 3145736 | tf_op jit(solution)/shard_map/ppermute | solution.py:72
  107.9 16.3 %collective-permute-start.23 = (bf16[128,2048]{1,0:T(8,128)(2,1)S(1)}, bf16[128,2048]{1,0:T(8,128)(2,1)S(1)}, u32[]{:S(2)}, u32[]{:S(2)}) collective-permute-start(bf16[128,2048]{1,0:T(8,128)(2,1)S(1)} %get-tuple-element.50), channel_id=1, source_target_pairs={{0,4},{1,5},{2,6},{3,7},{4,8},{5,9},{6,10},{7,11},{8,12},{9,13},{1... | collective-permute-start | bytes 1572872 | tf_op jit(solution)/shard_map/ppermute | solution.py:72
  108.7 15.5 %collective-permute-start.24 = (bf16[128,2048]{1,0:T(8,128)(2,1)S(1)}, bf16[128,2048]{1,0:T(8,128)(2,1)S(1)}, u32[]{:S(2)}, u32[]{:S(2)}) collective-permute-start(bf16[128,2048]{1,0:T(8,128)(2,1)S(1)} %get-tuple-element.51), channel_id=1, source_target_pairs={{0,12},{1,13},{2,14},{3,15},{4,0},{5,1},{6,2},{7,3},{8,4},{9,5},{1... | collective-permute-start | bytes 1572872 | tf_op jit(solution)/shard_map/ppermute | solution.py:72
  111.1 19.5 %collective-permute-start.25 = (bf16[128,2048]{1,0:T(8,128)(2,1)S(1)}, bf16[128,2048]{1,0:T(8,128)(2,1)S(1)}, u32[]{:S(2)}, u32[]{:S(2)}) collective-permute-start(bf16[128,2048]{1,0:T(8,128)(2,1)S(1)} %get-tuple-element.52), channel_id=1, source_target_pairs={{0,8},{1,9},{2,10},{3,11},{4,12},{5,13},{6,14},{7,15},{8,0},{9,1},... | collective-permute-start | bytes 1572872 | tf_op jit(solution)/shard_map/ppermute | solution.py:72
  137.6 10.1 %collective-permute-start.26 = (bf16[256,512]{1,0:T(8,128)(2,1)}, bf16[256,512]{1,0:T(8,128)(2,1)S(1)}, u32[]{:S(2)}, u32[]{:S(2)}) collective-permute-start(bf16[256,512]{1,0:T(8,128)(2,1)} %get-tuple-element.55), channel_id=1, source_target_pairs={{0,8},{1,9},{2,10},{3,11},{4,12},{5,13},{6,14},{7,15},{8,0},{9,1},... | collective-permute-start | bytes 786440 | tf_op jit(solution)/shard_map/ppermute | solution.py:80
  140.0 14.2 %collective-permute-start.27 = (bf16[256,512]{1,0:T(8,128)(2,1)}, bf16[256,512]{1,0:T(8,128)(2,1)S(1)}, u32[]{:S(2)}, u32[]{:S(2)}) collective-permute-start(bf16[256,512]{1,0:T(8,128)(2,1)} %get-tuple-element.56), channel_id=1, source_target_pairs={{0,4},{1,5},{2,6},{3,7},{4,8},{5,9},{6,10},{7,11},{8,12},{9,13},{1... | collective-permute-start | bytes 786440 | tf_op jit(solution)/shard_map/ppermute | solution.py:80
  140.7 13.4 %collective-permute-start.28 = (bf16[256,512]{1,0:T(8,128)(2,1)}, bf16[256,512]{1,0:T(8,128)(2,1)S(1)}, u32[]{:S(2)}, u32[]{:S(2)}) collective-permute-start(bf16[256,512]{1,0:T(8,128)(2,1)} %get-tuple-element.57), channel_id=1, source_target_pairs={{0,12},{1,13},{2,14},{3,15},{4,0},{5,1},{6,2},{7,3},{8,4},{9,5},{1... | collective-permute-start | bytes 786440 | tf_op jit(solution)/shard_map/ppermute | solution.py:80
  156.7 8.9 %collective-permute-start.30 = (bf16[256,512]{1,0:T(8,128)(2,1)S(1)}, bf16[256,512]{1,0:T(8,128)(2,1)S(1)}, u32[]{:S(2)}, u32[]{:S(2)}) collective-permute-start(bf16[256,512]{1,0:T(8,128)(2,1)S(1)} %add_convert_fusion.1.v0), channel_id=1, source_target_pairs={{0,3},{1,0},{2,1},{3,2},{4,7},{5,4},{6,5},{7,6},{8,11},{9,8},{10,9... | collective-permute-start | bytes 786440 | tf_op jit(solution)/shard_map/ppermute | solution.py:72
  169.3 16.2 %collective-permute-start.32 = (bf16[128,2048]{1,0:T(8,128)(2,1)S(1)}, bf16[128,2048]{1,0:T(8,128)(2,1)S(1)}, u32[]{:S(2)}, u32[]{:S(2)}) collective-permute-start(bf16[128,2048]{1,0:T(8,128)(2,1)S(1)} %get-tuple-element.59.e2), channel_id=1, source_target_pairs={{0,4},{1,5},{2,6},{3,7},{4,8},{5,9},{6,10},{7,11},{8,12},{9,13},{1... | collective-permute-start | bytes 1572872 | tf_op jit(solution)/shard_map/ppermute | solution.py:72
  169.6 19.0 %collective-permute-start.33 = (bf16[128,2048]{1,0:T(8,128)(2,1)S(1)}, bf16[128,2048]{1,0:T(8,128)(2,1)S(1)}, u32[]{:S(2)}, u32[]{:S(2)}) collective-permute-start(bf16[128,2048]{1,0:T(8,128)(2,1)S(1)} %get-tuple-element.60.e1), channel_id=1, source_target_pairs={{0,12},{1,13},{2,14},{3,15},{4,0},{5,1},{6,2},{7,3},{8,4},{9,5},{1... | collective-permute-start | bytes 1572872 | tf_op jit(solution)/shard_map/ppermute | solution.py:72
  172.5 16.2 %collective-permute-start.34 = (bf16[128,2048]{1,0:T(8,128)(2,1)S(1)}, bf16[128,2048]{1,0:T(8,128)(2,1)S(1)}, u32[]{:S(2)}, u32[]{:S(2)}) collective-permute-start(bf16[128,2048]{1,0:T(8,128)(2,1)S(1)} %get-tuple-element.61.e3), channel_id=1, source_target_pairs={{0,8},{1,9},{2,10},{3,11},{4,12},{5,13},{6,14},{7,15},{8,0},{9,1},... | collective-permute-start | bytes 1572872 | tf_op jit(solution)/shard_map/ppermute | solution.py:72
  182.1 11.1 %collective-permute-start.35 = (bf16[128,2048]{1,0:T(8,128)(2,1)}, bf16[128,2048]{1,0:T(8,128)(2,1)S(1)}, u32[]{:S(2)}, u32[]{:S(2)}) collective-permute-start(bf16[128,2048]{1,0:T(8,128)(2,1)} %get-tuple-element.64), channel_id=1, source_target_pairs={{0,8},{1,9},{2,10},{3,11},{4,12},{5,13},{6,14},{7,15},{8,0},{9,1},... | collective-permute-start | bytes 1572872 | tf_op jit(solution)/shard_map/ppermute | solution.py:72
  185.4 13.2 %collective-permute-start.36 = (bf16[128,2048]{1,0:T(8,128)(2,1)}, bf16[128,2048]{1,0:T(8,128)(2,1)S(1)}, u32[]{:S(2)}, u32[]{:S(2)}) collective-permute-start(bf16[128,2048]{1,0:T(8,128)(2,1)} %get-tuple-element.65), channel_id=1, source_target_pairs={{0,4},{1,5},{2,6},{3,7},{4,8},{5,9},{6,10},{7,11},{8,12},{9,13},{1... | collective-permute-start | bytes 1572872 | tf_op jit(solution)/shard_map/ppermute | solution.py:72
  185.4 13.2 %collective-permute-start.37 = (bf16[128,2048]{1,0:T(8,128)(2,1)}, bf16[128,2048]{1,0:T(8,128)(2,1)S(1)}, u32[]{:S(2)}, u32[]{:S(2)}) collective-permute-start(bf16[128,2048]{1,0:T(8,128)(2,1)} %get-tuple-element.66), channel_id=1, source_target_pairs={{0,12},{1,13},{2,14},{3,15},{4,0},{5,1},{6,2},{7,3},{8,4},{9,5},{1... | collective-permute-start | bytes 1572872 | tf_op jit(solution)/shard_map/ppermute | solution.py:72
  (34 other events, 413.1 us)
Sparse Core Ops, SparseCore 0:
  32.0 52.0 all-gather.1

commit v9 on v7

--- a/solution.py
+++ b/solution.py
@@ -227,40 +227,97 @@
     )(tab, dest, *visual, *text)
 
 
-def product_kernel(tab, e0, e1, e2, e3, gain, w0, w1, w2, w3a, w3b, own, left, right, far, scaled):
+def scaled_rows(gain, tab, j, rows):
+    return (rows[:, j * 512 : (j + 1) * 512].astype(F32) * gain[tab[j]]).astype(BF16)
+
+
+def text_kernel(tab, t0, t1, t2, t3, gain, w0, w1, w2, out, scaled):
     @pl.when(pl.program_id(0) == 0)
     def _():
-        for j in range(4):
-            at = slice(j * 512, (j + 1) * 512)
-            scale = gain[tab[j]]
-            for i2, rows in enumerate((e0, e1, e2, e3)):
-                scaled[i2 * 128 : (i2 + 1) * 128, at] = (rows[:, at].astype(F32) * scale).astype(BF16)
+        for i2, rows in enumerate((t0, t1, t2, t3)):
+            for j in range(3):
+                scaled[i2 * 128 : (i2 + 1) * 128, j * 512 : (j + 1) * 512] = scaled_rows(gain, tab, j, rows)
+
+    total = jnp.dot(scaled[:, 0:512], w0[...], preferred_element_type=F32)
+    total = total + jnp.dot(scaled[:, 512:1024], w1[...], preferred_element_type=F32)
+    out[...] = total + jnp.dot(scaled[:, 1024:1536], w2[...], preferred_element_type=F32)
+
+
+def text_far_kernel(tab, t0, t1, t2, t3, gain, near, w3a, w3b, out, scaled):
+    @pl.when(pl.program_id(0) == 0)
+    def _():
+        for i2, rows in enumerate((t0, t1, t2, t3)):
+            scaled[i2 * 128 : (i2 + 1) * 128, :] = scaled_rows(gain, tab, 3, rows)
+
+    total = near[...] + jnp.dot(scaled[:, 0:256], w3a[...], preferred_element_type=F32)
+    total = total + jnp.dot(scaled[:, 256:512], w3b[...], preferred_element_type=F32)
+    out[...] = total.astype(BF16)
+
+
+def block(count):
+    return pl.BlockSpec((count, 512), lambda n: (0, n))
+
+
+def text_product(tab, text, gain, weights):
+    return pl.pallas_call(
+        text_kernel,
+        out_shape=jax.ShapeDtypeStruct((512, 2048), F32),
+        grid=(4,),
+        in_specs=[SMEM] + [VMEM] * 5 + [block(512)] * 3,
+        out_specs=block(512),
+        scratch_shapes=[pltpu.VMEM((512, 1536), BF16)],
+        compiler_params=params(28),
+        cost_estimate=cost(3200 * 10**6, 14 * MIB),
+    )(tab, *text, gain, *weights)
+
+
+def text_far_product(tab, text, gain, near, weights):
+    return pl.pallas_call(
+        text_far_kernel,
+        out_shape=jax.ShapeDtypeStruct((512, 2048), BF16),
+        grid=(4,),
+        in_specs=[SMEM] + [VMEM] * 5 + [block(512)] + [block(256)] * 2,
+        out_specs=block(512),
+        scratch_shapes=[pltpu.VMEM((512, 512), BF16)],
+        compiler_params=params(28),
+        cost_estimate=cost(1100 * 10**6, 8 * MIB),
+    )(tab, *text, gain, near, *weights)
+
+
+def product_kernel(tab, dest, v0, v1, v2, v3, gain, text, w0, w1, w2, w3a, w3b, own, left, right, far, scaled, select):
+    @pl.when(pl.program_id(0) == 0)
+    def _():
+        for j, visual in enumerate((v0, v1, v2, v3)):
+            scaled[:, j * 512 : (j + 1) * 512] = (visual[...].astype(F32) * gain[tab[j]]).astype(BF16)
+        for i2 in range(4):
+            places = lax.broadcasted_iota(jnp.int32, (128, 256), 0) + tab[i2 * 4] * 128
+            select[i2 * 128 : (i2 + 1) * 128, :] = (places == dest[...]).astype(F32).astype(BF16)
 
     total = jnp.dot(scaled[:, 0:512], w0[...], preferred_element_type=F32)
     total = total + jnp.dot(scaled[:, 512:1024], w1[...], preferred_element_type=F32)
     total = total + jnp.dot(scaled[:, 1024:1536], w2[...], preferred_element_type=F32)
     total = total + jnp.dot(scaled[:, 1536:1792], w3a[...], preferred_element_type=F32)
     total = total + jnp.dot(scaled[:, 1792:2048], w3b[...], preferred_element_type=F32)
-    own[...] = total[0:128]
-    left[...] = total[128:256].astype(BF16)
-    right[...] = total[256:384].astype(BF16)
-    far[...] = total[384:512].astype(BF16)
-
-
-def product(tab, picked, gain, weights):
-    def block(count):
-        return pl.BlockSpec((count, 512), lambda n: (0, n))
-
+    total = total.astype(BF16)
+    for i2, out in ((3, far), (2, right), (1, left), (0, own)):
+        rows = slice(i2 * 128, (i2 + 1) * 128)
+        chosen = select[rows, :]
+        present = jnp.sum(chosen.astype(F32), axis=1, keepdims=True) > 0.0
+        picked = jnp.dot(chosen, total, preferred_element_type=F32).astype(BF16)
+        out[...] = jnp.where(present, picked, text[rows, :])
+
+
+def product(tab, dest, visual, gain, text, weights):
     return pl.pallas_call(
         product_kernel,
-        out_shape=[jax.ShapeDtypeStruct((128, 2048), F32)] + [jax.ShapeDtypeStruct((128, 2048), BF16)] * 3,
+        out_shape=[jax.ShapeDtypeStruct((128, 2048), BF16)] * 4,
         grid=(4,),
-        in_specs=[SMEM] + [VMEM] * 5 + [block(n) for n in (512, 512, 512, 256, 256)],
+        in_specs=[SMEM] + [VMEM] * 6 + [block(n) for n in (512, 512, 512, 512, 256, 256)],
         out_specs=[block(128)] * 4,
-        scratch_shapes=[pltpu.VMEM((512, 2048), BF16)],
-        compiler_params=params(56),
-        cost_estimate=cost(4300 * 10**6, 14 * MIB),
-    )(tab, *picked, gain, *weights)
+        scratch_shapes=[pltpu.VMEM((256, 2048), BF16), pltpu.VMEM((512, 256), BF16)],
+        compiler_params=params(28),
+        cost_estimate=cost(2700 * 10**6, 14 * MIB),
+    )(tab, dest, *visual, gain, text, *weights)
 
 
 def place_kernel(tab, e0, e1, e2, e3, out, scale, sems):
@@ -322,29 +379,31 @@
     own, to_left, to_right, to_far = pack(tab, text_embed[0, 0])
     hidden = up(tab, group, up_full, up_bias.reshape(16, 1, 320))
     units = (hidden, line(hidden, "x", 1), line(hidden, "x", -1), line(hidden, "x", 2))
-    moved = (*units, far_right, far_left, to_left, to_right, to_far)
-    *units, far_right, far_left, to_left, to_right, to_far = lax.optimization_barrier(moved)
-
-    weights = (kv_weight, kv_right, kv_left, hop(far_right, 1, 1), hop(far_left, 1, -1))
     text = (own, hop(to_right, 2, 1), hop(to_left, 2, -1), hop(to_far, 2, 2))
-    down_full = after(down_full, weights[3], weights[4], *text)
+    *units, far_right, far_left = lax.optimization_barrier((*units, far_right, far_left, *text))[:6]
+    far = (hop(far_right, 1, 1), hop(far_left, 1, -1))
+    gain = norm_gain.reshape(16, 1, 512)
+    text_sums = text_product(tab, text, gain, (kv_weight, kv_right, kv_left))
+    down_full, *far = lax.optimization_barrier((down_full, *far, text_sums))[:3]
     own, to_left, to_right, to_far = down(nat, units, down_full)
+    text_sums = text_far_product(tab, text, gain, after(text_sums, to_far), far)
     bias = lax.dynamic_slice_in_dim(down_bias, lax.axis_index("tp") * 512, 512, 0)
     total = own + bias
     for value in (line(to_far, "y", 2), line(to_right, "y", 1), line(to_left, "y", -1)):
         total = total + value.astype(F32)
     visual = total.astype(BF16)
-    visual = (visual, *around(visual, 1))
+    visual = (visual, *around(after(visual, text_sums), 1))
+    weights = (kv_weight, kv_right, kv_left, *far)
 
     live_rows = patch_counts[0, 0] // 4
     live = (jnp.arange(SLOT, dtype=jnp.int32)[None, :] < live_rows[:, None]).reshape(-1)
     dest = jnp.where(live, dest_pos[0, 0], -1)[None]
     picked = pick(tab, dest, visual, text)
     pieces = (picked[0], hop(picked[2], 2, 1), hop(picked[1], 2, -1), hop(picked[3], 2, 2))
-    own, to_left, to_right, to_far = product(tab, picked, norm_gain.reshape(16, 1, 512), weights)
+    own, to_left, to_right, to_far = product(tab, dest, visual, gain, text_sums, weights)
     sums = (hop(to_far, 2, 2), hop(to_right, 2, 1), hop(to_left, 2, -1))
     embedded, scale = place_rows(tab, pieces)
-    total = own
+    total = own.astype(F32)
     for value in sums:
         total = total + value.astype(F32)
     keys_values = (total * scale[:, :1] + kv_bias).astype(BF16)

time: 188 us -> 195 us (1.037)
  the two profiles are of different devices: /device:TPU:224 before, /device:TPU:32 now
where the time goes in v9:
time: 195 us; the launch traced here: 194 us
  waiting for transfers between devices  78.9 us (40%)
  starting transfers between devices  49.5 us (25%)
  Pallas kernels  36.2 us (19%)
  between operations  14.3 us (7%)
  local copies, waits for them, and re-layouts  13.3 us (7%)
    ppermute x22, waiting for transfers between devices, hop(): return lax.ppermute(value, ('mb', 'tp'), HOPS[which, step])  52.5 us
    ppermute x22, starting transfers between devices, hop(): return lax.ppermute(value, ('mb', 'tp'), HOPS[which, step])  35.1 us
    ppermute x1, waiting for transfers between devices, per_device(): down_part = lax.ppermute(down_weight, ('enc', 'mb', 'tp'), SHUFFLE)  18.3 us
    ppermute x6, starting transfers between devices, line(): return lax.ppermute(value, ('mb', 'tp'), LINES[axis, step])  11 us
    ppermute x6, waiting for transfers between devices, line(): return lax.ppermute(value, ('mb', 'tp'), LINES[axis, step])  7.47 us
    pallas_call x1, Pallas kernels, product(): pl.pallas_call(product_kernel, out_shape=[jax.ShapeDtypeStruct((128, 2048...  6.73 us
    pallas_call x1, Pallas kernels, down(): pl.pallas_call(down_kernel, out_shape=[jax.ShapeDtypeStruct((256, 512), F...  6.37 us
    pallas_call x1, Pallas kernels, text_product(): pl.pallas_call(text_kernel, out_shape=jax.ShapeDtypeStruct((512, 2048), F...  6.34 us
  transfers between devices with their start and end apart: 31, of which 16 were waited for; matrix products, arithmetic and copies ran while one was open for 4% of the time, Pallas kernels for 14%

profile of v9, /device:TPU:32, one launch (start us, length us, event | category | flops | bytes accessed | tf_op | source)
XLA Modules:
  0.0 193.8 jit_solution(5034861083611721326)
XLA Ops:
  17.4 3.2 %collective-permute-done.2 = bf16[16,5120]{1,0:T(8,128)(2,1)S(1)} collective-permute-done((bf16[16,5120]{1,0:T(8,128)(2,1)S(1)}, bf16[16,5120]{1,0:T(8,128)(2,1)S(1)}, u32[]{:S(2)}, u32[]{:S(2)}) %collective-permute-start.2) | collective-permute-done | bytes 163872 | tf_op jit(solution)/shard_map/ppermute | solution.py:52
  24.1 2.0 %collective-permute-start.5 = (bf16[64,5120]{1,0:T(8,128)(2,1)S(1)}, bf16[64,5120]{1,0:T(8,128)(2,1)}, u32[]{:S(2)}, u32[]{:S(2)}) collective-permute-start(bf16[64,5120]{1,0:T(8,128)(2,1)S(1)} %pad_maximum_fusion.s0), channel_id=1, source_target_pairs={{0,8},{1,9},{2,10},{3,11},{4,12},{5,13},{6,14},{7,15},{8,0},{9,1},... | collective-permute-start | bytes 1966088 | tf_op jit(solution)/shard_map/ppermute | solution.py:52
  26.0 3.3 %collective-permute-start.14 = (bf16[320,512]{1,0:T(8,128)(2,1)}, bf16[320,512]{1,0:T(8,128)(2,1)}, u32[]{:S(2)}, u32[]{:S(2)}) collective-permute-start(bf16[320,512]{1,0:T(8,128)(2,1)} %param.21), channel_id=1, source_target_pairs={{0,0},{1,16},{2,32},{3,48},{4,4},{5,20},{6,36},{7,52},{8,8},{9,24}... | collective-permute-start | bytes 983048 | tf_op jit(solution)/shard_map/ppermute | solution.py:369
  29.3 18.3 %collective-permute-done.14 = bf16[320,512]{1,0:T(8,128)(2,1)} collective-permute-done((bf16[320,512]{1,0:T(8,128)(2,1)}, bf16[320,512]{1,0:T(8,128)(2,1)}, u32[]{:S(2)}, u32[]{:S(2)}) %collective-permute-start.14) | collective-permute-done | bytes 327712 | tf_op jit(solution)/shard_map/ppermute | solution.py:369
  51.1 2.5 %shard_map.151 = (bf16[128,2048]{1,0:T(8,128)(2,1)S(1)}, bf16[128,2048]{1,0:T(8,128)(2,1)}, bf16[128,2048]{1,0:T(8,128)(2,1)}, bf16[128,2048]{1,0:T(8,128)(2,1)}) custom-call(s32[16]{0:T(128)S(1)} %get-tuple-element.65.tab, bf16[128,8192]{1,0:T(8,128)(2,1)S(1)} %bitcast.20, bf16[128,8192]{1,0:T(8,128)(2,1)S(1)} %bitcast.21, bf16[128,8192]{1,0:T(8,128)(2,1)S(1)} %bitcast.22, ...), custom_call_target="tpu_custom_call" | custom-call | bytes 4194304 | tf_op jit(solution)/shard_map/pallas_call | solution.py:115
  54.3 2.7 %collective-permute-start.12 = (bf16[128,2048]{1,0:T(8,128)(2,1)}, bf16[128,2048]{1,0:T(8,128)(2,1)}, u32[]{:S(2)}, u32[]{:S(2)}) collective-permute-start(bf16[128,2048]{1,0:T(8,128)(2,1)} %get-tuple-element.36), channel_id=1, source_target_pairs={{0,12},{1,13},{2,14},{3,15},{4,0},{5,1},{6,2},{7,3},{8,4},{9,5},{1... | collective-permute-start | bytes 1572872 | tf_op jit(solution)/shard_map/ppermute | solution.py:52
  57.6 5.5 %shard_map.150.h0 = bf16[256,320]{1,0:T(8,128)(2,1)} custom-call(s32[16]{0:T(128)} %copy-done.8, bf16[64,5120]{1,0:T(8,128)(2,1)} %copy-done.12, bf16[64,5120]{1,0:T(8,128)(2,1)} %copy-done.13, bf16[64,5120]{1,0:T(8,128)(2,1)} %collective-permute-done.4.s2, bf16[64,5120]{1,0:T(8,128)(2,1)} %collective-permute-done.5.s3, ...), custom_call_target="tpu_custom_call" | custom-call | flops 840000000 | bytes 6291456 | tf_op jit(solution)/shard_map/pallas_call | solution.py:153
  63.2 7.3 %collective-permute-done.11.t1.refs_1_ = bf16[128,2048]{1,0:T(8,128)(2,1)S(1)} collective-permute-done((bf16[128,2048]{1,0:T(8,128)(2,1)}, bf16[128,2048]{1,0:T(8,128)(2,1)S(1)}, u32[]{:S(2)}, u32[]{:S(2)}) %collective-permute-start.11) | collective-permute-done | bytes 524320 | tf_op jit(solution)/shard_map/ppermute | solution.py:52
  71.6 13.8 %collective-permute-done.10.w2 = bf16[512,2048]{1,0:T(8,128)(2,1)} collective-permute-done((bf16[512,2048]{1,0:T(8,128)(2,1)}, bf16[512,2048]{1,0:T(8,128)(2,1)}, u32[]{:S(2)}, u32[]{:S(2)}) %collective-permute-start.10) | collective-permute-done | bytes 2097184 | tf_op jit(solution)/shard_map/ppermute | solution.py:52
  85.4 3.7 %collective-permute-start.7 = (bf16[256,320]{1,0:T(8,128)(2,1)}, bf16[256,320]{1,0:T(8,128)(2,1)}, u32[]{:S(2)}, u32[]{:S(2)}) collective-permute-start(bf16[256,320]{1,0:T(8,128)(2,1)} %shard_map.150.h0), channel_id=1, source_target_pairs={{0,3},{1,0},{2,1},{3,2},{4,7},{5,4},{6,5},{7,6},{8,11},{9,8},{10,9... | collective-permute-start | bytes 491528 | tf_op jit(solution)/shard_map/ppermute | solution.py:60
  90.9 2.3 %slice.12 = bf16[256,2048]{1,0:T(8,128)(2,1)} slice(bf16[512,2048]{1,0:T(8,128)(2,1)} %collective-permute-done.9.w1), slice={[0:256], [0:2048]} | slice | bytes 2097152 | tf_op jit(solution)/shard_map/slice | solution.py:378
  93.2 2.4 %slice.13 = bf16[256,2048]{1,0:T(8,128)(2,1)} slice(bf16[512,2048]{1,0:T(8,128)(2,1)} %collective-permute-done.10.w2), slice={[256:512], [0:2048]} | slice | bytes 2097152 | tf_op jit(solution)/shard_map/slice | solution.py:378
  95.6 2.8 %collective-permute-done.8.h3 = bf16[256,320]{1,0:T(8,128)(2,1)} collective-permute-done((bf16[256,320]{1,0:T(8,128)(2,1)}, bf16[256,320]{1,0:T(8,128)(2,1)}, u32[]{:S(2)}, u32[]{:S(2)}) %collective-permute-start.8) | collective-permute-done | bytes 163872 | tf_op jit(solution)/shard_map/ppermute | solution.py:60
  98.4 3.2 %collective-permute-start.16 = (bf16[256,2048]{1,0:T(8,128)(2,1)}, bf16[256,2048]{1,0:T(8,128)(2,1)}, u32[]{:S(2)}, u32[]{:S(2)}) collective-permute-start(bf16[256,2048]{1,0:T(8,128)(2,1)} %slice.13), channel_id=1, source_target_pairs={{0,3},{1,0},{2,1},{3,2},{4,7},{5,4},{6,5},{7,6},{8,11},{9,8},{10,9... | collective-permute-start | bytes 3145736 | tf_op jit(solution)/shard_map/ppermute | solution.py:52
  102.4 6.3 %shard_map.152.near = f32[512,2048]{1,0:T(8,128)S(1)} custom-call(s32[16]{0:T(128)S(1)} %copy-done.9, bf16[128,2048]{1,0:T(8,128)(2,1)S(1)} %get-tuple-element.34.t0.refs_0_, bf16[128,2048]{1,0:T(8,128)(2,1)S(1)} %collective-permute-done.11.t1.refs_1_, bf16[128,2048]{1,0:T(8,128)(2,1)} %collective-permute-done.12.t2.refs_2_, ...), custom_call_target="tpu_custom_call" | custom-call | flops 3200000000 | bytes 14680064 | tf_op jit(solution)/shard_map/pallas_call | solution.py:262
  110.7 4.0 %collective-permute-done.15.w3a = bf16[256,2048]{1,0:T(8,128)(2,1)} collective-permute-done((bf16[256,2048]{1,0:T(8,128)(2,1)}, bf16[256,2048]{1,0:T(8,128)(2,1)}, u32[]{:S(2)}, u32[]{:S(2)}) %collective-permute-start.15) | collective-permute-done | bytes 1048608 | tf_op jit(solution)/shard_map/ppermute | solution.py:52
  114.7 6.4 %shard_map.153 = (f32[256,512]{1,0:T(8,128)}, bf16[256,512]{1,0:T(8,128)(2,1)}, bf16[256,512]{1,0:T(8,128)(2,1)}, bf16[256,512]{1,0:T(8,128)(2,1)}) custom-call(s32[16]{0:T(128)} %get-tuple-element.64.nat, bf16[256,320]{1,0:T(8,128)(2,1)} %shard_map.150.h0, bf16[256,320]{1,0:T(8,128)(2,1)} %copy-done.15, bf16[256,320]{1,0:T(8,128)(2,1)} %collective-permute-done.7.h2, ...), custom_call_target="tpu_custom_call" | custom-call | flops 1340000000 | bytes 8388608 | tf_op jit(solution)/shard_map/pallas_call | solution.py:189
  121.1 3.0 %collective-permute-start.17 = (bf16[256,512]{1,0:T(8,128)(2,1)}, bf16[256,512]{1,0:T(8,128)(2,1)S(1)}, u32[]{:S(2)}, u32[]{:S(2)}) collective-permute-start(bf16[256,512]{1,0:T(8,128)(2,1)} %get-tuple-element.47), channel_id=1, source_target_pairs={{0,8},{1,9},{2,10},{3,11},{4,12},{5,13},{6,14},{7,15},{8,0},{9,1},... | collective-permute-start | bytes 786440 | tf_op jit(solution)/shard_map/ppermute | solution.py:60
  125.1 2.3 %collective-permute-start.19 = (bf16[256,512]{1,0:T(8,128)(2,1)}, bf16[256,512]{1,0:T(8,128)(2,1)S(1)}, u32[]{:S(2)}, u32[]{:S(2)}) collective-permute-start(bf16[256,512]{1,0:T(8,128)(2,1)} %get-tuple-element.49), channel_id=1, source_target_pairs={{0,12},{1,13},{2,14},{3,15},{4,0},{5,1},{6,2},{7,3},{8,4},{9,5},{1... | collective-permute-start | bytes 786440 | tf_op jit(solution)/shard_map/ppermute | solution.py:60
  127.4 4.3 %shard_map.154.text = bf16[512,2048]{1,0:T(8,128)(2,1)S(1)} custom-call(s32[16]{0:T(128)S(1)} %copy-done.9, bf16[128,2048]{1,0:T(8,128)(2,1)S(1)} %get-tuple-element.34.t0.refs_0_, bf16[128,2048]{1,0:T(8,128)(2,1)S(1)} %collective-permute-done.11.t1.refs_1_, bf16[128,2048]{1,0:T(8,128)(2,1)} %collective-permute-done.12.t2.refs_2_, ...), custom_call_target="tpu_custom_call" | custom-call | flops 1100000000 | bytes 8388608 | tf_op jit(solution)/shard_map/pallas_call | solution.py:275
  133.1 3.5 %collective-permute-done.18 = bf16[256,512]{1,0:T(8,128)(2,1)S(1)} collective-permute-done((bf16[256,512]{1,0:T(8,128)(2,1)}, bf16[256,512]{1,0:T(8,128)(2,1)S(1)}, u32[]{:S(2)}, u32[]{:S(2)}) %collective-permute-start.18) | collective-permute-done | bytes 262176 | tf_op jit(solution)/shard_map/ppermute | solution.py:60
  138.0 3.2 %collective-permute-start.21 = (bf16[256,512]{1,0:T(8,128)(2,1)S(1)}, bf16[256,512]{1,0:T(8,128)(2,1)}, u32[]{:S(2)}, u32[]{:S(2)}) collective-permute-start(bf16[256,512]{1,0:T(8,128)(2,1)S(1)} %add_convert_fusion.1.v0), channel_id=1, source_target_pairs={{0,3},{1,0},{2,1},{3,2},{4,7},{5,4},{6,5},{7,6},{8,11},{9,8},{10,9... | collective-permute-start | bytes 786440 | tf_op jit(solution)/shard_map/ppermute | solution.py:52
  142.0 5.3 %collective-permute-done.20.v1 = bf16[256,512]{1,0:T(8,128)(2,1)} collective-permute-done((bf16[256,512]{1,0:T(8,128)(2,1)S(1)}, bf16[256,512]{1,0:T(8,128)(2,1)}, u32[]{:S(2)}, u32[]{:S(2)}) %collective-permute-start.20) | collective-permute-done | bytes 262176 | tf_op jit(solution)/shard_map/ppermute | solution.py:52
  148.2 4.7 %collective-permute-done.22.v3 = bf16[256,512]{1,0:T(8,128)(2,1)} collective-permute-done((bf16[256,512]{1,0:T(8,128)(2,1)S(1)}, bf16[256,512]{1,0:T(8,128)(2,1)}, u32[]{:S(2)}, u32[]{:S(2)}) %collective-permute-start.22) | collective-permute-done | bytes 262176 | tf_op jit(solution)/shard_map/ppermute | solution.py:52
  152.8 2.2 %shard_map.155 = (bf16[128,2048]{1,0:T(8,128)(2,1)S(1)}, bf16[128,2048]{1,0:T(8,128)(2,1)S(1)}, bf16[128,2048]{1,0:T(8,128)(2,1)S(1)}, bf16[128,2048]{1,0:T(8,128)(2,1)S(1)}) custom-call(s32[16]{0:T(128)S(1)} %copy-done.9, s32[1,256]{1,0:T(1,128)S(1)} %bitcast_select_fusion.dest, bf16[256,512]{1,0:T(8,128)(2,1)S(1)} %add_convert_fusion.1.v0, ...), custom_call_target="tpu_custom_call" | custom-call | flops 540000000 | bytes 6291456 | tf_op jit(solution)/shard_map/pallas_call | solution.py:220
  156.7 3.7 %collective-permute-start.24 = (bf16[128,2048]{1,0:T(8,128)(2,1)S(1)}, bf16[128,2048]{1,0:T(8,128)(2,1)S(1)}, u32[]{:S(2)}, u32[]{:S(2)}) collective-permute-start(bf16[128,2048]{1,0:T(8,128)(2,1)S(1)} %get-tuple-element.56), channel_id=1, source_target_pairs={{0,12},{1,13},{2,14},{3,15},{4,0},{5,1},{6,2},{7,3},{8,4},{9,5},{1... | collective-permute-start | bytes 1572872 | tf_op jit(solution)/shard_map/ppermute | solution.py:52
  161.8 6.7 %shard_map.157 = (bf16[128,2048]{1,0:T(8,128)(2,1)S(1)}, bf16[128,2048]{1,0:T(8,128)(2,1)S(1)}, bf16[128,2048]{1,0:T(8,128)(2,1)S(1)}, bf16[128,2048]{1,0:T(8,128)(2,1)S(1)}) custom-call(s32[16]{0:T(128)S(1)} %copy-done.9, s32[1,256]{1,0:T(1,128)S(1)} %bitcast_select_fusion.dest, bf16[256,512]{1,0:T(8,128)(2,1)S(1)} %add_convert_fusion.1.v0, ...), custom_call_target="tpu_custom_call" | custom-call | flops 2700000000 | bytes 14680064 | tf_op jit(solution)/shard_map/pallas_call | solution.py:311
  168.5 2.2 %collective-permute-start.26 = (bf16[128,2048]{1,0:T(8,128)(2,1)S(1)}, bf16[128,2048]{1,0:T(8,128)(2,1)S(1)}, u32[]{:S(2)}, u32[]{:S(2)}) collective-permute-start(bf16[128,2048]{1,0:T(8,128)(2,1)S(1)} %get-tuple-element.60), channel_id=1, source_target_pairs={{0,8},{1,9},{2,10},{3,11},{4,12},{5,13},{6,14},{7,15},{8,0},{9,1},... | collective-permute-start | bytes 1572872 | tf_op jit(solution)/shard_map/ppermute | solution.py:52
  170.8 3.2 %collective-permute-start.28 = (bf16[128,2048]{1,0:T(8,128)(2,1)S(1)}, bf16[128,2048]{1,0:T(8,128)(2,1)S(1)}, u32[]{:S(2)}, u32[]{:S(2)}) collective-permute-start(bf16[128,2048]{1,0:T(8,128)(2,1)S(1)} %get-tuple-element.62), channel_id=1, source_target_pairs={{0,12},{1,13},{2,14},{3,15},{4,0},{5,1},{6,2},{7,3},{8,4},{9,5},{1... | collective-permute-start | bytes 1572872 | tf_op jit(solution)/shard_map/ppermute | solution.py:52
  174.0 4.4 %collective-permute-done.24.e2 = bf16[128,2048]{1,0:T(8,128)(2,1)S(1)} collective-permute-done((bf16[128,2048]{1,0:T(8,128)(2,1)S(1)}, bf16[128,2048]{1,0:T(8,128)(2,1)S(1)}, u32[]{:S(2)}, u32[]{:S(2)}) %collective-permute-start.24) | collective-permute-done | bytes 524320 | tf_op jit(solution)/shard_map/ppermute | solution.py:52
  178.4 2.0 %shard_map.156 = (bf16[128,8192]{1,0:T(8,128)(2,1)}, f32[128,128]{1,0:T(8,128)S(1)}) custom-call(s32[16]{0:T(128)S(1)} %copy-done.9, bf16[128,2048]{1,0:T(8,128)(2,1)S(1)} %get-tuple-element.54.e0, bf16[128,2048]{1,0:T(8,128)(2,1)S(1)} %collective-permute-done.23.e1, bf16[128,2048]{1,0:T(8,128)(2,1)S(1)} %collective-permute-done.24.e2, ...), custom_call_target="tpu_custom_call" | custom-call | flops 4000000 | bytes 31457280 | tf_op jit(solution)/shard_map/pallas_call | solution.py:340
  180.5 5.3 %collective-permute-done.27 = bf16[128,2048]{1,0:T(8,128)(2,1)S(1)} collective-permute-done((bf16[128,2048]{1,0:T(8,128)(2,1)S(1)}, bf16[128,2048]{1,0:T(8,128)(2,1)S(1)}, u32[]{:S(2)}, u32[]{:S(2)}) %collective-permute-start.27) | collective-permute-done | bytes 524320 | tf_op jit(solution)/shard_map/ppermute | solution.py:52
  (94 shorter events, 33.6 us)
Async XLA Ops:
  7.2 43.9 %copy-start = (bf16[1,1,128,8192]{3,2,1,0:T(8,128)(2,1)S(1)}, bf16[1,1,128,8192]{3,2,1,0:T(8,128)(2,1)}, u32[]{:S(2)}) copy-start(bf16[1,1,128,8192]{3,2,1,0:T(8,128)(2,1)} %param.23) | copy-start | bytes 6291460
  7.2 50.4 %all-gather.3.cloned.1.call-start = ((), (), s32[]{:S(2)}) async-start(), calls=%async_computation | async-start | bytes 4177920 | tf_op jit(solution)/shard_map/all_gather | solution.py:368
  7.9 106.8 %all-gather.5.cloned.1.call-start = ((), (), s32[]{:S(2)}) async-start(), calls=%async_computation.1 | async-start | bytes 5570560 | tf_op jit(solution)/shard_map/all_gather | solution.py:374
  10.5 6.6 %collective-permute-start = (bf16[16,5120]{1,0:T(8,128)(2,1)S(1)}, bf16[16,5120]{1,0:T(8,128)(2,1)S(1)}, u32[]{:S(2)}, u32[]{:S(2)}) collective-permute-start(bf16[16,5120]{1,0:T(8,128)(2,1)S(1)} %shard_map.149), channel_id=1, source_target_pairs={{0,1},{1,2},{2,3},{3,0},{4,5},{5,6},{6,7},{7,4},{8,9},{9,10},{10,1... | collective-permute-start | bytes 491528 | tf_op jit(solution)/shard_map/ppermute | solution.py:52
  12.1 5.3 %collective-permute-start.1 = (bf16[16,5120]{1,0:T(8,128)(2,1)S(1)}, bf16[16,5120]{1,0:T(8,128)(2,1)S(1)}, u32[]{:S(2)}, u32[]{:S(2)}) collective-permute-start(bf16[16,5120]{1,0:T(8,128)(2,1)S(1)} %shard_map.149), channel_id=1, source_target_pairs={{0,3},{1,0},{2,1},{3,2},{4,7},{5,4},{6,5},{7,6},{8,11},{9,8},{10,9... | collective-permute-start | bytes 491528 | tf_op jit(solution)/shard_map/ppermute | solution.py:52
  13.9 6.8 %collective-permute-start.2 = (bf16[16,5120]{1,0:T(8,128)(2,1)S(1)}, bf16[16,5120]{1,0:T(8,128)(2,1)S(1)}, u32[]{:S(2)}, u32[]{:S(2)}) collective-permute-start(bf16[16,5120]{1,0:T(8,128)(2,1)S(1)} %shard_map.149), channel_id=1, source_target_pairs={{0,2},{1,3},{2,0},{3,1},{4,6},{5,7},{6,4},{7,5},{8,10},{9,11},{10,... | collective-permute-start | bytes 491528 | tf_op jit(solution)/shard_map/ppermute | solution.py:52
  20.7 26.9 %collective-permute-start.3 = (bf16[64,5120]{1,0:T(8,128)(2,1)S(1)}, bf16[64,5120]{1,0:T(8,128)(2,1)S(1)}, u32[]{:S(2)}, u32[]{:S(2)}) collective-permute-start(bf16[64,5120]{1,0:T(8,128)(2,1)S(1)} %pad_maximum_fusion.s0), channel_id=1, source_target_pairs={{0,4},{1,5},{2,6},{3,7},{4,8},{5,9},{6,10},{7,11},{8,12},{9,13},{1... | collective-permute-start | bytes 1966088 | tf_op jit(solution)/shard_map/ppermute | solution.py:52
  22.4 25.2 %collective-permute-start.4 = (bf16[64,5120]{1,0:T(8,128)(2,1)S(1)}, bf16[64,5120]{1,0:T(8,128)(2,1)}, u32[]{:S(2)}, u32[]{:S(2)}) collective-permute-start(bf16[64,5120]{1,0:T(8,128)(2,1)S(1)} %pad_maximum_fusion.s0), channel_id=1, source_target_pairs={{0,12},{1,13},{2,14},{3,15},{4,0},{5,1},{6,2},{7,3},{8,4},{9,5},{1... | collective-permute-start | bytes 1966088 | tf_op jit(solution)/shard_map/ppermute | solution.py:52
  24.1 23.6 %collective-permute-start.5 = (bf16[64,5120]{1,0:T(8,128)(2,1)S(1)}, bf16[64,5120]{1,0:T(8,128)(2,1)}, u32[]{:S(2)}, u32[]{:S(2)}) collective-permute-start(bf16[64,5120]{1,0:T(8,128)(2,1)S(1)} %pad_maximum_fusion.s0), channel_id=1, source_target_pairs={{0,8},{1,9},{2,10},{3,11},{4,12},{5,13},{6,14},{7,15},{8,0},{9,1},... | collective-permute-start | bytes 1966088 | tf_op jit(solution)/shard_map/ppermute | solution.py:52
  26.0 21.6 %collective-permute-start.14 = (bf16[320,512]{1,0:T(8,128)(2,1)}, bf16[320,512]{1,0:T(8,128)(2,1)}, u32[]{:S(2)}, u32[]{:S(2)}) collective-permute-start(bf16[320,512]{1,0:T(8,128)(2,1)} %param.21), channel_id=1, source_target_pairs={{0,0},{1,16},{2,32},{3,48},{4,4},{5,20},{6,36},{7,52},{8,8},{9,24}... | collective-permute-start | bytes 983048 | tf_op jit(solution)/shard_map/ppermute | solution.py:369
  47.6 37.7 %collective-permute-start.10 = (bf16[512,2048]{1,0:T(8,128)(2,1)}, bf16[512,2048]{1,0:T(8,128)(2,1)}, u32[]{:S(2)}, u32[]{:S(2)}) collective-permute-start(bf16[512,2048]{1,0:T(8,128)(2,1)} %w0.1), channel_id=1, source_target_pairs={{0,3},{1,0},{2,1},{3,2},{4,7},{5,4},{6,5},{7,6},{8,11},{9,8},{10,9... | collective-permute-start | bytes 6291464 | tf_op jit(solution)/shard_map/ppermute | solution.py:52
  48.9 42.0 %collective-permute-start.9 = (bf16[512,2048]{1,0:T(8,128)(2,1)}, bf16[512,2048]{1,0:T(8,128)(2,1)}, u32[]{:S(2)}, u32[]{:S(2)}) collective-permute-start(bf16[512,2048]{1,0:T(8,128)(2,1)} %w0.1), channel_id=1, source_target_pairs={{0,1},{1,2},{2,3},{3,0},{4,5},{5,6},{6,7},{7,4},{8,9},{9,10},{10,1... | collective-permute-start | bytes 6291464 | tf_op jit(solution)/shard_map/ppermute | solution.py:52
  53.6 16.9 %collective-permute-start.11 = (bf16[128,2048]{1,0:T(8,128)(2,1)}, bf16[128,2048]{1,0:T(8,128)(2,1)S(1)}, u32[]{:S(2)}, u32[]{:S(2)}) collective-permute-start(bf16[128,2048]{1,0:T(8,128)(2,1)} %get-tuple-element.35), channel_id=1, source_target_pairs={{0,4},{1,5},{2,6},{3,7},{4,8},{5,9},{6,10},{7,11},{8,12},{9,13},{1... | collective-permute-start | bytes 1572872 | tf_op jit(solution)/shard_map/ppermute | solution.py:52
  54.3 41.3 %collective-permute-start.12 = (bf16[128,2048]{1,0:T(8,128)(2,1)}, bf16[128,2048]{1,0:T(8,128)(2,1)}, u32[]{:S(2)}, u32[]{:S(2)}) collective-permute-start(bf16[128,2048]{1,0:T(8,128)(2,1)} %get-tuple-element.36), channel_id=1, source_target_pairs={{0,12},{1,13},{2,14},{3,15},{4,0},{5,1},{6,2},{7,3},{8,4},{9,5},{1... | collective-permute-start | bytes 1572872 | tf_op jit(solution)/shard_map/ppermute | solution.py:52
  56.9 38.7 %collective-permute-start.13 = (bf16[128,2048]{1,0:T(8,128)(2,1)}, bf16[128,2048]{1,0:T(8,128)(2,1)}, u32[]{:S(2)}, u32[]{:S(2)}) collective-permute-start(bf16[128,2048]{1,0:T(8,128)(2,1)} %get-tuple-element.37), channel_id=1, source_target_pairs={{0,8},{1,9},{2,10},{3,11},{4,12},{5,13},{6,14},{7,15},{8,0},{9,1},... | collective-permute-start | bytes 1572872 | tf_op jit(solution)/shard_map/ppermute | solution.py:52
  70.5 25.1 %collective-permute-start.6 = (bf16[256,320]{1,0:T(8,128)(2,1)}, bf16[256,320]{1,0:T(8,128)(2,1)S(1)}, u32[]{:S(2)}, u32[]{:S(2)}) collective-permute-start(bf16[256,320]{1,0:T(8,128)(2,1)} %shard_map.150.h0), channel_id=1, source_target_pairs={{0,1},{1,2},{2,3},{3,0},{4,5},{5,6},{6,7},{7,4},{8,9},{9,10},{10,1... | collective-permute-start | bytes 491528 | tf_op jit(solution)/shard_map/ppermute | solution.py:60
  85.4 10.2 %collective-permute-start.7 = (bf16[256,320]{1,0:T(8,128)(2,1)}, bf16[256,320]{1,0:T(8,128)(2,1)}, u32[]{:S(2)}, u32[]{:S(2)}) collective-permute-start(bf16[256,320]{1,0:T(8,128)(2,1)} %shard_map.150.h0), channel_id=1, source_target_pairs={{0,3},{1,0},{2,1},{3,2},{4,7},{5,4},{6,5},{7,6},{8,11},{9,8},{10,9... | collective-permute-start | bytes 491528 | tf_op jit(solution)/shard_map/ppermute | solution.py:60
  90.9 7.5 %collective-permute-start.8 = (bf16[256,320]{1,0:T(8,128)(2,1)}, bf16[256,320]{1,0:T(8,128)(2,1)}, u32[]{:S(2)}, u32[]{:S(2)}) collective-permute-start(bf16[256,320]{1,0:T(8,128)(2,1)} %shard_map.150.h0), channel_id=1, source_target_pairs={{0,2},{1,3},{2,0},{3,1},{4,6},{5,7},{6,4},{7,5},{8,10},{9,11},{10,... | collective-permute-start | bytes 491528 | tf_op jit(solution)/shard_map/ppermute | solution.py:60
  98.4 16.3 %collective-permute-start.15 = (bf16[256,2048]{1,0:T(8,128)(2,1)}, bf16[256,2048]{1,0:T(8,128)(2,1)}, u32[]{:S(2)}, u32[]{:S(2)}) collective-permute-start(bf16[256,2048]{1,0:T(8,128)(2,1)} %slice.12), channel_id=1, source_target_pairs={{0,1},{1,2},{2,3},{3,0},{4,5},{5,6},{6,7},{7,4},{8,9},{9,10},{10,1... | collective-permute-start | bytes 3145736 | tf_op jit(solution)/shard_map/ppermute | solution.py:52
  98.4 16.3 %collective-permute-start.16 = (bf16[256,2048]{1,0:T(8,128)(2,1)}, bf16[256,2048]{1,0:T(8,128)(2,1)}, u32[]{:S(2)}, u32[]{:S(2)}) collective-permute-start(bf16[256,2048]{1,0:T(8,128)(2,1)} %slice.13), channel_id=1, source_target_pairs={{0,3},{1,0},{2,1},{3,2},{4,7},{5,4},{6,5},{7,6},{8,11},{9,8},{10,9... | collective-permute-start | bytes 3145736 | tf_op jit(solution)/shard_map/ppermute | solution.py:52
  121.1 12.0 %collective-permute-start.17 = (bf16[256,512]{1,0:T(8,128)(2,1)}, bf16[256,512]{1,0:T(8,128)(2,1)S(1)}, u32[]{:S(2)}, u32[]{:S(2)}) collective-permute-start(bf16[256,512]{1,0:T(8,128)(2,1)} %get-tuple-element.47), channel_id=1, source_target_pairs={{0,8},{1,9},{2,10},{3,11},{4,12},{5,13},{6,14},{7,15},{8,0},{9,1},... | collective-permute-start | bytes 786440 | tf_op jit(solution)/shard_map/ppermute | solution.py:60
  124.2 12.4 %collective-permute-start.18 = (bf16[256,512]{1,0:T(8,128)(2,1)}, bf16[256,512]{1,0:T(8,128)(2,1)S(1)}, u32[]{:S(2)}, u32[]{:S(2)}) collective-permute-start(bf16[256,512]{1,0:T(8,128)(2,1)} %get-tuple-element.48), channel_id=1, source_target_pairs={{0,4},{1,5},{2,6},{3,7},{4,8},{5,9},{6,10},{7,11},{8,12},{9,13},{1... | collective-permute-start | bytes 786440 | tf_op jit(solution)/shard_map/ppermute | solution.py:60
  125.1 12.7 %collective-permute-start.19 = (bf16[256,512]{1,0:T(8,128)(2,1)}, bf16[256,512]{1,0:T(8,128)(2,1)S(1)}, u32[]{:S(2)}, u32[]{:S(2)}) collective-permute-start(bf16[256,512]{1,0:T(8,128)(2,1)} %get-tuple-element.49), channel_id=1, source_target_pairs={{0,12},{1,13},{2,14},{3,15},{4,0},{5,1},{6,2},{7,3},{8,4},{9,5},{1... | collective-permute-start | bytes 786440 | tf_op jit(solution)/shard_map/ppermute | solution.py:60
  137.9 9.4 %collective-permute-start.20 = (bf16[256,512]{1,0:T(8,128)(2,1)S(1)}, bf16[256,512]{1,0:T(8,128)(2,1)}, u32[]{:S(2)}, u32[]{:S(2)}) collective-permute-start(bf16[256,512]{1,0:T(8,128)(2,1)S(1)} %add_convert_fusion.1.v0), channel_id=1, source_target_pairs={{0,1},{1,2},{2,3},{3,0},{4,5},{5,6},{6,7},{7,4},{8,9},{9,10},{10,1... | collective-permute-start | bytes 786440 | tf_op jit(solution)/shard_map/ppermute | solution.py:52
  138.0 10.1 %collective-permute-start.21 = (bf16[256,512]{1,0:T(8,128)(2,1)S(1)}, bf16[256,512]{1,0:T(8,128)(2,1)}, u32[]{:S(2)}, u32[]{:S(2)}) collective-permute-start(bf16[256,512]{1,0:T(8,128)(2,1)S(1)} %add_convert_fusion.1.v0), channel_id=1, source_target_pairs={{0,3},{1,0},{2,1},{3,2},{4,7},{5,4},{6,5},{7,6},{8,11},{9,8},{10,9... | collective-permute-start | bytes 786440 | tf_op jit(solution)/shard_map/ppermute | solution.py:52
  141.3 11.6 %collective-permute-start.22 = (bf16[256,512]{1,0:T(8,128)(2,1)S(1)}, bf16[256,512]{1,0:T(8,128)(2,1)}, u32[]{:S(2)}, u32[]{:S(2)}) collective-permute-start(bf16[256,512]{1,0:T(8,128)(2,1)S(1)} %add_convert_fusion.1.v0), channel_id=1, source_target_pairs={{0,2},{1,3},{2,0},{3,1},{4,6},{5,7},{6,4},{7,5},{8,10},{9,11},{10,... | collective-permute-start | bytes 786440 | tf_op jit(solution)/shard_map/ppermute | solution.py:52
  155.0 15.7 %collective-permute-start.23 = (bf16[128,2048]{1,0:T(8,128)(2,1)S(1)}, bf16[128,2048]{1,0:T(8,128)(2,1)S(1)}, u32[]{:S(2)}, u32[]{:S(2)}) collective-permute-start(bf16[128,2048]{1,0:T(8,128)(2,1)S(1)} %get-tuple-element.55), channel_id=1, source_target_pairs={{0,4},{1,5},{2,6},{3,7},{4,8},{5,9},{6,10},{7,11},{8,12},{9,13},{1... | collective-permute-start | bytes 1572872 | tf_op jit(solution)/shard_map/ppermute | solution.py:52
  156.7 21.7 %collective-permute-start.24 = (bf16[128,2048]{1,0:T(8,128)(2,1)S(1)}, bf16[128,2048]{1,0:T(8,128)(2,1)S(1)}, u32[]{:S(2)}, u32[]{:S(2)}) collective-permute-start(bf16[128,2048]{1,0:T(8,128)(2,1)S(1)} %get-tuple-element.56), channel_id=1, source_target_pairs={{0,12},{1,13},{2,14},{3,15},{4,0},{5,1},{6,2},{7,3},{8,4},{9,5},{1... | collective-permute-start | bytes 1572872 | tf_op jit(solution)/shard_map/ppermute | solution.py:52
  160.4 18.0 %collective-permute-start.25 = (bf16[128,2048]{1,0:T(8,128)(2,1)S(1)}, bf16[128,2048]{1,0:T(8,128)(2,1)S(1)}, u32[]{:S(2)}, u32[]{:S(2)}) collective-permute-start(bf16[128,2048]{1,0:T(8,128)(2,1)S(1)} %get-tuple-element.57), channel_id=1, source_target_pairs={{0,8},{1,9},{2,10},{3,11},{4,12},{5,13},{6,14},{7,15},{8,0},{9,1},... | collective-permute-start | bytes 1572872 | tf_op jit(solution)/shard_map/ppermute | solution.py:52
  168.5 11.9 %collective-permute-start.26 = (bf16[128,2048]{1,0:T(8,128)(2,1)S(1)}, bf16[128,2048]{1,0:T(8,128)(2,1)S(1)}, u32[]{:S(2)}, u32[]{:S(2)}) collective-permute-start(bf16[128,2048]{1,0:T(8,128)(2,1)S(1)} %get-tuple-element.60), channel_id=1, source_target_pairs={{0,8},{1,9},{2,10},{3,11},{4,12},{5,13},{6,14},{7,15},{8,0},{9,1},... | collective-permute-start | bytes 1572872 | tf_op jit(solution)/shard_map/ppermute | solution.py:52
  170.7 15.0 %collective-permute-start.27 = (bf16[128,2048]{1,0:T(8,128)(2,1)S(1)}, bf16[128,2048]{1,0:T(8,128)(2,1)S(1)}, u32[]{:S(2)}, u32[]{:S(2)}) collective-permute-start(bf16[128,2048]{1,0:T(8,128)(2,1)S(1)} %get-tuple-element.61), channel_id=1, source_target_pairs={{0,4},{1,5},{2,6},{3,7},{4,8},{5,9},{6,10},{7,11},{8,12},{9,13},{1... | collective-permute-start | bytes 1572872 | tf_op jit(solution)/shard_map/ppermute | solution.py:52
  170.8 15.0 %collective-permute-start.28 = (bf16[128,2048]{1,0:T(8,128)(2,1)S(1)}, bf16[128,2048]{1,0:T(8,128)(2,1)S(1)}, u32[]{:S(2)}, u32[]{:S(2)}) collective-permute-start(bf16[128,2048]{1,0:T(8,128)(2,1)S(1)} %get-tuple-element.62), channel_id=1, source_target_pairs={{0,12},{1,13},{2,14},{3,15},{4,0},{5,1},{6,2},{7,3},{8,4},{9,5},{1... | collective-permute-start | bytes 1572872 | tf_op jit(solution)/shard_map/ppermute | solution.py:52
  (19 other events, 268.5 us)
Sparse Core Ops, SparseCore 0:
  9.8 46.6 all-gather.2
  58.3 43.2 all-gather.4

commit v10 on v9

--- a/solution.py
+++ b/solution.py
@@ -135,7 +135,9 @@
 
 def up_kernel(tab, s0, s1, s2, s3, weight, bias_ref, out_ref, rows, held, sems):
     copies = [(piece, rows.at[pl.ds(i * 64, 64)]) for i, piece in enumerate((s0, s1, s2, s3))]
-    copies += [(weight.at[pl.ds(k * 1024, 1024)], held.at[pl.ds(k * 1024, 1024)]) for k in range(5)]
+    copies += [
+        (weight.at[pl.ds(k * 1024, 1024), pl.ds(512, 320)], held.at[pl.ds(k * 1024, 1024)]) for k in range(5)
+    ]
     copies = start(copies, sems)
     for copy in copies[:4]:
         copy.wait()
@@ -171,7 +173,7 @@
         copies.append((piece, units.at[k]))
         for j in range(4):
             slot = nat[j * 4] // 4 * 4 + nat[k] % 4
-            source = weight.at[pl.ds(pl.multiple_of(slot * 320, 320), 320)]
+            source = weight.at[pl.ds(pl.multiple_of(slot * 320, 320), 320), pl.ds(0, 512)]
             copies.append((source, held.at[k, :, pl.ds(j * 512, 512)]))
     copies = start(copies, sems)
     total = 0.0
@@ -231,26 +233,18 @@
     return (rows[:, j * 512 : (j + 1) * 512].astype(F32) * gain[tab[j]]).astype(BF16)
 
 
-def text_kernel(tab, t0, t1, t2, t3, gain, w0, w1, w2, out, scaled):
+def text_kernel(tab, t0, t1, t2, t3, gain, w0, w1, w2, w3a, w3b, out, scaled):
     @pl.when(pl.program_id(0) == 0)
     def _():
         for i2, rows in enumerate((t0, t1, t2, t3)):
-            for j in range(3):
+            for j in range(4):
                 scaled[i2 * 128 : (i2 + 1) * 128, j * 512 : (j + 1) * 512] = scaled_rows(gain, tab, j, rows)
 
     total = jnp.dot(scaled[:, 0:512], w0[...], preferred_element_type=F32)
     total = total + jnp.dot(scaled[:, 512:1024], w1[...], preferred_element_type=F32)
-    out[...] = total + jnp.dot(scaled[:, 1024:1536], w2[...], preferred_element_type=F32)
-
-
-def text_far_kernel(tab, t0, t1, t2, t3, gain, near, w3a, w3b, out, scaled):
-    @pl.when(pl.program_id(0) == 0)
-    def _():
-        for i2, rows in enumerate((t0, t1, t2, t3)):
-            scaled[i2 * 128 : (i2 + 1) * 128, :] = scaled_rows(gain, tab, 3, rows)
-
-    total = near[...] + jnp.dot(scaled[:, 0:256], w3a[...], preferred_element_type=F32)
-    total = total + jnp.dot(scaled[:, 256:512], w3b[...], preferred_element_type=F32)
+    total = total + jnp.dot(scaled[:, 1024:1536], w2[...], preferred_element_type=F32)
+    total = total + jnp.dot(scaled[:, 1536:1792], w3a[...], preferred_element_type=F32)
+    total = total + jnp.dot(scaled[:, 1792:2048], w3b[...], preferred_element_type=F32)
     out[...] = total.astype(BF16)
 
 
@@ -261,27 +255,14 @@
 def text_product(tab, text, gain, weights):
     return pl.pallas_call(
         text_kernel,
-        out_shape=jax.ShapeDtypeStruct((512, 2048), F32),
-        grid=(4,),
-        in_specs=[SMEM] + [VMEM] * 5 + [block(512)] * 3,
-        out_specs=block(512),
-        scratch_shapes=[pltpu.VMEM((512, 1536), BF16)],
-        compiler_params=params(28),
-        cost_estimate=cost(3200 * 10**6, 14 * MIB),
-    )(tab, *text, gain, *weights)
-
-
-def text_far_product(tab, text, gain, near, weights):
-    return pl.pallas_call(
-        text_far_kernel,
         out_shape=jax.ShapeDtypeStruct((512, 2048), BF16),
         grid=(4,),
-        in_specs=[SMEM] + [VMEM] * 5 + [block(512)] + [block(256)] * 2,
+        in_specs=[SMEM] + [VMEM] * 5 + [block(n) for n in (512, 512, 512, 256, 256)],
         out_specs=block(512),
-        scratch_shapes=[pltpu.VMEM((512, 512), BF16)],
+        scratch_shapes=[pltpu.VMEM((512, 2048), BF16)],
         compiler_params=params(28),
-        cost_estimate=cost(1100 * 10**6, 8 * MIB),
-    )(tab, *text, gain, near, *weights)
+        cost_estimate=cost(4300 * 10**6, 14 * MIB),
+    )(tab, *text, gain, *weights)
 
 
 def product_kernel(tab, dest, v0, v1, v2, v3, gain, text, w0, w1, w2, w3a, w3b, own, left, right, far, scaled, select):
@@ -365,28 +346,28 @@
 ):
     tab = jnp.asarray(TABLE)[lax.axis_index("mb") * 16 + lax.axis_index("tp")]
     nat = jnp.asarray(TABLE)[lax.axis_index("tp")]
-    up_full = lax.all_gather(up_weight, ("enc", "mb"), axis=0, tiled=True)
     down_part = lax.ppermute(down_weight, ("enc", "mb", "tp"), SHUFFLE)
-
     merged = merge(patches[0, 0], merge_gain, merge_bias)
+    packed = jnp.concatenate([after(down_part, merged), up_weight], axis=1)
+    packed = lax.all_gather(packed, ("enc", "mb"), axis=0, tiled=True)
+
     near = jnp.concatenate([merged, *around(merged, 1)], axis=0)
     group = (near, *around(near, 2))
-    down_full = lax.all_gather(after(down_part, *group), ("enc", "mb"), axis=0, tiled=True)
-
     kv_weight = after(kv_weight, *group)
     kv_right, kv_left = hop(kv_weight, 1, 1), hop(kv_weight, 1, -1)
-    far_right, far_left = kv_right[:256], kv_left[256:]
     own, to_left, to_right, to_far = pack(tab, text_embed[0, 0])
-    hidden = up(tab, group, up_full, up_bias.reshape(16, 1, 320))
+    moved = lax.optimization_barrier((kv_right, kv_left, to_left, to_right, to_far))
+    kv_right, kv_left, to_left, to_right, to_far = moved
+    far = (hop(kv_right[:256], 1, 1), hop(kv_left[256:], 1, -1))
+    text = (own, hop(to_right, 2, 1), hop(to_left, 2, -1), hop(to_far, 2, 2))
+    weights = (kv_weight, kv_right, kv_left, *far)
+
+    packed = after(packed, *far, *text)
+    hidden = up(tab, group, packed, up_bias.reshape(16, 1, 320))
     units = (hidden, line(hidden, "x", 1), line(hidden, "x", -1), line(hidden, "x", 2))
-    text = (own, hop(to_right, 2, 1), hop(to_left, 2, -1), hop(to_far, 2, 2))
-    *units, far_right, far_left = lax.optimization_barrier((*units, far_right, far_left, *text))[:6]
-    far = (hop(far_right, 1, 1), hop(far_left, 1, -1))
     gain = norm_gain.reshape(16, 1, 512)
-    text_sums = text_product(tab, text, gain, (kv_weight, kv_right, kv_left))
-    down_full, *far = lax.optimization_barrier((down_full, *far, text_sums))[:3]
-    own, to_left, to_right, to_far = down(nat, units, down_full)
-    text_sums = text_far_product(tab, text, gain, after(text_sums, to_far), far)
+    text_sums = text_product(tab, (after(own, hidden), *text[1:]), gain, weights)
+    own, to_left, to_right, to_far = down(nat, units, after(packed, text_sums))
     bias = lax.dynamic_slice_in_dim(down_bias, lax.axis_index("tp") * 512, 512, 0)
     total = own + bias
     for value in (line(to_far, "y", 2), line(to_right, "y", 1), line(to_left, "y", -1)):

time: 195 us -> 210 us (1.077)
  waiting for transfers between devices: 78.9 us -> 91 us
  local copies, waits for them, and re-layouts: 13.3 us -> 18.3 us
  Pallas kernels: 36.2 us -> 32.5 us
  starting transfers between devices: 49.5 us -> 46 us
  other arithmetic: 1.47 us -> 4.56 us
    ppermute x22, waiting for transfers between devices: 52.5 us -> 74.9 us  [hop(): return lax.ppermute(value, ('mb', 'tp'), HOPS[which, step])]
    ppermute x1, waiting for transfers between devices: 18.3 us -> 7.5 us  [per_device(): down_part = lax.ppermute(down_weight, ('enc', 'mb', 'tp'), SHUFFLE)]
    unnamed x40 -> x64, local copies, waits for them, and re-layouts: 5.66 us -> 10.8 us
    pallas_call x2 -> x1, Pallas kernels: 10.7 us -> 7.17 us  [text_product(): pl.pallas_call(text_kernel, out_shape=jax.ShapeDtypeStruct((512, 2048), B...]
    ppermute x6, starting transfers between devices: 11 us -> 7.85 us  [line(): return lax.ppermute(value, ('mb', 'tp'), LINES[axis, step])]
  transfers between devices with their start and end apart: 31 -> 30, of which waited for: 16 -> 17; matrix products, arithmetic and copies ran while one was open for 4% -> 4% of each run, Pallas kernels for 14% -> 9%
where the time goes in v10:
time: 210 us; the launch traced here: 207 us
  waiting for transfers between devices  91 us (43%)
  starting transfers between devices  46 us (22%)
  Pallas kernels  32.5 us (15%)
  local copies, waits for them, and re-layouts  18.3 us (9%)
  between operations  14.4 us (7%)
  other arithmetic  4.56 us (2%)
    ppermute x22, waiting for transfers between devices, hop(): return lax.ppermute(value, ('mb', 'tp'), HOPS[which, step])  74.9 us
    ppermute x22, starting transfers between devices, hop(): return lax.ppermute(value, ('mb', 'tp'), HOPS[which, step])  33.7 us
    unnamed x64, local copies, waits for them, and re-layouts  10.8 us
    ppermute x6, waiting for transfers between devices, line(): return lax.ppermute(value, ('mb', 'tp'), LINES[axis, step])  8.54 us
    ppermute x6, starting transfers between devices, line(): return lax.ppermute(value, ('mb', 'tp'), LINES[axis, step])  7.85 us
    ppermute x1, waiting for transfers between devices, per_device(): down_part = lax.ppermute(down_weight, ('enc', 'mb', 'tp'), SHUFFLE)  7.5 us
    pallas_call x1, Pallas kernels, text_product(): pl.pallas_call(text_kernel, out_shape=jax.ShapeDtypeStruct((512, 2048), B...  7.17 us
    pallas_call x1, Pallas kernels, product(): pl.pallas_call(product_kernel, out_shape=[jax.ShapeDtypeStruct((128, 2048...  6.43 us
  transfers between devices with their start and end apart: 30, of which 17 were waited for; matrix products, arithmetic and copies ran while one was open for 4% of the time, Pallas kernels for 9%

profile of v10, /device:TPU:32, one launch (start us, length us, event | category | flops | bytes accessed | tf_op | source)
XLA Modules:
  0.0 206.8 jit_solution(10858622902914089352)
XLA Ops:
  7.2 4.5 %collective-permute-start.6 = (bf16[320,512]{1,0:T(8,128)(2,1)}, bf16[320,512]{1,0:T(8,128)(2,1)S(1)}, u32[]{:S(2)}, u32[]{:S(2)}) collective-permute-start(bf16[320,512]{1,0:T(8,128)(2,1)} %param.21), channel_id=1, source_target_pairs={{0,0},{1,16},{2,32},{3,48},{4,4},{5,20},{6,36},{7,52},{8,8},{9,24}... | collective-permute-start | bytes 983048 | tf_op jit(solution)/shard_map/ppermute | solution.py:349
  14.3 7.5 %collective-permute-done.6 = bf16[320,512]{1,0:T(8,128)(2,1)S(1)} collective-permute-done((bf16[320,512]{1,0:T(8,128)(2,1)}, bf16[320,512]{1,0:T(8,128)(2,1)S(1)}, u32[]{:S(2)}, u32[]{:S(2)}) %collective-permute-start.6) | collective-permute-done | bytes 327712 | tf_op jit(solution)/shard_map/ppermute | solution.py:349
  23.7 3.2 %collective-permute-start.1 = (bf16[16,5120]{1,0:T(8,128)(2,1)S(1)}, bf16[16,5120]{1,0:T(8,128)(2,1)S(1)}, u32[]{:S(2)}, u32[]{:S(2)}) collective-permute-start(bf16[16,5120]{1,0:T(8,128)(2,1)S(1)} %shard_map.149), channel_id=1, source_target_pairs={{0,3},{1,0},{2,1},{3,2},{4,7},{5,4},{6,5},{7,6},{8,11},{9,8},{10,9... | collective-permute-start | bytes 491528 | tf_op jit(solution)/shard_map/ppermute | solution.py:52
  26.9 3.3 %collective-permute-done = bf16[16,5120]{1,0:T(8,128)(2,1)S(1)} collective-permute-done((bf16[16,5120]{1,0:T(8,128)(2,1)S(1)}, bf16[16,5120]{1,0:T(8,128)(2,1)S(1)}, u32[]{:S(2)}, u32[]{:S(2)}) %collective-permute-start) | collective-permute-done | bytes 163872 | tf_op jit(solution)/shard_map/ppermute | solution.py:52
  31.5 3.3 %collective-permute-done.2 = bf16[16,5120]{1,0:T(8,128)(2,1)S(1)} collective-permute-done((bf16[16,5120]{1,0:T(8,128)(2,1)S(1)}, bf16[16,5120]{1,0:T(8,128)(2,1)S(1)}, u32[]{:S(2)}, u32[]{:S(2)}) %collective-permute-start.2) | collective-permute-done | bytes 163872 | tf_op jit(solution)/shard_map/ppermute | solution.py:52
  34.9 2.2 %collective-permute-start.3 = (bf16[64,5120]{1,0:T(8,128)(2,1)S(1)}, bf16[64,5120]{1,0:T(8,128)(2,1)S(1)}, u32[]{:S(2)}, u32[]{:S(2)}) collective-permute-start(bf16[64,5120]{1,0:T(8,128)(2,1)S(1)} %pad_maximum_fusion.s0), channel_id=1, source_target_pairs={{0,4},{1,5},{2,6},{3,7},{4,8},{5,9},{6,10},{7,11},{8,12},{9,13},{1... | collective-permute-start | bytes 1966088 | tf_op jit(solution)/shard_map/ppermute | solution.py:52
  38.7 2.1 %collective-permute-start.5 = (bf16[64,5120]{1,0:T(8,128)(2,1)S(1)}, bf16[64,5120]{1,0:T(8,128)(2,1)S(1)}, u32[]{:S(2)}, u32[]{:S(2)}) collective-permute-start(bf16[64,5120]{1,0:T(8,128)(2,1)S(1)} %pad_maximum_fusion.s0), channel_id=1, source_target_pairs={{0,8},{1,9},{2,10},{3,11},{4,12},{5,13},{6,14},{7,15},{8,0},{9,1},... | collective-permute-start | bytes 1966088 | tf_op jit(solution)/shard_map/ppermute | solution.py:52
  40.8 6.3 %collective-permute-done.3.s1 = bf16[64,5120]{1,0:T(8,128)(2,1)S(1)} collective-permute-done((bf16[64,5120]{1,0:T(8,128)(2,1)S(1)}, bf16[64,5120]{1,0:T(8,128)(2,1)S(1)}, u32[]{:S(2)}, u32[]{:S(2)}) %collective-permute-start.3) | collective-permute-done | bytes 655392 | tf_op jit(solution)/shard_map/ppermute | solution.py:52
  47.6 8.4 %collective-permute-done.5.s3 = bf16[64,5120]{1,0:T(8,128)(2,1)S(1)} collective-permute-done((bf16[64,5120]{1,0:T(8,128)(2,1)S(1)}, bf16[64,5120]{1,0:T(8,128)(2,1)S(1)}, u32[]{:S(2)}, u32[]{:S(2)}) %collective-permute-start.5) | collective-permute-done | bytes 655392 | tf_op jit(solution)/shard_map/ppermute | solution.py:52
  56.1 3.2 %collective-permute-start.8 = (bf16[512,2048]{1,0:T(8,128)(2,1)}, bf16[512,2048]{1,0:T(8,128)(2,1)}, u32[]{:S(2)}, u32[]{:S(2)}) collective-permute-start(bf16[512,2048]{1,0:T(8,128)(2,1)} %w0.1), channel_id=1, source_target_pairs={{0,3},{1,0},{2,1},{3,2},{4,7},{5,4},{6,5},{7,6},{8,11},{9,8},{10,9... | collective-permute-start | bytes 6291464 | tf_op jit(solution)/shard_map/ppermute | solution.py:52
  60.5 2.5 %shard_map.150 = (bf16[128,2048]{1,0:T(8,128)(2,1)S(1)}, bf16[128,2048]{1,0:T(8,128)(2,1)}, bf16[128,2048]{1,0:T(8,128)(2,1)}, bf16[128,2048]{1,0:T(8,128)(2,1)}) custom-call(s32[16]{0:T(128)S(1)} %get-tuple-element.61.tab, bf16[128,8192]{1,0:T(8,128)(2,1)S(1)} %bitcast.20, bf16[128,8192]{1,0:T(8,128)(2,1)S(1)} %bitcast.21, bf16[128,8192]{1,0:T(8,128)(2,1)S(1)} %bitcast.22, ...), custom_call_target="tpu_custom_call" | custom-call | bytes 4194304 | tf_op jit(solution)/shard_map/pallas_call | solution.py:115
  63.8 19.8 %collective-permute-done.7.w1 = bf16[512,2048]{1,0:T(8,128)(2,1)} collective-permute-done((bf16[512,2048]{1,0:T(8,128)(2,1)}, bf16[512,2048]{1,0:T(8,128)(2,1)}, u32[]{:S(2)}, u32[]{:S(2)}) %collective-permute-start.7) | collective-permute-done | bytes 2097184 | tf_op jit(solution)/shard_map/ppermute | solution.py:52
  83.6 2.3 %slice.10 = bf16[256,2048]{1,0:T(8,128)(2,1)} slice(bf16[512,2048]{1,0:T(8,128)(2,1)} %collective-permute-done.8.w2), slice={[256:512], [0:2048]} | slice | bytes 2097152 | tf_op jit(solution)/shard_map/slice | solution.py:361
  85.9 3.2 %collective-permute-start.10 = (bf16[256,2048]{1,0:T(8,128)(2,1)}, bf16[256,2048]{1,0:T(8,128)(2,1)S(1)}, u32[]{:S(2)}, u32[]{:S(2)}) collective-permute-start(bf16[256,2048]{1,0:T(8,128)(2,1)} %slice.10), channel_id=1, source_target_pairs={{0,3},{1,0},{2,1},{3,2},{4,7},{5,4},{6,5},{7,6},{8,11},{9,8},{10,9... | collective-permute-start | bytes 3145736 | tf_op jit(solution)/shard_map/ppermute | solution.py:52
  89.1 2.3 %slice.9 = bf16[256,2048]{1,0:T(8,128)(2,1)} slice(bf16[512,2048]{1,0:T(8,128)(2,1)} %collective-permute-done.7.w1), slice={[0:256], [0:2048]} | slice | bytes 2097152 | tf_op jit(solution)/shard_map/slice | solution.py:361
  95.9 15.4 %collective-permute-done.11.t1.refs_1_ = bf16[128,2048]{1,0:T(8,128)(2,1)S(1)} collective-permute-done((bf16[128,2048]{1,0:T(8,128)(2,1)}, bf16[128,2048]{1,0:T(8,128)(2,1)S(1)}, u32[]{:S(2)}, u32[]{:S(2)}) %collective-permute-start.11) | collective-permute-done | bytes 524320 | tf_op jit(solution)/shard_map/ppermute | solution.py:52
  113.9 6.2 %shard_map.151.h0 = bf16[256,320]{1,0:T(8,128)(2,1)} custom-call(s32[16]{0:T(128)} %copy-done.18, bf16[64,5120]{1,0:T(8,128)(2,1)} %copy-done.22, bf16[64,5120]{1,0:T(8,128)(2,1)} %copy-done.23, bf16[64,5120]{1,0:T(8,128)(2,1)} %copy-done.24, bf16[64,5120]{1,0:T(8,128)(2,1)} %copy-done.25, bf16[5120,832]{1,0:T(8,128)(2,1)} %all-gather.2.cloned.1.call-done.weight, ...), custom_call_target="tpu_custom_call" | custom-call | flops 840000000 | bytes 6291456 | tf_op jit(solution)/shard_map/pallas_call | solution.py:155
  120.2 3.2 %collective-permute-start.15 = (bf16[256,320]{1,0:T(8,128)(2,1)}, bf16[256,320]{1,0:T(8,128)(2,1)}, u32[]{:S(2)}, u32[]{:S(2)}) collective-permute-start(bf16[256,320]{1,0:T(8,128)(2,1)} %shard_map.151.h0), channel_id=1, source_target_pairs={{0,3},{1,0},{2,1},{3,2},{4,7},{5,4},{6,5},{7,6},{8,11},{9,8},{10,9... | collective-permute-start | bytes 491528 | tf_op jit(solution)/shard_map/ppermute | solution.py:60
  123.7 7.2 %shard_map.152.text = bf16[512,2048]{1,0:T(8,128)(2,1)S(1)} custom-call(s32[16]{0:T(128)S(1)} %copy-done.19, bf16[128,2048]{1,0:T(8,128)(2,1)S(1)} %copy-done.8, bf16[128,2048]{1,0:T(8,128)(2,1)S(1)} %copy-done.11, bf16[128,2048]{1,0:T(8,128)(2,1)S(1)} %copy-done.14, bf16[128,2048]{1,0:T(8,128)(2,1)} %collective-permute-done.13.t3.refs_3_, ...), custom_call_target="tpu_custom_call" | custom-call | flops 4300000256 | bytes 14680064 | tf_op jit(solution)/shard_map/pallas_call | solution.py:256
  132.9 5.9 %shard_map.153 = (f32[256,512]{1,0:T(8,128)}, bf16[256,512]{1,0:T(8,128)(2,1)}, bf16[256,512]{1,0:T(8,128)(2,1)}, bf16[256,512]{1,0:T(8,128)(2,1)}) custom-call(s32[16]{0:T(128)} %get-tuple-element.60.nat, bf16[256,320]{1,0:T(8,128)(2,1)} %shard_map.151.h0, bf16[256,320]{1,0:T(8,128)(2,1)} %copy-done.27, bf16[256,320]{1,0:T(8,128)(2,1)} %collective-permute-done.15.h2, ...), custom_call_target="tpu_custom_call" | custom-call | flops 1340000000 | bytes 8388608 | tf_op jit(solution)/shard_map/pallas_call | solution.py:191
  139.9 2.2 %collective-permute-start.18 = (bf16[256,512]{1,0:T(8,128)(2,1)}, bf16[256,512]{1,0:T(8,128)(2,1)}, u32[]{:S(2)}, u32[]{:S(2)}) collective-permute-start(bf16[256,512]{1,0:T(8,128)(2,1)} %get-tuple-element.47), channel_id=1, source_target_pairs={{0,4},{1,5},{2,6},{3,7},{4,8},{5,9},{6,10},{7,11},{8,12},{9,13},{1... | collective-permute-start | bytes 786440 | tf_op jit(solution)/shard_map/ppermute | solution.py:60
  143.9 4.2 %collective-permute-done.17 = bf16[256,512]{1,0:T(8,128)(2,1)S(1)} collective-permute-done((bf16[256,512]{1,0:T(8,128)(2,1)}, bf16[256,512]{1,0:T(8,128)(2,1)S(1)}, u32[]{:S(2)}, u32[]{:S(2)}) %collective-permute-start.17) | collective-permute-done | bytes 262176 | tf_op jit(solution)/shard_map/ppermute | solution.py:60
  148.1 2.8 %collective-permute-done.18 = bf16[256,512]{1,0:T(8,128)(2,1)} collective-permute-done((bf16[256,512]{1,0:T(8,128)(2,1)}, bf16[256,512]{1,0:T(8,128)(2,1)}, u32[]{:S(2)}, u32[]{:S(2)}) %collective-permute-start.18) | collective-permute-done | bytes 262176 | tf_op jit(solution)/shard_map/ppermute | solution.py:60
  154.0 3.2 %collective-permute-start.21 = (bf16[256,512]{1,0:T(8,128)(2,1)S(1)}, bf16[256,512]{1,0:T(8,128)(2,1)}, u32[]{:S(2)}, u32[]{:S(2)}) collective-permute-start(bf16[256,512]{1,0:T(8,128)(2,1)S(1)} %add_convert_fusion.1.v0), channel_id=1, source_target_pairs={{0,3},{1,0},{2,1},{3,2},{4,7},{5,4},{6,5},{7,6},{8,11},{9,8},{10,9... | collective-permute-start | bytes 786440 | tf_op jit(solution)/shard_map/ppermute | solution.py:52
  157.9 3.7 %collective-permute-done.20.v1 = bf16[256,512]{1,0:T(8,128)(2,1)} collective-permute-done((bf16[256,512]{1,0:T(8,128)(2,1)S(1)}, bf16[256,512]{1,0:T(8,128)(2,1)}, u32[]{:S(2)}, u32[]{:S(2)}) %collective-permute-start.20) | collective-permute-done | bytes 262176 | tf_op jit(solution)/shard_map/ppermute | solution.py:52
  161.6 2.2 %collective-permute-done.21.v2 = bf16[256,512]{1,0:T(8,128)(2,1)} collective-permute-done((bf16[256,512]{1,0:T(8,128)(2,1)S(1)}, bf16[256,512]{1,0:T(8,128)(2,1)}, u32[]{:S(2)}, u32[]{:S(2)}) %collective-permute-start.21) | collective-permute-done | bytes 262176 | tf_op jit(solution)/shard_map/ppermute | solution.py:52
  170.9 3.0 %collective-permute-start.24 = (bf16[128,2048]{1,0:T(8,128)(2,1)S(1)}, bf16[128,2048]{1,0:T(8,128)(2,1)S(1)}, u32[]{:S(2)}, u32[]{:S(2)}) collective-permute-start(bf16[128,2048]{1,0:T(8,128)(2,1)S(1)} %get-tuple-element.52), channel_id=1, source_target_pairs={{0,12},{1,13},{2,14},{3,15},{4,0},{5,1},{6,2},{7,3},{8,4},{9,5},{1... | collective-permute-start | bytes 1572872 | tf_op jit(solution)/shard_map/ppermute | solution.py:52
  174.7 6.4 %shard_map.156 = (bf16[128,2048]{1,0:T(8,128)(2,1)S(1)}, bf16[128,2048]{1,0:T(8,128)(2,1)S(1)}, bf16[128,2048]{1,0:T(8,128)(2,1)S(1)}, bf16[128,2048]{1,0:T(8,128)(2,1)S(1)}) custom-call(s32[16]{0:T(128)S(1)} %copy-done.19, s32[1,256]{1,0:T(1,128)S(1)} %bitcast_select_fusion.dest, bf16[256,512]{1,0:T(8,128)(2,1)S(1)} %add_convert_fusion.1.v0, ...), custom_call_target="tpu_custom_call" | custom-call | flops 2700000000 | bytes 14680064 | tf_op jit(solution)/shard_map/pallas_call | solution.py:292
  181.2 2.8 %collective-permute-start.26 = (bf16[128,2048]{1,0:T(8,128)(2,1)S(1)}, bf16[128,2048]{1,0:T(8,128)(2,1)S(1)}, u32[]{:S(2)}, u32[]{:S(2)}) collective-permute-start(bf16[128,2048]{1,0:T(8,128)(2,1)S(1)} %get-tuple-element.56), channel_id=1, source_target_pairs={{0,8},{1,9},{2,10},{3,11},{4,12},{5,13},{6,14},{7,15},{8,0},{9,1},... | collective-permute-start | bytes 1572872 | tf_op jit(solution)/shard_map/ppermute | solution.py:52
  183.9 3.2 %collective-permute-start.28 = (bf16[128,2048]{1,0:T(8,128)(2,1)S(1)}, bf16[128,2048]{1,0:T(8,128)(2,1)S(1)}, u32[]{:S(2)}, u32[]{:S(2)}) collective-permute-start(bf16[128,2048]{1,0:T(8,128)(2,1)S(1)} %get-tuple-element.58), channel_id=1, source_target_pairs={{0,12},{1,13},{2,14},{3,15},{4,0},{5,1},{6,2},{7,3},{8,4},{9,5},{1... | collective-permute-start | bytes 1572872 | tf_op jit(solution)/shard_map/ppermute | solution.py:52
  187.2 4.6 %collective-permute-done.24.e2 = bf16[128,2048]{1,0:T(8,128)(2,1)S(1)} collective-permute-done((bf16[128,2048]{1,0:T(8,128)(2,1)S(1)}, bf16[128,2048]{1,0:T(8,128)(2,1)S(1)}, u32[]{:S(2)}, u32[]{:S(2)}) %collective-permute-start.24) | collective-permute-done | bytes 524320 | tf_op jit(solution)/shard_map/ppermute | solution.py:52
  193.9 4.8 %collective-permute-done.27 = bf16[128,2048]{1,0:T(8,128)(2,1)S(1)} collective-permute-done((bf16[128,2048]{1,0:T(8,128)(2,1)S(1)}, bf16[128,2048]{1,0:T(8,128)(2,1)S(1)}, u32[]{:S(2)}, u32[]{:S(2)}) %collective-permute-start.27) | collective-permute-done | bytes 524320 | tf_op jit(solution)/shard_map/ppermute | solution.py:52
  (115 shorter events, 37.2 us)
Async XLA Ops:
  7.2 106.7 %all-gather.2.cloned.1.call-start = ((), (), s32[]{:S(2)}) async-start(), calls=%async_computation | async-start | bytes 9748480 | tf_op jit(solution)/shard_map/all_gather | solution.py:352
  7.2 14.6 %collective-permute-start.6 = (bf16[320,512]{1,0:T(8,128)(2,1)}, bf16[320,512]{1,0:T(8,128)(2,1)S(1)}, u32[]{:S(2)}, u32[]{:S(2)}) collective-permute-start(bf16[320,512]{1,0:T(8,128)(2,1)} %param.21), channel_id=1, source_target_pairs={{0,0},{1,16},{2,32},{3,48},{4,4},{5,20},{6,36},{7,52},{8,8},{9,24}... | collective-permute-start | bytes 983048 | tf_op jit(solution)/shard_map/ppermute | solution.py:349
  14.3 46.2 %copy-start = (bf16[1,1,128,8192]{3,2,1,0:T(8,128)(2,1)S(1)}, bf16[1,1,128,8192]{3,2,1,0:T(8,128)(2,1)}, u32[]{:S(2)}) copy-start(bf16[1,1,128,8192]{3,2,1,0:T(8,128)(2,1)} %param.23) | copy-start | bytes 6291460
  23.6 6.6 %collective-permute-start = (bf16[16,5120]{1,0:T(8,128)(2,1)S(1)}, bf16[16,5120]{1,0:T(8,128)(2,1)S(1)}, u32[]{:S(2)}, u32[]{:S(2)}) collective-permute-start(bf16[16,5120]{1,0:T(8,128)(2,1)S(1)} %shard_map.149), channel_id=1, source_target_pairs={{0,1},{1,2},{2,3},{3,0},{4,5},{5,6},{6,7},{7,4},{8,9},{9,10},{10,1... | collective-permute-start | bytes 491528 | tf_op jit(solution)/shard_map/ppermute | solution.py:52
  23.7 7.8 %collective-permute-start.1 = (bf16[16,5120]{1,0:T(8,128)(2,1)S(1)}, bf16[16,5120]{1,0:T(8,128)(2,1)S(1)}, u32[]{:S(2)}, u32[]{:S(2)}) collective-permute-start(bf16[16,5120]{1,0:T(8,128)(2,1)S(1)} %shard_map.149), channel_id=1, source_target_pairs={{0,3},{1,0},{2,1},{3,2},{4,7},{5,4},{6,5},{7,6},{8,11},{9,8},{10,9... | collective-permute-start | bytes 491528 | tf_op jit(solution)/shard_map/ppermute | solution.py:52
  26.9 7.9 %collective-permute-start.2 = (bf16[16,5120]{1,0:T(8,128)(2,1)S(1)}, bf16[16,5120]{1,0:T(8,128)(2,1)S(1)}, u32[]{:S(2)}, u32[]{:S(2)}) collective-permute-start(bf16[16,5120]{1,0:T(8,128)(2,1)S(1)} %shard_map.149), channel_id=1, source_target_pairs={{0,2},{1,3},{2,0},{3,1},{4,6},{5,7},{6,4},{7,5},{8,10},{9,11},{10,... | collective-permute-start | bytes 491528 | tf_op jit(solution)/shard_map/ppermute | solution.py:52
  34.9 12.3 %collective-permute-start.3 = (bf16[64,5120]{1,0:T(8,128)(2,1)S(1)}, bf16[64,5120]{1,0:T(8,128)(2,1)S(1)}, u32[]{:S(2)}, u32[]{:S(2)}) collective-permute-start(bf16[64,5120]{1,0:T(8,128)(2,1)S(1)} %pad_maximum_fusion.s0), channel_id=1, source_target_pairs={{0,4},{1,5},{2,6},{3,7},{4,8},{5,9},{6,10},{7,11},{8,12},{9,13},{1... | collective-permute-start | bytes 1966088 | tf_op jit(solution)/shard_map/ppermute | solution.py:52
  37.0 10.6 %collective-permute-start.4 = (bf16[64,5120]{1,0:T(8,128)(2,1)S(1)}, bf16[64,5120]{1,0:T(8,128)(2,1)S(1)}, u32[]{:S(2)}, u32[]{:S(2)}) collective-permute-start(bf16[64,5120]{1,0:T(8,128)(2,1)S(1)} %pad_maximum_fusion.s0), channel_id=1, source_target_pairs={{0,12},{1,13},{2,14},{3,15},{4,0},{5,1},{6,2},{7,3},{8,4},{9,5},{1... | collective-permute-start | bytes 1966088 | tf_op jit(solution)/shard_map/ppermute | solution.py:52
  38.7 17.3 %collective-permute-start.5 = (bf16[64,5120]{1,0:T(8,128)(2,1)S(1)}, bf16[64,5120]{1,0:T(8,128)(2,1)S(1)}, u32[]{:S(2)}, u32[]{:S(2)}) collective-permute-start(bf16[64,5120]{1,0:T(8,128)(2,1)S(1)} %pad_maximum_fusion.s0), channel_id=1, source_target_pairs={{0,8},{1,9},{2,10},{3,11},{4,12},{5,13},{6,14},{7,15},{8,0},{9,1},... | collective-permute-start | bytes 1966088 | tf_op jit(solution)/shard_map/ppermute | solution.py:52
  56.0 27.6 %collective-permute-start.7 = (bf16[512,2048]{1,0:T(8,128)(2,1)}, bf16[512,2048]{1,0:T(8,128)(2,1)}, u32[]{:S(2)}, u32[]{:S(2)}) collective-permute-start(bf16[512,2048]{1,0:T(8,128)(2,1)} %w0.1), channel_id=1, source_target_pairs={{0,1},{1,2},{2,3},{3,0},{4,5},{5,6},{6,7},{7,4},{8,9},{9,10},{10,1... | collective-permute-start | bytes 6291464 | tf_op jit(solution)/shard_map/ppermute | solution.py:52
  56.1 27.5 %collective-permute-start.8 = (bf16[512,2048]{1,0:T(8,128)(2,1)}, bf16[512,2048]{1,0:T(8,128)(2,1)}, u32[]{:S(2)}, u32[]{:S(2)}) collective-permute-start(bf16[512,2048]{1,0:T(8,128)(2,1)} %w0.1), channel_id=1, source_target_pairs={{0,3},{1,0},{2,1},{3,2},{4,7},{5,4},{6,5},{7,6},{8,11},{9,8},{10,9... | collective-permute-start | bytes 6291464 | tf_op jit(solution)/shard_map/ppermute | solution.py:52
  85.9 27.0 %collective-permute-start.10 = (bf16[256,2048]{1,0:T(8,128)(2,1)}, bf16[256,2048]{1,0:T(8,128)(2,1)S(1)}, u32[]{:S(2)}, u32[]{:S(2)}) collective-permute-start(bf16[256,2048]{1,0:T(8,128)(2,1)} %slice.10), channel_id=1, source_target_pairs={{0,3},{1,0},{2,1},{3,2},{4,7},{5,4},{6,5},{7,6},{8,11},{9,8},{10,9... | collective-permute-start | bytes 3145736 | tf_op jit(solution)/shard_map/ppermute | solution.py:52
  91.4 21.5 %collective-permute-start.9 = (bf16[256,2048]{1,0:T(8,128)(2,1)}, bf16[256,2048]{1,0:T(8,128)(2,1)S(1)}, u32[]{:S(2)}, u32[]{:S(2)}) collective-permute-start(bf16[256,2048]{1,0:T(8,128)(2,1)} %slice.9), channel_id=1, source_target_pairs={{0,1},{1,2},{2,3},{3,0},{4,5},{5,6},{6,7},{7,4},{8,9},{9,10},{10,1... | collective-permute-start | bytes 3145736 | tf_op jit(solution)/shard_map/ppermute | solution.py:52
  91.4 19.8 %collective-permute-start.11 = (bf16[128,2048]{1,0:T(8,128)(2,1)}, bf16[128,2048]{1,0:T(8,128)(2,1)S(1)}, u32[]{:S(2)}, u32[]{:S(2)}) collective-permute-start(bf16[128,2048]{1,0:T(8,128)(2,1)} %get-tuple-element.39), channel_id=1, source_target_pairs={{0,4},{1,5},{2,6},{3,7},{4,8},{5,9},{6,10},{7,11},{8,12},{9,13},{1... | collective-permute-start | bytes 1572872 | tf_op jit(solution)/shard_map/ppermute | solution.py:52
  93.1 18.9 %collective-permute-start.12 = (bf16[128,2048]{1,0:T(8,128)(2,1)}, bf16[128,2048]{1,0:T(8,128)(2,1)S(1)}, u32[]{:S(2)}, u32[]{:S(2)}) collective-permute-start(bf16[128,2048]{1,0:T(8,128)(2,1)} %get-tuple-element.40), channel_id=1, source_target_pairs={{0,12},{1,13},{2,14},{3,15},{4,0},{5,1},{6,2},{7,3},{8,4},{9,5},{1... | collective-permute-start | bytes 1572872 | tf_op jit(solution)/shard_map/ppermute | solution.py:52
  94.7 18.2 %collective-permute-start.13 = (bf16[128,2048]{1,0:T(8,128)(2,1)}, bf16[128,2048]{1,0:T(8,128)(2,1)}, u32[]{:S(2)}, u32[]{:S(2)}) collective-permute-start(bf16[128,2048]{1,0:T(8,128)(2,1)} %get-tuple-element.41), channel_id=1, source_target_pairs={{0,8},{1,9},{2,10},{3,11},{4,12},{5,13},{6,14},{7,15},{8,0},{9,1},... | collective-permute-start | bytes 1572872 | tf_op jit(solution)/shard_map/ppermute | solution.py:52
  120.1 12.1 %collective-permute-start.14 = (bf16[256,320]{1,0:T(8,128)(2,1)}, bf16[256,320]{1,0:T(8,128)(2,1)S(1)}, u32[]{:S(2)}, u32[]{:S(2)}) collective-permute-start(bf16[256,320]{1,0:T(8,128)(2,1)} %shard_map.151.h0), channel_id=1, source_target_pairs={{0,1},{1,2},{2,3},{3,0},{4,5},{5,6},{6,7},{7,4},{8,9},{9,10},{10,1... | collective-permute-start | bytes 491528 | tf_op jit(solution)/shard_map/ppermute | solution.py:60
  120.2 12.1 %collective-permute-start.15 = (bf16[256,320]{1,0:T(8,128)(2,1)}, bf16[256,320]{1,0:T(8,128)(2,1)}, u32[]{:S(2)}, u32[]{:S(2)}) collective-permute-start(bf16[256,320]{1,0:T(8,128)(2,1)} %shard_map.151.h0), channel_id=1, source_target_pairs={{0,3},{1,0},{2,1},{3,2},{4,7},{5,4},{6,5},{7,6},{8,11},{9,8},{10,9... | collective-permute-start | bytes 491528 | tf_op jit(solution)/shard_map/ppermute | solution.py:60
  123.4 8.8 %collective-permute-start.16 = (bf16[256,320]{1,0:T(8,128)(2,1)}, bf16[256,320]{1,0:T(8,128)(2,1)}, u32[]{:S(2)}, u32[]{:S(2)}) collective-permute-start(bf16[256,320]{1,0:T(8,128)(2,1)} %shard_map.151.h0), channel_id=1, source_target_pairs={{0,2},{1,3},{2,0},{3,1},{4,6},{5,7},{6,4},{7,5},{8,10},{9,11},{10,... | collective-permute-start | bytes 491528 | tf_op jit(solution)/shard_map/ppermute | solution.py:60
  138.9 19.0 %copy-start.30 = (s32[1,1,256]{2,1,0:T(1,128)S(1)}, s32[1,1,256]{2,1,0:T(1,128)}, u32[]{:S(2)}) copy-start(s32[1,1,256]{2,1,0:T(1,128)} %param.16) | copy-start | bytes 3076
  138.9 9.2 %collective-permute-start.17 = (bf16[256,512]{1,0:T(8,128)(2,1)}, bf16[256,512]{1,0:T(8,128)(2,1)S(1)}, u32[]{:S(2)}, u32[]{:S(2)}) collective-permute-start(bf16[256,512]{1,0:T(8,128)(2,1)} %get-tuple-element.46), channel_id=1, source_target_pairs={{0,8},{1,9},{2,10},{3,11},{4,12},{5,13},{6,14},{7,15},{8,0},{9,1},... | collective-permute-start | bytes 786440 | tf_op jit(solution)/shard_map/ppermute | solution.py:60
  139.9 11.0 %collective-permute-start.18 = (bf16[256,512]{1,0:T(8,128)(2,1)}, bf16[256,512]{1,0:T(8,128)(2,1)}, u32[]{:S(2)}, u32[]{:S(2)}) collective-permute-start(bf16[256,512]{1,0:T(8,128)(2,1)} %get-tuple-element.47), channel_id=1, source_target_pairs={{0,4},{1,5},{2,6},{3,7},{4,8},{5,9},{6,10},{7,11},{8,12},{9,13},{1... | collective-permute-start | bytes 786440 | tf_op jit(solution)/shard_map/ppermute | solution.py:60
  142.1 10.4 %collective-permute-start.19 = (bf16[256,512]{1,0:T(8,128)(2,1)}, bf16[256,512]{1,0:T(8,128)(2,1)}, u32[]{:S(2)}, u32[]{:S(2)}) collective-permute-start(bf16[256,512]{1,0:T(8,128)(2,1)} %get-tuple-element.48), channel_id=1, source_target_pairs={{0,12},{1,13},{2,14},{3,15},{4,0},{5,1},{6,2},{7,3},{8,4},{9,5},{1... | collective-permute-start | bytes 786440 | tf_op jit(solution)/shard_map/ppermute | solution.py:60
  153.9 7.8 %collective-permute-start.20 = (bf16[256,512]{1,0:T(8,128)(2,1)S(1)}, bf16[256,512]{1,0:T(8,128)(2,1)}, u32[]{:S(2)}, u32[]{:S(2)}) collective-permute-start(bf16[256,512]{1,0:T(8,128)(2,1)S(1)} %add_convert_fusion.1.v0), channel_id=1, source_target_pairs={{0,1},{1,2},{2,3},{3,0},{4,5},{5,6},{6,7},{7,4},{8,9},{9,10},{10,1... | collective-permute-start | bytes 786440 | tf_op jit(solution)/shard_map/ppermute | solution.py:52
  154.0 9.9 %collective-permute-start.21 = (bf16[256,512]{1,0:T(8,128)(2,1)S(1)}, bf16[256,512]{1,0:T(8,128)(2,1)}, u32[]{:S(2)}, u32[]{:S(2)}) collective-permute-start(bf16[256,512]{1,0:T(8,128)(2,1)S(1)} %add_convert_fusion.1.v0), channel_id=1, source_target_pairs={{0,3},{1,0},{2,1},{3,2},{4,7},{5,4},{6,5},{7,6},{8,11},{9,8},{10,9... | collective-permute-start | bytes 786440 | tf_op jit(solution)/shard_map/ppermute | solution.py:52
  157.2 8.0 %collective-permute-start.22 = (bf16[256,512]{1,0:T(8,128)(2,1)S(1)}, bf16[256,512]{1,0:T(8,128)(2,1)}, u32[]{:S(2)}, u32[]{:S(2)}) collective-permute-start(bf16[256,512]{1,0:T(8,128)(2,1)S(1)} %add_convert_fusion.1.v0), channel_id=1, source_target_pairs={{0,2},{1,3},{2,0},{3,1},{4,6},{5,7},{6,4},{7,5},{8,10},{9,11},{10,... | collective-permute-start | bytes 786440 | tf_op jit(solution)/shard_map/ppermute | solution.py:52
  170.3 13.6 %collective-permute-start.23 = (bf16[128,2048]{1,0:T(8,128)(2,1)S(1)}, bf16[128,2048]{1,0:T(8,128)(2,1)S(1)}, u32[]{:S(2)}, u32[]{:S(2)}) collective-permute-start(bf16[128,2048]{1,0:T(8,128)(2,1)S(1)} %get-tuple-element.51), channel_id=1, source_target_pairs={{0,4},{1,5},{2,6},{3,7},{4,8},{5,9},{6,10},{7,11},{8,12},{9,13},{1... | collective-permute-start | bytes 1572872 | tf_op jit(solution)/shard_map/ppermute | solution.py:52
  170.9 20.9 %collective-permute-start.24 = (bf16[128,2048]{1,0:T(8,128)(2,1)S(1)}, bf16[128,2048]{1,0:T(8,128)(2,1)S(1)}, u32[]{:S(2)}, u32[]{:S(2)}) collective-permute-start(bf16[128,2048]{1,0:T(8,128)(2,1)S(1)} %get-tuple-element.52), channel_id=1, source_target_pairs={{0,12},{1,13},{2,14},{3,15},{4,0},{5,1},{6,2},{7,3},{8,4},{9,5},{1... | collective-permute-start | bytes 1572872 | tf_op jit(solution)/shard_map/ppermute | solution.py:52
  173.9 17.9 %collective-permute-start.25 = (bf16[128,2048]{1,0:T(8,128)(2,1)S(1)}, bf16[128,2048]{1,0:T(8,128)(2,1)S(1)}, u32[]{:S(2)}, u32[]{:S(2)}) collective-permute-start(bf16[128,2048]{1,0:T(8,128)(2,1)S(1)} %get-tuple-element.53), channel_id=1, source_target_pairs={{0,8},{1,9},{2,10},{3,11},{4,12},{5,13},{6,14},{7,15},{8,0},{9,1},... | collective-permute-start | bytes 1572872 | tf_op jit(solution)/shard_map/ppermute | solution.py:52
  181.2 12.7 %collective-permute-start.26 = (bf16[128,2048]{1,0:T(8,128)(2,1)S(1)}, bf16[128,2048]{1,0:T(8,128)(2,1)S(1)}, u32[]{:S(2)}, u32[]{:S(2)}) collective-permute-start(bf16[128,2048]{1,0:T(8,128)(2,1)S(1)} %get-tuple-element.56), channel_id=1, source_target_pairs={{0,8},{1,9},{2,10},{3,11},{4,12},{5,13},{6,14},{7,15},{8,0},{9,1},... | collective-permute-start | bytes 1572872 | tf_op jit(solution)/shard_map/ppermute | solution.py:52
  183.9 14.8 %collective-permute-start.27 = (bf16[128,2048]{1,0:T(8,128)(2,1)S(1)}, bf16[128,2048]{1,0:T(8,128)(2,1)S(1)}, u32[]{:S(2)}, u32[]{:S(2)}) collective-permute-start(bf16[128,2048]{1,0:T(8,128)(2,1)S(1)} %get-tuple-element.57), channel_id=1, source_target_pairs={{0,4},{1,5},{2,6},{3,7},{4,8},{5,9},{6,10},{7,11},{8,12},{9,13},{1... | collective-permute-start | bytes 1572872 | tf_op jit(solution)/shard_map/ppermute | solution.py:52
  183.9 14.8 %collective-permute-start.28 = (bf16[128,2048]{1,0:T(8,128)(2,1)S(1)}, bf16[128,2048]{1,0:T(8,128)(2,1)S(1)}, u32[]{:S(2)}, u32[]{:S(2)}) collective-permute-start(bf16[128,2048]{1,0:T(8,128)(2,1)S(1)} %get-tuple-element.58), channel_id=1, source_target_pairs={{0,12},{1,13},{2,14},{3,15},{4,0},{5,1},{6,2},{7,3},{8,4},{9,5},{1... | collective-permute-start | bytes 1572872 | tf_op jit(solution)/shard_map/ppermute | solution.py:52
  (30 other events, 182.4 us)
Sparse Core Ops, SparseCore 0:
  23.7 60.0 all-gather.1

commit v11 on v7

--- a/solution.py
+++ b/solution.py
@@ -258,7 +258,7 @@
         in_specs=[SMEM] + [VMEM] * 5 + [block(n) for n in (512, 512, 512, 256, 256)],
         out_specs=[block(128)] * 4,
         scratch_shapes=[pltpu.VMEM((512, 2048), BF16)],
-        compiler_params=params(56),
+        compiler_params=params(28),
         cost_estimate=cost(4300 * 10**6, 14 * MIB),
     )(tab, *picked, gain, *weights)
 
@@ -313,6 +313,7 @@
 
     merged = merge(patches[0, 0], merge_gain, merge_bias)
     near = jnp.concatenate([merged, *around(merged, 1)], axis=0)
+    near, down_part = lax.optimization_barrier((near, down_part))
     group = (near, *around(near, 2))
     down_full = lax.all_gather(after(down_part, *group), ("enc", "mb"), axis=0, tiled=True)
 

time: 188 us -> 208 us (1.11)
  the two profiles are of different devices: /device:TPU:224 before, /device:TPU:32 now
where the time goes in v11:
time: 208 us; the launch traced here: 206 us
  waiting for transfers between devices  101 us (49%)
  starting transfers between devices  50.9 us (24%)
  Pallas kernels  23.5 us (11%)
  between operations  14.4 us (7%)
  local copies, waits for them, and re-layouts  13 us (6%)
  other arithmetic  2.53 us (1%)
    ppermute x22, waiting for transfers between devices, hop(): return lax.ppermute(value, ('mb', 'tp'), HOPS[which, step])  76.4 us
    ppermute x22, starting transfers between devices, hop(): return lax.ppermute(value, ('mb', 'tp'), HOPS[which, step])  36.8 us
    ppermute x6, waiting for transfers between devices, line(): return lax.ppermute(value, ('mb', 'tp'), LINES[axis, step])  13.1 us
    ppermute x1, waiting for transfers between devices, per_device(): down_part = lax.ppermute(down_weight, ('enc', 'mb', 'tp'), SHUFFLE)  11.3 us
    ppermute x6, starting transfers between devices, line(): return lax.ppermute(value, ('mb', 'tp'), LINES[axis, step])  9.21 us
    unnamed x50, local copies, waits for them, and re-layouts  8 us
    pallas_call x1, Pallas kernels, product(): pl.pallas_call(product_kernel, out_shape=[jax.ShapeDtypeStruct((128, 2048...  7 us
    pallas_call x1, Pallas kernels, down(): pl.pallas_call(down_kernel, out_shape=[jax.ShapeDtypeStruct((256, 512), F...  5.99 us
  transfers between devices with their start and end apart: 31, of which 16 were waited for; matrix products, arithmetic and copies ran while one was open for 3% of the time, Pallas kernels for 8%

profile of v11, /device:TPU:32, one launch (start us, length us, event | category | flops | bytes accessed | tf_op | source)
XLA Modules:
  0.0 205.8 jit_solution(1565784031928422567)
XLA Ops:
  13.9 1.8 collective-permute-start.2
  15.7 4.9 %collective-permute-start.3 = (bf16[320,512]{1,0:T(8,128)(2,1)}, bf16[320,512]{1,0:T(8,128)(2,1)S(1)}, u32[]{:S(2)}, u32[]{:S(2)}) collective-permute-start(bf16[320,512]{1,0:T(8,128)(2,1)} %param.21), channel_id=1, source_target_pairs={{0,0},{1,16},{2,32},{3,48},{4,4},{5,20},{6,36},{7,52},{8,8},{9,24}... | collective-permute-start | bytes 983048 | tf_op jit(solution)/shard_map/ppermute | solution.py:312
  20.7 11.3 %collective-permute-done.3 = bf16[320,512]{1,0:T(8,128)(2,1)S(1)} collective-permute-done((bf16[320,512]{1,0:T(8,128)(2,1)}, bf16[320,512]{1,0:T(8,128)(2,1)S(1)}, u32[]{:S(2)}, u32[]{:S(2)}) %collective-permute-start.3) | collective-permute-done | bytes 327712 | tf_op jit(solution)/shard_map/ppermute | solution.py:312
  32.1 1.8 collective-permute-start.4
  35.5 2.3 %collective-permute-start.6 = (bf16[64,5120]{1,0:T(8,128)(2,1)S(1)}, bf16[64,5120]{1,0:T(8,128)(2,1)S(1)}, u32[]{:S(2)}, u32[]{:S(2)}) collective-permute-start(bf16[64,5120]{1,0:T(8,128)(2,1)S(1)} %pad_maximum_fusion.s0), channel_id=1, source_target_pairs={{0,8},{1,9},{2,10},{3,11},{4,12},{5,13},{6,14},{7,15},{8,0},{9,1},... | collective-permute-start | bytes 1966088 | tf_op jit(solution)/shard_map/ppermute | solution.py:52
  37.8 6.3 %collective-permute-done.4.s1 = bf16[64,5120]{1,0:T(8,128)(2,1)S(1)} collective-permute-done((bf16[64,5120]{1,0:T(8,128)(2,1)S(1)}, bf16[64,5120]{1,0:T(8,128)(2,1)S(1)}, u32[]{:S(2)}, u32[]{:S(2)}) %collective-permute-start.4) | collective-permute-done | bytes 655392 | tf_op jit(solution)/shard_map/ppermute | solution.py:52
  44.4 8.1 %collective-permute-done.6.s3 = bf16[64,5120]{1,0:T(8,128)(2,1)S(1)} collective-permute-done((bf16[64,5120]{1,0:T(8,128)(2,1)S(1)}, bf16[64,5120]{1,0:T(8,128)(2,1)S(1)}, u32[]{:S(2)}, u32[]{:S(2)}) %collective-permute-start.6) | collective-permute-done | bytes 655392 | tf_op jit(solution)/shard_map/ppermute | solution.py:52
  53.5 3.2 %collective-permute-start.11 = (bf16[512,2048]{1,0:T(8,128)(2,1)}, bf16[512,2048]{1,0:T(8,128)(2,1)}, u32[]{:S(2)}, u32[]{:S(2)}) collective-permute-start(bf16[512,2048]{1,0:T(8,128)(2,1)} %w0), channel_id=1, source_target_pairs={{0,3},{1,0},{2,1},{3,2},{4,7},{5,4},{6,5},{7,6},{8,11},{9,8},{10,9... | collective-permute-start | bytes 6291464 | tf_op jit(solution)/shard_map/ppermute | solution.py:52
  58.7 5.7 %shard_map.150.h0 = bf16[256,320]{1,0:T(8,128)(2,1)} custom-call(s32[16]{0:T(128)} %get-tuple-element.67.tab, bf16[64,5120]{1,0:T(8,128)(2,1)} %copy-done.13, bf16[64,5120]{1,0:T(8,128)(2,1)} %copy-done.14, bf16[64,5120]{1,0:T(8,128)(2,1)} %copy-done.15, bf16[64,5120]{1,0:T(8,128)(2,1)} %copy-done.16, bf16[5120,320]{1,0:T(8,128)(2,1)} %all-gather.3.cloned.1.call-done.weight, ...), custom_call_target="tpu_custom_call" | custom-call | flops 840000000 | bytes 6291456 | tf_op jit(solution)/shard_map/pallas_call | solution.py:153
  64.5 3.2 %collective-permute-start.8 = (bf16[256,320]{1,0:T(8,128)(2,1)}, bf16[256,320]{1,0:T(8,128)(2,1)S(1)}, u32[]{:S(2)}, u32[]{:S(2)}) collective-permute-start(bf16[256,320]{1,0:T(8,128)(2,1)} %shard_map.150.h0), channel_id=1, source_target_pairs={{0,3},{1,0},{2,1},{3,2},{4,7},{5,4},{6,5},{7,6},{8,11},{9,8},{10,9... | collective-permute-start | bytes 491528 | tf_op jit(solution)/shard_map/ppermute | solution.py:60
  69.0 19.6 %collective-permute-done.10.w1 = bf16[512,2048]{1,0:T(8,128)(2,1)S(1)} collective-permute-done((bf16[512,2048]{1,0:T(8,128)(2,1)}, bf16[512,2048]{1,0:T(8,128)(2,1)S(1)}, u32[]{:S(2)}, u32[]{:S(2)}) %collective-permute-start.10) | collective-permute-done | bytes 2097184 | tf_op jit(solution)/shard_map/ppermute | solution.py:52
  88.8 2.0 slice.13
  90.7 7.7 %collective-permute-done.7.h1 = bf16[256,320]{1,0:T(8,128)(2,1)S(1)} collective-permute-done((bf16[256,320]{1,0:T(8,128)(2,1)}, bf16[256,320]{1,0:T(8,128)(2,1)S(1)}, u32[]{:S(2)}, u32[]{:S(2)}) %collective-permute-start.7) | collective-permute-done | bytes 163872 | tf_op jit(solution)/shard_map/ppermute | solution.py:60
  98.6 3.2 %collective-permute-start.13 = (bf16[256,2048]{1,0:T(8,128)(2,1)S(1)}, bf16[256,2048]{1,0:T(8,128)(2,1)S(1)}, u32[]{:S(2)}, u32[]{:S(2)}) collective-permute-start(bf16[256,2048]{1,0:T(8,128)(2,1)S(1)} %slice.13), channel_id=1, source_target_pairs={{0,3},{1,0},{2,1},{3,2},{4,7},{5,4},{6,5},{7,6},{8,11},{9,8},{10,9... | collective-permute-start | bytes 3145736 | tf_op jit(solution)/shard_map/ppermute | solution.py:52
  101.8 3.6 %collective-permute-start.14 = (bf16[128,2048]{1,0:T(8,128)(2,1)S(1)}, bf16[128,2048]{1,0:T(8,128)(2,1)S(1)}, u32[]{:S(2)}, u32[]{:S(2)}) collective-permute-start(bf16[128,2048]{1,0:T(8,128)(2,1)S(1)} %get-tuple-element.48), channel_id=1, source_target_pairs={{0,4},{1,5},{2,6},{3,7},{4,8},{5,9},{6,10},{7,11},{8,12},{9,13},{1... | collective-permute-start | bytes 1572872 | tf_op jit(solution)/shard_map/ppermute | solution.py:52
  105.4 2.1 %collective-permute-start.16 = (bf16[128,2048]{1,0:T(8,128)(2,1)S(1)}, bf16[128,2048]{1,0:T(8,128)(2,1)S(1)}, u32[]{:S(2)}, u32[]{:S(2)}) collective-permute-start(bf16[128,2048]{1,0:T(8,128)(2,1)S(1)} %get-tuple-element.50), channel_id=1, source_target_pairs={{0,8},{1,9},{2,10},{3,11},{4,12},{5,13},{6,14},{7,15},{8,0},{9,1},... | collective-permute-start | bytes 1572872 | tf_op jit(solution)/shard_map/ppermute | solution.py:52
  107.5 6.2 %collective-permute-done.14.refs_1_ = bf16[128,2048]{1,0:T(8,128)(2,1)S(1)} collective-permute-done((bf16[128,2048]{1,0:T(8,128)(2,1)S(1)}, bf16[128,2048]{1,0:T(8,128)(2,1)S(1)}, u32[]{:S(2)}, u32[]{:S(2)}) %collective-permute-start.14) | collective-permute-done | bytes 524320 | tf_op jit(solution)/shard_map/ppermute | solution.py:52
  113.6 3.3 %collective-permute-done.15.refs_2_ = bf16[128,2048]{1,0:T(8,128)(2,1)S(1)} collective-permute-done((bf16[128,2048]{1,0:T(8,128)(2,1)S(1)}, bf16[128,2048]{1,0:T(8,128)(2,1)S(1)}, u32[]{:S(2)}, u32[]{:S(2)}) %collective-permute-start.15) | collective-permute-done | bytes 524320 | tf_op jit(solution)/shard_map/ppermute | solution.py:52
  116.9 7.8 %collective-permute-done.16.refs_3_ = bf16[128,2048]{1,0:T(8,128)(2,1)S(1)} collective-permute-done((bf16[128,2048]{1,0:T(8,128)(2,1)S(1)}, bf16[128,2048]{1,0:T(8,128)(2,1)S(1)}, u32[]{:S(2)}, u32[]{:S(2)}) %collective-permute-start.16) | collective-permute-done | bytes 524320 | tf_op jit(solution)/shard_map/ppermute | solution.py:52
  126.8 6.0 %shard_map.152 = (f32[256,512]{1,0:T(8,128)}, bf16[256,512]{1,0:T(8,128)(2,1)}, bf16[256,512]{1,0:T(8,128)(2,1)}, bf16[256,512]{1,0:T(8,128)(2,1)}) custom-call(s32[16]{0:T(128)} %get-tuple-element.66.nat, bf16[256,320]{1,0:T(8,128)(2,1)} %shard_map.150.h0, bf16[256,320]{1,0:T(8,128)(2,1)} %copy-done.18, bf16[256,320]{1,0:T(8,128)(2,1)} %copy-done.19, ...), custom_call_target="tpu_custom_call" | custom-call | flops 1340000000 | bytes 8388608 | tf_op jit(solution)/shard_map/pallas_call | solution.py:189
  132.8 2.7 %collective-permute-start.17 = (bf16[256,512]{1,0:T(8,128)(2,1)}, bf16[256,512]{1,0:T(8,128)(2,1)S(1)}, u32[]{:S(2)}, u32[]{:S(2)}) collective-permute-start(bf16[256,512]{1,0:T(8,128)(2,1)} %get-tuple-element.53), channel_id=1, source_target_pairs={{0,8},{1,9},{2,10},{3,11},{4,12},{5,13},{6,14},{7,15},{8,0},{9,1},... | collective-permute-start | bytes 786440 | tf_op jit(solution)/shard_map/ppermute | solution.py:60
  135.5 2.0 collective-permute-start.18
  141.0 2.8 %collective-permute-done.18 = bf16[256,512]{1,0:T(8,128)(2,1)S(1)} collective-permute-done((bf16[256,512]{1,0:T(8,128)(2,1)}, bf16[256,512]{1,0:T(8,128)(2,1)S(1)}, u32[]{:S(2)}, u32[]{:S(2)}) %collective-permute-start.18) | collective-permute-done | bytes 262176 | tf_op jit(solution)/shard_map/ppermute | solution.py:60
  146.1 3.2 %collective-permute-start.21 = (bf16[256,512]{1,0:T(8,128)(2,1)S(1)}, bf16[256,512]{1,0:T(8,128)(2,1)S(1)}, u32[]{:S(2)}, u32[]{:S(2)}) collective-permute-start(bf16[256,512]{1,0:T(8,128)(2,1)S(1)} %add_convert_fusion.1.v0), channel_id=1, source_target_pairs={{0,3},{1,0},{2,1},{3,2},{4,7},{5,4},{6,5},{7,6},{8,11},{9,8},{10,9... | collective-permute-start | bytes 786440 | tf_op jit(solution)/shard_map/ppermute | solution.py:52
  149.5 17.1 %collective-permute-done.20.v1 = bf16[256,512]{1,0:T(8,128)(2,1)S(1)} collective-permute-done((bf16[256,512]{1,0:T(8,128)(2,1)S(1)}, bf16[256,512]{1,0:T(8,128)(2,1)S(1)}, u32[]{:S(2)}, u32[]{:S(2)}) %collective-permute-start.20) | collective-permute-done | bytes 262176 | tf_op jit(solution)/shard_map/ppermute | solution.py:52
  168.2 3.1 %collective-permute-start.24 = (bf16[128,2048]{1,0:T(8,128)(2,1)S(1)}, bf16[128,2048]{1,0:T(8,128)(2,1)S(1)}, u32[]{:S(2)}, u32[]{:S(2)}) collective-permute-start(bf16[128,2048]{1,0:T(8,128)(2,1)S(1)} %get-tuple-element.58.e1), channel_id=1, source_target_pairs={{0,12},{1,13},{2,14},{3,15},{4,0},{5,1},{6,2},{7,3},{8,4},{9,5},{1... | collective-permute-start | bytes 1572872 | tf_op jit(solution)/shard_map/ppermute | solution.py:52
  174.1 7.0 %shard_map.155 = (f32[128,2048]{1,0:T(8,128)S(1)}, bf16[128,2048]{1,0:T(8,128)(2,1)S(1)}, bf16[128,2048]{1,0:T(8,128)(2,1)S(1)}, bf16[128,2048]{1,0:T(8,128)(2,1)S(1)}) custom-call(s32[16]{0:T(128)S(1)} %copy-done.4, bf16[128,2048]{1,0:T(8,128)(2,1)S(1)} %get-tuple-element.56.e0, bf16[128,2048]{1,0:T(8,128)(2,1)S(1)} %get-tuple-element.58.e1, ...), custom_call_target="tpu_custom_call" | custom-call | flops 4300000256 | bytes 14680064 | tf_op jit(solution)/shard_map/pallas_call | solution.py:254
  181.1 3.8 %collective-permute-start.26 = (bf16[128,2048]{1,0:T(8,128)(2,1)S(1)}, bf16[128,2048]{1,0:T(8,128)(2,1)S(1)}, u32[]{:S(2)}, u32[]{:S(2)}) collective-permute-start(bf16[128,2048]{1,0:T(8,128)(2,1)S(1)} %get-tuple-element.62), channel_id=1, source_target_pairs={{0,8},{1,9},{2,10},{3,11},{4,12},{5,13},{6,14},{7,15},{8,0},{9,1},... | collective-permute-start | bytes 1572872 | tf_op jit(solution)/shard_map/ppermute | solution.py:52
  185.0 3.2 %collective-permute-start.28 = (bf16[128,2048]{1,0:T(8,128)(2,1)S(1)}, bf16[128,2048]{1,0:T(8,128)(2,1)S(1)}, u32[]{:S(2)}, u32[]{:S(2)}) collective-permute-start(bf16[128,2048]{1,0:T(8,128)(2,1)S(1)} %get-tuple-element.64), channel_id=1, source_target_pairs={{0,12},{1,13},{2,14},{3,15},{4,0},{5,1},{6,2},{7,3},{8,4},{9,5},{1... | collective-permute-start | bytes 1572872 | tf_op jit(solution)/shard_map/ppermute | solution.py:52
  188.2 2.0 shard_map.154
  190.3 1.9 collective-permute-done.26
  192.2 5.5 %collective-permute-done.27 = bf16[128,2048]{1,0:T(8,128)(2,1)S(1)} collective-permute-done((bf16[128,2048]{1,0:T(8,128)(2,1)S(1)}, bf16[128,2048]{1,0:T(8,128)(2,1)S(1)}, u32[]{:S(2)}, u32[]{:S(2)}) %collective-permute-start.27) | collective-permute-done | bytes 524320 | tf_op jit(solution)/shard_map/ppermute | solution.py:52
  (102 shorter events, 27.0 us)
Async XLA Ops:
  7.2 49.5 %copy-start.21 = (f32[5120]{0:T(1024)S(1)}, f32[5120]{0:T(1024)}, u32[]{:S(2)}) copy-start(f32[5120]{0:T(1024)} %param.20) | copy-start | bytes 61444
  7.2 51.5 %all-gather.3.cloned.1.call-start = ((), (), s32[]{:S(2)}) async-start(), calls=%async_computation | async-start | bytes 4177920 | tf_op jit(solution)/shard_map/all_gather | solution.py:311
  7.9 118.9 %all-gather.5.cloned.1.call-start = ((), (), s32[]{:S(2)}) async-start(), calls=%async_computation.1 | async-start | bytes 5570560 | tf_op jit(solution)/shard_map/all_gather | solution.py:318
  10.5 10.0 %collective-permute-start = (bf16[16,5120]{1,0:T(8,128)(2,1)S(1)}, bf16[16,5120]{1,0:T(8,128)(2,1)S(1)}, u32[]{:S(2)}, u32[]{:S(2)}) collective-permute-start(bf16[16,5120]{1,0:T(8,128)(2,1)S(1)} %shard_map.149), channel_id=1, source_target_pairs={{0,1},{1,2},{2,3},{3,0},{4,5},{5,6},{6,7},{7,4},{8,9},{9,10},{10,1... | collective-permute-start | bytes 491528 | tf_op jit(solution)/shard_map/ppermute | solution.py:52
  12.1 8.5 %collective-permute-start.1 = (bf16[16,5120]{1,0:T(8,128)(2,1)S(1)}, bf16[16,5120]{1,0:T(8,128)(2,1)S(1)}, u32[]{:S(2)}, u32[]{:S(2)}) collective-permute-start(bf16[16,5120]{1,0:T(8,128)(2,1)S(1)} %shard_map.149), channel_id=1, source_target_pairs={{0,3},{1,0},{2,1},{3,2},{4,7},{5,4},{6,5},{7,6},{8,11},{9,8},{10,9... | collective-permute-start | bytes 491528 | tf_op jit(solution)/shard_map/ppermute | solution.py:52
  13.9 6.8 %collective-permute-start.2 = (bf16[16,5120]{1,0:T(8,128)(2,1)S(1)}, bf16[16,5120]{1,0:T(8,128)(2,1)S(1)}, u32[]{:S(2)}, u32[]{:S(2)}) collective-permute-start(bf16[16,5120]{1,0:T(8,128)(2,1)S(1)} %shard_map.149), channel_id=1, source_target_pairs={{0,2},{1,3},{2,0},{3,1},{4,6},{5,7},{6,4},{7,5},{8,10},{9,11},{10,... | collective-permute-start | bytes 491528 | tf_op jit(solution)/shard_map/ppermute | solution.py:52
  15.7 16.4 %collective-permute-start.3 = (bf16[320,512]{1,0:T(8,128)(2,1)}, bf16[320,512]{1,0:T(8,128)(2,1)S(1)}, u32[]{:S(2)}, u32[]{:S(2)}) collective-permute-start(bf16[320,512]{1,0:T(8,128)(2,1)} %param.21), channel_id=1, source_target_pairs={{0,0},{1,16},{2,32},{3,48},{4,4},{5,20},{6,36},{7,52},{8,8},{9,24}... | collective-permute-start | bytes 983048 | tf_op jit(solution)/shard_map/ppermute | solution.py:312
  32.1 12.0 %collective-permute-start.4 = (bf16[64,5120]{1,0:T(8,128)(2,1)S(1)}, bf16[64,5120]{1,0:T(8,128)(2,1)S(1)}, u32[]{:S(2)}, u32[]{:S(2)}) collective-permute-start(bf16[64,5120]{1,0:T(8,128)(2,1)S(1)} %pad_maximum_fusion.s0), channel_id=1, source_target_pairs={{0,4},{1,5},{2,6},{3,7},{4,8},{5,9},{6,10},{7,11},{8,12},{9,13},{1... | collective-permute-start | bytes 1966088 | tf_op jit(solution)/shard_map/ppermute | solution.py:52
  33.8 10.6 %collective-permute-start.5 = (bf16[64,5120]{1,0:T(8,128)(2,1)S(1)}, bf16[64,5120]{1,0:T(8,128)(2,1)S(1)}, u32[]{:S(2)}, u32[]{:S(2)}) collective-permute-start(bf16[64,5120]{1,0:T(8,128)(2,1)S(1)} %pad_maximum_fusion.s0), channel_id=1, source_target_pairs={{0,12},{1,13},{2,14},{3,15},{4,0},{5,1},{6,2},{7,3},{8,4},{9,5},{1... | collective-permute-start | bytes 1966088 | tf_op jit(solution)/shard_map/ppermute | solution.py:52
  35.5 17.0 %collective-permute-start.6 = (bf16[64,5120]{1,0:T(8,128)(2,1)S(1)}, bf16[64,5120]{1,0:T(8,128)(2,1)S(1)}, u32[]{:S(2)}, u32[]{:S(2)}) collective-permute-start(bf16[64,5120]{1,0:T(8,128)(2,1)S(1)} %pad_maximum_fusion.s0), channel_id=1, source_target_pairs={{0,8},{1,9},{2,10},{3,11},{4,12},{5,13},{6,14},{7,15},{8,0},{9,1},... | collective-permute-start | bytes 1966088 | tf_op jit(solution)/shard_map/ppermute | solution.py:52
  53.4 35.3 %collective-permute-start.10 = (bf16[512,2048]{1,0:T(8,128)(2,1)}, bf16[512,2048]{1,0:T(8,128)(2,1)S(1)}, u32[]{:S(2)}, u32[]{:S(2)}) collective-permute-start(bf16[512,2048]{1,0:T(8,128)(2,1)} %w0), channel_id=1, source_target_pairs={{0,1},{1,2},{2,3},{3,0},{4,5},{5,6},{6,7},{7,4},{8,9},{9,10},{10,1... | collective-permute-start | bytes 6291464 | tf_op jit(solution)/shard_map/ppermute | solution.py:52
  53.5 35.3 %collective-permute-start.11 = (bf16[512,2048]{1,0:T(8,128)(2,1)}, bf16[512,2048]{1,0:T(8,128)(2,1)}, u32[]{:S(2)}, u32[]{:S(2)}) collective-permute-start(bf16[512,2048]{1,0:T(8,128)(2,1)} %w0), channel_id=1, source_target_pairs={{0,3},{1,0},{2,1},{3,2},{4,7},{5,4},{6,5},{7,6},{8,11},{9,8},{10,9... | collective-permute-start | bytes 6291464 | tf_op jit(solution)/shard_map/ppermute | solution.py:52
  64.4 34.0 %collective-permute-start.7 = (bf16[256,320]{1,0:T(8,128)(2,1)}, bf16[256,320]{1,0:T(8,128)(2,1)S(1)}, u32[]{:S(2)}, u32[]{:S(2)}) collective-permute-start(bf16[256,320]{1,0:T(8,128)(2,1)} %shard_map.150.h0), channel_id=1, source_target_pairs={{0,1},{1,2},{2,3},{3,0},{4,5},{5,6},{6,7},{7,4},{8,9},{9,10},{10,1... | collective-permute-start | bytes 491528 | tf_op jit(solution)/shard_map/ppermute | solution.py:60
  64.5 34.0 %collective-permute-start.8 = (bf16[256,320]{1,0:T(8,128)(2,1)}, bf16[256,320]{1,0:T(8,128)(2,1)S(1)}, u32[]{:S(2)}, u32[]{:S(2)}) collective-permute-start(bf16[256,320]{1,0:T(8,128)(2,1)} %shard_map.150.h0), channel_id=1, source_target_pairs={{0,3},{1,0},{2,1},{3,2},{4,7},{5,4},{6,5},{7,6},{8,11},{9,8},{10,9... | collective-permute-start | bytes 491528 | tf_op jit(solution)/shard_map/ppermute | solution.py:60
  67.8 30.7 %collective-permute-start.9 = (bf16[256,320]{1,0:T(8,128)(2,1)}, bf16[256,320]{1,0:T(8,128)(2,1)S(1)}, u32[]{:S(2)}, u32[]{:S(2)}) collective-permute-start(bf16[256,320]{1,0:T(8,128)(2,1)} %shard_map.150.h0), channel_id=1, source_target_pairs={{0,2},{1,3},{2,0},{3,1},{4,6},{5,7},{6,4},{7,5},{8,10},{9,11},{10,... | collective-permute-start | bytes 491528 | tf_op jit(solution)/shard_map/ppermute | solution.py:60
  98.5 26.3 %collective-permute-start.12 = (bf16[256,2048]{1,0:T(8,128)(2,1)S(1)}, bf16[256,2048]{1,0:T(8,128)(2,1)S(1)}, u32[]{:S(2)}, u32[]{:S(2)}) collective-permute-start(bf16[256,2048]{1,0:T(8,128)(2,1)S(1)} %slice.12), channel_id=1, source_target_pairs={{0,1},{1,2},{2,3},{3,0},{4,5},{5,6},{6,7},{7,4},{8,9},{9,10},{10,1... | collective-permute-start | bytes 3145736 | tf_op jit(solution)/shard_map/ppermute | solution.py:52
  98.6 27.2 %collective-permute-start.13 = (bf16[256,2048]{1,0:T(8,128)(2,1)S(1)}, bf16[256,2048]{1,0:T(8,128)(2,1)S(1)}, u32[]{:S(2)}, u32[]{:S(2)}) collective-permute-start(bf16[256,2048]{1,0:T(8,128)(2,1)S(1)} %slice.13), channel_id=1, source_target_pairs={{0,3},{1,0},{2,1},{3,2},{4,7},{5,4},{6,5},{7,6},{8,11},{9,8},{10,9... | collective-permute-start | bytes 3145736 | tf_op jit(solution)/shard_map/ppermute | solution.py:52
  101.8 11.8 %collective-permute-start.14 = (bf16[128,2048]{1,0:T(8,128)(2,1)S(1)}, bf16[128,2048]{1,0:T(8,128)(2,1)S(1)}, u32[]{:S(2)}, u32[]{:S(2)}) collective-permute-start(bf16[128,2048]{1,0:T(8,128)(2,1)S(1)} %get-tuple-element.48), channel_id=1, source_target_pairs={{0,4},{1,5},{2,6},{3,7},{4,8},{5,9},{6,10},{7,11},{8,12},{9,13},{1... | collective-permute-start | bytes 1572872 | tf_op jit(solution)/shard_map/ppermute | solution.py:52
  105.4 11.5 %collective-permute-start.15 = (bf16[128,2048]{1,0:T(8,128)(2,1)S(1)}, bf16[128,2048]{1,0:T(8,128)(2,1)S(1)}, u32[]{:S(2)}, u32[]{:S(2)}) collective-permute-start(bf16[128,2048]{1,0:T(8,128)(2,1)S(1)} %get-tuple-element.49), channel_id=1, source_target_pairs={{0,12},{1,13},{2,14},{3,15},{4,0},{5,1},{6,2},{7,3},{8,4},{9,5},{1... | collective-permute-start | bytes 1572872 | tf_op jit(solution)/shard_map/ppermute | solution.py:52
  105.4 19.4 %collective-permute-start.16 = (bf16[128,2048]{1,0:T(8,128)(2,1)S(1)}, bf16[128,2048]{1,0:T(8,128)(2,1)S(1)}, u32[]{:S(2)}, u32[]{:S(2)}) collective-permute-start(bf16[128,2048]{1,0:T(8,128)(2,1)S(1)} %get-tuple-element.50), channel_id=1, source_target_pairs={{0,8},{1,9},{2,10},{3,11},{4,12},{5,13},{6,14},{7,15},{8,0},{9,1},... | collective-permute-start | bytes 1572872 | tf_op jit(solution)/shard_map/ppermute | solution.py:52
  132.8 8.2 %collective-permute-start.17 = (bf16[256,512]{1,0:T(8,128)(2,1)}, bf16[256,512]{1,0:T(8,128)(2,1)S(1)}, u32[]{:S(2)}, u32[]{:S(2)}) collective-permute-start(bf16[256,512]{1,0:T(8,128)(2,1)} %get-tuple-element.53), channel_id=1, source_target_pairs={{0,8},{1,9},{2,10},{3,11},{4,12},{5,13},{6,14},{7,15},{8,0},{9,1},... | collective-permute-start | bytes 786440 | tf_op jit(solution)/shard_map/ppermute | solution.py:60
  135.5 8.3 %collective-permute-start.18 = (bf16[256,512]{1,0:T(8,128)(2,1)}, bf16[256,512]{1,0:T(8,128)(2,1)S(1)}, u32[]{:S(2)}, u32[]{:S(2)}) collective-permute-start(bf16[256,512]{1,0:T(8,128)(2,1)} %get-tuple-element.54), channel_id=1, source_target_pairs={{0,4},{1,5},{2,6},{3,7},{4,8},{5,9},{6,10},{7,11},{8,12},{9,13},{1... | collective-permute-start | bytes 786440 | tf_op jit(solution)/shard_map/ppermute | solution.py:60
  137.4 7.4 %collective-permute-start.19 = (bf16[256,512]{1,0:T(8,128)(2,1)}, bf16[256,512]{1,0:T(8,128)(2,1)S(1)}, u32[]{:S(2)}, u32[]{:S(2)}) collective-permute-start(bf16[256,512]{1,0:T(8,128)(2,1)} %get-tuple-element.55), channel_id=1, source_target_pairs={{0,12},{1,13},{2,14},{3,15},{4,0},{5,1},{6,2},{7,3},{8,4},{9,5},{1... | collective-permute-start | bytes 786440 | tf_op jit(solution)/shard_map/ppermute | solution.py:60
  146.0 20.7 %collective-permute-start.20 = (bf16[256,512]{1,0:T(8,128)(2,1)S(1)}, bf16[256,512]{1,0:T(8,128)(2,1)S(1)}, u32[]{:S(2)}, u32[]{:S(2)}) collective-permute-start(bf16[256,512]{1,0:T(8,128)(2,1)S(1)} %add_convert_fusion.1.v0), channel_id=1, source_target_pairs={{0,1},{1,2},{2,3},{3,0},{4,5},{5,6},{6,7},{7,4},{8,9},{9,10},{10,1... | collective-permute-start | bytes 786440 | tf_op jit(solution)/shard_map/ppermute | solution.py:52
  146.1 20.6 %collective-permute-start.21 = (bf16[256,512]{1,0:T(8,128)(2,1)S(1)}, bf16[256,512]{1,0:T(8,128)(2,1)S(1)}, u32[]{:S(2)}, u32[]{:S(2)}) collective-permute-start(bf16[256,512]{1,0:T(8,128)(2,1)S(1)} %add_convert_fusion.1.v0), channel_id=1, source_target_pairs={{0,3},{1,0},{2,1},{3,2},{4,7},{5,4},{6,5},{7,6},{8,11},{9,8},{10,9... | collective-permute-start | bytes 786440 | tf_op jit(solution)/shard_map/ppermute | solution.py:52
  149.3 17.4 %collective-permute-start.22 = (bf16[256,512]{1,0:T(8,128)(2,1)S(1)}, bf16[256,512]{1,0:T(8,128)(2,1)S(1)}, u32[]{:S(2)}, u32[]{:S(2)}) collective-permute-start(bf16[256,512]{1,0:T(8,128)(2,1)S(1)} %add_convert_fusion.1.v0), channel_id=1, source_target_pairs={{0,2},{1,3},{2,0},{3,1},{4,6},{5,7},{6,4},{7,5},{8,10},{9,11},{10,... | collective-permute-start | bytes 786440 | tf_op jit(solution)/shard_map/ppermute | solution.py:52
  168.0 17.0 %collective-permute-start.23 = (bf16[128,2048]{1,0:T(8,128)(2,1)S(1)}, bf16[128,2048]{1,0:T(8,128)(2,1)S(1)}, u32[]{:S(2)}, u32[]{:S(2)}) collective-permute-start(bf16[128,2048]{1,0:T(8,128)(2,1)S(1)} %get-tuple-element.57.e2), channel_id=1, source_target_pairs={{0,4},{1,5},{2,6},{3,7},{4,8},{5,9},{6,10},{7,11},{8,12},{9,13},{1... | collective-permute-start | bytes 1572872 | tf_op jit(solution)/shard_map/ppermute | solution.py:52
  168.2 20.0 %collective-permute-start.24 = (bf16[128,2048]{1,0:T(8,128)(2,1)S(1)}, bf16[128,2048]{1,0:T(8,128)(2,1)S(1)}, u32[]{:S(2)}, u32[]{:S(2)}) collective-permute-start(bf16[128,2048]{1,0:T(8,128)(2,1)S(1)} %get-tuple-element.58.e1), channel_id=1, source_target_pairs={{0,12},{1,13},{2,14},{3,15},{4,0},{5,1},{6,2},{7,3},{8,4},{9,5},{1... | collective-permute-start | bytes 1572872 | tf_op jit(solution)/shard_map/ppermute | solution.py:52
  171.3 16.9 %collective-permute-start.25 = (bf16[128,2048]{1,0:T(8,128)(2,1)S(1)}, bf16[128,2048]{1,0:T(8,128)(2,1)S(1)}, u32[]{:S(2)}, u32[]{:S(2)}) collective-permute-start(bf16[128,2048]{1,0:T(8,128)(2,1)S(1)} %get-tuple-element.59.e3), channel_id=1, source_target_pairs={{0,8},{1,9},{2,10},{3,11},{4,12},{5,13},{6,14},{7,15},{8,0},{9,1},... | collective-permute-start | bytes 1572872 | tf_op jit(solution)/shard_map/ppermute | solution.py:52
  181.1 11.1 %collective-permute-start.26 = (bf16[128,2048]{1,0:T(8,128)(2,1)S(1)}, bf16[128,2048]{1,0:T(8,128)(2,1)S(1)}, u32[]{:S(2)}, u32[]{:S(2)}) collective-permute-start(bf16[128,2048]{1,0:T(8,128)(2,1)S(1)} %get-tuple-element.62), channel_id=1, source_target_pairs={{0,8},{1,9},{2,10},{3,11},{4,12},{5,13},{6,14},{7,15},{8,0},{9,1},... | collective-permute-start | bytes 1572872 | tf_op jit(solution)/shard_map/ppermute | solution.py:52
  185.0 12.8 %collective-permute-start.27 = (bf16[128,2048]{1,0:T(8,128)(2,1)S(1)}, bf16[128,2048]{1,0:T(8,128)(2,1)S(1)}, u32[]{:S(2)}, u32[]{:S(2)}) collective-permute-start(bf16[128,2048]{1,0:T(8,128)(2,1)S(1)} %get-tuple-element.63), channel_id=1, source_target_pairs={{0,4},{1,5},{2,6},{3,7},{4,8},{5,9},{6,10},{7,11},{8,12},{9,13},{1... | collective-permute-start | bytes 1572872 | tf_op jit(solution)/shard_map/ppermute | solution.py:52
  185.0 12.8 %collective-permute-start.28 = (bf16[128,2048]{1,0:T(8,128)(2,1)S(1)}, bf16[128,2048]{1,0:T(8,128)(2,1)S(1)}, u32[]{:S(2)}, u32[]{:S(2)}) collective-permute-start(bf16[128,2048]{1,0:T(8,128)(2,1)S(1)} %get-tuple-element.64), channel_id=1, source_target_pairs={{0,12},{1,13},{2,14},{3,15},{4,0},{5,1},{6,2},{7,3},{8,4},{9,5},{1... | collective-permute-start | bytes 1572872 | tf_op jit(solution)/shard_map/ppermute | solution.py:52
  (24 other events, 316.2 us)
Sparse Core Ops, SparseCore 0:
  9.8 45.4 all-gather.2
  57.7 43.0 all-gather.4

commit v12 on v7

--- a/solution.py
+++ b/solution.py
@@ -53,7 +53,8 @@
 
 
 def around(value, which):
-    return hop(value, which, 1), hop(value, which, -1), hop(value, which, 2)
+    far = hop(value, which, 2)
+    return hop(value, which, 1), hop(value, which, -1), far
 
 
 def line(value, axis, step):
@@ -172,13 +173,11 @@
         for j in range(4):
             slot = nat[j * 4] // 4 * 4 + nat[k] % 4
             source = weight.at[pl.ds(pl.multiple_of(slot * 320, 320), 320)]
-            copies.append((source, held.at[k, :, pl.ds(j * 512, 512)]))
-    copies = start(copies, sems)
-    total = 0.0
-    for k in range(4):
-        for copy in copies[k * 5 : k * 5 + 5]:
-            copy.wait()
-        total = total + jnp.dot(units[k], held[k], preferred_element_type=F32)
+            copies.append((source, held.at[pl.ds(k * 320, 320), pl.ds(j * 512, 512)]))
+    for copy in start(copies, sems):
+        copy.wait()
+    rows = jnp.concatenate([units[k] for k in range(4)], axis=1)
+    total = jnp.dot(rows, held[...], preferred_element_type=F32)
     own[...] = total[:, 0:512]
     left[...] = total[:, 512:1024].astype(BF16)
     right[...] = total[:, 1024:1536].astype(BF16)
@@ -193,7 +192,7 @@
         out_specs=[VMEM] * 4,
         scratch_shapes=[
             pltpu.VMEM((4, 256, 320), BF16),
-            pltpu.VMEM((4, 320, 2048), BF16),
+            pltpu.VMEM((1280, 2048), BF16),
             pltpu.SemaphoreType.DMA((20,)),
         ],
         compiler_params=params(56),
@@ -227,37 +226,47 @@
     )(tab, dest, *visual, *text)
 
 
-def product_kernel(tab, e0, e1, e2, e3, gain, w0, w1, w2, w3a, w3b, own, left, right, far, scaled):
-    @pl.when(pl.program_id(0) == 0)
-    def _():
-        for j in range(4):
-            at = slice(j * 512, (j + 1) * 512)
-            scale = gain[tab[j]]
-            for i2, rows in enumerate((e0, e1, e2, e3)):
-                scaled[i2 * 128 : (i2 + 1) * 128, at] = (rows[:, at].astype(F32) * scale).astype(BF16)
-
-    total = jnp.dot(scaled[:, 0:512], w0[...], preferred_element_type=F32)
-    total = total + jnp.dot(scaled[:, 512:1024], w1[...], preferred_element_type=F32)
-    total = total + jnp.dot(scaled[:, 1024:1536], w2[...], preferred_element_type=F32)
-    total = total + jnp.dot(scaled[:, 1536:1792], w3a[...], preferred_element_type=F32)
-    total = total + jnp.dot(scaled[:, 1792:2048], w3b[...], preferred_element_type=F32)
-    own[...] = total[0:128]
-    left[...] = total[128:256].astype(BF16)
-    right[...] = total[256:384].astype(BF16)
-    far[...] = total[384:512].astype(BF16)
+def product_kernel(tab, e0, e1, e2, e3, gain, *refs):
+    weights, outs, (scaled, held, sems) = refs[:5], refs[5:9], refs[9:]
+
+    def fetch(n):
+        copies, row = [], 0
+        for i, weight in enumerate(weights):
+            count = weight.shape[0]
+            source = weight.at[:, pl.ds(n * 512, 512)]
+            copies.append(pltpu.make_async_copy(source, held.at[n % 2, pl.ds(row, count)], sems.at[n % 2, i]))
+            row += count
+        for copy in copies:
+            copy.start()
+        return copies
+
+    copies = fetch(0)
+    for j in range(4):
+        at = slice(j * 512, (j + 1) * 512)
+        scale = gain[tab[j]]
+        for i2, rows in enumerate((e0, e1, e2, e3)):
+            scaled[i2 * 128 : (i2 + 1) * 128, at] = (rows[:, at].astype(F32) * scale).astype(BF16)
+    for n in range(4):
+        later = fetch(n + 1) if n < 3 else []
+        for copy in copies:
+            copy.wait()
+        copies = later
+        total = jnp.dot(scaled[...], held[n % 2], preferred_element_type=F32)
+        for i2, out in enumerate(outs):
+            out[:, n * 512 : (n + 1) * 512] = total[i2 * 128 : (i2 + 1) * 128].astype(out.dtype)
 
 
 def product(tab, picked, gain, weights):
-    def block(count):
-        return pl.BlockSpec((count, 512), lambda n: (0, n))
-
     return pl.pallas_call(
         product_kernel,
         out_shape=[jax.ShapeDtypeStruct((128, 2048), F32)] + [jax.ShapeDtypeStruct((128, 2048), BF16)] * 3,
-        grid=(4,),
-        in_specs=[SMEM] + [VMEM] * 5 + [block(n) for n in (512, 512, 512, 256, 256)],
-        out_specs=[block(128)] * 4,
-        scratch_shapes=[pltpu.VMEM((512, 2048), BF16)],
+        in_specs=[SMEM] + [VMEM] * 5 + [ANY] * 5,
+        out_specs=[VMEM] * 4,
+        scratch_shapes=[
+            pltpu.VMEM((512, 2048), BF16),
+            pltpu.VMEM((2, 2048, 512), BF16),
+            pltpu.SemaphoreType.DMA((2, 5)),
+        ],
         compiler_params=params(56),
         cost_estimate=cost(4300 * 10**6, 14 * MIB),
     )(tab, *picked, gain, *weights)
@@ -321,12 +330,14 @@
     far_right, far_left = kv_right[:256], kv_left[256:]
     own, to_left, to_right, to_far = pack(tab, text_embed[0, 0])
     hidden = up(tab, group, up_full, up_bias.reshape(16, 1, 320))
-    units = (hidden, line(hidden, "x", 1), line(hidden, "x", -1), line(hidden, "x", 2))
+    far = line(hidden, "x", 2)
+    units = (hidden, line(hidden, "x", 1), line(hidden, "x", -1), far)
     moved = (*units, far_right, far_left, to_left, to_right, to_far)
     *units, far_right, far_left, to_left, to_right, to_far = lax.optimization_barrier(moved)
 
     weights = (kv_weight, kv_right, kv_left, hop(far_right, 1, 1), hop(far_left, 1, -1))
-    text = (own, hop(to_right, 2, 1), hop(to_left, 2, -1), hop(to_far, 2, 2))
+    far = hop(to_far, 2, 2)
+    text = (own, hop(to_right, 2, 1), hop(to_left, 2, -1), far)
     down_full = after(down_full, weights[3], weights[4], *text)
     own, to_left, to_right, to_far = down(nat, units, down_full)
     bias = lax.dynamic_slice_in_dim(down_bias, lax.axis_index("tp") * 512, 512, 0)
@@ -340,7 +351,8 @@
     live = (jnp.arange(SLOT, dtype=jnp.int32)[None, :] < live_rows[:, None]).reshape(-1)
     dest = jnp.where(live, dest_pos[0, 0], -1)[None]
     picked = pick(tab, dest, visual, text)
-    pieces = (picked[0], hop(picked[2], 2, 1), hop(picked[1], 2, -1), hop(picked[3], 2, 2))
+    far = hop(picked[3], 2, 2)
+    pieces = (picked[0], hop(picked[2], 2, 1), hop(picked[1], 2, -1), far)
     own, to_left, to_right, to_far = product(tab, picked, norm_gain.reshape(16, 1, 512), weights)
     sums = (hop(to_far, 2, 2), hop(to_right, 2, 1), hop(to_left, 2, -1))
     embedded, scale = place_rows(tab, pieces)

time: 188 us -> 188 us (level)
  transfers between devices with their start and end apart: 31 -> 31, of which waited for: 19 -> 20; matrix products, arithmetic and copies ran while one was open for 3% -> 3% of each run, Pallas kernels for 10% -> 10%
where the time goes in v12:
time: 188 us; the launch traced here: 187 us
  waiting for transfers between devices  80.5 us (43%)
  starting transfers between devices  53.7 us (29%)
  Pallas kernels  26.1 us (14%)
  between operations  14.4 us (8%)
  local copies, waits for them, and re-layouts  10.4 us (6%)
  other arithmetic  2.49 us (1%)
    ppermute x22, waiting for transfers between devices, hop(): return lax.ppermute(value, ('mb', 'tp'), HOPS[which, step])  50.3 us
    ppermute x22, starting transfers between devices, hop(): return lax.ppermute(value, ('mb', 'tp'), HOPS[which, step])  39.1 us
    ppermute x1, waiting for transfers between devices, per_device(): down_part = lax.ppermute(down_weight, ('enc', 'mb', 'tp'), SHUFFLE)  17.3 us
    ppermute x6, waiting for transfers between devices, line(): return lax.ppermute(value, ('mb', 'tp'), LINES[axis, step])  11.3 us
    ppermute x6, starting transfers between devices, line(): return lax.ppermute(value, ('mb', 'tp'), LINES[axis, step])  10.3 us
    pallas_call x1, Pallas kernels, product(): pl.pallas_call(product_kernel, out_shape=[jax.ShapeDtypeStruct((128, 2048...  9.65 us
    pallas_call x1, Pallas kernels, down(): pl.pallas_call(down_kernel, out_shape=[jax.ShapeDtypeStruct((256, 512), F...  5.94 us
    pallas_call x1, Pallas kernels, up(): pl.pallas_call(up_kernel, out_shape=jax.ShapeDtypeStruct((256, 320), BF16...  5.68 us
  transfers between devices with their start and end apart: 31, of which 20 were waited for; matrix products, arithmetic and copies ran while one was open for 3% of the time, Pallas kernels for 10%

profile of v12, /device:TPU:224, one launch (start us, length us, event | category | flops | bytes accessed | tf_op | source)
XLA Modules:
  0.0 187.5 jit_solution(2759245753201006841)
XLA Ops:
  12.1 1.7 collective-permute-start.1
  13.9 1.8 collective-permute-start.2
  17.4 3.2 %collective-permute-done.2 = bf16[16,5120]{1,0:T(8,128)(2,1)S(1)} collective-permute-done((bf16[16,5120]{1,0:T(8,128)(2,1)S(1)}, bf16[16,5120]{1,0:T(8,128)(2,1)S(1)}, u32[]{:S(2)}, u32[]{:S(2)}) %collective-permute-start.2) | collective-permute-done | bytes 163872 | tf_op jit(solution)/shard_map/ppermute | solution.py:52
  22.4 1.7 collective-permute-start.4
  24.1 2.0 %collective-permute-start.5 = (bf16[64,5120]{1,0:T(8,128)(2,1)S(1)}, bf16[64,5120]{1,0:T(8,128)(2,1)S(1)}, u32[]{:S(2)}, u32[]{:S(2)}) collective-permute-start(bf16[64,5120]{1,0:T(8,128)(2,1)S(1)} %pad_maximum_fusion.s0), channel_id=1, source_target_pairs={{0,8},{1,9},{2,10},{3,11},{4,12},{5,13},{6,14},{7,15},{8,0},{9,1},... | collective-permute-start | bytes 1966088 | tf_op jit(solution)/shard_map/ppermute | solution.py:52
  26.0 4.2 %collective-permute-start.11 = (bf16[320,512]{1,0:T(8,128)(2,1)}, bf16[320,512]{1,0:T(8,128)(2,1)S(1)}, u32[]{:S(2)}, u32[]{:S(2)}) collective-permute-start(bf16[320,512]{1,0:T(8,128)(2,1)} %param.21), channel_id=1, source_target_pairs={{0,0},{1,16},{2,32},{3,48},{4,4},{5,20},{6,36},{7,52},{8,8},{9,24}... | collective-permute-start | bytes 983048 | tf_op jit(solution)/shard_map/ppermute | solution.py:321
  30.2 17.3 %collective-permute-done.11 = bf16[320,512]{1,0:T(8,128)(2,1)S(1)} collective-permute-done((bf16[320,512]{1,0:T(8,128)(2,1)}, bf16[320,512]{1,0:T(8,128)(2,1)S(1)}, u32[]{:S(2)}, u32[]{:S(2)}) %collective-permute-start.11) | collective-permute-done | bytes 327712 | tf_op jit(solution)/shard_map/ppermute | solution.py:321
  48.3 3.2 %collective-permute-start.10 = (bf16[512,2048]{1,0:T(8,128)(2,1)}, bf16[512,2048]{1,0:T(8,128)(2,1)}, u32[]{:S(2)}, u32[]{:S(2)}) collective-permute-start(bf16[512,2048]{1,0:T(8,128)(2,1)} %refs_0_), channel_id=1, source_target_pairs={{0,3},{1,0},{2,1},{3,2},{4,7},{5,4},{6,5},{7,6},{8,11},{9,8},{10,9... | collective-permute-start | bytes 6291464 | tf_op jit(solution)/shard_map/ppermute | solution.py:52
  54.5 5.7 %shard_map.150.h0 = bf16[256,320]{1,0:T(8,128)(2,1)} custom-call(s32[16]{0:T(128)} %get-tuple-element.63.tab, bf16[64,5120]{1,0:T(8,128)(2,1)} %copy-done.11, bf16[64,5120]{1,0:T(8,128)(2,1)} %copy-done.13, bf16[64,5120]{1,0:T(8,128)(2,1)} %copy-done.14, bf16[64,5120]{1,0:T(8,128)(2,1)} %copy-done.15, bf16[5120,320]{1,0:T(8,128)(2,1)} %all-gather.3.cloned.1.call-done.weight, ...), custom_call_target="tpu_custom_call" | custom-call | flops 840000000 | bytes 6291456 | tf_op jit(solution)/shard_map/pallas_call | solution.py:154
  60.6 2.9 %collective-permute-start.7 = (bf16[256,320]{1,0:T(8,128)(2,1)}, bf16[256,320]{1,0:T(8,128)(2,1)S(1)}, u32[]{:S(2)}, u32[]{:S(2)}) collective-permute-start(bf16[256,320]{1,0:T(8,128)(2,1)} %shard_map.150.h0), channel_id=1, source_target_pairs={{0,3},{1,0},{2,1},{3,2},{4,7},{5,4},{6,5},{7,6},{8,11},{9,8},{10,9... | collective-permute-start | bytes 491528 | tf_op jit(solution)/shard_map/ppermute | solution.py:61
  63.5 2.1 %collective-permute-start.8 = (bf16[256,320]{1,0:T(8,128)(2,1)}, bf16[256,320]{1,0:T(8,128)(2,1)S(1)}, u32[]{:S(2)}, u32[]{:S(2)}) collective-permute-start(bf16[256,320]{1,0:T(8,128)(2,1)} %shard_map.150.h0), channel_id=1, source_target_pairs={{0,2},{1,3},{2,0},{3,1},{4,6},{5,7},{6,4},{7,5},{8,10},{9,11},{10,... | collective-permute-start | bytes 491528 | tf_op jit(solution)/shard_map/ppermute | solution.py:61
  66.9 13.1 %collective-permute-done.9.refs_1_ = bf16[512,2048]{1,0:T(8,128)(2,1)} collective-permute-done((bf16[512,2048]{1,0:T(8,128)(2,1)}, bf16[512,2048]{1,0:T(8,128)(2,1)}, u32[]{:S(2)}, u32[]{:S(2)}) %collective-permute-start.9) | collective-permute-done | bytes 2097184 | tf_op jit(solution)/shard_map/ppermute | solution.py:52
  82.7 1.7 collective-permute-done.6.h1
  85.4 2.1 %collective-permute-start.12 = (bf16[256,2048]{1,0:T(8,128)(2,1)S(1)}, bf16[256,2048]{1,0:T(8,128)(2,1)S(1)}, u32[]{:S(2)}, u32[]{:S(2)}) collective-permute-start(bf16[256,2048]{1,0:T(8,128)(2,1)S(1)} %slice.12), channel_id=1, source_target_pairs={{0,1},{1,2},{2,3},{3,0},{4,5},{5,6},{6,7},{7,4},{8,9},{9,10},{10,1... | collective-permute-start | bytes 3145736 | tf_op jit(solution)/shard_map/ppermute | solution.py:52
  87.4 1.8 collective-permute-start.13
  89.3 2.1 %collective-permute-start.14 = (bf16[128,2048]{1,0:T(8,128)(2,1)S(1)}, bf16[128,2048]{1,0:T(8,128)(2,1)S(1)}, u32[]{:S(2)}, u32[]{:S(2)}) collective-permute-start(bf16[128,2048]{1,0:T(8,128)(2,1)S(1)} %get-tuple-element.44), channel_id=1, source_target_pairs={{0,4},{1,5},{2,6},{3,7},{4,8},{5,9},{6,10},{7,11},{8,12},{9,13},{1... | collective-permute-start | bytes 1572872 | tf_op jit(solution)/shard_map/ppermute | solution.py:52
  93.9 5.8 %collective-permute-done.14.refs_1_ = bf16[128,2048]{1,0:T(8,128)(2,1)S(1)} collective-permute-done((bf16[128,2048]{1,0:T(8,128)(2,1)S(1)}, bf16[128,2048]{1,0:T(8,128)(2,1)S(1)}, u32[]{:S(2)}, u32[]{:S(2)}) %collective-permute-start.14) | collective-permute-done | bytes 524320 | tf_op jit(solution)/shard_map/ppermute | solution.py:52
  100.6 5.3 %collective-permute-done.16.refs_3_ = bf16[128,2048]{1,0:T(8,128)(2,1)S(1)} collective-permute-done((bf16[128,2048]{1,0:T(8,128)(2,1)S(1)}, bf16[128,2048]{1,0:T(8,128)(2,1)S(1)}, u32[]{:S(2)}, u32[]{:S(2)}) %collective-permute-start.16) | collective-permute-done | bytes 524320 | tf_op jit(solution)/shard_map/ppermute | solution.py:52
  107.7 5.9 %shard_map.152 = (f32[256,512]{1,0:T(8,128)}, bf16[256,512]{1,0:T(8,128)(2,1)}, bf16[256,512]{1,0:T(8,128)(2,1)}, bf16[256,512]{1,0:T(8,128)(2,1)}) custom-call(s32[16]{0:T(128)} %get-tuple-element.62.nat, bf16[256,320]{1,0:T(8,128)(2,1)} %shard_map.150.h0, bf16[256,320]{1,0:T(8,128)(2,1)} %copy-done.17, bf16[256,320]{1,0:T(8,128)(2,1)} %copy-done.18, ...), custom_call_target="tpu_custom_call" | custom-call | flops 1340000000 | bytes 8388608 | tf_op jit(solution)/shard_map/pallas_call | solution.py:188
  116.8 1.7 collective-permute-start.19
  119.3 3.0 %collective-permute-done.17 = bf16[256,512]{1,0:T(8,128)(2,1)S(1)} collective-permute-done((bf16[256,512]{1,0:T(8,128)(2,1)}, bf16[256,512]{1,0:T(8,128)(2,1)S(1)}, u32[]{:S(2)}, u32[]{:S(2)}) %collective-permute-start.17) | collective-permute-done | bytes 262176 | tf_op jit(solution)/shard_map/ppermute | solution.py:61
  122.2 5.6 %collective-permute-done.18 = bf16[256,512]{1,0:T(8,128)(2,1)S(1)} collective-permute-done((bf16[256,512]{1,0:T(8,128)(2,1)}, bf16[256,512]{1,0:T(8,128)(2,1)S(1)}, u32[]{:S(2)}, u32[]{:S(2)}) %collective-permute-start.18) | collective-permute-done | bytes 262176 | tf_op jit(solution)/shard_map/ppermute | solution.py:61
  129.2 3.2 %collective-permute-start.21 = (bf16[256,512]{1,0:T(8,128)(2,1)S(1)}, bf16[256,512]{1,0:T(8,128)(2,1)S(1)}, u32[]{:S(2)}, u32[]{:S(2)}) collective-permute-start(bf16[256,512]{1,0:T(8,128)(2,1)S(1)} %add_convert_fusion.1.v0), channel_id=1, source_target_pairs={{0,3},{1,0},{2,1},{3,2},{4,7},{5,4},{6,5},{7,6},{8,11},{9,8},{10,9... | collective-permute-start | bytes 786440 | tf_op jit(solution)/shard_map/ppermute | solution.py:52
  132.8 4.8 %collective-permute-done.20.v1 = bf16[256,512]{1,0:T(8,128)(2,1)S(1)} collective-permute-done((bf16[256,512]{1,0:T(8,128)(2,1)S(1)}, bf16[256,512]{1,0:T(8,128)(2,1)S(1)}, u32[]{:S(2)}, u32[]{:S(2)}) %collective-permute-start.20) | collective-permute-done | bytes 262176 | tf_op jit(solution)/shard_map/ppermute | solution.py:52
  138.8 4.3 %collective-permute-done.22.v3 = bf16[256,512]{1,0:T(8,128)(2,1)S(1)} collective-permute-done((bf16[256,512]{1,0:T(8,128)(2,1)S(1)}, bf16[256,512]{1,0:T(8,128)(2,1)S(1)}, u32[]{:S(2)}, u32[]{:S(2)}) %collective-permute-start.22) | collective-permute-done | bytes 262176 | tf_op jit(solution)/shard_map/ppermute | solution.py:52
  146.2 5.6 %collective-permute-start.24 = (bf16[128,2048]{1,0:T(8,128)(2,1)S(1)}, bf16[128,2048]{1,0:T(8,128)(2,1)S(1)}, u32[]{:S(2)}, u32[]{:S(2)}) collective-permute-start(bf16[128,2048]{1,0:T(8,128)(2,1)S(1)} %get-tuple-element.54.e1), channel_id=1, source_target_pairs={{0,12},{1,13},{2,14},{3,15},{4,0},{5,1},{6,2},{7,3},{8,4},{9,5},{1... | collective-permute-start | bytes 1572872 | tf_op jit(solution)/shard_map/ppermute | solution.py:52
  153.2 9.6 %shard_map.155 = (f32[128,2048]{1,0:T(8,128)}, bf16[128,2048]{1,0:T(8,128)(2,1)}, bf16[128,2048]{1,0:T(8,128)(2,1)}, bf16[128,2048]{1,0:T(8,128)(2,1)}) custom-call(s32[16]{0:T(128)} %get-tuple-element.63.tab, bf16[128,2048]{1,0:T(8,128)(2,1)} %copy-done.1, bf16[128,2048]{1,0:T(8,128)(2,1)} %copy-done.9, bf16[128,2048]{1,0:T(8,128)(2,1)} %copy-done.10, ...), custom_call_target="tpu_custom_call" | custom-call | flops 4300000256 | bytes 14680064 | tf_op jit(solution)/shard_map/pallas_call | solution.py:260
  162.9 2.2 %collective-permute-start.26 = (bf16[128,2048]{1,0:T(8,128)(2,1)}, bf16[128,2048]{1,0:T(8,128)(2,1)S(1)}, u32[]{:S(2)}, u32[]{:S(2)}) collective-permute-start(bf16[128,2048]{1,0:T(8,128)(2,1)} %get-tuple-element.58), channel_id=1, source_target_pairs={{0,8},{1,9},{2,10},{3,11},{4,12},{5,13},{6,14},{7,15},{8,0},{9,1},... | collective-permute-start | bytes 1572872 | tf_op jit(solution)/shard_map/ppermute | solution.py:52
  165.1 3.2 %collective-permute-start.28 = (bf16[128,2048]{1,0:T(8,128)(2,1)}, bf16[128,2048]{1,0:T(8,128)(2,1)S(1)}, u32[]{:S(2)}, u32[]{:S(2)}) collective-permute-start(bf16[128,2048]{1,0:T(8,128)(2,1)} %get-tuple-element.60), channel_id=1, source_target_pairs={{0,12},{1,13},{2,14},{3,15},{4,0},{5,1},{6,2},{7,3},{8,4},{9,5},{1... | collective-permute-start | bytes 1572872 | tf_op jit(solution)/shard_map/ppermute | solution.py:52
  168.4 2.0 %shard_map.154 = (bf16[128,8192]{1,0:T(8,128)(2,1)}, f32[128,128]{1,0:T(8,128)S(1)}) custom-call(s32[16]{0:T(128)S(1)} %copy-done.5, bf16[128,2048]{1,0:T(8,128)(2,1)S(1)} %copy-done.2, bf16[128,2048]{1,0:T(8,128)(2,1)S(1)} %collective-permute-done.23.e1, bf16[128,2048]{1,0:T(8,128)(2,1)S(1)} %collective-permute-done.24.e2, ...), custom_call_target="tpu_custom_call" | custom-call | flops 4000000 | bytes 31457280 | tf_op jit(solution)/shard_map/pallas_call | solution.py:292
  170.5 3.5 %collective-permute-done.26 = bf16[128,2048]{1,0:T(8,128)(2,1)S(1)} collective-permute-done((bf16[128,2048]{1,0:T(8,128)(2,1)}, bf16[128,2048]{1,0:T(8,128)(2,1)S(1)}, u32[]{:S(2)}, u32[]{:S(2)}) %collective-permute-start.26) | collective-permute-done | bytes 524320 | tf_op jit(solution)/shard_map/ppermute | solution.py:52
  174.0 5.5 %collective-permute-done.27 = bf16[128,2048]{1,0:T(8,128)(2,1)S(1)} collective-permute-done((bf16[128,2048]{1,0:T(8,128)(2,1)}, bf16[128,2048]{1,0:T(8,128)(2,1)S(1)}, u32[]{:S(2)}, u32[]{:S(2)}) %collective-permute-start.27) | collective-permute-done | bytes 524320 | tf_op jit(solution)/shard_map/ppermute | solution.py:52
  (102 shorter events, 35.0 us)
Async XLA Ops:
  7.2 44.4 %copy-start.20 = (f32[5120]{0:T(1024)S(1)}, f32[5120]{0:T(1024)}, u32[]{:S(2)}) copy-start(f32[5120]{0:T(1024)} %param.20) | copy-start | bytes 61444
  7.2 47.3 %all-gather.3.cloned.1.call-start = ((), (), s32[]{:S(2)}) async-start(), calls=%async_computation | async-start | bytes 4177920 | tf_op jit(solution)/shard_map/all_gather | solution.py:320
  7.9 99.7 %all-gather.5.cloned.1.call-start = ((), (), s32[]{:S(2)}) async-start(), calls=%async_computation.1 | async-start | bytes 5570560 | tf_op jit(solution)/shard_map/all_gather | solution.py:326
  10.5 6.6 %collective-permute-start = (bf16[16,5120]{1,0:T(8,128)(2,1)S(1)}, bf16[16,5120]{1,0:T(8,128)(2,1)S(1)}, u32[]{:S(2)}, u32[]{:S(2)}) collective-permute-start(bf16[16,5120]{1,0:T(8,128)(2,1)S(1)} %shard_map.149), channel_id=1, source_target_pairs={{0,1},{1,2},{2,3},{3,0},{4,5},{5,6},{6,7},{7,4},{8,9},{9,10},{10,1... | collective-permute-start | bytes 491528 | tf_op jit(solution)/shard_map/ppermute | solution.py:52
  12.1 5.3 %collective-permute-start.1 = (bf16[16,5120]{1,0:T(8,128)(2,1)S(1)}, bf16[16,5120]{1,0:T(8,128)(2,1)S(1)}, u32[]{:S(2)}, u32[]{:S(2)}) collective-permute-start(bf16[16,5120]{1,0:T(8,128)(2,1)S(1)} %shard_map.149), channel_id=1, source_target_pairs={{0,3},{1,0},{2,1},{3,2},{4,7},{5,4},{6,5},{7,6},{8,11},{9,8},{10,9... | collective-permute-start | bytes 491528 | tf_op jit(solution)/shard_map/ppermute | solution.py:52
  13.9 6.8 %collective-permute-start.2 = (bf16[16,5120]{1,0:T(8,128)(2,1)S(1)}, bf16[16,5120]{1,0:T(8,128)(2,1)S(1)}, u32[]{:S(2)}, u32[]{:S(2)}) collective-permute-start(bf16[16,5120]{1,0:T(8,128)(2,1)S(1)} %shard_map.149), channel_id=1, source_target_pairs={{0,2},{1,3},{2,0},{3,1},{4,6},{5,7},{6,4},{7,5},{8,10},{9,11},{10,... | collective-permute-start | bytes 491528 | tf_op jit(solution)/shard_map/ppermute | solution.py:52
  20.7 26.7 %collective-permute-start.3 = (bf16[64,5120]{1,0:T(8,128)(2,1)S(1)}, bf16[64,5120]{1,0:T(8,128)(2,1)S(1)}, u32[]{:S(2)}, u32[]{:S(2)}) collective-permute-start(bf16[64,5120]{1,0:T(8,128)(2,1)S(1)} %pad_maximum_fusion.s0), channel_id=1, source_target_pairs={{0,4},{1,5},{2,6},{3,7},{4,8},{5,9},{6,10},{7,11},{8,12},{9,13},{1... | collective-permute-start | bytes 1966088 | tf_op jit(solution)/shard_map/ppermute | solution.py:52
  22.4 25.1 %collective-permute-start.4 = (bf16[64,5120]{1,0:T(8,128)(2,1)S(1)}, bf16[64,5120]{1,0:T(8,128)(2,1)S(1)}, u32[]{:S(2)}, u32[]{:S(2)}) collective-permute-start(bf16[64,5120]{1,0:T(8,128)(2,1)S(1)} %pad_maximum_fusion.s0), channel_id=1, source_target_pairs={{0,12},{1,13},{2,14},{3,15},{4,0},{5,1},{6,2},{7,3},{8,4},{9,5},{1... | collective-permute-start | bytes 1966088 | tf_op jit(solution)/shard_map/ppermute | solution.py:52
  24.1 23.5 %collective-permute-start.5 = (bf16[64,5120]{1,0:T(8,128)(2,1)S(1)}, bf16[64,5120]{1,0:T(8,128)(2,1)S(1)}, u32[]{:S(2)}, u32[]{:S(2)}) collective-permute-start(bf16[64,5120]{1,0:T(8,128)(2,1)S(1)} %pad_maximum_fusion.s0), channel_id=1, source_target_pairs={{0,8},{1,9},{2,10},{3,11},{4,12},{5,13},{6,14},{7,15},{8,0},{9,1},... | collective-permute-start | bytes 1966088 | tf_op jit(solution)/shard_map/ppermute | solution.py:52
  26.0 21.4 %collective-permute-start.11 = (bf16[320,512]{1,0:T(8,128)(2,1)}, bf16[320,512]{1,0:T(8,128)(2,1)S(1)}, u32[]{:S(2)}, u32[]{:S(2)}) collective-permute-start(bf16[320,512]{1,0:T(8,128)(2,1)} %param.21), channel_id=1, source_target_pairs={{0,0},{1,16},{2,32},{3,48},{4,4},{5,20},{6,36},{7,52},{8,8},{9,24}... | collective-permute-start | bytes 983048 | tf_op jit(solution)/shard_map/ppermute | solution.py:321
  48.2 31.9 %collective-permute-start.9 = (bf16[512,2048]{1,0:T(8,128)(2,1)}, bf16[512,2048]{1,0:T(8,128)(2,1)}, u32[]{:S(2)}, u32[]{:S(2)}) collective-permute-start(bf16[512,2048]{1,0:T(8,128)(2,1)} %refs_0_), channel_id=1, source_target_pairs={{0,1},{1,2},{2,3},{3,0},{4,5},{5,6},{6,7},{7,4},{8,9},{9,10},{10,1... | collective-permute-start | bytes 6291464 | tf_op jit(solution)/shard_map/ppermute | solution.py:52
  48.3 33.1 %collective-permute-start.10 = (bf16[512,2048]{1,0:T(8,128)(2,1)}, bf16[512,2048]{1,0:T(8,128)(2,1)}, u32[]{:S(2)}, u32[]{:S(2)}) collective-permute-start(bf16[512,2048]{1,0:T(8,128)(2,1)} %refs_0_), channel_id=1, source_target_pairs={{0,3},{1,0},{2,1},{3,2},{4,7},{5,4},{6,5},{7,6},{8,11},{9,8},{10,9... | collective-permute-start | bytes 6291464 | tf_op jit(solution)/shard_map/ppermute | solution.py:52
  60.2 24.3 %collective-permute-start.6 = (bf16[256,320]{1,0:T(8,128)(2,1)}, bf16[256,320]{1,0:T(8,128)(2,1)S(1)}, u32[]{:S(2)}, u32[]{:S(2)}) collective-permute-start(bf16[256,320]{1,0:T(8,128)(2,1)} %shard_map.150.h0), channel_id=1, source_target_pairs={{0,1},{1,2},{2,3},{3,0},{4,5},{5,6},{6,7},{7,4},{8,9},{9,10},{10,1... | collective-permute-start | bytes 491528 | tf_op jit(solution)/shard_map/ppermute | solution.py:61
  60.6 24.7 %collective-permute-start.7 = (bf16[256,320]{1,0:T(8,128)(2,1)}, bf16[256,320]{1,0:T(8,128)(2,1)S(1)}, u32[]{:S(2)}, u32[]{:S(2)}) collective-permute-start(bf16[256,320]{1,0:T(8,128)(2,1)} %shard_map.150.h0), channel_id=1, source_target_pairs={{0,3},{1,0},{2,1},{3,2},{4,7},{5,4},{6,5},{7,6},{8,11},{9,8},{10,9... | collective-permute-start | bytes 491528 | tf_op jit(solution)/shard_map/ppermute | solution.py:61
  63.5 21.8 %collective-permute-start.8 = (bf16[256,320]{1,0:T(8,128)(2,1)}, bf16[256,320]{1,0:T(8,128)(2,1)S(1)}, u32[]{:S(2)}, u32[]{:S(2)}) collective-permute-start(bf16[256,320]{1,0:T(8,128)(2,1)} %shard_map.150.h0), channel_id=1, source_target_pairs={{0,2},{1,3},{2,0},{3,1},{4,6},{5,7},{6,4},{7,5},{8,10},{9,11},{10,... | collective-permute-start | bytes 491528 | tf_op jit(solution)/shard_map/ppermute | solution.py:61
  85.4 21.3 %collective-permute-start.12 = (bf16[256,2048]{1,0:T(8,128)(2,1)S(1)}, bf16[256,2048]{1,0:T(8,128)(2,1)S(1)}, u32[]{:S(2)}, u32[]{:S(2)}) collective-permute-start(bf16[256,2048]{1,0:T(8,128)(2,1)S(1)} %slice.12), channel_id=1, source_target_pairs={{0,1},{1,2},{2,3},{3,0},{4,5},{5,6},{6,7},{7,4},{8,9},{9,10},{10,1... | collective-permute-start | bytes 3145736 | tf_op jit(solution)/shard_map/ppermute | solution.py:52
  87.4 20.2 %collective-permute-start.13 = (bf16[256,2048]{1,0:T(8,128)(2,1)S(1)}, bf16[256,2048]{1,0:T(8,128)(2,1)}, u32[]{:S(2)}, u32[]{:S(2)}) collective-permute-start(bf16[256,2048]{1,0:T(8,128)(2,1)S(1)} %slice.13), channel_id=1, source_target_pairs={{0,3},{1,0},{2,1},{3,2},{4,7},{5,4},{6,5},{7,6},{8,11},{9,8},{10,9... | collective-permute-start | bytes 3145736 | tf_op jit(solution)/shard_map/ppermute | solution.py:52
  89.3 10.4 %collective-permute-start.14 = (bf16[128,2048]{1,0:T(8,128)(2,1)S(1)}, bf16[128,2048]{1,0:T(8,128)(2,1)S(1)}, u32[]{:S(2)}, u32[]{:S(2)}) collective-permute-start(bf16[128,2048]{1,0:T(8,128)(2,1)S(1)} %get-tuple-element.44), channel_id=1, source_target_pairs={{0,4},{1,5},{2,6},{3,7},{4,8},{5,9},{6,10},{7,11},{8,12},{9,13},{1... | collective-permute-start | bytes 1572872 | tf_op jit(solution)/shard_map/ppermute | solution.py:52
  91.4 9.2 %collective-permute-start.15 = (bf16[128,2048]{1,0:T(8,128)(2,1)S(1)}, bf16[128,2048]{1,0:T(8,128)(2,1)S(1)}, u32[]{:S(2)}, u32[]{:S(2)}) collective-permute-start(bf16[128,2048]{1,0:T(8,128)(2,1)S(1)} %get-tuple-element.45), channel_id=1, source_target_pairs={{0,12},{1,13},{2,14},{3,15},{4,0},{5,1},{6,2},{7,3},{8,4},{9,5},{1... | collective-permute-start | bytes 1572872 | tf_op jit(solution)/shard_map/ppermute | solution.py:52
  92.5 13.4 %collective-permute-start.16 = (bf16[128,2048]{1,0:T(8,128)(2,1)S(1)}, bf16[128,2048]{1,0:T(8,128)(2,1)S(1)}, u32[]{:S(2)}, u32[]{:S(2)}) collective-permute-start(bf16[128,2048]{1,0:T(8,128)(2,1)S(1)} %get-tuple-element.46), channel_id=1, source_target_pairs={{0,8},{1,9},{2,10},{3,11},{4,12},{5,13},{6,14},{7,15},{8,0},{9,1},... | collective-permute-start | bytes 1572872 | tf_op jit(solution)/shard_map/ppermute | solution.py:52
  113.6 8.6 %collective-permute-start.17 = (bf16[256,512]{1,0:T(8,128)(2,1)}, bf16[256,512]{1,0:T(8,128)(2,1)S(1)}, u32[]{:S(2)}, u32[]{:S(2)}) collective-permute-start(bf16[256,512]{1,0:T(8,128)(2,1)} %get-tuple-element.49), channel_id=1, source_target_pairs={{0,8},{1,9},{2,10},{3,11},{4,12},{5,13},{6,14},{7,15},{8,0},{9,1},... | collective-permute-start | bytes 786440 | tf_op jit(solution)/shard_map/ppermute | solution.py:61
  115.3 12.6 %collective-permute-start.18 = (bf16[256,512]{1,0:T(8,128)(2,1)}, bf16[256,512]{1,0:T(8,128)(2,1)S(1)}, u32[]{:S(2)}, u32[]{:S(2)}) collective-permute-start(bf16[256,512]{1,0:T(8,128)(2,1)} %get-tuple-element.50), channel_id=1, source_target_pairs={{0,4},{1,5},{2,6},{3,7},{4,8},{5,9},{6,10},{7,11},{8,12},{9,13},{1... | collective-permute-start | bytes 786440 | tf_op jit(solution)/shard_map/ppermute | solution.py:61
  116.8 11.1 %collective-permute-start.19 = (bf16[256,512]{1,0:T(8,128)(2,1)}, bf16[256,512]{1,0:T(8,128)(2,1)S(1)}, u32[]{:S(2)}, u32[]{:S(2)}) collective-permute-start(bf16[256,512]{1,0:T(8,128)(2,1)} %get-tuple-element.51), channel_id=1, source_target_pairs={{0,12},{1,13},{2,14},{3,15},{4,0},{5,1},{6,2},{7,3},{8,4},{9,5},{1... | collective-permute-start | bytes 786440 | tf_op jit(solution)/shard_map/ppermute | solution.py:61
  129.1 8.4 %collective-permute-start.20 = (bf16[256,512]{1,0:T(8,128)(2,1)S(1)}, bf16[256,512]{1,0:T(8,128)(2,1)S(1)}, u32[]{:S(2)}, u32[]{:S(2)}) collective-permute-start(bf16[256,512]{1,0:T(8,128)(2,1)S(1)} %add_convert_fusion.1.v0), channel_id=1, source_target_pairs={{0,1},{1,2},{2,3},{3,0},{4,5},{5,6},{6,7},{7,4},{8,9},{9,10},{10,1... | collective-permute-start | bytes 786440 | tf_op jit(solution)/shard_map/ppermute | solution.py:52
  129.2 9.6 %collective-permute-start.21 = (bf16[256,512]{1,0:T(8,128)(2,1)S(1)}, bf16[256,512]{1,0:T(8,128)(2,1)S(1)}, u32[]{:S(2)}, u32[]{:S(2)}) collective-permute-start(bf16[256,512]{1,0:T(8,128)(2,1)S(1)} %add_convert_fusion.1.v0), channel_id=1, source_target_pairs={{0,3},{1,0},{2,1},{3,2},{4,7},{5,4},{6,5},{7,6},{8,11},{9,8},{10,9... | collective-permute-start | bytes 786440 | tf_op jit(solution)/shard_map/ppermute | solution.py:52
  132.4 10.7 %collective-permute-start.22 = (bf16[256,512]{1,0:T(8,128)(2,1)S(1)}, bf16[256,512]{1,0:T(8,128)(2,1)S(1)}, u32[]{:S(2)}, u32[]{:S(2)}) collective-permute-start(bf16[256,512]{1,0:T(8,128)(2,1)S(1)} %add_convert_fusion.1.v0), channel_id=1, source_target_pairs={{0,2},{1,3},{2,0},{3,1},{4,6},{5,7},{6,4},{7,5},{8,10},{9,11},{10,... | collective-permute-start | bytes 786440 | tf_op jit(solution)/shard_map/ppermute | solution.py:52
  145.2 19.9 %collective-permute-start.23 = (bf16[128,2048]{1,0:T(8,128)(2,1)S(1)}, bf16[128,2048]{1,0:T(8,128)(2,1)S(1)}, u32[]{:S(2)}, u32[]{:S(2)}) collective-permute-start(bf16[128,2048]{1,0:T(8,128)(2,1)S(1)} %get-tuple-element.53.e2), channel_id=1, source_target_pairs={{0,4},{1,5},{2,6},{3,7},{4,8},{5,9},{6,10},{7,11},{8,12},{9,13},{1... | collective-permute-start | bytes 1572872 | tf_op jit(solution)/shard_map/ppermute | solution.py:52
  146.2 22.2 %collective-permute-start.24 = (bf16[128,2048]{1,0:T(8,128)(2,1)S(1)}, bf16[128,2048]{1,0:T(8,128)(2,1)S(1)}, u32[]{:S(2)}, u32[]{:S(2)}) collective-permute-start(bf16[128,2048]{1,0:T(8,128)(2,1)S(1)} %get-tuple-element.54.e1), channel_id=1, source_target_pairs={{0,12},{1,13},{2,14},{3,15},{4,0},{5,1},{6,2},{7,3},{8,4},{9,5},{1... | collective-permute-start | bytes 1572872 | tf_op jit(solution)/shard_map/ppermute | solution.py:52
  151.8 16.6 %collective-permute-start.25 = (bf16[128,2048]{1,0:T(8,128)(2,1)S(1)}, bf16[128,2048]{1,0:T(8,128)(2,1)S(1)}, u32[]{:S(2)}, u32[]{:S(2)}) collective-permute-start(bf16[128,2048]{1,0:T(8,128)(2,1)S(1)} %get-tuple-element.55.e3), channel_id=1, source_target_pairs={{0,8},{1,9},{2,10},{3,11},{4,12},{5,13},{6,14},{7,15},{8,0},{9,1},... | collective-permute-start | bytes 1572872 | tf_op jit(solution)/shard_map/ppermute | solution.py:52
  162.9 11.1 %collective-permute-start.26 = (bf16[128,2048]{1,0:T(8,128)(2,1)}, bf16[128,2048]{1,0:T(8,128)(2,1)S(1)}, u32[]{:S(2)}, u32[]{:S(2)}) collective-permute-start(bf16[128,2048]{1,0:T(8,128)(2,1)} %get-tuple-element.58), channel_id=1, source_target_pairs={{0,8},{1,9},{2,10},{3,11},{4,12},{5,13},{6,14},{7,15},{8,0},{9,1},... | collective-permute-start | bytes 1572872 | tf_op jit(solution)/shard_map/ppermute | solution.py:52
  165.1 14.4 %collective-permute-start.27 = (bf16[128,2048]{1,0:T(8,128)(2,1)}, bf16[128,2048]{1,0:T(8,128)(2,1)S(1)}, u32[]{:S(2)}, u32[]{:S(2)}) collective-permute-start(bf16[128,2048]{1,0:T(8,128)(2,1)} %get-tuple-element.59), channel_id=1, source_target_pairs={{0,4},{1,5},{2,6},{3,7},{4,8},{5,9},{6,10},{7,11},{8,12},{9,13},{1... | collective-permute-start | bytes 1572872 | tf_op jit(solution)/shard_map/ppermute | solution.py:52
  165.1 14.4 %collective-permute-start.28 = (bf16[128,2048]{1,0:T(8,128)(2,1)}, bf16[128,2048]{1,0:T(8,128)(2,1)S(1)}, u32[]{:S(2)}, u32[]{:S(2)}) collective-permute-start(bf16[128,2048]{1,0:T(8,128)(2,1)} %get-tuple-element.60), channel_id=1, source_target_pairs={{0,12},{1,13},{2,14},{3,15},{4,0},{5,1},{6,2},{7,3},{8,4},{9,5},{1... | collective-permute-start | bytes 1572872 | tf_op jit(solution)/shard_map/ppermute | solution.py:52
  (24 other events, 273.9 us)
Sparse Core Ops, SparseCore 0:
  9.8 44.6 all-gather.2
  56.9 42.2 all-gather.4

commit v13 on v7

--- a/solution.py
+++ b/solution.py
@@ -327,8 +327,8 @@
 
     weights = (kv_weight, kv_right, kv_left, hop(far_right, 1, 1), hop(far_left, 1, -1))
     text = (own, hop(to_right, 2, 1), hop(to_left, 2, -1), hop(to_far, 2, 2))
-    down_full = after(down_full, weights[3], weights[4], *text)
-    own, to_left, to_right, to_far = down(nat, units, down_full)
+    own, *parts = down(nat, units, after(down_full, text[1]))
+    to_left, to_right, to_far = lax.optimization_barrier((*parts, *text[2:], *weights[3:]))[:3]
     bias = lax.dynamic_slice_in_dim(down_bias, lax.axis_index("tp") * 512, 512, 0)
     total = own + bias
     for value in (line(to_far, "y", 2), line(to_right, "y", 1), line(to_left, "y", -1)):

time: 188 us -> 178 us (0.947)
  the two profiles are of different devices: /device:TPU:224 before, /device:TPU:32 now
where the time goes in v13:
time: 178 us; the launch traced here: 177 us
  waiting for transfers between devices  72.5 us (41%)
  starting transfers between devices  49.5 us (28%)
  Pallas kernels  26.8 us (15%)
  between operations  14.3 us (8%)
  local copies, waits for them, and re-layouts  11.6 us (7%)
  other arithmetic  2.47 us (1%)
    ppermute x22, waiting for transfers between devices, hop(): return lax.ppermute(value, ('mb', 'tp'), HOPS[which, step])  41.8 us
    ppermute x22, starting transfers between devices, hop(): return lax.ppermute(value, ('mb', 'tp'), HOPS[which, step])  36.3 us
    ppermute x1, waiting for transfers between devices, per_device(): down_part = lax.ppermute(down_weight, ('enc', 'mb', 'tp'), SHUFFLE)  18.2 us
    ppermute x6, starting transfers between devices, line(): return lax.ppermute(value, ('mb', 'tp'), LINES[axis, step])  9.85 us
    pallas_call x1, Pallas kernels, product(): pl.pallas_call(product_kernel, out_shape=[jax.ShapeDtypeStruct((128, 2048...  9.27 us
    ppermute x6, waiting for transfers between devices, line(): return lax.ppermute(value, ('mb', 'tp'), LINES[axis, step])  8.93 us
    pallas_call x1, Pallas kernels, down(): pl.pallas_call(down_kernel, out_shape=[jax.ShapeDtypeStruct((256, 512), F...  5.97 us
    pallas_call x1, Pallas kernels, up(): pl.pallas_call(up_kernel, out_shape=jax.ShapeDtypeStruct((256, 320), BF16...  5.69 us
  transfers between devices with their start and end apart: 31, of which 16 were waited for; matrix products, arithmetic and copies ran while one was open for 4% of the time, Pallas kernels for 14%

profile of v13, /device:TPU:32, one launch (start us, length us, event | category | flops | bytes accessed | tf_op | source)
XLA Modules:
  0.0 177.2 jit_solution(18399187337050993548)
XLA Ops:
  13.9 1.8 %collective-permute-start.2 = (bf16[16,5120]{1,0:T(8,128)(2,1)S(1)}, bf16[16,5120]{1,0:T(8,128)(2,1)S(1)}, u32[]{:S(2)}, u32[]{:S(2)}) collective-permute-start(bf16[16,5120]{1,0:T(8,128)(2,1)S(1)} %shard_map.149), channel_id=1, source_target_pairs={{0,2},{1,3},{2,0},{3,1},{4,6},{5,7},{6,4},{7,5},{8,10},{9,11},{10,... | collective-permute-start | bytes 491528 | tf_op jit(solution)/shard_map/ppermute | solution.py:52
  17.4 3.2 %collective-permute-done.2 = bf16[16,5120]{1,0:T(8,128)(2,1)S(1)} collective-permute-done((bf16[16,5120]{1,0:T(8,128)(2,1)S(1)}, bf16[16,5120]{1,0:T(8,128)(2,1)S(1)}, u32[]{:S(2)}, u32[]{:S(2)}) %collective-permute-start.2) | collective-permute-done | bytes 163872 | tf_op jit(solution)/shard_map/ppermute | solution.py:52
  24.1 2.0 %collective-permute-start.5 = (bf16[64,5120]{1,0:T(8,128)(2,1)S(1)}, bf16[64,5120]{1,0:T(8,128)(2,1)S(1)}, u32[]{:S(2)}, u32[]{:S(2)}) collective-permute-start(bf16[64,5120]{1,0:T(8,128)(2,1)S(1)} %pad_maximum_fusion.s0), channel_id=1, source_target_pairs={{0,8},{1,9},{2,10},{3,11},{4,12},{5,13},{6,14},{7,15},{8,0},{9,1},... | collective-permute-start | bytes 1966088 | tf_op jit(solution)/shard_map/ppermute | solution.py:52
  26.0 3.3 %collective-permute-start.11 = (bf16[320,512]{1,0:T(8,128)(2,1)}, bf16[320,512]{1,0:T(8,128)(2,1)S(1)}, u32[]{:S(2)}, u32[]{:S(2)}) collective-permute-start(bf16[320,512]{1,0:T(8,128)(2,1)} %param.21), channel_id=1, source_target_pairs={{0,0},{1,16},{2,32},{3,48},{4,4},{5,20},{6,36},{7,52},{8,8},{9,24}... | collective-permute-start | bytes 983048 | tf_op jit(solution)/shard_map/ppermute | solution.py:312
  29.3 18.2 %collective-permute-done.11 = bf16[320,512]{1,0:T(8,128)(2,1)S(1)} collective-permute-done((bf16[320,512]{1,0:T(8,128)(2,1)}, bf16[320,512]{1,0:T(8,128)(2,1)S(1)}, u32[]{:S(2)}, u32[]{:S(2)}) %collective-permute-start.11) | collective-permute-done | bytes 327712 | tf_op jit(solution)/shard_map/ppermute | solution.py:312
  48.3 3.2 %collective-permute-start.10 = (bf16[512,2048]{1,0:T(8,128)(2,1)}, bf16[512,2048]{1,0:T(8,128)(2,1)}, u32[]{:S(2)}, u32[]{:S(2)}) collective-permute-start(bf16[512,2048]{1,0:T(8,128)(2,1)} %w0), channel_id=1, source_target_pairs={{0,3},{1,0},{2,1},{3,2},{4,7},{5,4},{6,5},{7,6},{8,11},{9,8},{10,9... | collective-permute-start | bytes 6291464 | tf_op jit(solution)/shard_map/ppermute | solution.py:52
  53.6 2.9 %all-gather.3.cloned.1.call-done.weight = bf16[5120,320]{1,0:T(8,128)(2,1)} async-done(((bf16[320,320]{1,0:T(8,128)(2,1)}), bf16[5120,320]{1,0:T(8,128)(2,1)}) %all-gather.3.cloned.1.call-update) | async-done | bytes 3276816 | tf_op jit(solution)/shard_map/all_gather | solution.py:311
  56.5 5.7 %shard_map.150.h0 = bf16[256,320]{1,0:T(8,128)(2,1)} custom-call(s32[16]{0:T(128)} %get-tuple-element.69.tab, bf16[64,5120]{1,0:T(8,128)(2,1)} %copy-done.11, bf16[64,5120]{1,0:T(8,128)(2,1)} %copy-done.13, bf16[64,5120]{1,0:T(8,128)(2,1)} %copy-done.14, bf16[64,5120]{1,0:T(8,128)(2,1)} %copy-done.15, bf16[5120,320]{1,0:T(8,128)(2,1)} %all-gather.3.cloned.1.call-done.weight, ...), custom_call_target="tpu_custom_call" | custom-call | flops 840000000 | bytes 6291456 | tf_op jit(solution)/shard_map/pallas_call | solution.py:153
  62.2 2.7 %collective-permute-start.6 = (bf16[256,320]{1,0:T(8,128)(2,1)}, bf16[256,320]{1,0:T(8,128)(2,1)S(1)}, u32[]{:S(2)}, u32[]{:S(2)}) collective-permute-start(bf16[256,320]{1,0:T(8,128)(2,1)} %shard_map.150.h0), channel_id=1, source_target_pairs={{0,1},{1,2},{2,3},{3,0},{4,5},{5,6},{6,7},{7,4},{8,9},{9,10},{10,1... | collective-permute-start | bytes 491528 | tf_op jit(solution)/shard_map/ppermute | solution.py:60
  65.9 2.5 %collective-permute-start.8 = (bf16[256,320]{1,0:T(8,128)(2,1)}, bf16[256,320]{1,0:T(8,128)(2,1)S(1)}, u32[]{:S(2)}, u32[]{:S(2)}) collective-permute-start(bf16[256,320]{1,0:T(8,128)(2,1)} %shard_map.150.h0), channel_id=1, source_target_pairs={{0,2},{1,3},{2,0},{3,1},{4,6},{5,7},{6,4},{7,5},{8,10},{9,11},{10,... | collective-permute-start | bytes 491528 | tf_op jit(solution)/shard_map/ppermute | solution.py:60
  68.4 2.3 %shard_map.151 = (bf16[128,2048]{1,0:T(8,128)(2,1)S(1)}, bf16[128,2048]{1,0:T(8,128)(2,1)}, bf16[128,2048]{1,0:T(8,128)(2,1)S(1)}, bf16[128,2048]{1,0:T(8,128)(2,1)S(1)}) custom-call(s32[16]{0:T(128)S(1)} %copy-done.4, bf16[128,8192]{1,0:T(8,128)(2,1)S(1)} %bitcast.20, bf16[128,8192]{1,0:T(8,128)(2,1)S(1)} %bitcast.21, bf16[128,8192]{1,0:T(8,128)(2,1)S(1)} %bitcast.22, ...), custom_call_target="tpu_custom_call" | custom-call | bytes 4194304 | tf_op jit(solution)/shard_map/pallas_call | solution.py:115
  70.7 9.4 %collective-permute-done.9.w1 = bf16[512,2048]{1,0:T(8,128)(2,1)} collective-permute-done((bf16[512,2048]{1,0:T(8,128)(2,1)}, bf16[512,2048]{1,0:T(8,128)(2,1)}, u32[]{:S(2)}, u32[]{:S(2)}) %collective-permute-start.9) | collective-permute-done | bytes 2097184 | tf_op jit(solution)/shard_map/ppermute | solution.py:52
  80.1 2.3 %slice.12 = bf16[256,2048]{1,0:T(8,128)(2,1)} slice(bf16[512,2048]{1,0:T(8,128)(2,1)} %collective-permute-done.9.w1), slice={[0:256], [0:2048]} | slice | bytes 2097152 | tf_op jit(solution)/shard_map/slice | solution.py:321
  82.4 2.4 %slice.13 = bf16[256,2048]{1,0:T(8,128)(2,1)} slice(bf16[512,2048]{1,0:T(8,128)(2,1)} %collective-permute-done.10.w2), slice={[256:512], [0:2048]} | slice | bytes 2097152 | tf_op jit(solution)/shard_map/slice | solution.py:321
  85.2 3.6 %collective-permute-start.16 = (bf16[256,2048]{1,0:T(8,128)(2,1)}, bf16[256,2048]{1,0:T(8,128)(2,1)}, u32[]{:S(2)}, u32[]{:S(2)}) collective-permute-start(bf16[256,2048]{1,0:T(8,128)(2,1)} %slice.13), channel_id=1, source_target_pairs={{0,3},{1,0},{2,1},{3,2},{4,7},{5,4},{6,5},{7,6},{8,11},{9,8},{10,9... | collective-permute-start | bytes 3145736 | tf_op jit(solution)/shard_map/ppermute | solution.py:52
  88.9 3.2 %collective-permute-start.13 = (bf16[128,2048]{1,0:T(8,128)(2,1)}, bf16[128,2048]{1,0:T(8,128)(2,1)S(1)}, u32[]{:S(2)}, u32[]{:S(2)}) collective-permute-start(bf16[128,2048]{1,0:T(8,128)(2,1)} %get-tuple-element.50), channel_id=1, source_target_pairs={{0,12},{1,13},{2,14},{3,15},{4,0},{5,1},{6,2},{7,3},{8,4},{9,5},{1... | collective-permute-start | bytes 1572872 | tf_op jit(solution)/shard_map/ppermute | solution.py:52
  92.1 12.8 %collective-permute-done.12.refs_1_ = bf16[128,2048]{1,0:T(8,128)(2,1)S(1)} collective-permute-done((bf16[128,2048]{1,0:T(8,128)(2,1)S(1)}, bf16[128,2048]{1,0:T(8,128)(2,1)S(1)}, u32[]{:S(2)}, u32[]{:S(2)}) %collective-permute-start.12) | collective-permute-done | bytes 524320 | tf_op jit(solution)/shard_map/ppermute | solution.py:52
  104.9 6.0 %shard_map.152 = (f32[256,512]{1,0:T(8,128)}, bf16[256,512]{1,0:T(8,128)(2,1)}, bf16[256,512]{1,0:T(8,128)(2,1)}, bf16[256,512]{1,0:T(8,128)(2,1)}) custom-call(s32[16]{0:T(128)} %get-tuple-element.68.nat, bf16[256,320]{1,0:T(8,128)(2,1)} %shard_map.150.h0, bf16[256,320]{1,0:T(8,128)(2,1)} %copy-done.17, bf16[256,320]{1,0:T(8,128)(2,1)} %copy-done.18, ...), custom_call_target="tpu_custom_call" | custom-call | flops 1340000000 | bytes 8388608 | tf_op jit(solution)/shard_map/pallas_call | solution.py:189
  112.0 2.7 %collective-permute-start.19 = (bf16[256,512]{1,0:T(8,128)(2,1)}, bf16[256,512]{1,0:T(8,128)(2,1)S(1)}, u32[]{:S(2)}, u32[]{:S(2)}) collective-permute-start(bf16[256,512]{1,0:T(8,128)(2,1)} %get-tuple-element.56), channel_id=1, source_target_pairs={{0,12},{1,13},{2,14},{3,15},{4,0},{5,1},{6,2},{7,3},{8,4},{9,5},{1... | collective-permute-start | bytes 786440 | tf_op jit(solution)/shard_map/ppermute | solution.py:60
  115.4 6.0 %collective-permute-done.17 = bf16[256,512]{1,0:T(8,128)(2,1)S(1)} collective-permute-done((bf16[256,512]{1,0:T(8,128)(2,1)}, bf16[256,512]{1,0:T(8,128)(2,1)S(1)}, u32[]{:S(2)}, u32[]{:S(2)}) %collective-permute-start.17) | collective-permute-done | bytes 262176 | tf_op jit(solution)/shard_map/ppermute | solution.py:60
  121.4 2.7 %collective-permute-done.18 = bf16[256,512]{1,0:T(8,128)(2,1)S(1)} collective-permute-done((bf16[256,512]{1,0:T(8,128)(2,1)}, bf16[256,512]{1,0:T(8,128)(2,1)S(1)}, u32[]{:S(2)}, u32[]{:S(2)}) %collective-permute-start.18) | collective-permute-done | bytes 262176 | tf_op jit(solution)/shard_map/ppermute | solution.py:60
  127.0 1.7 collective-permute-start.21
  128.8 1.8 collective-permute-start.22
  130.7 2.4 %collective-permute-done.20.v1 = bf16[256,512]{1,0:T(8,128)(2,1)S(1)} collective-permute-done((bf16[256,512]{1,0:T(8,128)(2,1)S(1)}, bf16[256,512]{1,0:T(8,128)(2,1)S(1)}, u32[]{:S(2)}, u32[]{:S(2)}) %collective-permute-start.20) | collective-permute-done | bytes 262176 | tf_op jit(solution)/shard_map/ppermute | solution.py:52
  133.1 2.4 %collective-permute-done.21.v2 = bf16[256,512]{1,0:T(8,128)(2,1)S(1)} collective-permute-done((bf16[256,512]{1,0:T(8,128)(2,1)S(1)}, bf16[256,512]{1,0:T(8,128)(2,1)S(1)}, u32[]{:S(2)}, u32[]{:S(2)}) %collective-permute-start.21) | collective-permute-done | bytes 262176 | tf_op jit(solution)/shard_map/ppermute | solution.py:52
  140.4 1.8 %collective-permute-start.24 = (bf16[128,2048]{1,0:T(8,128)(2,1)S(1)}, bf16[128,2048]{1,0:T(8,128)(2,1)S(1)}, u32[]{:S(2)}, u32[]{:S(2)}) collective-permute-start(bf16[128,2048]{1,0:T(8,128)(2,1)S(1)} %get-tuple-element.60.e1), channel_id=1, source_target_pairs={{0,12},{1,13},{2,14},{3,15},{4,0},{5,1},{6,2},{7,3},{8,4},{9,5},{1... | collective-permute-start | bytes 1572872 | tf_op jit(solution)/shard_map/ppermute | solution.py:52
  143.1 9.3 %shard_map.155 = (f32[128,2048]{1,0:T(8,128)}, bf16[128,2048]{1,0:T(8,128)(2,1)}, bf16[128,2048]{1,0:T(8,128)(2,1)}, bf16[128,2048]{1,0:T(8,128)(2,1)}) custom-call(s32[16]{0:T(128)} %get-tuple-element.69.tab, bf16[128,2048]{1,0:T(8,128)(2,1)} %copy-done.1, bf16[128,2048]{1,0:T(8,128)(2,1)} %copy-done.9, bf16[128,2048]{1,0:T(8,128)(2,1)} %copy-done.10, ...), custom_call_target="tpu_custom_call" | custom-call | flops 4300000256 | bytes 14680064 | tf_op jit(solution)/shard_map/pallas_call | solution.py:254
  152.4 3.0 %collective-permute-start.26 = (bf16[128,2048]{1,0:T(8,128)(2,1)}, bf16[128,2048]{1,0:T(8,128)(2,1)S(1)}, u32[]{:S(2)}, u32[]{:S(2)}) collective-permute-start(bf16[128,2048]{1,0:T(8,128)(2,1)} %get-tuple-element.64), channel_id=1, source_target_pairs={{0,8},{1,9},{2,10},{3,11},{4,12},{5,13},{6,14},{7,15},{8,0},{9,1},... | collective-permute-start | bytes 1572872 | tf_op jit(solution)/shard_map/ppermute | solution.py:52
  155.6 3.0 %collective-permute-start.28 = (bf16[128,2048]{1,0:T(8,128)(2,1)}, bf16[128,2048]{1,0:T(8,128)(2,1)S(1)}, u32[]{:S(2)}, u32[]{:S(2)}) collective-permute-start(bf16[128,2048]{1,0:T(8,128)(2,1)} %get-tuple-element.66), channel_id=1, source_target_pairs={{0,12},{1,13},{2,14},{3,15},{4,0},{5,1},{6,2},{7,3},{8,4},{9,5},{1... | collective-permute-start | bytes 1572872 | tf_op jit(solution)/shard_map/ppermute | solution.py:52
  158.6 2.0 %shard_map.154 = (bf16[128,8192]{1,0:T(8,128)(2,1)}, f32[128,128]{1,0:T(8,128)S(1)}) custom-call(s32[16]{0:T(128)S(1)} %copy-done.5, bf16[128,2048]{1,0:T(8,128)(2,1)S(1)} %copy-done.2, bf16[128,2048]{1,0:T(8,128)(2,1)S(1)} %collective-permute-done.23.e1, bf16[128,2048]{1,0:T(8,128)(2,1)S(1)} %collective-permute-done.24.e2, ...), custom_call_target="tpu_custom_call" | custom-call | flops 4000000 | bytes 31457280 | tf_op jit(solution)/shard_map/pallas_call | solution.py:283
  160.7 3.0 %collective-permute-done.26 = bf16[128,2048]{1,0:T(8,128)(2,1)S(1)} collective-permute-done((bf16[128,2048]{1,0:T(8,128)(2,1)}, bf16[128,2048]{1,0:T(8,128)(2,1)S(1)}, u32[]{:S(2)}, u32[]{:S(2)}) %collective-permute-start.26) | collective-permute-done | bytes 524320 | tf_op jit(solution)/shard_map/ppermute | solution.py:52
  163.7 5.5 %collective-permute-done.27 = bf16[128,2048]{1,0:T(8,128)(2,1)S(1)} collective-permute-done((bf16[128,2048]{1,0:T(8,128)(2,1)}, bf16[128,2048]{1,0:T(8,128)(2,1)S(1)}, u32[]{:S(2)}, u32[]{:S(2)}) %collective-permute-start.27) | collective-permute-done | bytes 524320 | tf_op jit(solution)/shard_map/ppermute | solution.py:52
  (100 shorter events, 28.2 us)
Async XLA Ops:
  7.2 44.4 %copy-start.20 = (f32[5120]{0:T(1024)S(1)}, f32[5120]{0:T(1024)}, u32[]{:S(2)}) copy-start(f32[5120]{0:T(1024)} %param.20) | copy-start | bytes 61444
  7.2 49.3 %all-gather.3.cloned.1.call-start = ((), (), s32[]{:S(2)}) async-start(), calls=%async_computation | async-start | bytes 4177920 | tf_op jit(solution)/shard_map/all_gather | solution.py:311
  7.9 97.0 %all-gather.5.cloned.1.call-start = ((), (), s32[]{:S(2)}) async-start(), calls=%async_computation.1 | async-start | bytes 5570560 | tf_op jit(solution)/shard_map/all_gather | solution.py:317
  10.5 6.6 %collective-permute-start = (bf16[16,5120]{1,0:T(8,128)(2,1)S(1)}, bf16[16,5120]{1,0:T(8,128)(2,1)S(1)}, u32[]{:S(2)}, u32[]{:S(2)}) collective-permute-start(bf16[16,5120]{1,0:T(8,128)(2,1)S(1)} %shard_map.149), channel_id=1, source_target_pairs={{0,1},{1,2},{2,3},{3,0},{4,5},{5,6},{6,7},{7,4},{8,9},{9,10},{10,1... | collective-permute-start | bytes 491528 | tf_op jit(solution)/shard_map/ppermute | solution.py:52
  12.1 5.3 %collective-permute-start.1 = (bf16[16,5120]{1,0:T(8,128)(2,1)S(1)}, bf16[16,5120]{1,0:T(8,128)(2,1)S(1)}, u32[]{:S(2)}, u32[]{:S(2)}) collective-permute-start(bf16[16,5120]{1,0:T(8,128)(2,1)S(1)} %shard_map.149), channel_id=1, source_target_pairs={{0,3},{1,0},{2,1},{3,2},{4,7},{5,4},{6,5},{7,6},{8,11},{9,8},{10,9... | collective-permute-start | bytes 491528 | tf_op jit(solution)/shard_map/ppermute | solution.py:52
  13.9 6.8 %collective-permute-start.2 = (bf16[16,5120]{1,0:T(8,128)(2,1)S(1)}, bf16[16,5120]{1,0:T(8,128)(2,1)S(1)}, u32[]{:S(2)}, u32[]{:S(2)}) collective-permute-start(bf16[16,5120]{1,0:T(8,128)(2,1)S(1)} %shard_map.149), channel_id=1, source_target_pairs={{0,2},{1,3},{2,0},{3,1},{4,6},{5,7},{6,4},{7,5},{8,10},{9,11},{10,... | collective-permute-start | bytes 491528 | tf_op jit(solution)/shard_map/ppermute | solution.py:52
  20.7 26.7 %collective-permute-start.3 = (bf16[64,5120]{1,0:T(8,128)(2,1)S(1)}, bf16[64,5120]{1,0:T(8,128)(2,1)S(1)}, u32[]{:S(2)}, u32[]{:S(2)}) collective-permute-start(bf16[64,5120]{1,0:T(8,128)(2,1)S(1)} %pad_maximum_fusion.s0), channel_id=1, source_target_pairs={{0,4},{1,5},{2,6},{3,7},{4,8},{5,9},{6,10},{7,11},{8,12},{9,13},{1... | collective-permute-start | bytes 1966088 | tf_op jit(solution)/shard_map/ppermute | solution.py:52
  22.4 25.1 %collective-permute-start.4 = (bf16[64,5120]{1,0:T(8,128)(2,1)S(1)}, bf16[64,5120]{1,0:T(8,128)(2,1)S(1)}, u32[]{:S(2)}, u32[]{:S(2)}) collective-permute-start(bf16[64,5120]{1,0:T(8,128)(2,1)S(1)} %pad_maximum_fusion.s0), channel_id=1, source_target_pairs={{0,12},{1,13},{2,14},{3,15},{4,0},{5,1},{6,2},{7,3},{8,4},{9,5},{1... | collective-permute-start | bytes 1966088 | tf_op jit(solution)/shard_map/ppermute | solution.py:52
  24.1 23.5 %collective-permute-start.5 = (bf16[64,5120]{1,0:T(8,128)(2,1)S(1)}, bf16[64,5120]{1,0:T(8,128)(2,1)S(1)}, u32[]{:S(2)}, u32[]{:S(2)}) collective-permute-start(bf16[64,5120]{1,0:T(8,128)(2,1)S(1)} %pad_maximum_fusion.s0), channel_id=1, source_target_pairs={{0,8},{1,9},{2,10},{3,11},{4,12},{5,13},{6,14},{7,15},{8,0},{9,1},... | collective-permute-start | bytes 1966088 | tf_op jit(solution)/shard_map/ppermute | solution.py:52
  26.0 21.4 %collective-permute-start.11 = (bf16[320,512]{1,0:T(8,128)(2,1)}, bf16[320,512]{1,0:T(8,128)(2,1)S(1)}, u32[]{:S(2)}, u32[]{:S(2)}) collective-permute-start(bf16[320,512]{1,0:T(8,128)(2,1)} %param.21), channel_id=1, source_target_pairs={{0,0},{1,16},{2,32},{3,48},{4,4},{5,20},{6,36},{7,52},{8,8},{9,24}... | collective-permute-start | bytes 983048 | tf_op jit(solution)/shard_map/ppermute | solution.py:312
  48.2 31.9 %collective-permute-start.9 = (bf16[512,2048]{1,0:T(8,128)(2,1)}, bf16[512,2048]{1,0:T(8,128)(2,1)}, u32[]{:S(2)}, u32[]{:S(2)}) collective-permute-start(bf16[512,2048]{1,0:T(8,128)(2,1)} %w0), channel_id=1, source_target_pairs={{0,1},{1,2},{2,3},{3,0},{4,5},{5,6},{6,7},{7,4},{8,9},{9,10},{10,1... | collective-permute-start | bytes 6291464 | tf_op jit(solution)/shard_map/ppermute | solution.py:52
  48.3 34.1 %collective-permute-start.10 = (bf16[512,2048]{1,0:T(8,128)(2,1)}, bf16[512,2048]{1,0:T(8,128)(2,1)}, u32[]{:S(2)}, u32[]{:S(2)}) collective-permute-start(bf16[512,2048]{1,0:T(8,128)(2,1)} %w0), channel_id=1, source_target_pairs={{0,3},{1,0},{2,1},{3,2},{4,7},{5,4},{6,5},{7,6},{8,11},{9,8},{10,9... | collective-permute-start | bytes 6291464 | tf_op jit(solution)/shard_map/ppermute | solution.py:52
  62.2 22.6 %collective-permute-start.6 = (bf16[256,320]{1,0:T(8,128)(2,1)}, bf16[256,320]{1,0:T(8,128)(2,1)S(1)}, u32[]{:S(2)}, u32[]{:S(2)}) collective-permute-start(bf16[256,320]{1,0:T(8,128)(2,1)} %shard_map.150.h0), channel_id=1, source_target_pairs={{0,1},{1,2},{2,3},{3,0},{4,5},{5,6},{6,7},{7,4},{8,9},{9,10},{10,1... | collective-permute-start | bytes 491528 | tf_op jit(solution)/shard_map/ppermute | solution.py:60
  65.0 20.0 %collective-permute-start.7 = (bf16[256,320]{1,0:T(8,128)(2,1)}, bf16[256,320]{1,0:T(8,128)(2,1)S(1)}, u32[]{:S(2)}, u32[]{:S(2)}) collective-permute-start(bf16[256,320]{1,0:T(8,128)(2,1)} %shard_map.150.h0), channel_id=1, source_target_pairs={{0,3},{1,0},{2,1},{3,2},{4,7},{5,4},{6,5},{7,6},{8,11},{9,8},{10,9... | collective-permute-start | bytes 491528 | tf_op jit(solution)/shard_map/ppermute | solution.py:60
  65.9 19.0 %collective-permute-start.8 = (bf16[256,320]{1,0:T(8,128)(2,1)}, bf16[256,320]{1,0:T(8,128)(2,1)S(1)}, u32[]{:S(2)}, u32[]{:S(2)}) collective-permute-start(bf16[256,320]{1,0:T(8,128)(2,1)} %shard_map.150.h0), channel_id=1, source_target_pairs={{0,2},{1,3},{2,0},{3,1},{4,6},{5,7},{6,4},{7,5},{8,10},{9,11},{10,... | collective-permute-start | bytes 491528 | tf_op jit(solution)/shard_map/ppermute | solution.py:60
  84.9 26.0 %collective-permute-start.15 = (bf16[256,2048]{1,0:T(8,128)(2,1)}, bf16[256,2048]{1,0:T(8,128)(2,1)}, u32[]{:S(2)}, u32[]{:S(2)}) collective-permute-start(bf16[256,2048]{1,0:T(8,128)(2,1)} %slice.12), channel_id=1, source_target_pairs={{0,1},{1,2},{2,3},{3,0},{4,5},{5,6},{6,7},{7,4},{8,9},{9,10},{10,1... | collective-permute-start | bytes 3145736 | tf_op jit(solution)/shard_map/ppermute | solution.py:52
  85.2 25.7 %collective-permute-start.16 = (bf16[256,2048]{1,0:T(8,128)(2,1)}, bf16[256,2048]{1,0:T(8,128)(2,1)}, u32[]{:S(2)}, u32[]{:S(2)}) collective-permute-start(bf16[256,2048]{1,0:T(8,128)(2,1)} %slice.13), channel_id=1, source_target_pairs={{0,3},{1,0},{2,1},{3,2},{4,7},{5,4},{6,5},{7,6},{8,11},{9,8},{10,9... | collective-permute-start | bytes 3145736 | tf_op jit(solution)/shard_map/ppermute | solution.py:52
  88.9 16.0 %collective-permute-start.12 = (bf16[128,2048]{1,0:T(8,128)(2,1)S(1)}, bf16[128,2048]{1,0:T(8,128)(2,1)S(1)}, u32[]{:S(2)}, u32[]{:S(2)}) collective-permute-start(bf16[128,2048]{1,0:T(8,128)(2,1)S(1)} %get-tuple-element.44), channel_id=1, source_target_pairs={{0,4},{1,5},{2,6},{3,7},{4,8},{5,9},{6,10},{7,11},{8,12},{9,13},{1... | collective-permute-start | bytes 1572872 | tf_op jit(solution)/shard_map/ppermute | solution.py:52
  88.9 22.0 %collective-permute-start.13 = (bf16[128,2048]{1,0:T(8,128)(2,1)}, bf16[128,2048]{1,0:T(8,128)(2,1)S(1)}, u32[]{:S(2)}, u32[]{:S(2)}) collective-permute-start(bf16[128,2048]{1,0:T(8,128)(2,1)} %get-tuple-element.50), channel_id=1, source_target_pairs={{0,12},{1,13},{2,14},{3,15},{4,0},{5,1},{6,2},{7,3},{8,4},{9,5},{1... | collective-permute-start | bytes 1572872 | tf_op jit(solution)/shard_map/ppermute | solution.py:52
  92.1 18.8 %collective-permute-start.14 = (bf16[128,2048]{1,0:T(8,128)(2,1)S(1)}, bf16[128,2048]{1,0:T(8,128)(2,1)S(1)}, u32[]{:S(2)}, u32[]{:S(2)}) collective-permute-start(bf16[128,2048]{1,0:T(8,128)(2,1)S(1)} %get-tuple-element.51), channel_id=1, source_target_pairs={{0,8},{1,9},{2,10},{3,11},{4,12},{5,13},{6,14},{7,15},{8,0},{9,1},... | collective-permute-start | bytes 1572872 | tf_op jit(solution)/shard_map/ppermute | solution.py:52
  110.9 10.5 %collective-permute-start.17 = (bf16[256,512]{1,0:T(8,128)(2,1)}, bf16[256,512]{1,0:T(8,128)(2,1)S(1)}, u32[]{:S(2)}, u32[]{:S(2)}) collective-permute-start(bf16[256,512]{1,0:T(8,128)(2,1)} %get-tuple-element.54), channel_id=1, source_target_pairs={{0,8},{1,9},{2,10},{3,11},{4,12},{5,13},{6,14},{7,15},{8,0},{9,1},... | collective-permute-start | bytes 786440 | tf_op jit(solution)/shard_map/ppermute | solution.py:60
  111.4 12.8 %collective-permute-start.18 = (bf16[256,512]{1,0:T(8,128)(2,1)}, bf16[256,512]{1,0:T(8,128)(2,1)S(1)}, u32[]{:S(2)}, u32[]{:S(2)}) collective-permute-start(bf16[256,512]{1,0:T(8,128)(2,1)} %get-tuple-element.55), channel_id=1, source_target_pairs={{0,4},{1,5},{2,6},{3,7},{4,8},{5,9},{6,10},{7,11},{8,12},{9,13},{1... | collective-permute-start | bytes 786440 | tf_op jit(solution)/shard_map/ppermute | solution.py:60
  112.0 12.3 %collective-permute-start.19 = (bf16[256,512]{1,0:T(8,128)(2,1)}, bf16[256,512]{1,0:T(8,128)(2,1)S(1)}, u32[]{:S(2)}, u32[]{:S(2)}) collective-permute-start(bf16[256,512]{1,0:T(8,128)(2,1)} %get-tuple-element.56), channel_id=1, source_target_pairs={{0,12},{1,13},{2,14},{3,15},{4,0},{5,1},{6,2},{7,3},{8,4},{9,5},{1... | collective-permute-start | bytes 786440 | tf_op jit(solution)/shard_map/ppermute | solution.py:60
  125.4 7.7 %collective-permute-start.20 = (bf16[256,512]{1,0:T(8,128)(2,1)S(1)}, bf16[256,512]{1,0:T(8,128)(2,1)S(1)}, u32[]{:S(2)}, u32[]{:S(2)}) collective-permute-start(bf16[256,512]{1,0:T(8,128)(2,1)S(1)} %add_convert_fusion.1.v0), channel_id=1, source_target_pairs={{0,1},{1,2},{2,3},{3,0},{4,5},{5,6},{6,7},{7,4},{8,9},{9,10},{10,1... | collective-permute-start | bytes 786440 | tf_op jit(solution)/shard_map/ppermute | solution.py:52
  127.0 8.5 %collective-permute-start.21 = (bf16[256,512]{1,0:T(8,128)(2,1)S(1)}, bf16[256,512]{1,0:T(8,128)(2,1)S(1)}, u32[]{:S(2)}, u32[]{:S(2)}) collective-permute-start(bf16[256,512]{1,0:T(8,128)(2,1)S(1)} %add_convert_fusion.1.v0), channel_id=1, source_target_pairs={{0,3},{1,0},{2,1},{3,2},{4,7},{5,4},{6,5},{7,6},{8,11},{9,8},{10,9... | collective-permute-start | bytes 786440 | tf_op jit(solution)/shard_map/ppermute | solution.py:52
  128.8 8.1 %collective-permute-start.22 = (bf16[256,512]{1,0:T(8,128)(2,1)S(1)}, bf16[256,512]{1,0:T(8,128)(2,1)S(1)}, u32[]{:S(2)}, u32[]{:S(2)}) collective-permute-start(bf16[256,512]{1,0:T(8,128)(2,1)S(1)} %add_convert_fusion.1.v0), channel_id=1, source_target_pairs={{0,2},{1,3},{2,0},{3,1},{4,6},{5,7},{6,4},{7,5},{8,10},{9,11},{10,... | collective-permute-start | bytes 786440 | tf_op jit(solution)/shard_map/ppermute | solution.py:52
  139.0 16.6 %collective-permute-start.23 = (bf16[128,2048]{1,0:T(8,128)(2,1)S(1)}, bf16[128,2048]{1,0:T(8,128)(2,1)S(1)}, u32[]{:S(2)}, u32[]{:S(2)}) collective-permute-start(bf16[128,2048]{1,0:T(8,128)(2,1)S(1)} %get-tuple-element.59.e2), channel_id=1, source_target_pairs={{0,4},{1,5},{2,6},{3,7},{4,8},{5,9},{6,10},{7,11},{8,12},{9,13},{1... | collective-permute-start | bytes 1572872 | tf_op jit(solution)/shard_map/ppermute | solution.py:52
  140.4 18.2 %collective-permute-start.24 = (bf16[128,2048]{1,0:T(8,128)(2,1)S(1)}, bf16[128,2048]{1,0:T(8,128)(2,1)S(1)}, u32[]{:S(2)}, u32[]{:S(2)}) collective-permute-start(bf16[128,2048]{1,0:T(8,128)(2,1)S(1)} %get-tuple-element.60.e1), channel_id=1, source_target_pairs={{0,12},{1,13},{2,14},{3,15},{4,0},{5,1},{6,2},{7,3},{8,4},{9,5},{1... | collective-permute-start | bytes 1572872 | tf_op jit(solution)/shard_map/ppermute | solution.py:52
  142.2 16.4 %collective-permute-start.25 = (bf16[128,2048]{1,0:T(8,128)(2,1)S(1)}, bf16[128,2048]{1,0:T(8,128)(2,1)S(1)}, u32[]{:S(2)}, u32[]{:S(2)}) collective-permute-start(bf16[128,2048]{1,0:T(8,128)(2,1)S(1)} %get-tuple-element.61.e3), channel_id=1, source_target_pairs={{0,8},{1,9},{2,10},{3,11},{4,12},{5,13},{6,14},{7,15},{8,0},{9,1},... | collective-permute-start | bytes 1572872 | tf_op jit(solution)/shard_map/ppermute | solution.py:52
  152.4 11.3 %collective-permute-start.26 = (bf16[128,2048]{1,0:T(8,128)(2,1)}, bf16[128,2048]{1,0:T(8,128)(2,1)S(1)}, u32[]{:S(2)}, u32[]{:S(2)}) collective-permute-start(bf16[128,2048]{1,0:T(8,128)(2,1)} %get-tuple-element.64), channel_id=1, source_target_pairs={{0,8},{1,9},{2,10},{3,11},{4,12},{5,13},{6,14},{7,15},{8,0},{9,1},... | collective-permute-start | bytes 1572872 | tf_op jit(solution)/shard_map/ppermute | solution.py:52
  155.4 13.8 %collective-permute-start.27 = (bf16[128,2048]{1,0:T(8,128)(2,1)}, bf16[128,2048]{1,0:T(8,128)(2,1)S(1)}, u32[]{:S(2)}, u32[]{:S(2)}) collective-permute-start(bf16[128,2048]{1,0:T(8,128)(2,1)} %get-tuple-element.65), channel_id=1, source_target_pairs={{0,4},{1,5},{2,6},{3,7},{4,8},{5,9},{6,10},{7,11},{8,12},{9,13},{1... | collective-permute-start | bytes 1572872 | tf_op jit(solution)/shard_map/ppermute | solution.py:52
  155.6 13.6 %collective-permute-start.28 = (bf16[128,2048]{1,0:T(8,128)(2,1)}, bf16[128,2048]{1,0:T(8,128)(2,1)S(1)}, u32[]{:S(2)}, u32[]{:S(2)}) collective-permute-start(bf16[128,2048]{1,0:T(8,128)(2,1)} %get-tuple-element.66), channel_id=1, source_target_pairs={{0,12},{1,13},{2,14},{3,15},{4,0},{5,1},{6,2},{7,3},{8,4},{9,5},{1... | collective-permute-start | bytes 1572872 | tf_op jit(solution)/shard_map/ppermute | solution.py:52
  (23 other events, 263.7 us)
Sparse Core Ops, SparseCore 0:
  9.8 46.6 all-gather.2
  58.9 43.2 all-gather.4

commit v14 on v13

--- a/solution.py
+++ b/solution.py
@@ -227,40 +227,51 @@
     )(tab, dest, *visual, *text)
 
 
-def product_kernel(tab, e0, e1, e2, e3, gain, w0, w1, w2, w3a, w3b, own, left, right, far, scaled):
-    @pl.when(pl.program_id(0) == 0)
-    def _():
-        for j in range(4):
-            at = slice(j * 512, (j + 1) * 512)
-            scale = gain[tab[j]]
-            for i2, rows in enumerate((e0, e1, e2, e3)):
-                scaled[i2 * 128 : (i2 + 1) * 128, at] = (rows[:, at].astype(F32) * scale).astype(BF16)
-
-    total = jnp.dot(scaled[:, 0:512], w0[...], preferred_element_type=F32)
-    total = total + jnp.dot(scaled[:, 512:1024], w1[...], preferred_element_type=F32)
-    total = total + jnp.dot(scaled[:, 1024:1536], w2[...], preferred_element_type=F32)
-    total = total + jnp.dot(scaled[:, 1536:1792], w3a[...], preferred_element_type=F32)
-    total = total + jnp.dot(scaled[:, 1792:2048], w3b[...], preferred_element_type=F32)
-    own[...] = total[0:128]
-    left[...] = total[128:256].astype(BF16)
-    right[...] = total[256:384].astype(BF16)
-    far[...] = total[384:512].astype(BF16)
-
-
-def product(tab, picked, gain, weights):
-    def block(count):
-        return pl.BlockSpec((count, 512), lambda n: (0, n))
-
+def stack_kernel(w0, w1, w2, w3a, w3b, out, sems):
+    copies, row = [], 0
+    for weight in (w0, w1, w2, w3a, w3b):
+        count = weight.shape[0]
+        copies.append((weight, out.at[pl.ds(row, count)]))
+        row += count
+    for copy in start(copies, sems):
+        copy.wait()
+
+
+def stack(weights):
+    return pl.pallas_call(
+        stack_kernel,
+        out_shape=jax.ShapeDtypeStruct((2048, 2048), BF16),
+        in_specs=[ANY] * 5,
+        out_specs=VMEM,
+        scratch_shapes=[pltpu.SemaphoreType.DMA((5,))],
+        compiler_params=params(16),
+        cost_estimate=cost(0, 16 * MIB),
+    )(*weights)
+
+
+def product_kernel(tab, e0, e1, e2, e3, gain, weight, own, left, right, far, scaled):
+    for j in range(4):
+        at = slice(j * 512, (j + 1) * 512)
+        scale = gain[tab[j]]
+        for i2, rows in enumerate((e0, e1, e2, e3)):
+            scaled[i2 * 128 : (i2 + 1) * 128, at] = (rows[:, at].astype(F32) * scale).astype(BF16)
+    for n in range(4):
+        at = slice(n * 512, (n + 1) * 512)
+        total = jnp.dot(scaled[...], weight[:, at], preferred_element_type=F32)
+        for i2, out in enumerate((own, left, right, far)):
+            out[:, at] = total[i2 * 128 : (i2 + 1) * 128].astype(out.dtype)
+
+
+def product(tab, picked, gain, weight):
     return pl.pallas_call(
         product_kernel,
         out_shape=[jax.ShapeDtypeStruct((128, 2048), F32)] + [jax.ShapeDtypeStruct((128, 2048), BF16)] * 3,
-        grid=(4,),
-        in_specs=[SMEM] + [VMEM] * 5 + [block(n) for n in (512, 512, 512, 256, 256)],
-        out_specs=[block(128)] * 4,
+        in_specs=[SMEM] + [VMEM] * 6,
+        out_specs=[VMEM] * 4,
         scratch_shapes=[pltpu.VMEM((512, 2048), BF16)],
-        compiler_params=params(56),
+        compiler_params=params(28),
         cost_estimate=cost(4300 * 10**6, 14 * MIB),
-    )(tab, *picked, gain, *weights)
+    )(tab, *picked, gain, weight)
 
 
 def place_kernel(tab, e0, e1, e2, e3, out, scale, sems):
@@ -328,13 +339,14 @@
     weights = (kv_weight, kv_right, kv_left, hop(far_right, 1, 1), hop(far_left, 1, -1))
     text = (own, hop(to_right, 2, 1), hop(to_left, 2, -1), hop(to_far, 2, 2))
     own, *parts = down(nat, units, after(down_full, text[1]))
-    to_left, to_right, to_far = lax.optimization_barrier((*parts, *text[2:], *weights[3:]))[:3]
+    moved = lax.optimization_barrier((*parts, *weights[3:], *text[2:]))
+    (to_left, to_right, to_far), weights = moved[:3], stack((*weights[:3], *moved[3:5]))
     bias = lax.dynamic_slice_in_dim(down_bias, lax.axis_index("tp") * 512, 512, 0)
     total = own + bias
     for value in (line(to_far, "y", 2), line(to_right, "y", 1), line(to_left, "y", -1)):
         total = total + value.astype(F32)
     visual = total.astype(BF16)
-    visual = (visual, *around(visual, 1))
+    visual = (visual, *around(after(visual, weights), 1))
 
     live_rows = patch_counts[0, 0] // 4
     live = (jnp.arange(SLOT, dtype=jnp.int32)[None, :] < live_rows[:, None]).reshape(-1)

time: 178 us -> 191 us (1.073)
  the two profiles are of different devices: /device:TPU:32 before, /device:TPU:230 now
where the time goes in v14:
time: 191 us; the launch traced here: 190 us
  starting transfers between devices  65.7 us (34%)
  waiting for transfers between devices  60.3 us (32%)
  Pallas kernels  25.5 us (13%)
  local copies, waits for them, and re-layouts  21.8 us (11%)
  between operations  14.3 us (7%)
  other arithmetic  2.48 us (1%)
    ppermute x22, starting transfers between devices, hop(): return lax.ppermute(value, ('mb', 'tp'), HOPS[which, step])  53.8 us
    ppermute x22, waiting for transfers between devices, hop(): return lax.ppermute(value, ('mb', 'tp'), HOPS[which, step])  41.6 us
    unnamed x52, local copies, waits for them, and re-layouts  15.4 us
    ppermute x1, waiting for transfers between devices, per_device(): down_part = lax.ppermute(down_weight, ('enc', 'mb', 'tp'), SHUFFLE)  15.3 us
    ppermute x6, starting transfers between devices, line(): return lax.ppermute(value, ('mb', 'tp'), LINES[axis, step])  9.96 us
    pallas_call x1, Pallas kernels, down(): pl.pallas_call(down_kernel, out_shape=[jax.ShapeDtypeStruct((256, 512), F...  5.95 us
    pallas_call x1, Pallas kernels, up(): pl.pallas_call(up_kernel, out_shape=jax.ShapeDtypeStruct((256, 320), BF16...  5.7 us
    pallas_call x1, Pallas kernels, product(): pl.pallas_call(product_kernel, out_shape=[jax.ShapeDtypeStruct((128, 2048...  5.07 us
  transfers between devices with their start and end apart: 31, of which 13 were waited for; matrix products, arithmetic and copies ran while one was open for 3% of the time, Pallas kernels for 12%

profile of v14, /device:TPU:230, one launch (start us, length us, event | category | flops | bytes accessed | tf_op | source)
XLA Modules:
  0.0 190.1 jit_solution(10943279033125428860)
XLA Ops:
  12.0 3.2 %collective-permute-start = (bf16[16,5120]{1,0:T(8,128)(2,1)S(1)}, bf16[16,5120]{1,0:T(8,128)(2,1)S(1)}, u32[]{:S(2)}, u32[]{:S(2)}) collective-permute-start(bf16[16,5120]{1,0:T(8,128)(2,1)S(1)} %shard_map.149), channel_id=1, source_target_pairs={{0,1},{1,2},{2,3},{3,0},{4,5},{5,6},{6,7},{7,4},{8,9},{9,10},{10,1... | collective-permute-start | bytes 491528 | tf_op jit(solution)/shard_map/ppermute | solution.py:52
  15.3 2.2 %collective-permute-done.2 = bf16[16,5120]{1,0:T(8,128)(2,1)S(1)} collective-permute-done((bf16[16,5120]{1,0:T(8,128)(2,1)S(1)}, bf16[16,5120]{1,0:T(8,128)(2,1)S(1)}, u32[]{:S(2)}, u32[]{:S(2)}) %collective-permute-start.2) | collective-permute-done | bytes 163872 | tf_op jit(solution)/shard_map/ppermute | solution.py:52
  19.3 3.3 %collective-permute-start.5 = (bf16[64,5120]{1,0:T(8,128)(2,1)S(1)}, bf16[64,5120]{1,0:T(8,128)(2,1)S(1)}, u32[]{:S(2)}, u32[]{:S(2)}) collective-permute-start(bf16[64,5120]{1,0:T(8,128)(2,1)S(1)} %pad_maximum_fusion.s0), channel_id=1, source_target_pairs={{0,8},{1,9},{2,10},{3,11},{4,12},{5,13},{6,14},{7,15},{8,0},{9,1},... | collective-permute-start | bytes 1966088 | tf_op jit(solution)/shard_map/ppermute | solution.py:52
  24.6 1.9 %collective-permute-start.11 = (bf16[320,512]{1,0:T(8,128)(2,1)}, bf16[320,512]{1,0:T(8,128)(2,1)S(1)}, u32[]{:S(2)}, u32[]{:S(2)}) collective-permute-start(bf16[320,512]{1,0:T(8,128)(2,1)} %param.21), channel_id=1, source_target_pairs={{0,0},{1,16},{2,32},{3,48},{4,4},{5,20},{6,36},{7,52},{8,8},{9,24}... | collective-permute-start | bytes 983048 | tf_op jit(solution)/shard_map/ppermute | solution.py:323
  26.5 15.3 %collective-permute-done.11 = bf16[320,512]{1,0:T(8,128)(2,1)S(1)} collective-permute-done((bf16[320,512]{1,0:T(8,128)(2,1)}, bf16[320,512]{1,0:T(8,128)(2,1)S(1)}, u32[]{:S(2)}, u32[]{:S(2)}) %collective-permute-start.11) | collective-permute-done | bytes 327712 | tf_op jit(solution)/shard_map/ppermute | solution.py:323
  43.2 6.3 %collective-permute-start.9 = (bf16[512,2048]{1,0:T(8,128)(2,1)}, bf16[512,2048]{1,0:T(8,128)(2,1)}, u32[]{:S(2)}, u32[]{:S(2)}) collective-permute-start(bf16[512,2048]{1,0:T(8,128)(2,1)} %w0), channel_id=1, source_target_pairs={{0,1},{1,2},{2,3},{3,0},{4,5},{5,6},{6,7},{7,4},{8,9},{9,10},{10,1... | collective-permute-start | bytes 6291464 | tf_op jit(solution)/shard_map/ppermute | solution.py:52
  51.6 2.6 %all-gather.3.cloned.1.call-done.weight = bf16[5120,320]{1,0:T(8,128)(2,1)} async-done(((bf16[320,320]{1,0:T(8,128)(2,1)}), bf16[5120,320]{1,0:T(8,128)(2,1)}) %all-gather.3.cloned.1.call-update) | async-done | bytes 3276816 | tf_op jit(solution)/shard_map/all_gather | solution.py:322
  54.2 5.7 %shard_map.150.h0 = bf16[256,320]{1,0:T(8,128)(2,1)} custom-call(s32[16]{0:T(128)} %get-tuple-element.75.tab, bf16[64,5120]{1,0:T(8,128)(2,1)} %copy-done.13, bf16[64,5120]{1,0:T(8,128)(2,1)} %copy-done.16, bf16[64,5120]{1,0:T(8,128)(2,1)} %copy-done.15, bf16[64,5120]{1,0:T(8,128)(2,1)} %copy-done.14, bf16[5120,320]{1,0:T(8,128)(2,1)} %all-gather.3.cloned.1.call-done.weight, ...), custom_call_target="tpu_custom_call" | custom-call | flops 840000000 | bytes 6291456 | tf_op jit(solution)/shard_map/pallas_call | solution.py:153
  59.9 2.2 %collective-permute-start.8 = (bf16[256,320]{1,0:T(8,128)(2,1)}, bf16[256,320]{1,0:T(8,128)(2,1)S(1)}, u32[]{:S(2)}, u32[]{:S(2)}) collective-permute-start(bf16[256,320]{1,0:T(8,128)(2,1)} %shard_map.150.h0), channel_id=1, source_target_pairs={{0,2},{1,3},{2,0},{3,1},{4,6},{5,7},{6,4},{7,5},{8,10},{9,11},{10,... | collective-permute-start | bytes 491528 | tf_op jit(solution)/shard_map/ppermute | solution.py:60
  62.1 3.2 %collective-permute-start.6 = (bf16[256,320]{1,0:T(8,128)(2,1)}, bf16[256,320]{1,0:T(8,128)(2,1)S(1)}, u32[]{:S(2)}, u32[]{:S(2)}) collective-permute-start(bf16[256,320]{1,0:T(8,128)(2,1)} %shard_map.150.h0), channel_id=1, source_target_pairs={{0,1},{1,2},{2,3},{3,0},{4,5},{5,6},{6,7},{7,4},{8,9},{9,10},{10,1... | collective-permute-start | bytes 491528 | tf_op jit(solution)/shard_map/ppermute | solution.py:60
  65.4 2.4 %shard_map.151 = (bf16[128,2048]{1,0:T(8,128)(2,1)S(1)}, bf16[128,2048]{1,0:T(8,128)(2,1)}, bf16[128,2048]{1,0:T(8,128)(2,1)S(1)}, bf16[128,2048]{1,0:T(8,128)(2,1)}) custom-call(s32[16]{0:T(128)S(1)} %copy-done.9, bf16[128,8192]{1,0:T(8,128)(2,1)S(1)} %bitcast.20, bf16[128,8192]{1,0:T(8,128)(2,1)S(1)} %bitcast.21, bf16[128,8192]{1,0:T(8,128)(2,1)S(1)} %bitcast.22, ...), custom_call_target="tpu_custom_call" | custom-call | bytes 4194304 | tf_op jit(solution)/shard_map/pallas_call | solution.py:115
  67.8 10.1 %collective-permute-done.10.w2 = bf16[512,2048]{1,0:T(8,128)(2,1)S(1)} collective-permute-done((bf16[512,2048]{1,0:T(8,128)(2,1)}, bf16[512,2048]{1,0:T(8,128)(2,1)S(1)}, u32[]{:S(2)}, u32[]{:S(2)}) %collective-permute-start.10) | collective-permute-done | bytes 2097184 | tf_op jit(solution)/shard_map/ppermute | solution.py:52
  79.7 2.3 %slice.12 = bf16[256,2048]{1,0:T(8,128)(2,1)} slice(bf16[512,2048]{1,0:T(8,128)(2,1)} %collective-permute-done.9.w1), slice={[0:256], [0:2048]} | slice | bytes 2097152 | tf_op jit(solution)/shard_map/slice | solution.py:332
  82.8 3.7 %collective-permute-start.13 = (bf16[256,2048]{1,0:T(8,128)(2,1)}, bf16[256,2048]{1,0:T(8,128)(2,1)S(1)}, u32[]{:S(2)}, u32[]{:S(2)}) collective-permute-start(bf16[256,2048]{1,0:T(8,128)(2,1)} %slice.12), channel_id=1, source_target_pairs={{0,1},{1,2},{2,3},{3,0},{4,5},{5,6},{6,7},{7,4},{8,9},{9,10},{10,1... | collective-permute-start | bytes 3145736 | tf_op jit(solution)/shard_map/ppermute | solution.py:52
  88.3 7.6 %collective-permute-start.15 = (bf16[128,2048]{1,0:T(8,128)(2,1)}, bf16[128,2048]{1,0:T(8,128)(2,1)}, u32[]{:S(2)}, u32[]{:S(2)}) collective-permute-start(bf16[128,2048]{1,0:T(8,128)(2,1)} %get-tuple-element.55), channel_id=1, source_target_pairs={{0,12},{1,13},{2,14},{3,15},{4,0},{5,1},{6,2},{7,3},{8,4},{9,5},{1... | collective-permute-start | bytes 1572872 | tf_op jit(solution)/shard_map/ppermute | solution.py:52
  97.4 5.7 %collective-permute-done.12.refs_1_ = bf16[128,2048]{1,0:T(8,128)(2,1)S(1)} collective-permute-done((bf16[128,2048]{1,0:T(8,128)(2,1)S(1)}, bf16[128,2048]{1,0:T(8,128)(2,1)S(1)}, u32[]{:S(2)}, u32[]{:S(2)}) %collective-permute-start.12) | collective-permute-done | bytes 524320 | tf_op jit(solution)/shard_map/ppermute | solution.py:52
  103.9 6.0 %shard_map.152 = (f32[256,512]{1,0:T(8,128)}, bf16[256,512]{1,0:T(8,128)(2,1)}, bf16[256,512]{1,0:T(8,128)(2,1)}, bf16[256,512]{1,0:T(8,128)(2,1)}) custom-call(s32[16]{0:T(128)} %get-tuple-element.74.nat, bf16[256,320]{1,0:T(8,128)(2,1)} %shard_map.150.h0, bf16[256,320]{1,0:T(8,128)(2,1)} %copy-done.21, bf16[256,320]{1,0:T(8,128)(2,1)} %copy-done.20, ...), custom_call_target="tpu_custom_call" | custom-call | flops 1340000000 | bytes 8388608 | tf_op jit(solution)/shard_map/pallas_call | solution.py:189
  111.0 2.2 %collective-permute-start.18 = (bf16[256,512]{1,0:T(8,128)(2,1)}, bf16[256,512]{1,0:T(8,128)(2,1)}, u32[]{:S(2)}, u32[]{:S(2)}) collective-permute-start(bf16[256,512]{1,0:T(8,128)(2,1)} %get-tuple-element.58), channel_id=1, source_target_pairs={{0,4},{1,5},{2,6},{3,7},{4,8},{5,9},{6,10},{7,11},{8,12},{9,13},{1... | collective-permute-start | bytes 786440 | tf_op jit(solution)/shard_map/ppermute | solution.py:60
  117.2 2.1 %shard_map.153.weight = bf16[2048,2048]{1,0:T(8,128)(2,1)S(1)} custom-call(bf16[512,2048]{1,0:T(8,128)(2,1)S(1)} %copy-done.3, bf16[512,2048]{1,0:T(8,128)(2,1)} %collective-permute-done.9.w1, bf16[512,2048]{1,0:T(8,128)(2,1)S(1)} %collective-permute-done.10.w2, bf16[256,2048]{1,0:T(8,128)(2,1)S(1)} %collective-permute-done.13.w3a, ...), custom_call_target="tpu_custom_call" | custom-call | bytes 16777216 | tf_op jit(solution)/shard_map/pallas_call | solution.py:241
  119.3 3.3 %copy-done.1 = bf16[2048,2048]{1,0:T(8,128)(2,1)} copy-done((bf16[2048,2048]{1,0:T(8,128)(2,1)}, bf16[2048,2048]{1,0:T(8,128)(2,1)S(1)}, u32[]{:S(2)}) %copy-start.1) | copy-done | bytes 8388632
  125.4 10.4 %collective-permute-start.21 = (bf16[256,512]{1,0:T(8,128)(2,1)S(1)}, bf16[256,512]{1,0:T(8,128)(2,1)S(1)}, u32[]{:S(2)}, u32[]{:S(2)}) collective-permute-start(bf16[256,512]{1,0:T(8,128)(2,1)S(1)} %add_convert_fusion.1.v0), channel_id=1, source_target_pairs={{0,3},{1,0},{2,1},{3,2},{4,7},{5,4},{6,5},{7,6},{8,11},{9,8},{10,9... | collective-permute-start | bytes 786440 | tf_op jit(solution)/shard_map/ppermute | solution.py:52
  136.0 5.0 %collective-permute-done.21.v2 = bf16[256,512]{1,0:T(8,128)(2,1)S(1)} collective-permute-done((bf16[256,512]{1,0:T(8,128)(2,1)S(1)}, bf16[256,512]{1,0:T(8,128)(2,1)S(1)}, u32[]{:S(2)}, u32[]{:S(2)}) %collective-permute-start.21) | collective-permute-done | bytes 262176 | tf_op jit(solution)/shard_map/ppermute | solution.py:52
  140.9 6.9 %collective-permute-done.20.v1 = bf16[256,512]{1,0:T(8,128)(2,1)S(1)} collective-permute-done((bf16[256,512]{1,0:T(8,128)(2,1)S(1)}, bf16[256,512]{1,0:T(8,128)(2,1)S(1)}, u32[]{:S(2)}, u32[]{:S(2)}) %collective-permute-start.20) | collective-permute-done | bytes 262176 | tf_op jit(solution)/shard_map/ppermute | solution.py:52
  149.9 2.0 %shard_map.154 = (bf16[128,2048]{1,0:T(8,128)(2,1)S(1)}, bf16[128,2048]{1,0:T(8,128)(2,1)S(1)}, bf16[128,2048]{1,0:T(8,128)(2,1)S(1)}, bf16[128,2048]{1,0:T(8,128)(2,1)S(1)}) custom-call(s32[16]{0:T(128)S(1)} %copy-done.9, s32[1,256]{1,0:T(1,128)S(1)} %bitcast_select_fusion.dest, bf16[256,512]{1,0:T(8,128)(2,1)S(1)} %add_convert_fusion.1.v0, ...), custom_call_target="tpu_custom_call" | custom-call | flops 540000000 | bytes 6291456 | tf_op jit(solution)/shard_map/pallas_call | solution.py:220
  153.1 2.8 %collective-permute-start.24 = (bf16[128,2048]{1,0:T(8,128)(2,1)S(1)}, bf16[128,2048]{1,0:T(8,128)(2,1)S(1)}, u32[]{:S(2)}, u32[]{:S(2)}) collective-permute-start(bf16[128,2048]{1,0:T(8,128)(2,1)S(1)} %get-tuple-element.66.e1), channel_id=1, source_target_pairs={{0,12},{1,13},{2,14},{3,15},{4,0},{5,1},{6,2},{7,3},{8,4},{9,5},{1... | collective-permute-start | bytes 1572872 | tf_op jit(solution)/shard_map/ppermute | solution.py:52
  157.3 3.4 %copy-done.2 = bf16[2048,2048]{1,0:T(8,128)(2,1)S(1)} copy-done((bf16[2048,2048]{1,0:T(8,128)(2,1)S(1)}, bf16[2048,2048]{1,0:T(8,128)(2,1)}, u32[]{:S(2)}) %copy-start.2) | copy-done | bytes 8388632
  160.7 5.1 %shard_map.156 = (f32[128,2048]{1,0:T(8,128)S(1)}, bf16[128,2048]{1,0:T(8,128)(2,1)S(1)}, bf16[128,2048]{1,0:T(8,128)(2,1)S(1)}, bf16[128,2048]{1,0:T(8,128)(2,1)S(1)}) custom-call(s32[16]{0:T(128)S(1)} %copy-done.9, bf16[128,2048]{1,0:T(8,128)(2,1)S(1)} %get-tuple-element.64.e0, bf16[128,2048]{1,0:T(8,128)(2,1)S(1)} %get-tuple-element.66.e1, ...), custom_call_target="tpu_custom_call" | custom-call | flops 4300000256 | bytes 14680064 | tf_op jit(solution)/shard_map/pallas_call | solution.py:266
  165.8 2.2 %collective-permute-start.26 = (bf16[128,2048]{1,0:T(8,128)(2,1)S(1)}, bf16[128,2048]{1,0:T(8,128)(2,1)S(1)}, u32[]{:S(2)}, u32[]{:S(2)}) collective-permute-start(bf16[128,2048]{1,0:T(8,128)(2,1)S(1)} %get-tuple-element.70), channel_id=1, source_target_pairs={{0,8},{1,9},{2,10},{3,11},{4,12},{5,13},{6,14},{7,15},{8,0},{9,1},... | collective-permute-start | bytes 1572872 | tf_op jit(solution)/shard_map/ppermute | solution.py:52
  168.0 3.2 %collective-permute-start.28 = (bf16[128,2048]{1,0:T(8,128)(2,1)S(1)}, bf16[128,2048]{1,0:T(8,128)(2,1)S(1)}, u32[]{:S(2)}, u32[]{:S(2)}) collective-permute-start(bf16[128,2048]{1,0:T(8,128)(2,1)S(1)} %get-tuple-element.72), channel_id=1, source_target_pairs={{0,12},{1,13},{2,14},{3,15},{4,0},{5,1},{6,2},{7,3},{8,4},{9,5},{1... | collective-permute-start | bytes 1572872 | tf_op jit(solution)/shard_map/ppermute | solution.py:52
  171.2 2.6 %collective-permute-done.24.e2 = bf16[128,2048]{1,0:T(8,128)(2,1)S(1)} collective-permute-done((bf16[128,2048]{1,0:T(8,128)(2,1)S(1)}, bf16[128,2048]{1,0:T(8,128)(2,1)S(1)}, u32[]{:S(2)}, u32[]{:S(2)}) %collective-permute-start.24) | collective-permute-done | bytes 524320 | tf_op jit(solution)/shard_map/ppermute | solution.py:52
  173.9 2.0 %shard_map.155 = (bf16[128,8192]{1,0:T(8,128)(2,1)}, f32[128,128]{1,0:T(8,128)S(1)}) custom-call(s32[16]{0:T(128)S(1)} %copy-done.9, bf16[128,2048]{1,0:T(8,128)(2,1)S(1)} %get-tuple-element.64.e0, bf16[128,2048]{1,0:T(8,128)(2,1)S(1)} %collective-permute-done.23.e1, bf16[128,2048]{1,0:T(8,128)(2,1)S(1)} %collective-permute-done.24.e2, ...), custom_call_target="tpu_custom_call" | custom-call | flops 4000000 | bytes 31457280 | tf_op jit(solution)/shard_map/pallas_call | solution.py:294
  176.6 5.5 %collective-permute-done.27 = bf16[128,2048]{1,0:T(8,128)(2,1)S(1)} collective-permute-done((bf16[128,2048]{1,0:T(8,128)(2,1)S(1)}, bf16[128,2048]{1,0:T(8,128)(2,1)S(1)}, u32[]{:S(2)}, u32[]{:S(2)}) %collective-permute-start.27) | collective-permute-done | bytes 524320 | tf_op jit(solution)/shard_map/ppermute | solution.py:52
  (105 shorter events, 33.4 us)
Async XLA Ops:
  7.2 42.3 %copy-start.22 = (f32[5120]{0:T(1024)S(1)}, f32[5120]{0:T(1024)}, u32[]{:S(2)}) copy-start(f32[5120]{0:T(1024)} %param.20) | copy-start | bytes 61444
  7.2 47.0 %all-gather.3.cloned.1.call-start = ((), (), s32[]{:S(2)}) async-start(), calls=%async_computation | async-start | bytes 4177920 | tf_op jit(solution)/shard_map/all_gather | solution.py:322
  7.9 96.0 %all-gather.5.cloned.1.call-start = ((), (), s32[]{:S(2)}) async-start(), calls=%async_computation.1 | async-start | bytes 5570560 | tf_op jit(solution)/shard_map/all_gather | solution.py:328
  10.5 7.0 %collective-permute-start.2 = (bf16[16,5120]{1,0:T(8,128)(2,1)S(1)}, bf16[16,5120]{1,0:T(8,128)(2,1)S(1)}, u32[]{:S(2)}, u32[]{:S(2)}) collective-permute-start(bf16[16,5120]{1,0:T(8,128)(2,1)S(1)} %shard_map.149), channel_id=1, source_target_pairs={{0,2},{1,3},{2,0},{3,1},{4,6},{5,7},{6,4},{7,5},{8,10},{9,11},{10,... | collective-permute-start | bytes 491528 | tf_op jit(solution)/shard_map/ppermute | solution.py:52
  12.0 7.2 %collective-permute-start.1 = (bf16[16,5120]{1,0:T(8,128)(2,1)S(1)}, bf16[16,5120]{1,0:T(8,128)(2,1)S(1)}, u32[]{:S(2)}, u32[]{:S(2)}) collective-permute-start(bf16[16,5120]{1,0:T(8,128)(2,1)S(1)} %shard_map.149), channel_id=1, source_target_pairs={{0,3},{1,0},{2,1},{3,2},{4,7},{5,4},{6,5},{7,6},{8,11},{9,8},{10,9... | collective-permute-start | bytes 491528 | tf_op jit(solution)/shard_map/ppermute | solution.py:52
  12.0 7.2 %collective-permute-start = (bf16[16,5120]{1,0:T(8,128)(2,1)S(1)}, bf16[16,5120]{1,0:T(8,128)(2,1)S(1)}, u32[]{:S(2)}, u32[]{:S(2)}) collective-permute-start(bf16[16,5120]{1,0:T(8,128)(2,1)S(1)} %shard_map.149), channel_id=1, source_target_pairs={{0,1},{1,2},{2,3},{3,0},{4,5},{5,6},{6,7},{7,4},{8,9},{9,10},{10,1... | collective-permute-start | bytes 491528 | tf_op jit(solution)/shard_map/ppermute | solution.py:52
  19.3 22.6 %collective-permute-start.5 = (bf16[64,5120]{1,0:T(8,128)(2,1)S(1)}, bf16[64,5120]{1,0:T(8,128)(2,1)S(1)}, u32[]{:S(2)}, u32[]{:S(2)}) collective-permute-start(bf16[64,5120]{1,0:T(8,128)(2,1)S(1)} %pad_maximum_fusion.s0), channel_id=1, source_target_pairs={{0,8},{1,9},{2,10},{3,11},{4,12},{5,13},{6,14},{7,15},{8,0},{9,1},... | collective-permute-start | bytes 1966088 | tf_op jit(solution)/shard_map/ppermute | solution.py:52
  22.6 19.3 %collective-permute-start.4 = (bf16[64,5120]{1,0:T(8,128)(2,1)S(1)}, bf16[64,5120]{1,0:T(8,128)(2,1)S(1)}, u32[]{:S(2)}, u32[]{:S(2)}) collective-permute-start(bf16[64,5120]{1,0:T(8,128)(2,1)S(1)} %pad_maximum_fusion.s0), channel_id=1, source_target_pairs={{0,12},{1,13},{2,14},{3,15},{4,0},{5,1},{6,2},{7,3},{8,4},{9,5},{1... | collective-permute-start | bytes 1966088 | tf_op jit(solution)/shard_map/ppermute | solution.py:52
  23.6 18.2 %collective-permute-start.3 = (bf16[64,5120]{1,0:T(8,128)(2,1)S(1)}, bf16[64,5120]{1,0:T(8,128)(2,1)S(1)}, u32[]{:S(2)}, u32[]{:S(2)}) collective-permute-start(bf16[64,5120]{1,0:T(8,128)(2,1)S(1)} %pad_maximum_fusion.s0), channel_id=1, source_target_pairs={{0,4},{1,5},{2,6},{3,7},{4,8},{5,9},{6,10},{7,11},{8,12},{9,13},{1... | collective-permute-start | bytes 1966088 | tf_op jit(solution)/shard_map/ppermute | solution.py:52
  24.6 17.2 %collective-permute-start.11 = (bf16[320,512]{1,0:T(8,128)(2,1)}, bf16[320,512]{1,0:T(8,128)(2,1)S(1)}, u32[]{:S(2)}, u32[]{:S(2)}) collective-permute-start(bf16[320,512]{1,0:T(8,128)(2,1)} %param.21), channel_id=1, source_target_pairs={{0,0},{1,16},{2,32},{3,48},{4,4},{5,20},{6,36},{7,52},{8,8},{9,24}... | collective-permute-start | bytes 983048 | tf_op jit(solution)/shard_map/ppermute | solution.py:323
  43.1 34.8 %collective-permute-start.10 = (bf16[512,2048]{1,0:T(8,128)(2,1)}, bf16[512,2048]{1,0:T(8,128)(2,1)S(1)}, u32[]{:S(2)}, u32[]{:S(2)}) collective-permute-start(bf16[512,2048]{1,0:T(8,128)(2,1)} %w0), channel_id=1, source_target_pairs={{0,3},{1,0},{2,1},{3,2},{4,7},{5,4},{6,5},{7,6},{8,11},{9,8},{10,9... | collective-permute-start | bytes 6291464 | tf_op jit(solution)/shard_map/ppermute | solution.py:52
  43.2 36.5 %collective-permute-start.9 = (bf16[512,2048]{1,0:T(8,128)(2,1)}, bf16[512,2048]{1,0:T(8,128)(2,1)}, u32[]{:S(2)}, u32[]{:S(2)}) collective-permute-start(bf16[512,2048]{1,0:T(8,128)(2,1)} %w0), channel_id=1, source_target_pairs={{0,1},{1,2},{2,3},{3,0},{4,5},{5,6},{6,7},{7,4},{8,9},{9,10},{10,1... | collective-permute-start | bytes 6291464 | tf_op jit(solution)/shard_map/ppermute | solution.py:52
  59.9 22.1 %collective-permute-start.8 = (bf16[256,320]{1,0:T(8,128)(2,1)}, bf16[256,320]{1,0:T(8,128)(2,1)S(1)}, u32[]{:S(2)}, u32[]{:S(2)}) collective-permute-start(bf16[256,320]{1,0:T(8,128)(2,1)} %shard_map.150.h0), channel_id=1, source_target_pairs={{0,2},{1,3},{2,0},{3,1},{4,6},{5,7},{6,4},{7,5},{8,10},{9,11},{10,... | collective-permute-start | bytes 491528 | tf_op jit(solution)/shard_map/ppermute | solution.py:60
  62.1 19.9 %collective-permute-start.7 = (bf16[256,320]{1,0:T(8,128)(2,1)}, bf16[256,320]{1,0:T(8,128)(2,1)S(1)}, u32[]{:S(2)}, u32[]{:S(2)}) collective-permute-start(bf16[256,320]{1,0:T(8,128)(2,1)} %shard_map.150.h0), channel_id=1, source_target_pairs={{0,3},{1,0},{2,1},{3,2},{4,7},{5,4},{6,5},{7,6},{8,11},{9,8},{10,9... | collective-permute-start | bytes 491528 | tf_op jit(solution)/shard_map/ppermute | solution.py:60
  62.1 20.0 %collective-permute-start.6 = (bf16[256,320]{1,0:T(8,128)(2,1)}, bf16[256,320]{1,0:T(8,128)(2,1)S(1)}, u32[]{:S(2)}, u32[]{:S(2)}) collective-permute-start(bf16[256,320]{1,0:T(8,128)(2,1)} %shard_map.150.h0), channel_id=1, source_target_pairs={{0,1},{1,2},{2,3},{3,0},{4,5},{5,6},{6,7},{7,4},{8,9},{9,10},{10,1... | collective-permute-start | bytes 491528 | tf_op jit(solution)/shard_map/ppermute | solution.py:60
  82.8 27.5 %collective-permute-start.13 = (bf16[256,2048]{1,0:T(8,128)(2,1)}, bf16[256,2048]{1,0:T(8,128)(2,1)S(1)}, u32[]{:S(2)}, u32[]{:S(2)}) collective-permute-start(bf16[256,2048]{1,0:T(8,128)(2,1)} %slice.12), channel_id=1, source_target_pairs={{0,1},{1,2},{2,3},{3,0},{4,5},{5,6},{6,7},{7,4},{8,9},{9,10},{10,1... | collective-permute-start | bytes 3145736 | tf_op jit(solution)/shard_map/ppermute | solution.py:52
  86.5 23.8 %collective-permute-start.14 = (bf16[256,2048]{1,0:T(8,128)(2,1)}, bf16[256,2048]{1,0:T(8,128)(2,1)}, u32[]{:S(2)}, u32[]{:S(2)}) collective-permute-start(bf16[256,2048]{1,0:T(8,128)(2,1)} %slice.13), channel_id=1, source_target_pairs={{0,3},{1,0},{2,1},{3,2},{4,7},{5,4},{6,5},{7,6},{8,11},{9,8},{10,9... | collective-permute-start | bytes 3145736 | tf_op jit(solution)/shard_map/ppermute | solution.py:52
  86.5 16.5 %collective-permute-start.12 = (bf16[128,2048]{1,0:T(8,128)(2,1)S(1)}, bf16[128,2048]{1,0:T(8,128)(2,1)S(1)}, u32[]{:S(2)}, u32[]{:S(2)}) collective-permute-start(bf16[128,2048]{1,0:T(8,128)(2,1)S(1)} %get-tuple-element.47), channel_id=1, source_target_pairs={{0,4},{1,5},{2,6},{3,7},{4,8},{5,9},{6,10},{7,11},{8,12},{9,13},{1... | collective-permute-start | bytes 1572872 | tf_op jit(solution)/shard_map/ppermute | solution.py:52
  88.3 21.5 %collective-permute-start.15 = (bf16[128,2048]{1,0:T(8,128)(2,1)}, bf16[128,2048]{1,0:T(8,128)(2,1)}, u32[]{:S(2)}, u32[]{:S(2)}) collective-permute-start(bf16[128,2048]{1,0:T(8,128)(2,1)} %get-tuple-element.55), channel_id=1, source_target_pairs={{0,12},{1,13},{2,14},{3,15},{4,0},{5,1},{6,2},{7,3},{8,4},{9,5},{1... | collective-permute-start | bytes 1572872 | tf_op jit(solution)/shard_map/ppermute | solution.py:52
  95.9 14.4 %collective-permute-start.16 = (bf16[128,2048]{1,0:T(8,128)(2,1)}, bf16[128,2048]{1,0:T(8,128)(2,1)}, u32[]{:S(2)}, u32[]{:S(2)}) collective-permute-start(bf16[128,2048]{1,0:T(8,128)(2,1)} %get-tuple-element.56), channel_id=1, source_target_pairs={{0,8},{1,9},{2,10},{3,11},{4,12},{5,13},{6,14},{7,15},{8,0},{9,1},... | collective-permute-start | bytes 1572872 | tf_op jit(solution)/shard_map/ppermute | solution.py:52
  110.3 12.3 %collective-permute-start.17 = (bf16[256,512]{1,0:T(8,128)(2,1)}, bf16[256,512]{1,0:T(8,128)(2,1)S(1)}, u32[]{:S(2)}, u32[]{:S(2)}) collective-permute-start(bf16[256,512]{1,0:T(8,128)(2,1)} %get-tuple-element.57), channel_id=1, source_target_pairs={{0,8},{1,9},{2,10},{3,11},{4,12},{5,13},{6,14},{7,15},{8,0},{9,1},... | collective-permute-start | bytes 786440 | tf_op jit(solution)/shard_map/ppermute | solution.py:60
  111.0 11.6 %collective-permute-start.18 = (bf16[256,512]{1,0:T(8,128)(2,1)}, bf16[256,512]{1,0:T(8,128)(2,1)}, u32[]{:S(2)}, u32[]{:S(2)}) collective-permute-start(bf16[256,512]{1,0:T(8,128)(2,1)} %get-tuple-element.58), channel_id=1, source_target_pairs={{0,4},{1,5},{2,6},{3,7},{4,8},{5,9},{6,10},{7,11},{8,12},{9,13},{1... | collective-permute-start | bytes 786440 | tf_op jit(solution)/shard_map/ppermute | solution.py:60
  113.2 9.4 %collective-permute-start.19 = (bf16[256,512]{1,0:T(8,128)(2,1)}, bf16[256,512]{1,0:T(8,128)(2,1)}, u32[]{:S(2)}, u32[]{:S(2)}) collective-permute-start(bf16[256,512]{1,0:T(8,128)(2,1)} %get-tuple-element.59), channel_id=1, source_target_pairs={{0,12},{1,13},{2,14},{3,15},{4,0},{5,1},{6,2},{7,3},{8,4},{9,5},{1... | collective-permute-start | bytes 786440 | tf_op jit(solution)/shard_map/ppermute | solution.py:60
  123.8 12.1 %collective-permute-start.22 = (bf16[256,512]{1,0:T(8,128)(2,1)S(1)}, bf16[256,512]{1,0:T(8,128)(2,1)S(1)}, u32[]{:S(2)}, u32[]{:S(2)}) collective-permute-start(bf16[256,512]{1,0:T(8,128)(2,1)S(1)} %add_convert_fusion.1.v0), channel_id=1, source_target_pairs={{0,2},{1,3},{2,0},{3,1},{4,6},{5,7},{6,4},{7,5},{8,10},{9,11},{10,... | collective-permute-start | bytes 786440 | tf_op jit(solution)/shard_map/ppermute | solution.py:52
  125.4 15.5 %collective-permute-start.21 = (bf16[256,512]{1,0:T(8,128)(2,1)S(1)}, bf16[256,512]{1,0:T(8,128)(2,1)S(1)}, u32[]{:S(2)}, u32[]{:S(2)}) collective-permute-start(bf16[256,512]{1,0:T(8,128)(2,1)S(1)} %add_convert_fusion.1.v0), channel_id=1, source_target_pairs={{0,3},{1,0},{2,1},{3,2},{4,7},{5,4},{6,5},{7,6},{8,11},{9,8},{10,9... | collective-permute-start | bytes 786440 | tf_op jit(solution)/shard_map/ppermute | solution.py:52
  135.8 12.1 %collective-permute-start.20 = (bf16[256,512]{1,0:T(8,128)(2,1)S(1)}, bf16[256,512]{1,0:T(8,128)(2,1)S(1)}, u32[]{:S(2)}, u32[]{:S(2)}) collective-permute-start(bf16[256,512]{1,0:T(8,128)(2,1)S(1)} %add_convert_fusion.1.v0), channel_id=1, source_target_pairs={{0,1},{1,2},{2,3},{3,0},{4,5},{5,6},{6,7},{7,4},{8,9},{9,10},{10,1... | collective-permute-start | bytes 786440 | tf_op jit(solution)/shard_map/ppermute | solution.py:52
  151.9 16.1 %collective-permute-start.23 = (bf16[128,2048]{1,0:T(8,128)(2,1)S(1)}, bf16[128,2048]{1,0:T(8,128)(2,1)S(1)}, u32[]{:S(2)}, u32[]{:S(2)}) collective-permute-start(bf16[128,2048]{1,0:T(8,128)(2,1)S(1)} %get-tuple-element.65.e2), channel_id=1, source_target_pairs={{0,4},{1,5},{2,6},{3,7},{4,8},{5,9},{6,10},{7,11},{8,12},{9,13},{1... | collective-permute-start | bytes 1572872 | tf_op jit(solution)/shard_map/ppermute | solution.py:52
  153.1 20.7 %collective-permute-start.24 = (bf16[128,2048]{1,0:T(8,128)(2,1)S(1)}, bf16[128,2048]{1,0:T(8,128)(2,1)S(1)}, u32[]{:S(2)}, u32[]{:S(2)}) collective-permute-start(bf16[128,2048]{1,0:T(8,128)(2,1)S(1)} %get-tuple-element.66.e1), channel_id=1, source_target_pairs={{0,12},{1,13},{2,14},{3,15},{4,0},{5,1},{6,2},{7,3},{8,4},{9,5},{1... | collective-permute-start | bytes 1572872 | tf_op jit(solution)/shard_map/ppermute | solution.py:52
  155.9 18.0 %collective-permute-start.25 = (bf16[128,2048]{1,0:T(8,128)(2,1)S(1)}, bf16[128,2048]{1,0:T(8,128)(2,1)S(1)}, u32[]{:S(2)}, u32[]{:S(2)}) collective-permute-start(bf16[128,2048]{1,0:T(8,128)(2,1)S(1)} %get-tuple-element.67.e3), channel_id=1, source_target_pairs={{0,8},{1,9},{2,10},{3,11},{4,12},{5,13},{6,14},{7,15},{8,0},{9,1},... | collective-permute-start | bytes 1572872 | tf_op jit(solution)/shard_map/ppermute | solution.py:52
  165.8 10.9 %collective-permute-start.26 = (bf16[128,2048]{1,0:T(8,128)(2,1)S(1)}, bf16[128,2048]{1,0:T(8,128)(2,1)S(1)}, u32[]{:S(2)}, u32[]{:S(2)}) collective-permute-start(bf16[128,2048]{1,0:T(8,128)(2,1)S(1)} %get-tuple-element.70), channel_id=1, source_target_pairs={{0,8},{1,9},{2,10},{3,11},{4,12},{5,13},{6,14},{7,15},{8,0},{9,1},... | collective-permute-start | bytes 1572872 | tf_op jit(solution)/shard_map/ppermute | solution.py:52
  168.0 14.1 %collective-permute-start.27 = (bf16[128,2048]{1,0:T(8,128)(2,1)S(1)}, bf16[128,2048]{1,0:T(8,128)(2,1)S(1)}, u32[]{:S(2)}, u32[]{:S(2)}) collective-permute-start(bf16[128,2048]{1,0:T(8,128)(2,1)S(1)} %get-tuple-element.71), channel_id=1, source_target_pairs={{0,4},{1,5},{2,6},{3,7},{4,8},{5,9},{6,10},{7,11},{8,12},{9,13},{1... | collective-permute-start | bytes 1572872 | tf_op jit(solution)/shard_map/ppermute | solution.py:52
  168.0 14.1 %collective-permute-start.28 = (bf16[128,2048]{1,0:T(8,128)(2,1)S(1)}, bf16[128,2048]{1,0:T(8,128)(2,1)S(1)}, u32[]{:S(2)}, u32[]{:S(2)}) collective-permute-start(bf16[128,2048]{1,0:T(8,128)(2,1)S(1)} %get-tuple-element.72), channel_id=1, source_target_pairs={{0,12},{1,13},{2,14},{3,15},{4,0},{5,1},{6,2},{7,3},{8,4},{9,5},{1... | collective-permute-start | bytes 1572872 | tf_op jit(solution)/shard_map/ppermute | solution.py:52
  (25 other events, 231.6 us)
Sparse Core Ops, SparseCore 0:
  9.8 44.2 all-gather.2
  56.6 42.7 all-gather.4
